TPU v7x, 32 devices: a whole 2x2x4 slice. The times are simulated.
32 devices in a mesh: tile: 8 (over z, x), chan: 4 (over y, core).
Axes of the slice: x: 2, y: 2, z: 4, core: 2. Of those that a mesh axis runs over, the one named last changes fastest.
Arguments:
- inputs: bfloat16 [8, 256, 1024], P('tile', 'chan'), may hold values from -6 to 6
- grad_out: bfloat16 [8, 256, 1024], P('tile', 'chan'), may hold values from -6 to 6
- kernel: bfloat16 [25, 256], P(None, 'chan'), may hold values from -1.25 to 1.25
- w_in: bfloat16 [256, 1024], replicated, may hold values from -0.375 to 0.375
- w_out: bfloat16 [1024, 256], replicated, may hold values from -0.1875 to 0.1875
- neighbours: int32 [8, 8], replicated, may hold values from 0 to 7, as said below
- rotations: int32 [8, 8], replicated, may hold values from 0 to 3, as said below
Outputs:
- outputs: bfloat16 [8, 256, 1024], P('tile', 'chan')
- grad_in: bfloat16 [8, 256, 1024], P('tile', 'chan')
- grad_w_in: float32 [256, 1024], replicated
- grad_w_out: float32 [1024, 256], replicated
- grad_kernel: float32 [25, 256], replicated
Inputs may be any that keep to these rules, and one draw needn't show every extreme that they name: neighbours[t, d] is the tile that borders tile t in direction d; for every tile t and direction d exactly one tile s has neighbours[s, d] = t, namely s = neighbours[t, 7 - d]. rotations[t, d] is the number of quarter turns that brings the bordering tile into tile t's frame.
All inputs are finite; a program needn't handle non-finite values.
Results may differ from a plain program's by a relative error of at most 0.006.
Values may be sent and summed in bfloat16 or wider, within the bound.
No kernel may reach another device: no remote copies, remote signals or barrier semaphores. Data moves between devices by JAX's collectives and lax.ppermute only.
A program may use at most 64 MiB of HBM per device.

v0:
```python
import functools
import math

import jax
import jax.numpy as jnp
from jax import lax
from jax.experimental import pallas as pl
from jax.experimental.pallas import tpu as pltpu
from jax.sharding import PartitionSpec as P

KSIZE = 5
HALO = KSIZE // 2
LANES = 128
SIDES = (0, 2, 3, 4, 5, 7)
BF16 = jnp.bfloat16
F32 = jnp.float32

VMEM = pl.BlockSpec(memory_space=pltpu.VMEM)
SMEM = pl.BlockSpec(memory_space=pltpu.SMEM)


def call(kernel, outs, scratch=(), limit=32):
    def run(*args):
        specs = [SMEM if a.ndim == 1 and a.dtype == jnp.int32 else VMEM for a in args]
        return pl.pallas_call(
            kernel,
            out_shape=[jax.ShapeDtypeStruct(s, d) for s, d in outs],
            in_specs=specs,
            out_specs=[VMEM] * len(outs),
            scratch_shapes=list(scratch),
            compiler_params=pltpu.CompilerParams(vmem_limit_bytes=limit * 1024 * 1024),
        )(*args)

    return run


def dot(a, b):
    return lax.dot_general(a, b, (((1,), (0,)), ((), ())), preferred_element_type=F32)


def dot_nt(a, b):
    return lax.dot_general(a, b, (((1,), (1,)), ((), ())), preferred_element_type=F32)


def one_hot(index, rows):
    row = lax.broadcasted_iota(jnp.int32, (rows, index.shape[1]), 0)
    return jnp.where(row == index, 1.0, 0.0).astype(BF16)


def rim_pixels(edge):
    band_len = HALO * edge
    lane = lax.broadcasted_iota(jnp.int32, (1, 4 * band_len), 1)
    band, at = lane // band_len, lane % band_len
    side = (at // HALO) * edge + at % HALO
    pixel = jnp.where(band == 0, at, (edge - HALO) * edge + at)
    return jnp.where(band == 2, side, jnp.where(band == 3, side + edge - HALO, pixel))


def rim_lane(row, col, edge):
    band_len = HALO * edge
    side = jnp.where(col < HALO, 2 * band_len + row * HALO + col,
                     3 * band_len + row * HALO + col - (edge - HALO))
    side = jnp.where(row >= edge - HALO, band_len + (row - (edge - HALO)) * edge + col, side)
    return jnp.where(row < HALO, row * edge + col, side)


def turned_lane(row, col, quarter, edge):
    last = edge - 1
    from_row = jnp.where(quarter == 1, col, jnp.where(
        quarter == 2, last - row, jnp.where(quarter == 3, last - col, row)))
    from_col = jnp.where(quarter == 1, last - row, jnp.where(
        quarter == 2, last - col, jnp.where(quarter == 3, row, col)))
    return rim_lane(from_row, from_col, edge)


def row_halo_maps(top_turn, bottom_turn, edge):
    rim = 4 * HALO * edge
    lane = lax.broadcasted_iota(jnp.int32, (1, LANES), 1)
    up = lane - (LANES - HALO * edge)
    top = turned_lane(edge - HALO + up // edge, up % edge, top_turn, edge)
    low = turned_lane(lane // edge, lane % edge, bottom_turn, edge)
    top = jnp.where(up >= 0, top, -1)
    low = jnp.where(lane < HALO * edge, low, -1)
    return one_hot(top, rim), one_hot(low, rim)


def side_map(turns, edge):
    rim = 4 * HALO * edge
    lane = lax.broadcasted_iota(jnp.int32, (1, 2 * LANES), 1)
    row, k = lane // (2 * HALO), lane % (2 * HALO)
    above, below, right = row < HALO, row >= HALO + edge, k >= HALO
    b_row = jnp.where(above, edge - HALO + row, jnp.where(below, row - HALO - edge, row - HALO))
    b_col = jnp.where(right, k - HALO, edge - HALO + k)
    slot = jnp.where(above, 0, jnp.where(below, 4, 2)) + right.astype(jnp.int32)
    quarter = jnp.zeros_like(slot)
    for position in range(len(SIDES)):
        quarter = jnp.where(slot == position, turns[position], quarter)
    index = slot * rim + turned_lane(b_row, b_col, quarter, edge)
    index = jnp.where(row < edge + 2 * HALO, index, -1)
    return one_hot(index, len(SIDES) * rim)


def spread_map(edge, wide):
    lane = lax.broadcasted_iota(jnp.int32, (1, wide), 1)
    row = lane // edge - (LANES // edge - HALO)
    col = lane % edge
    right_row, left_row = row - 1, row + 1
    rows = edge + 2 * HALO
    right = jnp.where((right_row >= 0) & (right_row < rows), right_row * 2 * HALO + HALO + col, -1)
    left = jnp.where((left_row >= 0) & (left_row < rows),
                     left_row * 2 * HALO + col - (edge - HALO), -1)
    index = jnp.where(col < HALO, right, jnp.where(col >= edge - HALO, left, -1))
    return one_hot(index, 2 * LANES)


def side_mask(shift, shape, edge):
    col = lax.broadcasted_iota(jnp.int32, shape, 1) % edge
    return col < shift if shift > 0 else col >= edge + shift


def roll(values, shift):
    size = values.shape[1]
    return values if shift % size == 0 else pltpu.roll(values, shift % size, axis=1)


def pack_kernel(edge, x_ref, rim_ref):
    pixels = x_ref.shape[1]
    pick = one_hot(rim_pixels(edge), pixels)
    rim = dot(x_ref[...], pick).astype(BF16)
    rim_ref[...] = jnp.broadcast_to(rim[None], rim_ref.shape)


def conv_kernel(edge, place_ref, nb_ref, rot_ref, x_ref, rims_ref, taps_ref,
                hidden_ref, padded_ref, side_ref, gathered):
    channels, pixels = x_ref.shape
    wide = pixels + 2 * LANES
    rim = rims_ref.shape[2]
    first = place_ref[0] * 8
    nb = [nb_ref[first + d] for d in range(8)]
    rot = [rot_ref[first + d] for d in range(8)]
    top, low = row_halo_maps(rot[1], rot[6], edge)
    padded_ref[:, :LANES] = dot(rims_ref[nb[1]], top).astype(BF16)
    padded_ref[:, LANES + pixels:] = dot(rims_ref[nb[6]], low).astype(BF16)
    padded_ref[:, LANES:LANES + pixels] = x_ref[...]
    for position, d in enumerate(SIDES):
        gathered[:, position * rim:(position + 1) * rim] = rims_ref[nb[d]]
    packed = dot(gathered[...], side_map([rot[d] for d in SIDES], edge)).astype(BF16)
    side_ref[...] = dot(packed, spread_map(edge, wide)).astype(BF16)

    def block(i, carry):
        at = pl.multiple_of(i * 16, 16)
        xs = padded_ref[pl.ds(at, 16), :].astype(F32)
        hs = side_ref[pl.ds(at, 16), :].astype(F32)
        halves = []
        for half in (0, 8):
            x, h = xs[half:half + 8], hs[half:half + 8]
            sums = [None] * KSIZE
            for b in range(KSIZE):
                shift = b - HALO
                moved = x
                if shift:
                    moved = roll(jnp.where(side_mask(shift, x.shape, edge), h, x), -shift)
                for a in range(KSIZE):
                    tap = taps_ref[a * KSIZE + b, pl.ds(at + half, 8), :]
                    term = jnp.tile(tap, (1, wide // LANES)) * moved
                    sums[a] = term if sums[a] is None else sums[a] + term
            total = None
            for a in range(KSIZE):
                part = roll(sums[a], -(a - HALO) * edge)[:, LANES:LANES + pixels]
                total = part if total is None else total + part
            halves.append(total)
        hidden_ref[pl.ds(at, 16), :] = jnp.concatenate(halves, axis=0).astype(BF16)
        return carry

    lax.fori_loop(0, channels // 16, block, 0)


def gelu_parts(pre, grad_act):
    cumul = 0.5 * (1.0 + lax.erf(pre * 0.7071067811865476))
    slope = cumul + pre * jnp.exp(-0.5 * pre * pre) * 0.3989422804014327
    return (pre * cumul).astype(BF16), (grad_act * slope).astype(BF16)


def hidden_block(w_in_t, w_out, feats_ref, cot_ref, pre, slope, act, gpre):
    pre[...] = dot(w_in_t, feats_ref[...])
    slope[...] = dot(w_out, cot_ref[...])

    def rows(i, carry):
        at = pl.multiple_of(i * 16, 16)
        act[pl.ds(at, 16), :], gpre[pl.ds(at, 16), :] = gelu_parts(
            pre[pl.ds(at, 16), :], slope[pl.ds(at, 16), :])
        return carry

    lax.fori_loop(0, pre.shape[0] // 16, rows, 0)


def weight_kernel(place_ref, feats_ref, cot_ref, w_in_t_ref, w_out_ref, out_ref,
                  pre, slope, act, gpre):
    units = pre.shape[0]
    full = feats_ref.shape[0]
    at = pl.multiple_of(place_ref[1] * units, units)
    hidden_block(w_in_t_ref[pl.ds(at, units), :], w_out_ref[pl.ds(at, units), :],
                 feats_ref, cot_ref, pre, slope, act, gpre)
    part_in = dot_nt(feats_ref[...], gpre[...]).astype(BF16)
    part_out = dot_nt(act[...], cot_ref[...]).astype(BF16)
    used = 0
    for column in range(0, units, LANES):
        out_ref[used:used + full, :] = part_in[:, column:column + LANES]
        used += full
    for column in range(0, full, LANES):
        out_ref[used:used + units, :] = part_out[:, column:column + LANES]
        used += units
    if used < out_ref.shape[0]:
        out_ref[used:, :] = jnp.zeros((out_ref.shape[0] - used, LANES), BF16)


def point_kernel(feats_ref, cot_ref, w_in_t_ref, w_out_ref, w_in_own_ref, w_out_own_ref, x_ref,
                 out_ref, grad_ref, pre, slope, act, gpre):
    units = pre.shape[0]
    hidden = w_out_ref.shape[0]
    branch = grad = None
    for at in range(0, hidden, units):
        hidden_block(w_in_t_ref[at:at + units, :], w_out_ref[at:at + units, :],
                     feats_ref, cot_ref, pre, slope, act, gpre)
        more = dot(w_out_own_ref[:, at:at + units], act[...])
        branch = more if branch is None else branch + more
        more = dot(w_in_own_ref[:, at:at + units], gpre[...])
        grad = more if grad is None else grad + more
    out_ref[...] = (x_ref[...].astype(F32) + branch.astype(BF16).astype(F32)).astype(BF16)
    grad_ref[...] = grad.astype(BF16)


def back_kernel(edge, place_ref, nb_ref, rot_ref, grad_ref, cot_ref, padded_ref, side_ref, taps_ref,
                accum_ref, send_ref, d_row, d_side, tap_grads, gathered):
    channels, pixels = grad_ref.shape
    wide = pixels + 2 * LANES
    tiles = send_ref.shape[0]
    rim = gathered.shape[2]
    lane = lax.broadcasted_iota(jnp.int32, (8, LANES), 1)

    def block(i, carry):
        at = pl.multiple_of(i * 16, 16)
        gs = grad_ref[pl.ds(at, 16), :].astype(F32)
        xs = padded_ref[pl.ds(at, 16), :].astype(F32)
        hs = side_ref[pl.ds(at, 16), :].astype(F32)
        edges = jnp.zeros((8, LANES), F32)
        rows, sides = [], []
        for half in (0, 8):
            x, h = xs[half:half + 8], hs[half:half + 8]
            g = jnp.concatenate([edges, gs[half:half + 8], edges], axis=1)
            turned = [roll(g, (a - HALO) * edge) for a in range(KSIZE)]
            d_x = d_h = None
            sums = jnp.zeros((8, LANES), F32)
            for b in range(KSIZE):
                shift = b - HALO
                moved = x
                if shift:
                    mask = side_mask(shift, x.shape, edge)
                    moved = roll(jnp.where(mask, h, x), -shift)
                back = None
                for a in range(KSIZE):
                    tap = taps_ref[a * KSIZE + b, pl.ds(at + half, 8), :]
                    term = jnp.tile(tap, (1, wide // LANES)) * turned[a]
                    back = term if back is None else back + term
                    product = turned[a] * moved
                    line = product[:, :LANES]
                    for column in range(LANES, wide, LANES):
                        line = line + product[:, column:column + LANES]
                    sums = jnp.where(lane == a * KSIZE + b,
                                     jnp.sum(line, axis=1, keepdims=True), sums)
                back = roll(back, shift)
                if shift:
                    inside = jnp.where(mask, 0.0, back)
                    outside = jnp.where(mask, back, 0.0)
                    d_h = outside if d_h is None else d_h + outside
                    d_x = inside if d_x is None else d_x + inside
                else:
                    d_x = back if d_x is None else d_x + back
            tap_grads[pl.ds(at + half, 8), :] = sums
            rows.append(d_x)
            sides.append(d_h)
        d_x = jnp.concatenate(rows, axis=0)
        accum_ref[pl.ds(at, 16), :] = (
            d_x[:, LANES:LANES + pixels] + cot_ref[pl.ds(at, 16), :].astype(F32))
        d_row[pl.ds(at, 16), :LANES] = d_x[:, :LANES].astype(BF16)
        d_row[pl.ds(at, 16), LANES:] = d_x[:, LANES + pixels:].astype(BF16)
        d_side[pl.ds(at, 16), :] = jnp.concatenate(sides, axis=0).astype(BF16)
        return carry

    lax.fori_loop(0, channels // 16, block, 0)

    first = place_ref[0] * 8
    nb = [nb_ref[first + d] for d in range(8)]
    rot = [rot_ref[first + d] for d in range(8)]
    gathered[...] = jnp.zeros(gathered.shape, F32)
    top, low = row_halo_maps(rot[1], rot[6], edge)
    gathered[nb[1]] += dot_nt(d_row[:, :LANES], top)
    gathered[nb[6]] += dot_nt(d_row[:, LANES:], low)
    packed = dot_nt(d_side[...], spread_map(edge, wide)).astype(BF16)
    picks = side_map([rot[d] for d in SIDES], edge)
    for position, d in enumerate(SIDES):
        gathered[nb[d]] += dot_nt(packed, picks[position * rim:(position + 1) * rim, :])
    sums = split_parts(tap_grads[...])

    def store(t, carry):
        send_ref[t, :, :rim] = gathered[t].astype(BF16)
        send_ref[t, :, rim:] = sums
        return carry

    lax.fori_loop(0, tiles, store, 0)


def split_parts(values):
    high = values.astype(BF16)
    left = (values - high.astype(F32)).astype(BF16).astype(F32)
    lane = lax.broadcasted_iota(jnp.int32, values.shape, 1)
    return jnp.where(lane < LANES // 2, high.astype(F32), roll(left, LANES // 2)).astype(BF16)


def join_parts(values):
    return values + roll(values, LANES // 2)


def border_kernel(edge, recv_ref, accum_ref, grad_ref, tap_ref):
    tiles, channels, _ = recv_ref.shape
    pixels = accum_ref.shape[1]
    rim = 4 * HALO * edge
    total = lax.fori_loop(
        0, tiles, lambda t, so_far: so_far + recv_ref[t].astype(F32),
        jnp.zeros(recv_ref.shape[1:], F32))
    rims = total[:, :rim]
    high = rims.astype(BF16)
    low = (rims - high.astype(F32)).astype(BF16)
    pick = one_hot(rim_pixels(edge), pixels)
    grad_ref[...] = (accum_ref[...] + dot_nt(high, pick) + dot_nt(low, pick)).astype(BF16)
    tap_ref[...] = split_parts(join_parts(total[:, rim:]))


def sum_kernel(recv_ref, out_ref):
    total = lax.fori_loop(
        0, recv_ref.shape[0], lambda t, so_far: so_far + recv_ref[t].astype(F32),
        jnp.zeros(recv_ref.shape[1:], F32))
    out_ref[...] = jnp.broadcast_to(total.astype(BF16)[None], out_ref.shape)


def final_kernel(groups, scale, place_ref, *refs):
    pieces, taps = refs[:groups], refs[groups:2 * groups]
    g_in_ref, g_out_ref, g_tap_ref, all_taps = refs[2 * groups:]
    full, hidden = g_in_ref.shape
    units = hidden // groups
    channels = taps[0].shape[0]
    for k in range(groups):
        owner = place_ref[1] ^ k
        start = pl.multiple_of(owner * units, units)
        used = 0
        for column in range(0, units, LANES):
            g_in_ref[:, pl.ds(pl.multiple_of(start + column, LANES), LANES)] = (
                pieces[k][used:used + full, :].astype(F32) * scale)
            used += full
        for column in range(0, full, LANES):
            g_out_ref[pl.ds(start, units), column:column + LANES] = (
                pieces[k][used:used + units, :].astype(F32) * scale)
            used += units
        all_taps[pl.ds(pl.multiple_of(owner * channels, channels), channels), :] = (
            join_parts(taps[k][...].astype(F32)) * scale)
    g_tap_ref[...] = all_taps[...].T[:KSIZE * KSIZE, :]


def gather_pieces(own, groups):
    pieces = {0: own}
    bit = groups // 2
    while bit:
        swap = [(i, i ^ bit) for i in range(groups)]
        for k in list(pieces):
            pieces[k ^ bit] = lax.ppermute(pieces[k], "chan", swap)
        bit //= 2
    return [pieces[k] for k in range(groups)]


def swap_rows(values):
    return lax.all_to_all(values, "tile", 0, 0, tiled=True)


def body(inputs, grad_out, kernel, w_in, w_out, neighbours, rotations):
    channels, pixels = inputs.shape[1:]
    edge = math.isqrt(pixels)
    full, hidden = w_in.shape
    groups = lax.axis_size("chan")
    tiles = lax.axis_size("tile")
    wide = pixels + 2 * LANES
    rim = 4 * HALO * edge
    units = hidden // groups
    scale = (tiles * pixels) ** -0.5
    place = jnp.stack([lax.axis_index("tile"), lax.axis_index("chan")]).astype(jnp.int32)
    nb, rot = neighbours.reshape(-1), rotations.reshape(-1)
    x, cot = inputs[0], grad_out[0]

    [rims] = call(functools.partial(pack_kernel, edge), [((tiles, channels, rim), BF16)])(x)
    rims = swap_rows(rims)
    cots = lax.all_gather(cot, "chan", axis=0, tiled=True)
    taps = jnp.broadcast_to(kernel.astype(F32)[:, :, None], (KSIZE * KSIZE, channels, LANES))
    w_in_t = w_in.T
    start = place[1] * channels
    w_in_own = lax.dynamic_slice_in_dim(w_in, start, channels, 0)
    w_out_own = lax.dynamic_slice_in_dim(w_out, start, channels, 1).T

    hid, padded, side = call(
        functools.partial(conv_kernel, edge),
        [((channels, pixels), BF16), ((channels, wide), BF16), ((channels, wide), BF16)],
        [pltpu.VMEM((channels, len(SIDES) * rim), BF16)],
    )(place, nb, rot, x, rims, taps)
    feats = lax.all_gather(hid, "chan", axis=0, tiled=True)

    used = 2 * full * units // LANES
    share = -(-used // (16 * tiles)) * 16
    scratch = [pltpu.VMEM((units, pixels), F32), pltpu.VMEM((units, pixels), F32),
               pltpu.VMEM((units, pixels), BF16), pltpu.VMEM((units, pixels), BF16)]
    [part] = call(weight_kernel, [((tiles * share, LANES), BF16)], scratch)(
        place, feats, cots, w_in_t, w_out)
    part = swap_rows(part.reshape(tiles, share, LANES))

    outputs, grad_hid = call(
        point_kernel, [((channels, pixels), BF16)] * 2, scratch
    )(feats, cots, w_in_t, w_out, w_in_own, w_out_own, x)

    [mine] = call(sum_kernel, [((tiles, share, LANES), BF16)])(part)
    weights = swap_rows(mine).reshape(tiles * share, LANES)

    accum, border = call(
        functools.partial(back_kernel, edge),
        [((channels, pixels), F32), ((tiles, channels, rim + LANES), BF16)],
        [pltpu.VMEM((channels, 2 * LANES), BF16), pltpu.VMEM((channels, wide), BF16),
         pltpu.VMEM((channels, LANES), F32), pltpu.VMEM((tiles, channels, rim), F32)],
    )(place, nb, rot, grad_hid, cot, padded, side, taps)
    border = swap_rows(border)
    pieces = gather_pieces(weights, groups)
    grad_in, tap_part = call(
        functools.partial(border_kernel, edge),
        [((channels, pixels), BF16), ((channels, LANES), BF16)],
    )(border, accum)
    tap_pieces = gather_pieces(tap_part, groups)
    grads = call(
        functools.partial(final_kernel, groups, scale),
        [((full, hidden), F32), ((hidden, full), F32), ((KSIZE * KSIZE, full), F32)],
        [pltpu.VMEM((full, LANES), F32)],
    )(place, *pieces, *tap_pieces)
    return (outputs[None], grad_in[None], *grads)


def solution(mesh):
    return jax.shard_map(
        body,
        mesh=mesh,
        in_specs=(
            P("tile", "chan", None),
            P("tile", "chan", None),
            P(None, "chan"),
            P(),
            P(),
            P(),
            P(),
        ),
        out_specs=(P("tile", "chan", None), P("tile", "chan", None), P(), P(), P()),
        check_vma=False,
    )
```

profile of v0, /device:TPU:0, one launch (start us, length us, event | category | flops | bytes accessed | tf_op | source)
XLA Modules:
  0.0 91.9 jit_solution(15274185601069489618)
XLA Ops:
  0.6 0.9 copy-done.1
  1.5 0.9 %shard_map.110 = bf16[8,64,256]{2,1,0:T(8,128)(2,1)} custom-call(bf16[64,1024]{1,0:T(8,128)(2,1)S(1)} %bitcast.15), custom_call_target="tpu_custom_call" | custom-call | tf_op jit(solution)/shard_map/pallas_call | solution.py:25
  2.5 7.3 %all-to-all-start = ((bf16[8,64,256]{2,1,0:T(8,128)(2,1)}), bf16[8,64,256]{2,1,0:T(8,128)(2,1)S(1)}, u32[]{:S(2)}, u32[]{:S(2)}) async-start(bf16[8,64,256]{2,1,0:T(8,128)(2,1)} %shard_map.110), calls=%async_computation | async-start | bytes 524288 | tf_op jit(solution)/shard_map/all_to_all | solution.py:381
  11.5 7.3 %all-gather = bf16[1,256,1024]{2,1,0:T(8,128)(2,1)S(1)} all-gather(bf16[1,64,1024]{2,1,0:T(8,128)(2,1)S(1)} %copy-done.3), channel_id=2, replica_groups=mesh['tile'=8,'chan'=4] {'chan'}, dimensions={1}, use_global_device_ids=true | all-gather | bytes 655360 | tf_op jit(solution)/shard_map/all_gather | solution.py:400
  19.7 2.3 %shard_map.111 = (bf16[64,1024]{1,0:T(8,128)(2,1)S(1)}, bf16[64,1280]{1,0:T(8,128)(2,1)S(1)}, bf16[64,1280]{1,0:T(8,128)(2,1)S(1)}) custom-call(s32[2]{0:T(128)S(1)} %pad_add_fusion.place_ref, s32[64]{0:T(128)S(1)} %reshape.23.nb_ref, s32[64]{0:T(128)S(1)} %reshape.24.rot_ref, bf16[64,1024]{1,0:T(8,128)(2,1)S(1)} %bitcast.16, ...), custom_call_target="tpu_custom_call" | custom-call | tf_op jit(solution)/shard_map/pallas_call | solution.py:25
  22.7 7.4 %all_gather.6.feats_ref = bf16[256,1024]{1,0:T(8,128)(2,1)S(1)} all-gather(bf16[64,1024]{1,0:T(8,128)(2,1)S(1)} %get-tuple-element.17), channel_id=1, replica_groups=mesh['tile'=8,'chan'=4] {'chan'}, dimensions={0}, use_global_device_ids=true | all-gather | bytes 655360 | tf_op jit(solution)/shard_map/all_gather | solution.py:412
  30.1 2.0 %shard_map.115 = bf16[1024,128]{1,0:T(8,128)(2,1)S(1)} custom-call(s32[2]{0:T(128)S(1)} %pad_add_fusion.place_ref, bf16[256,1024]{1,0:T(8,128)(2,1)S(1)} %all_gather.6.feats_ref, bf16[256,1024]{1,0:T(8,128)(2,1)S(1)} %bitcast.11, bf16[1024,256]{1,0:T(8,128)(2,1)S(1)} %bitcast.13, bf16[1024,256]{1,0:T(8,128)(2,1)S(1)} %copy-done), custom_call_target="tpu_custom_call" | custom-call | tf_op jit(solution)/shard_map/pallas_call | solution.py:25
  32.1 15.2 %all_to_all.20.recv_ref = bf16[8,128,128]{2,1,0:T(8,128)(2,1)S(1)} all-to-all(bf16[8,128,128]{2,1,0:T(8,128)(2,1)S(1)} %bitcast.18), channel_id=1, replica_groups=mesh['tile'=8,'chan'=4] {'tile'}, dimensions={0} | all-to-all | bytes 524288 | tf_op jit(solution)/shard_map/all_to_all | solution.py:381
  47.3 0.8 shard_map.116
  48.1 3.6 %all-to-all-start.3 = ((bf16[8,128,128]{2,1,0:T(8,128)(2,1)}), bf16[8,128,128]{2,1,0:T(8,128)(2,1)S(1)}, u32[]{:S(2)}, u32[]{:S(2)}) async-start(bf16[8,128,128]{2,1,0:T(8,128)(2,1)} %shard_map.116), calls=%async_computation.3 | async-start | bytes 524288 | tf_op jit(solution)/shard_map/all_to_all | solution.py:381
  51.7 0.8 constant_dynamic-slice_fusion
  52.5 1.7 %copy.14 = bf16[1024,64]{0,1:T(8,128)(2,1)} copy(bf16[1024,64]{1,0:T(8,128)(2,1)} %constant_dynamic-slice_fusion) | data formatting | bytes 262144
  54.3 0.9 %constant_dynamic-slice_fusion.1.w_in_own_ref = bf16[64,1024]{1,0:T(8,128)(2,1)S(1)} fusion(bf16[256,1024]{1,0:T(8,128)(2,1)} %param.10, s32[]{:T(128)S(6)} %select_n.4), kind=kLoop, calls=%fused_computation.2 | loop fusion | bytes 262148 | tf_op jit(solution)/shard_map/dynamic_slice | solution.py:404
  55.2 5.5 %shard_map.112 = (bf16[64,1024]{1,0:T(8,128)(2,1)}, bf16[64,1024]{1,0:T(8,128)(2,1)S(1)}) custom-call(bf16[256,1024]{1,0:T(8,128)(2,1)S(1)} %all_gather.6.feats_ref, bf16[256,1024]{1,0:T(8,128)(2,1)S(1)} %bitcast.12, bf16[1024,256]{1,0:T(8,128)(2,1)S(1)} %bitcast.14, bf16[1024,256]{1,0:T(8,128)(2,1)S(1)} %copy-done, ...), custom_call_target="tpu_custom_call" | custom-call | tf_op jit(solution)/shard_map/pallas_call | solution.py:25
  60.8 5.6 %shard_map.113 = (f32[64,1024]{1,0:T(8,128)S(1)}, bf16[8,64,384]{2,1,0:T(8,128)(2,1)}) custom-call(s32[2]{0:T(128)S(1)} %pad_add_fusion.place_ref, s32[64]{0:T(128)S(1)} %reshape.23.nb_ref, s32[64]{0:T(128)S(1)} %reshape.24.rot_ref, bf16[64,1024]{1,0:T(8,128)(2,1)S(1)} %get-tuple-element.19.grad_ref, bf16[64,1024]{1,0:T(8,128)(2,1)S(1)} %bitcast.22, ...), custom_call_target="tpu_custom_call" | custom-call | tf_op jit(solution)/shard_map/pallas_call | solution.py:25
  66.4 6.0 %all-to-all-start.1 = ((bf16[8,64,384]{2,1,0:T(8,128)(2,1)}), bf16[8,64,384]{2,1,0:T(8,128)(2,1)S(1)}, u32[]{:S(2)}, u32[]{:S(2)}) async-start(bf16[8,64,384]{2,1,0:T(8,128)(2,1)} %get-tuple-element.22), calls=%async_computation.1 | async-start | bytes 786432 | tf_op jit(solution)/shard_map/all_to_all | solution.py:381
  72.4 0.8 collective-permute-start.1
  73.3 6.4 %collective-permute-done.1.refs_2_ = bf16[1024,128]{1,0:T(8,128)(2,1)S(1)} collective-permute-done((bf16[1024,128]{1,0:T(8,128)(2,1)S(1)}, bf16[1024,128]{1,0:T(8,128)(2,1)S(1)}, u32[]{:S(2)}, u32[]{:S(2)}) %collective-permute-start.1) | collective-permute-done | bytes 262176 | tf_op jit(solution)/shard_map/ppermute | solution.py:375
  79.7 4.0 %all-to-all-done.1.recv_ref = bf16[8,64,384]{2,1,0:T(8,128)(2,1)S(1)} async-done(((bf16[8,64,384]{2,1,0:T(8,128)(2,1)}), bf16[8,64,384]{2,1,0:T(8,128)(2,1)S(1)}, u32[]{:S(2)}, u32[]{:S(2)}) %all-to-all-start.1) | async-done | bytes 393248 | tf_op jit(solution)/shard_map/all_to_all | solution.py:381
  83.6 1.2 %shard_map.114 = (bf16[64,1024]{1,0:T(8,128)(2,1)}, bf16[64,128]{1,0:T(8,128)(2,1)S(1)}) custom-call(bf16[8,64,384]{2,1,0:T(8,128)(2,1)S(1)} %all-to-all-done.1.recv_ref, f32[64,1024]{1,0:T(8,128)S(1)} %get-tuple-element.23.accum_ref), custom_call_target="tpu_custom_call" | custom-call | tf_op jit(solution)/shard_map/pallas_call | solution.py:25
  84.9 0.8 collective-permute-start.4
  85.7 2.9 %collective-permute-done.4.refs_6_ = bf16[64,128]{1,0:T(8,128)(2,1)S(1)} collective-permute-done((bf16[64,128]{1,0:T(8,128)(2,1)S(1)}, bf16[64,128]{1,0:T(8,128)(2,1)S(1)}, u32[]{:S(2)}, u32[]{:S(2)}) %collective-permute-start.4) | collective-permute-done | bytes 16416 | tf_op jit(solution)/shard_map/ppermute | solution.py:375
  88.6 1.2 %collective-permute-done.5.refs_7_ = bf16[64,128]{1,0:T(8,128)(2,1)S(1)} collective-permute-done((bf16[64,128]{1,0:T(8,128)(2,1)S(1)}, bf16[64,128]{1,0:T(8,128)(2,1)S(1)}, u32[]{:S(2)}, u32[]{:S(2)}) %collective-permute-start.5) | collective-permute-done | bytes 16416 | tf_op jit(solution)/shard_map/ppermute | solution.py:375
  89.8 2.0 %shard_map.117 = (f32[256,1024]{1,0:T(8,128)}, f32[1024,256]{1,0:T(8,128)}, f32[25,256]{1,0:T(8,128)}) custom-call(s32[2]{0:T(128)S(1)} %pad_add_fusion.place_ref, bf16[1024,128]{1,0:T(8,128)(2,1)S(1)} %bitcast.21, bf16[1024,128]{1,0:T(8,128)(2,1)S(1)} %collective-permute-done.refs_1_, bf16[1024,128]{1,0:T(8,128)(2,1)S(1)} %collective-permute-done.1.refs_2_, ...), custom_call_target="tpu_custom_call" | custom-call | tf_op jit(solution)/shard_map/pallas_call | solution.py:25
  (39 shorter events, 3.3 us)
Async XLA Ops:
  0.6 0.9 copy-start.1
  1.5 9.0 %copy-start.9 = (bf16[256,1024]{1,0:T(8,128)(2,1)S(1)}, bf16[256,1024]{1,0:T(8,128)(2,1)}, u32[]{:S(2)}) copy-start(bf16[256,1024]{1,0:T(8,128)(2,1)} %param.10) | copy-start | bytes 1572868
  2.5 16.3 %all-to-all-start = ((bf16[8,64,256]{2,1,0:T(8,128)(2,1)}), bf16[8,64,256]{2,1,0:T(8,128)(2,1)S(1)}, u32[]{:S(2)}, u32[]{:S(2)}) async-start(bf16[8,64,256]{2,1,0:T(8,128)(2,1)} %shard_map.110), calls=%async_computation | async-start | bytes 524288 | tf_op jit(solution)/shard_map/all_to_all | solution.py:381
  9.7 0.7 copy-start.11
  9.7 0.8 copy-start.12
  10.6 0.9 copy-start.3
  11.5 7.3 %copy-start.10 = (bf16[25,64]{1,0:T(8,128)(2,1)S(1)}, bf16[25,64]{1,0:T(8,128)(2,1)}, u32[]{:S(2)}) copy-start(bf16[25,64]{1,0:T(8,128)(2,1)} %param.9) | copy-start | bytes 9604
  18.8 0.9 copy-start.2
  22.0 0.7 copy-start.7
  22.7 7.4 %copy-start.5 = (bf16[64,1280]{1,0:T(8,128)(2,1)}, bf16[64,1280]{1,0:T(8,128)(2,1)S(1)}, u32[]{:S(2)}) copy-start(bf16[64,1280]{1,0:T(8,128)(2,1)S(1)} %get-tuple-element.20.padded_ref) | copy-start | bytes 491524
  22.7 7.4 %copy-start = (bf16[1024,256]{1,0:T(8,128)(2,1)S(1)}, bf16[1024,256]{1,0:T(8,128)(2,1)}, u32[]{:S(2)}) copy-start(bf16[1024,256]{1,0:T(8,128)(2,1)} %w_out_ref.3) | copy-start | bytes 1572868
  48.1 18.3 %all-to-all-start.3 = ((bf16[8,128,128]{2,1,0:T(8,128)(2,1)}), bf16[8,128,128]{2,1,0:T(8,128)(2,1)S(1)}, u32[]{:S(2)}, u32[]{:S(2)}) async-start(bf16[8,128,128]{2,1,0:T(8,128)(2,1)} %shard_map.116), calls=%async_computation.3 | async-start | bytes 524288 | tf_op jit(solution)/shard_map/all_to_all | solution.py:381
  54.3 1.0 %copy-start.4 = (bf16[1024,64]{0,1:T(8,128)(2,1)S(1)}, bf16[1024,64]{0,1:T(8,128)(2,1)}, u32[]{:S(2)}) copy-start(bf16[1024,64]{0,1:T(8,128)(2,1)} %copy.14) | copy-start | bytes 393220
  55.2 5.5 %copy-start.6 = (bf16[64,1280]{1,0:T(8,128)(2,1)S(1)}, bf16[64,1280]{1,0:T(8,128)(2,1)}, u32[]{:S(2)}) copy-start(bf16[64,1280]{1,0:T(8,128)(2,1)} %copy-done.5) | copy-start | bytes 491524
  55.2 5.5 %copy-start.8 = (bf16[64,1280]{1,0:T(8,128)(2,1)S(1)}, bf16[64,1280]{1,0:T(8,128)(2,1)}, u32[]{:S(2)}) copy-start(bf16[64,1280]{1,0:T(8,128)(2,1)} %copy-done.7) | copy-start | bytes 491524
  66.4 17.2 %all-to-all-start.1 = ((bf16[8,64,384]{2,1,0:T(8,128)(2,1)}), bf16[8,64,384]{2,1,0:T(8,128)(2,1)S(1)}, u32[]{:S(2)}, u32[]{:S(2)}) async-start(bf16[8,64,384]{2,1,0:T(8,128)(2,1)} %get-tuple-element.22), calls=%async_computation.1 | async-start | bytes 786432 | tf_op jit(solution)/shard_map/all_to_all | solution.py:381
  72.4 7.3 %collective-permute-start.1 = (bf16[1024,128]{1,0:T(8,128)(2,1)S(1)}, bf16[1024,128]{1,0:T(8,128)(2,1)S(1)}, u32[]{:S(2)}, u32[]{:S(2)}) collective-permute-start(bf16[1024,128]{1,0:T(8,128)(2,1)S(1)} %bitcast.19), channel_id=1, source_target_pairs={{0,2},{1,3},{2,0},{3,1},{4,6},{5,7},{6,4},{7,5},{8,10},{9,11},{10,... | collective-permute-start | bytes 786440 | tf_op jit(solution)/shard_map/ppermute | solution.py:375
  73.2 16.6 %collective-permute-start = (bf16[1024,128]{1,0:T(8,128)(2,1)S(1)}, bf16[1024,128]{1,0:T(8,128)(2,1)S(1)}, u32[]{:S(2)}, u32[]{:S(2)}) collective-permute-start(bf16[1024,128]{1,0:T(8,128)(2,1)S(1)} %bitcast.20), channel_id=1, source_target_pairs={{0,1},{1,0},{2,3},{3,2},{4,5},{5,4},{6,7},{7,6},{8,9},{9,8},{10,11... | collective-permute-start | bytes 786440 | tf_op jit(solution)/shard_map/ppermute | solution.py:375
  79.7 10.1 %collective-permute-start.2 = (bf16[1024,128]{1,0:T(8,128)(2,1)S(1)}, bf16[1024,128]{1,0:T(8,128)(2,1)S(1)}, u32[]{:S(2)}, u32[]{:S(2)}) collective-permute-start(bf16[1024,128]{1,0:T(8,128)(2,1)S(1)} %collective-permute-done.1.refs_2_), channel_id=1, source_target_pairs={{0,1},{1,0},{2,3},{3,2},{4,5},{5,4},{6,7},{7,6},{8,9},{9,8},{10,11... | collective-permute-start | bytes 786440 | tf_op jit(solution)/shard_map/ppermute | solution.py:375
  84.9 3.7 %collective-permute-start.4 = (bf16[64,128]{1,0:T(8,128)(2,1)S(1)}, bf16[64,128]{1,0:T(8,128)(2,1)S(1)}, u32[]{:S(2)}, u32[]{:S(2)}) collective-permute-start(bf16[64,128]{1,0:T(8,128)(2,1)S(1)} %get-tuple-element.25.refs_4_), channel_id=1, source_target_pairs={{0,2},{1,3},{2,0},{3,1},{4,6},{5,7},{6,4},{7,5},{8,10},{9,11},{10,... | collective-permute-start | bytes 49160 | tf_op jit(solution)/shard_map/ppermute | solution.py:375
  85.7 2.9 %collective-permute-start.3 = (bf16[64,128]{1,0:T(8,128)(2,1)S(1)}, bf16[64,128]{1,0:T(8,128)(2,1)S(1)}, u32[]{:S(2)}, u32[]{:S(2)}) collective-permute-start(bf16[64,128]{1,0:T(8,128)(2,1)S(1)} %get-tuple-element.25.refs_4_), channel_id=1, source_target_pairs={{0,1},{1,0},{2,3},{3,2},{4,5},{5,4},{6,7},{7,6},{8,9},{9,8},{10,11... | collective-permute-start | bytes 49160 | tf_op jit(solution)/shard_map/ppermute | solution.py:375
  88.6 1.2 %collective-permute-start.5 = (bf16[64,128]{1,0:T(8,128)(2,1)S(1)}, bf16[64,128]{1,0:T(8,128)(2,1)S(1)}, u32[]{:S(2)}, u32[]{:S(2)}) collective-permute-start(bf16[64,128]{1,0:T(8,128)(2,1)S(1)} %collective-permute-done.4.refs_6_), channel_id=1, source_target_pairs={{0,1},{1,0},{2,3},{3,2},{4,5},{5,4},{6,7},{7,6},{8,9},{9,8},{10,11... | collective-permute-start | bytes 49160 | tf_op jit(solution)/shard_map/ppermute | solution.py:375
where the time goes:
time: 92.5 us; the launch traced here: 91.9 us
  blocking collectives  29.9 us (32%)
  Pallas kernels  20.4 us (22%)
  starting transfers between devices  18.5 us (20%)
  waiting for transfers between devices  14.5 us (16%)
  local copies, waits for them, and re-layouts  7.66 us (8%)
    pallas_call x8, Pallas kernels, run(): pl.pallas_call(kernel, out_shape=[jax.ShapeDtypeStruct(s, d) for s, d in...  20.4 us
    all_to_all x3, starting transfers between devices, swap_rows(): return lax.all_to_all(values, 'tile', 0, 0, tiled=True)  16.8 us
    all_to_all x1, blocking collectives, swap_rows(): return lax.all_to_all(values, 'tile', 0, 0, tiled=True)  15.2 us
    ppermute x6, waiting for transfers between devices, gather_pieces(): pieces[k ^ bit] = lax.ppermute(pieces[k], 'chan', swap)  10.5 us
    all_gather x1, blocking collectives, body(): feats = lax.all_gather(hid, 'chan', axis=0, tiled=True)  7.41 us
    all_gather x1, blocking collectives, body(): cots = lax.all_gather(cot, 'chan', axis=0, tiled=True)  7.32 us
    unnamed x28, local copies, waits for them, and re-layouts  5.44 us
    all_to_all x3, waiting for transfers between devices, swap_rows(): return lax.all_to_all(values, 'tile', 0, 0, tiled=True)  3.96 us
  transfers between devices with their start and end apart: 9, of which 4 were waited for; matrix products, arithmetic and copies ran while one was open for 4% of the time, Pallas kernels for 13%

commit v1 on v0

--- a/solution.py
+++ b/solution.py
@@ -19,7 +19,7 @@
 SMEM = pl.BlockSpec(memory_space=pltpu.SMEM)
 
 
-def call(kernel, outs, scratch=(), limit=32):
+def call(kernel, outs, scratch=(), limit=16):
     def run(*args):
         specs = [SMEM if a.ndim == 1 and a.dtype == jnp.int32 else VMEM for a in args]
         return pl.pallas_call(
@@ -194,8 +194,8 @@
     lax.fori_loop(0, pre.shape[0] // 16, rows, 0)
 
 
-def weight_kernel(place_ref, feats_ref, cot_ref, w_in_t_ref, w_out_ref, out_ref,
-                  pre, slope, act, gpre):
+def weight_kernel(place_ref, feats_ref, cot_ref, w_in_t_ref, w_out_ref, out_ref, act, gpre,
+                  pre, slope):
     units = pre.shape[0]
     full = feats_ref.shape[0]
     at = pl.multiple_of(place_ref[1] * units, units)
@@ -214,80 +214,114 @@
         out_ref[used:, :] = jnp.zeros((out_ref.shape[0] - used, LANES), BF16)
 
 
-def point_kernel(feats_ref, cot_ref, w_in_t_ref, w_out_ref, w_in_own_ref, w_out_own_ref, x_ref,
-                 out_ref, grad_ref, pre, slope, act, gpre):
+def point_kernel(groups, place_ref, feats_ref, cot_ref, w_in_t_ref, w_out_ref, w_in_own_ref,
+                 w_out_own_ref, act_own, gpre_own, x_ref, out_ref, grad_ref,
+                 pre, slope, act, gpre):
     units = pre.shape[0]
-    hidden = w_out_ref.shape[0]
-    branch = grad = None
-    for at in range(0, hidden, units):
-        hidden_block(w_in_t_ref[at:at + units, :], w_out_ref[at:at + units, :],
+
+    def start(k):
+        return pl.multiple_of((place_ref[1] ^ k) * units, units)
+
+    mine = pl.ds(start(0), units)
+    branch = dot(w_out_own_ref[:, mine], act_own[...])
+    grad = dot(w_in_own_ref[:, mine], gpre_own[...])
+    for k in range(1, groups):
+        part = pl.ds(start(k), units)
+        hidden_block(w_in_t_ref[part, :], w_out_ref[part, :],
                      feats_ref, cot_ref, pre, slope, act, gpre)
-        more = dot(w_out_own_ref[:, at:at + units], act[...])
-        branch = more if branch is None else branch + more
-        more = dot(w_in_own_ref[:, at:at + units], gpre[...])
-        grad = more if grad is None else grad + more
+        branch = branch + dot(w_out_own_ref[:, part], act[...])
+        grad = grad + dot(w_in_own_ref[:, part], gpre[...])
     out_ref[...] = (x_ref[...].astype(F32) + branch.astype(BF16).astype(F32)).astype(BF16)
     grad_ref[...] = grad.astype(BF16)
 
 
+def prep_kernel(place_ref, w_in_ref, w_out_ref, w_in_t_ref, w_in_own_ref, w_out_own_ref):
+    channels = w_in_own_ref.shape[0]
+    start = place_ref[1] * channels
+    w_in_t_ref[...] = w_in_ref[...].astype(F32).T.astype(BF16)
+    w_in_own_ref[...] = w_in_ref[pl.ds(pl.multiple_of(start, channels), channels), :]
+    row = lax.broadcasted_iota(jnp.int32, (channels, w_out_ref.shape[1]), 0)
+    column = lax.broadcasted_iota(jnp.int32, (channels, w_out_ref.shape[1]), 1)
+    pick = jnp.where(column == row + start, 1.0, 0.0).astype(BF16)
+    w_out_own_ref[...] = dot_nt(pick, w_out_ref[...]).astype(BF16)
+
+
+def join_kernel(place_ref, *refs):
+    pieces, out_ref = refs[:-1], refs[-1]
+    channels = pieces[0].shape[0]
+    for k, piece in enumerate(pieces):
+        start = pl.multiple_of((place_ref[1] ^ k) * channels, channels)
+        out_ref[pl.ds(start, channels), :] = piece[...]
+
+
 def back_kernel(edge, place_ref, nb_ref, rot_ref, grad_ref, cot_ref, padded_ref, side_ref, taps_ref,
-                accum_ref, send_ref, d_row, d_side, tap_grads, gathered):
+                accum_ref, send_ref, tap_ref, d_row, d_side, turned_all, moved_all, gathered):
     channels, pixels = grad_ref.shape
     wide = pixels + 2 * LANES
-    tiles = send_ref.shape[0]
-    rim = gathered.shape[2]
-    lane = lax.broadcasted_iota(jnp.int32, (8, LANES), 1)
-
-    def block(i, carry):
-        at = pl.multiple_of(i * 16, 16)
-        gs = grad_ref[pl.ds(at, 16), :].astype(F32)
-        xs = padded_ref[pl.ds(at, 16), :].astype(F32)
-        hs = side_ref[pl.ds(at, 16), :].astype(F32)
-        edges = jnp.zeros((8, LANES), F32)
+    tiles, _, rim = send_ref.shape
+    slots = tap_ref.shape[0]
+    moved_all[KSIZE * 16:, :] = jnp.zeros((LANES - KSIZE * 16, wide), BF16)
+    tap_ref[...] = jnp.zeros(tap_ref.shape, BF16)
+    same = (lax.broadcasted_iota(jnp.int32, (16, KSIZE * LANES), 1) % 16
+            == lax.broadcasted_iota(jnp.int32, (16, KSIZE * LANES), 0))
+    line = lax.broadcasted_iota(jnp.int32, (KSIZE * LANES, LANES), 0)
+    tap = lax.broadcasted_iota(jnp.int32, (KSIZE * LANES, LANES), 1)
+    used = line % LANES < KSIZE * 16
+    pick = jnp.where(used & (line // LANES * KSIZE + line % LANES // 16 == tap), 1.0, 0.0).astype(BF16)
+
+    for block in range(channels // 16):
+        at = block * 16
+        gs = grad_ref[at:at + 16, :].astype(F32)
+        xs = padded_ref[at:at + 16, :].astype(F32)
+        hs = side_ref[at:at + 16, :].astype(F32)
+        zeros = jnp.zeros((8, LANES), F32)
+        turned_rows, moved_rows = [[] for _ in range(KSIZE)], [[] for _ in range(KSIZE)]
         rows, sides = [], []
         for half in (0, 8):
             x, h = xs[half:half + 8], hs[half:half + 8]
-            g = jnp.concatenate([edges, gs[half:half + 8], edges], axis=1)
+            g = jnp.concatenate([zeros, gs[half:half + 8], zeros], axis=1)
             turned = [roll(g, (a - HALO) * edge) for a in range(KSIZE)]
             d_x = d_h = None
-            sums = jnp.zeros((8, LANES), F32)
             for b in range(KSIZE):
                 shift = b - HALO
-                moved = x
+                back = None
+                for a in range(KSIZE):
+                    weight = taps_ref[a * KSIZE + b, at + half:at + half + 8, :]
+                    term = jnp.tile(weight, (1, wide // LANES)) * turned[a]
+                    back = term if back is None else back + term
+                back = roll(back, shift)
                 if shift:
                     mask = side_mask(shift, x.shape, edge)
-                    moved = roll(jnp.where(mask, h, x), -shift)
-                back = None
-                for a in range(KSIZE):
-                    tap = taps_ref[a * KSIZE + b, pl.ds(at + half, 8), :]
-                    term = jnp.tile(tap, (1, wide // LANES)) * turned[a]
-                    back = term if back is None else back + term
-                    product = turned[a] * moved
-                    line = product[:, :LANES]
-                    for column in range(LANES, wide, LANES):
-                        line = line + product[:, column:column + LANES]
-                    sums = jnp.where(lane == a * KSIZE + b,
-                                     jnp.sum(line, axis=1, keepdims=True), sums)
-                back = roll(back, shift)
-                if shift:
+                    moved_rows[b].append(roll(jnp.where(mask, h, x), -shift))
                     inside = jnp.where(mask, 0.0, back)
                     outside = jnp.where(mask, back, 0.0)
                     d_h = outside if d_h is None else d_h + outside
                     d_x = inside if d_x is None else d_x + inside
                 else:
+                    moved_rows[b].append(x)
                     d_x = back if d_x is None else d_x + back
-            tap_grads[pl.ds(at + half, 8), :] = sums
+            for a in range(KSIZE):
+                turned_rows[a].append(turned[a])
             rows.append(d_x)
             sides.append(d_h)
         d_x = jnp.concatenate(rows, axis=0)
-        accum_ref[pl.ds(at, 16), :] = (
-            d_x[:, LANES:LANES + pixels] + cot_ref[pl.ds(at, 16), :].astype(F32))
-        d_row[pl.ds(at, 16), :LANES] = d_x[:, :LANES].astype(BF16)
-        d_row[pl.ds(at, 16), LANES:] = d_x[:, LANES + pixels:].astype(BF16)
-        d_side[pl.ds(at, 16), :] = jnp.concatenate(sides, axis=0).astype(BF16)
-        return carry
-
-    lax.fori_loop(0, channels // 16, block, 0)
+        accum_ref[at:at + 16, :] = (
+            d_x[:, LANES:LANES + pixels] + cot_ref[at:at + 16, :].astype(F32))
+        d_row[at:at + 16, :LANES] = d_x[:, :LANES].astype(BF16)
+        d_row[at:at + 16, LANES:] = d_x[:, LANES + pixels:].astype(BF16)
+        d_side[at:at + 16, :] = jnp.concatenate(sides, axis=0).astype(BF16)
+        for a in range(KSIZE):
+            turned_all[a * 16:a * 16 + 16, :] = jnp.concatenate(turned_rows[a], axis=0).astype(BF16)
+            moved_all[a * 16:a * 16 + 16, :] = jnp.concatenate(moved_rows[a], axis=0).astype(BF16)
+        products = dot_nt(turned_all[...], moved_all[...])
+        side_by_side = jnp.concatenate(
+            [products[a * 16:a * 16 + 16, :] for a in range(KSIZE)], axis=1)
+        found = dot(jnp.where(same, side_by_side, 0.0).astype(BF16), pick)
+        lane = lax.broadcasted_iota(jnp.int32, (16, LANES), 1)
+        place = block % 4
+        placed = jnp.where(lane // 32 == place, roll(found, 32 * place), 0.0)
+        slot = slice(block // 4 * 16, block // 4 * 16 + 16)
+        tap_ref[slot, :] = (tap_ref[slot, :].astype(F32) + placed).astype(BF16)
 
     first = place_ref[0] * 8
     nb = [nb_ref[first + d] for d in range(8)]
@@ -300,70 +334,78 @@
     picks = side_map([rot[d] for d in SIDES], edge)
     for position, d in enumerate(SIDES):
         gathered[nb[d]] += dot_nt(packed, picks[position * rim:(position + 1) * rim, :])
-    sums = split_parts(tap_grads[...])
 
     def store(t, carry):
-        send_ref[t, :, :rim] = gathered[t].astype(BF16)
-        send_ref[t, :, rim:] = sums
+        send_ref[t] = gathered[t].astype(BF16)
         return carry
 
     lax.fori_loop(0, tiles, store, 0)
 
 
-def split_parts(values):
-    high = values.astype(BF16)
-    left = (values - high.astype(F32)).astype(BF16).astype(F32)
-    lane = lax.broadcasted_iota(jnp.int32, values.shape, 1)
-    return jnp.where(lane < LANES // 2, high.astype(F32), roll(left, LANES // 2)).astype(BF16)
-
-
-def join_parts(values):
-    return values + roll(values, LANES // 2)
-
-
-def border_kernel(edge, recv_ref, accum_ref, grad_ref, tap_ref):
-    tiles, channels, _ = recv_ref.shape
+def border_kernel(edge, recv_ref, accum_ref, grad_ref):
     pixels = accum_ref.shape[1]
-    rim = 4 * HALO * edge
-    total = lax.fori_loop(
-        0, tiles, lambda t, so_far: so_far + recv_ref[t].astype(F32),
-        jnp.zeros(recv_ref.shape[1:], F32))
-    rims = total[:, :rim]
+    rims = total_of(recv_ref)
     high = rims.astype(BF16)
     low = (rims - high.astype(F32)).astype(BF16)
     pick = one_hot(rim_pixels(edge), pixels)
     grad_ref[...] = (accum_ref[...] + dot_nt(high, pick) + dot_nt(low, pick)).astype(BF16)
-    tap_ref[...] = split_parts(join_parts(total[:, rim:]))
-
-
-def sum_kernel(recv_ref, out_ref):
-    total = lax.fori_loop(
-        0, recv_ref.shape[0], lambda t, so_far: so_far + recv_ref[t].astype(F32),
-        jnp.zeros(recv_ref.shape[1:], F32))
-    out_ref[...] = jnp.broadcast_to(total.astype(BF16)[None], out_ref.shape)
-
-
-def final_kernel(groups, scale, place_ref, *refs):
-    pieces, taps = refs[:groups], refs[groups:2 * groups]
-    g_in_ref, g_out_ref, g_tap_ref, all_taps = refs[2 * groups:]
+
+
+def total_of(ref):
+    return lax.fori_loop(1, ref.shape[0], lambda t, so_far: so_far + ref[t].astype(F32),
+                         ref[0].astype(F32))
+
+
+def sum_kernel(recv_ref, tap_ref, out_ref):
+    share = recv_ref.shape[1]
+    total = total_of(recv_ref).astype(BF16)
+
+    def store(t, carry):
+        out_ref[t, :share, :] = total
+        out_ref[t, share:, :] = tap_ref[...]
+        return carry
+
+    lax.fori_loop(0, out_ref.shape[0], store, 0)
+
+
+def final_kernel(groups, share, channels, scale, place_ref, *refs):
+    pieces = refs[:groups]
+    g_in_ref, g_out_ref, g_tap_ref, all_taps = refs[groups:]
     full, hidden = g_in_ref.shape
     units = hidden // groups
-    channels = taps[0].shape[0]
+    tiles, rows, _ = pieces[0].shape
     for k in range(groups):
         owner = place_ref[1] ^ k
         start = pl.multiple_of(owner * units, units)
-        used = 0
-        for column in range(0, units, LANES):
-            g_in_ref[:, pl.ds(pl.multiple_of(start + column, LANES), LANES)] = (
-                pieces[k][used:used + full, :].astype(F32) * scale)
-            used += full
-        for column in range(0, full, LANES):
-            g_out_ref[pl.ds(start, units), column:column + LANES] = (
-                pieces[k][used:used + units, :].astype(F32) * scale)
-            used += units
-        all_taps[pl.ds(pl.multiple_of(owner * channels, channels), channels), :] = (
-            join_parts(taps[k][...].astype(F32)) * scale)
+        for tile in range(tiles):
+            for row, count, column, at, into_in in chunks(tile, share, units, full):
+                values = pieces[k][tile, row:row + count, :].astype(F32) * scale
+                if into_in:
+                    g_in_ref[at:at + count, pl.ds(pl.multiple_of(start + column, LANES), LANES)] = values
+                else:
+                    g_out_ref[pl.ds(pl.multiple_of(start + at, 16), count), column:column + LANES] = values
+        taps = pieces[k][0, share:, :].astype(F32)
+        for tile in range(1, tiles):
+            taps = taps + pieces[k][tile, share:, :].astype(F32)
+        taps = taps * scale
+        for block in range(channels // 16):
+            values = taps[block // 4 * 16:block // 4 * 16 + 16, :]
+            into = pl.ds(pl.multiple_of(owner * channels + block * 16, 16), 16)
+            all_taps[into, :] = roll(values, -32 * (block % 4))
     g_tap_ref[...] = all_taps[...].T[:KSIZE * KSIZE, :]
+
+
+def chunks(tile, share, units, full):
+    inside, found = units // LANES * full, []
+    row, end = tile * share, min((tile + 1) * share, 2 * units * full // LANES)
+    while row < end:
+        height = full if row < inside else units
+        offset = row if row < inside else row - inside
+        column, at = offset // height * LANES, offset % height
+        count = min(end - row, height - at)
+        found.append((row - tile * share, count, column, at, row < inside))
+        row += count
+    return found
 
 
 def gather_pieces(own, groups):
@@ -396,13 +438,16 @@
     x, cot = inputs[0], grad_out[0]
 
     [rims] = call(functools.partial(pack_kernel, edge), [((tiles, channels, rim), BF16)])(x)
+    rims, kernel, w_in, w_out = lax.optimization_barrier((rims, kernel, w_in, w_out))
     rims = swap_rows(rims)
-    cots = lax.all_gather(cot, "chan", axis=0, tiled=True)
+    cot_pieces = gather_pieces(cot, groups)
     taps = jnp.broadcast_to(kernel.astype(F32)[:, :, None], (KSIZE * KSIZE, channels, LANES))
-    w_in_t = w_in.T
-    start = place[1] * channels
-    w_in_own = lax.dynamic_slice_in_dim(w_in, start, channels, 0)
-    w_out_own = lax.dynamic_slice_in_dim(w_out, start, channels, 1).T
+    w_in_t, w_in_own, w_out_own = call(
+        prep_kernel, [((hidden, full), BF16)] + [((channels, hidden), BF16)] * 2
+    )(place, w_in, w_out)
+    [cots] = call(join_kernel, [((full, pixels), BF16)])(place, *cot_pieces)
+    rims, cots, taps, w_in_t, w_in_own, w_out_own = lax.optimization_barrier(
+        (rims, cots, taps, w_in_t, w_in_own, w_out_own))
 
     hid, padded, side = call(
         functools.partial(conv_kernel, edge),
@@ -413,37 +458,37 @@
 
     used = 2 * full * units // LANES
     share = -(-used // (16 * tiles)) * 16
-    scratch = [pltpu.VMEM((units, pixels), F32), pltpu.VMEM((units, pixels), F32),
-               pltpu.VMEM((units, pixels), BF16), pltpu.VMEM((units, pixels), BF16)]
-    [part] = call(weight_kernel, [((tiles * share, LANES), BF16)], scratch)(
+    tap_rows = -(-channels // 64) * 16
+    values = [pltpu.VMEM((units, pixels), F32)] * 2
+    rounded = [((units, pixels), BF16)] * 2
+    part, act, gpre = call(weight_kernel, [((tiles * share, LANES), BF16)] + rounded, values)(
         place, feats, cots, w_in_t, w_out)
     part = swap_rows(part.reshape(tiles, share, LANES))
 
     outputs, grad_hid = call(
-        point_kernel, [((channels, pixels), BF16)] * 2, scratch
-    )(feats, cots, w_in_t, w_out, w_in_own, w_out_own, x)
-
-    [mine] = call(sum_kernel, [((tiles, share, LANES), BF16)])(part)
-    weights = swap_rows(mine).reshape(tiles * share, LANES)
-
-    accum, border = call(
+        functools.partial(point_kernel, groups), [((channels, pixels), BF16)] * 2,
+        values + [pltpu.VMEM(s, d) for s, d in rounded],
+    )(place, feats, cots, w_in_t, w_out, w_in_own, w_out_own, act, gpre, x)
+    accum, border, tap_part = call(
         functools.partial(back_kernel, edge),
-        [((channels, pixels), F32), ((tiles, channels, rim + LANES), BF16)],
+        [((channels, pixels), F32), ((tiles, channels, rim), BF16), ((tap_rows, LANES), BF16)],
         [pltpu.VMEM((channels, 2 * LANES), BF16), pltpu.VMEM((channels, wide), BF16),
-         pltpu.VMEM((channels, LANES), F32), pltpu.VMEM((tiles, channels, rim), F32)],
+         pltpu.VMEM((KSIZE * 16, wide), BF16), pltpu.VMEM((LANES, wide), BF16),
+         pltpu.VMEM((tiles, channels, rim), F32)],
     )(place, nb, rot, grad_hid, cot, padded, side, taps)
+
+    [mine] = call(sum_kernel, [((tiles, share + tap_rows, LANES), BF16)])(part, tap_part)
+    mine, border = lax.optimization_barrier((mine, border))
+    weights = swap_rows(mine)
     border = swap_rows(border)
     pieces = gather_pieces(weights, groups)
-    grad_in, tap_part = call(
-        functools.partial(border_kernel, edge),
-        [((channels, pixels), BF16), ((channels, LANES), BF16)],
-    )(border, accum)
-    tap_pieces = gather_pieces(tap_part, groups)
+    [grad_in] = call(
+        functools.partial(border_kernel, edge), [((channels, pixels), BF16)])(border, accum)
     grads = call(
-        functools.partial(final_kernel, groups, scale),
+        functools.partial(final_kernel, groups, share, channels, scale),
         [((full, hidden), F32), ((hidden, full), F32), ((KSIZE * KSIZE, full), F32)],
         [pltpu.VMEM((full, LANES), F32)],
-    )(place, *pieces, *tap_pieces)
+    )(place, *pieces)
     return (outputs[None], grad_in[None], *grads)
 
 

time: 92.5 us -> 88.3 us (0.955)
  blocking collectives: 29.9 us -> 23.5 us
  local copies, waits for them, and re-layouts: 7.66 us -> 12.7 us
  waiting for transfers between devices: 14.5 us -> 11.5 us
  starting transfers between devices: 18.5 us -> 19.9 us
  Pallas kernels: 20.4 us -> 19.1 us
    all_gather x1 -> x0, blocking collectives: 7.32 us -> none  [body(): cots = lax.all_gather(cot, 'chan', axis=0, tiled=True)]
    unnamed x28 -> x42, local copies, waits for them, and re-layouts: 5.44 us -> 12.2 us
    ppermute x6, waiting for transfers between devices: 10.5 us -> 5.16 us  [gather_pieces(): pieces[k ^ bit] = lax.ppermute(pieces[k], 'chan', swap)]
    all_to_all x3, waiting for transfers between devices: 3.96 us -> 6.38 us  [swap_rows(): return lax.all_to_all(values, 'tile', 0, 0, tiled=True)]
    dynamic_slice x2 -> x0, local copies, waits for them, and re-layouts: 1.79 us -> none  [the longest x1 0.95 us: body(): w_in_own = lax.dynamic_slice_in_dim(w_in, start, channels, 0)]
    ppermute x6, starting transfers between devices: 1.68 us -> 3.18 us  [gather_pieces(): pieces[k ^ bit] = lax.ppermute(pieces[k], 'chan', swap)]
    pallas_call x8 -> x10, Pallas kernels: 20.4 us -> 19.1 us  [run(): pl.pallas_call(kernel, out_shape=[jax.ShapeDtypeStruct(s, d) for s, d in...]
  transfers between devices with their start and end apart: 9 -> 9, of which waited for: 4 -> 3; matrix products, arithmetic and copies ran while one was open for 4% -> 0% of each run, Pallas kernels for 13% -> 13%
where the time goes in v1:
time: 88.3 us; the launch traced here: 87.6 us
  blocking collectives  23.5 us (27%)
  starting transfers between devices  19.9 us (23%)
  Pallas kernels  19.1 us (22%)
  local copies, waits for them, and re-layouts  12.7 us (14%)
  waiting for transfers between devices  11.5 us (13%)
    pallas_call x10, Pallas kernels, run(): pl.pallas_call(kernel, out_shape=[jax.ShapeDtypeStruct(s, d) for s, d in...  19.1 us
    all_to_all x3, starting transfers between devices, swap_rows(): return lax.all_to_all(values, 'tile', 0, 0, tiled=True)  16.7 us
    all_to_all x1, blocking collectives, swap_rows(): return lax.all_to_all(values, 'tile', 0, 0, tiled=True)  16.1 us
    unnamed x42, local copies, waits for them, and re-layouts  12.2 us
    all_gather x1, blocking collectives, body(): feats = lax.all_gather(hid, 'chan', axis=0, tiled=True)  7.44 us
    all_to_all x3, waiting for transfers between devices, swap_rows(): return lax.all_to_all(values, 'tile', 0, 0, tiled=True)  6.38 us
    ppermute x6, waiting for transfers between devices, gather_pieces(): pieces[k ^ bit] = lax.ppermute(pieces[k], 'chan', swap)  5.16 us
    ppermute x6, starting transfers between devices, gather_pieces(): pieces[k ^ bit] = lax.ppermute(pieces[k], 'chan', swap)  3.18 us
  transfers between devices with their start and end apart: 9, of which 3 were waited for; matrix products, arithmetic and copies ran while one was open for 0% of the time, Pallas kernels for 13%

profile of v1, /device:TPU:0, one launch (start us, length us, event | category | flops | bytes accessed | tf_op | source)
XLA Modules:
  0.0 87.6 jit_solution(15808118063189895018)
XLA Ops:
  0.7 1.0 %copy-done.1 = bf16[1,64,1024]{2,1,0:T(8,128)(2,1)S(1)} copy-done((bf16[1,64,1024]{2,1,0:T(8,128)(2,1)S(1)}, bf16[1,64,1024]{2,1,0:T(8,128)(2,1)}, u32[]{:S(2)}) %copy-start.1) | copy-done | bytes 131096
  1.6 0.9 %shard_map.110 = bf16[8,64,256]{2,1,0:T(8,128)(2,1)} custom-call(bf16[64,1024]{1,0:T(8,128)(2,1)S(1)} %bitcast.7), custom_call_target="tpu_custom_call" | custom-call | tf_op jit(solution)/shard_map/pallas_call | solution.py:25
  2.5 7.4 %all-to-all-start = ((bf16[8,64,256]{2,1,0:T(8,128)(2,1)}), bf16[8,64,256]{2,1,0:T(8,128)(2,1)S(1)}, u32[]{:S(2)}, u32[]{:S(2)}) async-start(bf16[8,64,256]{2,1,0:T(8,128)(2,1)} %shard_map.110), calls=%async_computation | async-start | bytes 524288 | tf_op jit(solution)/shard_map/all_to_all | solution.py:423
  9.9 1.6 %collective-permute-start.1 = (bf16[64,1024]{1,0:T(8,128)(2,1)S(1)}, bf16[64,1024]{1,0:T(8,128)(2,1)S(1)}, u32[]{:S(2)}, u32[]{:S(2)}) collective-permute-start(bf16[64,1024]{1,0:T(8,128)(2,1)S(1)} %bitcast.10), channel_id=1, source_target_pairs={{0,2},{1,3},{2,0},{3,1},{4,6},{5,7},{6,4},{7,5},{8,10},{9,11},{10,... | collective-permute-start | bytes 393224 | tf_op jit(solution)/shard_map/ppermute | solution.py:417
  11.5 3.4 %collective-permute-done.1.refs_2_ = bf16[64,1024]{1,0:T(8,128)(2,1)S(1)} collective-permute-done((bf16[64,1024]{1,0:T(8,128)(2,1)S(1)}, bf16[64,1024]{1,0:T(8,128)(2,1)S(1)}, u32[]{:S(2)}, u32[]{:S(2)}) %collective-permute-start.1) | collective-permute-done | bytes 131104 | tf_op jit(solution)/shard_map/ppermute | solution.py:417
  15.9 1.0 %copy-done.3 = bf16[256,1024]{1,0:T(8,128)(2,1)S(1)} copy-done((bf16[256,1024]{1,0:T(8,128)(2,1)S(1)}, bf16[256,1024]{1,0:T(8,128)(2,1)}, u32[]{:S(2)}) %copy-start.3) | copy-done | bytes 524312
  16.9 0.8 shard_map.112
  20.7 2.3 %shard_map.113 = (bf16[64,1024]{1,0:T(8,128)(2,1)S(1)}, bf16[64,1280]{1,0:T(8,128)(2,1)S(1)}, bf16[64,1280]{1,0:T(8,128)(2,1)S(1)}) custom-call(s32[2]{0:T(128)S(1)} %pad_add_fusion.place_ref, s32[64]{0:T(128)S(1)} %reshape.20.nb_ref, s32[64]{0:T(128)S(1)} %reshape.21.rot_ref, bf16[64,1024]{1,0:T(8,128)(2,1)S(1)} %bitcast.8, ...), custom_call_target="tpu_custom_call" | custom-call | tf_op jit(solution)/shard_map/pallas_call | solution.py:25
  24.3 7.4 %all_gather.3.feats_ref = bf16[256,1024]{1,0:T(8,128)(2,1)S(1)} all-gather(bf16[64,1024]{1,0:T(8,128)(2,1)S(1)} %get-tuple-element.43), channel_id=1, replica_groups=mesh['tile'=8,'chan'=4] {'chan'}, dimensions={0}, use_global_device_ids=true | all-gather | bytes 655360 | tf_op jit(solution)/shard_map/all_gather | solution.py:457
  31.7 2.0 %shard_map.114 = (bf16[1024,128]{1,0:T(8,128)(2,1)S(1)}, bf16[256,1024]{1,0:T(8,128)(2,1)S(1)}, bf16[256,1024]{1,0:T(8,128)(2,1)S(1)}) custom-call(s32[2]{0:T(128)S(1)} %pad_add_fusion.place_ref, bf16[256,1024]{1,0:T(8,128)(2,1)S(1)} %all_gather.3.feats_ref, bf16[256,1024]{1,0:T(8,128)(2,1)S(1)} %shard_map.111.cot_ref, ...), custom_call_target="tpu_custom_call" | custom-call | tf_op jit(solution)/shard_map/pallas_call | solution.py:25
  36.0 5.9 %all-to-all-start.1 = ((bf16[8,128,128]{2,1,0:T(8,128)(2,1)}), bf16[8,128,128]{2,1,0:T(8,128)(2,1)S(1)}, u32[]{:S(2)}, u32[]{:S(2)}) async-start(bf16[8,128,128]{2,1,0:T(8,128)(2,1)} %bitcast.14), calls=%async_computation.1 | async-start | bytes 524288 | tf_op jit(solution)/shard_map/all_to_all | solution.py:423
  42.0 1.0 %copy-done.6 = bf16[256,1024]{1,0:T(8,128)(2,1)S(1)} copy-done((bf16[256,1024]{1,0:T(8,128)(2,1)S(1)}, bf16[256,1024]{1,0:T(8,128)(2,1)}, u32[]{:S(2)}) %copy-start.6) | copy-done | bytes 524312
  43.0 1.0 %copy-done.8 = bf16[256,1024]{1,0:T(8,128)(2,1)S(1)} copy-done((bf16[256,1024]{1,0:T(8,128)(2,1)S(1)}, bf16[256,1024]{1,0:T(8,128)(2,1)}, u32[]{:S(2)}) %copy-start.8) | copy-done | bytes 524312
  44.0 0.9 %copy-done.15 = bf16[64,1024]{1,0:T(8,128)(2,1)S(1)} copy-done((bf16[64,1024]{1,0:T(8,128)(2,1)S(1)}, bf16[64,1024]{1,0:T(8,128)(2,1)}, u32[]{:S(2)}) %copy-start.15) | copy-done | bytes 131096
  45.0 0.9 %copy-done.17 = bf16[64,1024]{1,0:T(8,128)(2,1)S(1)} copy-done((bf16[64,1024]{1,0:T(8,128)(2,1)S(1)}, bf16[64,1024]{1,0:T(8,128)(2,1)}, u32[]{:S(2)}) %copy-start.17) | copy-done | bytes 131096
  45.9 5.1 %shard_map.115 = (bf16[64,1024]{1,0:T(8,128)(2,1)}, bf16[64,1024]{1,0:T(8,128)(2,1)S(1)}) custom-call(s32[2]{0:T(128)S(1)} %pad_add_fusion.place_ref, bf16[256,1024]{1,0:T(8,128)(2,1)S(1)} %all_gather.3.feats_ref, bf16[256,1024]{1,0:T(8,128)(2,1)S(1)} %shard_map.111.cot_ref, bf16[1024,256]{1,0:T(8,128)(2,1)S(1)} %get-tuple-element.45.w_in_t_ref, ...), custom_call_target="tpu_custom_call" | custom-call | tf_op jit(solution)/shard_map/pallas_call | solution.py:25
  50.9 4.1 %shard_map.116 = (f32[64,1024]{1,0:T(8,128)S(1)}, bf16[8,64,256]{2,1,0:T(8,128)(2,1)}, bf16[16,128]{1,0:T(8,128)(2,1)S(1)}) custom-call(s32[2]{0:T(128)S(1)} %pad_add_fusion.place_ref, s32[64]{0:T(128)S(1)} %reshape.20.nb_ref, s32[64]{0:T(128)S(1)} %reshape.21.rot_ref, bf16[64,1024]{1,0:T(8,128)(2,1)S(1)} %get-tuple-element.52.grad_ref, ...), custom_call_target="tpu_custom_call" | custom-call | tf_op jit(solution)/shard_map/pallas_call | solution.py:25
  55.1 16.1 %all_to_all.20.refs_0_ = bf16[8,144,128]{2,1,0:T(8,128)(2,1)S(1)} all-to-all(bf16[8,144,128]{2,1,0:T(8,128)(2,1)S(1)} %shard_map.117), channel_id=1, replica_groups=mesh['tile'=8,'chan'=4] {'tile'}, dimensions={0} | all-to-all | bytes 589824 | tf_op jit(solution)/shard_map/all_to_all | solution.py:423
  71.2 1.5 %collective-permute-start.4 = (bf16[8,144,128]{2,1,0:T(8,128)(2,1)S(1)}, bf16[8,144,128]{2,1,0:T(8,128)(2,1)S(1)}, u32[]{:S(2)}, u32[]{:S(2)}) collective-permute-start(bf16[8,144,128]{2,1,0:T(8,128)(2,1)S(1)} %all_to_all.20.refs_0_), channel_id=1, source_target_pairs={{0,2},{1,3},{2,0},{3,1},{4,6},{5,7},{6,4},{7,5},{8,10},{9,11},{10,... | collective-permute-start | bytes 884744 | tf_op jit(solution)/shard_map/ppermute | solution.py:417
  72.7 3.4 %all-to-all-start.2 = ((bf16[8,64,256]{2,1,0:T(8,128)(2,1)}), bf16[8,64,256]{2,1,0:T(8,128)(2,1)S(1)}, u32[]{:S(2)}, u32[]{:S(2)}) async-start(bf16[8,64,256]{2,1,0:T(8,128)(2,1)} %get-tuple-element.57), calls=%async_computation.2 | async-start | bytes 524288 | tf_op jit(solution)/shard_map/all_to_all | solution.py:423
  76.2 1.7 %collective-permute-done.4.refs_2_ = bf16[8,144,128]{2,1,0:T(8,128)(2,1)S(1)} collective-permute-done((bf16[8,144,128]{2,1,0:T(8,128)(2,1)S(1)}, bf16[8,144,128]{2,1,0:T(8,128)(2,1)S(1)}, u32[]{:S(2)}, u32[]{:S(2)}) %collective-permute-start.4) | collective-permute-done | bytes 294944 | tf_op jit(solution)/shard_map/ppermute | solution.py:417
  77.9 6.4 %all-to-all-done.2.recv_ref = bf16[8,64,256]{2,1,0:T(8,128)(2,1)S(1)} async-done(((bf16[8,64,256]{2,1,0:T(8,128)(2,1)}), bf16[8,64,256]{2,1,0:T(8,128)(2,1)S(1)}, u32[]{:S(2)}, u32[]{:S(2)}) %all-to-all-start.2) | async-done | bytes 262176 | tf_op jit(solution)/shard_map/all_to_all | solution.py:423
  84.3 1.2 %shard_map.118 = bf16[64,1024]{1,0:T(8,128)(2,1)} custom-call(bf16[8,64,256]{2,1,0:T(8,128)(2,1)S(1)} %all-to-all-done.2.recv_ref, f32[64,1024]{1,0:T(8,128)S(1)} %get-tuple-element.58.accum_ref), custom_call_target="tpu_custom_call" | custom-call | tf_op jit(solution)/shard_map/pallas_call | solution.py:25
  85.5 2.1 %shard_map.119 = (f32[256,1024]{1,0:T(8,128)}, f32[1024,256]{1,0:T(8,128)}, f32[25,256]{1,0:T(8,128)}) custom-call(s32[2]{0:T(128)S(1)} %pad_add_fusion.place_ref, bf16[8,144,128]{2,1,0:T(8,128)(2,1)S(1)} %all_to_all.20.refs_0_, bf16[8,144,128]{2,1,0:T(8,128)(2,1)S(1)} %collective-permute-done.3.refs_1_, ...), custom_call_target="tpu_custom_call" | custom-call | tf_op jit(solution)/shard_map/pallas_call | solution.py:25
  (52 shorter events, 7.6 us)
Async XLA Ops:
  0.6 15.3 %copy-start = (bf16[1024,256]{1,0:T(8,128)(2,1)S(1)}, bf16[1024,256]{1,0:T(8,128)(2,1)}, u32[]{:S(2)}) copy-start(bf16[1024,256]{1,0:T(8,128)(2,1)} %w_out_ref.2) | copy-start | bytes 1572868
  0.6 1.0 %copy-start.1 = (bf16[1,64,1024]{2,1,0:T(8,128)(2,1)S(1)}, bf16[1,64,1024]{2,1,0:T(8,128)(2,1)}, u32[]{:S(2)}) copy-start(bf16[1,64,1024]{2,1,0:T(8,128)(2,1)} %param.7) | copy-start | bytes 393220
  2.5 7.4 %copy-start.4 = (bf16[1,64,1024]{2,1,0:T(8,128)(2,1)S(1)}, bf16[1,64,1024]{2,1,0:T(8,128)(2,1)}, u32[]{:S(2)}) copy-start(bf16[1,64,1024]{2,1,0:T(8,128)(2,1)} %param.8) | copy-start | bytes 393220
  2.5 17.1 %all-to-all-start = ((bf16[8,64,256]{2,1,0:T(8,128)(2,1)}), bf16[8,64,256]{2,1,0:T(8,128)(2,1)S(1)}, u32[]{:S(2)}, u32[]{:S(2)}) async-start(bf16[8,64,256]{2,1,0:T(8,128)(2,1)} %shard_map.110), calls=%async_computation | async-start | bytes 524288 | tf_op jit(solution)/shard_map/all_to_all | solution.py:423
  9.9 5.0 %collective-permute-start.1 = (bf16[64,1024]{1,0:T(8,128)(2,1)S(1)}, bf16[64,1024]{1,0:T(8,128)(2,1)S(1)}, u32[]{:S(2)}, u32[]{:S(2)}) collective-permute-start(bf16[64,1024]{1,0:T(8,128)(2,1)S(1)} %bitcast.10), channel_id=1, source_target_pairs={{0,2},{1,3},{2,0},{3,1},{4,6},{5,7},{6,4},{7,5},{8,10},{9,11},{10,... | collective-permute-start | bytes 393224 | tf_op jit(solution)/shard_map/ppermute | solution.py:417
  11.5 7.6 %collective-permute-start = (bf16[64,1024]{1,0:T(8,128)(2,1)S(1)}, bf16[64,1024]{1,0:T(8,128)(2,1)S(1)}, u32[]{:S(2)}, u32[]{:S(2)}) collective-permute-start(bf16[64,1024]{1,0:T(8,128)(2,1)S(1)} %bitcast.11), channel_id=1, source_target_pairs={{0,1},{1,0},{2,3},{3,2},{4,5},{5,4},{6,7},{7,6},{8,9},{9,8},{10,11... | collective-permute-start | bytes 393224 | tf_op jit(solution)/shard_map/ppermute | solution.py:417
  15.0 4.1 %collective-permute-start.2 = (bf16[64,1024]{1,0:T(8,128)(2,1)S(1)}, bf16[64,1024]{1,0:T(8,128)(2,1)S(1)}, u32[]{:S(2)}, u32[]{:S(2)}) collective-permute-start(bf16[64,1024]{1,0:T(8,128)(2,1)S(1)} %collective-permute-done.1.refs_2_), channel_id=1, source_target_pairs={{0,1},{1,0},{2,3},{3,2},{4,5},{5,4},{6,7},{7,6},{8,9},{9,8},{10,11... | collective-permute-start | bytes 393224 | tf_op jit(solution)/shard_map/ppermute | solution.py:417
  15.0 0.8 copy-start.20
  15.9 1.0 %copy-start.3 = (bf16[256,1024]{1,0:T(8,128)(2,1)S(1)}, bf16[256,1024]{1,0:T(8,128)(2,1)}, u32[]{:S(2)}) copy-start(bf16[256,1024]{1,0:T(8,128)(2,1)} %w_in_ref) | copy-start | bytes 1572868
  19.8 0.9 %copy-start.2 = (bf16[1,64,1024]{2,1,0:T(8,128)(2,1)S(1)}, bf16[1,64,1024]{2,1,0:T(8,128)(2,1)}, u32[]{:S(2)}) copy-start(bf16[1,64,1024]{2,1,0:T(8,128)(2,1)} %param.7) | copy-start | bytes 393220
  33.7 0.8 copy-start.5
  34.5 0.8 copy-start.7
  35.3 0.7 copy-start.9
  36.0 19.0 %all-to-all-start.1 = ((bf16[8,128,128]{2,1,0:T(8,128)(2,1)}), bf16[8,128,128]{2,1,0:T(8,128)(2,1)S(1)}, u32[]{:S(2)}, u32[]{:S(2)}) async-start(bf16[8,128,128]{2,1,0:T(8,128)(2,1)} %bitcast.14), calls=%async_computation.1 | async-start | bytes 524288 | tf_op jit(solution)/shard_map/all_to_all | solution.py:423
  42.0 1.0 %copy-start.6 = (bf16[256,1024]{1,0:T(8,128)(2,1)S(1)}, bf16[256,1024]{1,0:T(8,128)(2,1)}, u32[]{:S(2)}) copy-start(bf16[256,1024]{1,0:T(8,128)(2,1)} %copy-done.5) | copy-start | bytes 1572868
  43.0 1.0 %copy-start.8 = (bf16[256,1024]{1,0:T(8,128)(2,1)S(1)}, bf16[256,1024]{1,0:T(8,128)(2,1)}, u32[]{:S(2)}) copy-start(bf16[256,1024]{1,0:T(8,128)(2,1)} %copy-done.7) | copy-start | bytes 1572868
  44.0 0.9 %copy-start.15 = (bf16[64,1024]{1,0:T(8,128)(2,1)S(1)}, bf16[64,1024]{1,0:T(8,128)(2,1)}, u32[]{:S(2)}) copy-start(bf16[64,1024]{1,0:T(8,128)(2,1)} %copy-done.14) | copy-start | bytes 393220
  44.9 0.9 %copy-start.17 = (bf16[64,1024]{1,0:T(8,128)(2,1)S(1)}, bf16[64,1024]{1,0:T(8,128)(2,1)}, u32[]{:S(2)}) copy-start(bf16[64,1024]{1,0:T(8,128)(2,1)} %copy-done.16) | copy-start | bytes 393220
  45.9 5.1 %copy-start.11 = (bf16[64,1280]{1,0:T(8,128)(2,1)S(1)}, bf16[64,1280]{1,0:T(8,128)(2,1)}, u32[]{:S(2)}) copy-start(bf16[64,1280]{1,0:T(8,128)(2,1)} %copy-done.10) | copy-start | bytes 491524
  45.9 5.1 %copy-start.13 = (bf16[64,1280]{1,0:T(8,128)(2,1)S(1)}, bf16[64,1280]{1,0:T(8,128)(2,1)}, u32[]{:S(2)}) copy-start(bf16[64,1280]{1,0:T(8,128)(2,1)} %copy-done.12) | copy-start | bytes 491524
  71.2 6.7 %collective-permute-start.4 = (bf16[8,144,128]{2,1,0:T(8,128)(2,1)S(1)}, bf16[8,144,128]{2,1,0:T(8,128)(2,1)S(1)}, u32[]{:S(2)}, u32[]{:S(2)}) collective-permute-start(bf16[8,144,128]{2,1,0:T(8,128)(2,1)S(1)} %all_to_all.20.refs_0_), channel_id=1, source_target_pairs={{0,2},{1,3},{2,0},{3,1},{4,6},{5,7},{6,4},{7,5},{8,10},{9,11},{10,... | collective-permute-start | bytes 884744 | tf_op jit(solution)/shard_map/ppermute | solution.py:417
  72.7 11.6 %all-to-all-start.2 = ((bf16[8,64,256]{2,1,0:T(8,128)(2,1)}), bf16[8,64,256]{2,1,0:T(8,128)(2,1)S(1)}, u32[]{:S(2)}, u32[]{:S(2)}) async-start(bf16[8,64,256]{2,1,0:T(8,128)(2,1)} %get-tuple-element.57), calls=%async_computation.2 | async-start | bytes 524288 | tf_op jit(solution)/shard_map/all_to_all | solution.py:423
  76.2 9.4 %collective-permute-start.3 = (bf16[8,144,128]{2,1,0:T(8,128)(2,1)S(1)}, bf16[8,144,128]{2,1,0:T(8,128)(2,1)S(1)}, u32[]{:S(2)}, u32[]{:S(2)}) collective-permute-start(bf16[8,144,128]{2,1,0:T(8,128)(2,1)S(1)} %all_to_all.20.refs_0_), channel_id=1, source_target_pairs={{0,1},{1,0},{2,3},{3,2},{4,5},{5,4},{6,7},{7,6},{8,9},{9,8},{10,11... | collective-permute-start | bytes 884744 | tf_op jit(solution)/shard_map/ppermute | solution.py:417
  77.9 7.6 %collective-permute-start.5 = (bf16[8,144,128]{2,1,0:T(8,128)(2,1)S(1)}, bf16[8,144,128]{2,1,0:T(8,128)(2,1)S(1)}, u32[]{:S(2)}, u32[]{:S(2)}) collective-permute-start(bf16[8,144,128]{2,1,0:T(8,128)(2,1)S(1)} %collective-permute-done.4.refs_2_), channel_id=1, source_target_pairs={{0,1},{1,0},{2,3},{3,2},{4,5},{5,4},{6,7},{7,6},{8,9},{9,8},{10,11... | collective-permute-start | bytes 884744 | tf_op jit(solution)/shard_map/ppermute | solution.py:417
  (6 other events, 4.0 us)

commit v2 on v1

--- a/solution.py
+++ b/solution.py
@@ -15,23 +15,70 @@
 BF16 = jnp.bfloat16
 F32 = jnp.float32
 
-VMEM = pl.BlockSpec(memory_space=pltpu.VMEM)
-SMEM = pl.BlockSpec(memory_space=pltpu.SMEM)
-
-
-def call(kernel, outs, scratch=(), limit=16):
-    def run(*args):
-        specs = [SMEM if a.ndim == 1 and a.dtype == jnp.int32 else VMEM for a in args]
-        return pl.pallas_call(
-            kernel,
-            out_shape=[jax.ShapeDtypeStruct(s, d) for s, d in outs],
-            in_specs=specs,
-            out_specs=[VMEM] * len(outs),
-            scratch_shapes=list(scratch),
-            compiler_params=pltpu.CompilerParams(vmem_limit_bytes=limit * 1024 * 1024),
-        )(*args)
-
-    return run
+SCALAR, NEAR, FAR, RAW = "scalar", "near", "far", "raw"
+SPACES = {SCALAR: pltpu.SMEM, NEAR: pltpu.VMEM, FAR: pltpu.HBM, RAW: pltpu.HBM}
+
+
+class Loaded:
+    def __init__(self, ref, copy=None):
+        self.ref, self.copy = ref, copy
+        if copy is not None:
+            copy.start()
+
+    def get(self):
+        if self.copy is not None:
+            self.copy.wait()
+            self.copy = None
+        return self.ref
+
+
+class Stored:
+    def __init__(self, ref, copy):
+        self.ref, self.copy, self.started = ref, copy, False
+
+    def send(self):
+        if not self.started:
+            self.copy.start()
+            self.started = True
+
+
+def call(kernel, ins, outs, scratch=(), limit=16):
+    buffers = []
+    for shape, dtype, place in [(a.shape, a.dtype, p) for a, p in ins] + list(outs):
+        if place == FAR:
+            buffers += [pltpu.VMEM(shape, dtype), pltpu.SemaphoreType.DMA]
+
+    def run(*refs):
+        ends = len(ins), len(ins) + len(outs), len(ins) + len(outs) + len(buffers)
+        spare = list(refs[ends[1]:ends[2]])
+        operands, results = [], []
+        for ref, (_, place) in zip(refs, ins):
+            if place == FAR:
+                buffer, sem = spare.pop(0), spare.pop(0)
+                operands.append(Loaded(buffer, pltpu.make_async_copy(ref, buffer, sem)))
+            else:
+                operands.append(Loaded(ref) if place == NEAR else ref)
+        for ref, (_, _, place) in zip(refs[ends[0]:], outs):
+            if place == FAR:
+                buffer, sem = spare.pop(0), spare.pop(0)
+                results.append(Stored(buffer, pltpu.make_async_copy(buffer, ref, sem)))
+            else:
+                results.append(ref)
+        kernel(*operands, *results, *refs[ends[2]:])
+        far = [result for result in results if isinstance(result, Stored)]
+        for result in far:
+            result.send()
+        for result in far:
+            result.copy.wait()
+
+    return pl.pallas_call(
+        run,
+        out_shape=[jax.ShapeDtypeStruct(s, d) for s, d, _ in outs],
+        in_specs=[pl.BlockSpec(memory_space=SPACES[p]) for _, p in ins],
+        out_specs=[pl.BlockSpec(memory_space=SPACES[p]) for _, _, p in outs],
+        scratch_shapes=buffers + list(scratch),
+        compiler_params=pltpu.CompilerParams(vmem_limit_bytes=limit * 1024 * 1024),
+    )(*[a for a, _ in ins])
 
 
 def dot(a, b):
@@ -123,16 +170,17 @@
     return values if shift % size == 0 else pltpu.roll(values, shift % size, axis=1)
 
 
-def pack_kernel(edge, x_ref, rim_ref):
-    pixels = x_ref.shape[1]
-    pick = one_hot(rim_pixels(edge), pixels)
-    rim = dot(x_ref[...], pick).astype(BF16)
-    rim_ref[...] = jnp.broadcast_to(rim[None], rim_ref.shape)
-
-
-def conv_kernel(edge, place_ref, nb_ref, rot_ref, x_ref, rims_ref, taps_ref,
-                hidden_ref, padded_ref, side_ref, gathered):
-    channels, pixels = x_ref.shape
+def pack_kernel(edge, x, rims):
+    pick = one_hot(rim_pixels(edge), edge * edge)
+    rim = dot(x.get()[...], pick).astype(BF16)
+    rims.ref[...] = jnp.broadcast_to(rim[None], rims.ref.shape)
+
+
+def conv_kernel(edge, place_ref, nb_ref, rot_ref, x, rims, taps,
+                hidden_ref, padded, side, gathered):
+    padded_ref, side_ref = padded.ref, side.ref
+    rims_ref, taps_ref = rims.get(), taps.get()
+    channels, pixels = hidden_ref.shape
     wide = pixels + 2 * LANES
     rim = rims_ref.shape[2]
     first = place_ref[0] * 8
@@ -141,11 +189,13 @@
     top, low = row_halo_maps(rot[1], rot[6], edge)
     padded_ref[:, :LANES] = dot(rims_ref[nb[1]], top).astype(BF16)
     padded_ref[:, LANES + pixels:] = dot(rims_ref[nb[6]], low).astype(BF16)
-    padded_ref[:, LANES:LANES + pixels] = x_ref[...]
+    padded_ref[:, LANES:LANES + pixels] = x.get()[...]
+    padded.send()
     for position, d in enumerate(SIDES):
         gathered[:, position * rim:(position + 1) * rim] = rims_ref[nb[d]]
     packed = dot(gathered[...], side_map([rot[d] for d in SIDES], edge)).astype(BF16)
     side_ref[...] = dot(packed, spread_map(edge, wide)).astype(BF16)
+    side.send()
 
     def block(i, carry):
         at = pl.multiple_of(i * 16, 16)
@@ -181,9 +231,9 @@
     return (pre * cumul).astype(BF16), (grad_act * slope).astype(BF16)
 
 
-def hidden_block(w_in_t, w_out, feats_ref, cot_ref, pre, slope, act, gpre):
-    pre[...] = dot(w_in_t, feats_ref[...])
-    slope[...] = dot(w_out, cot_ref[...])
+def hidden_block(w_in_t, w_out, feats, cots, pre, slope, act, gpre):
+    pre[...] = dot(w_in_t, feats[...])
+    slope[...] = dot(w_out, cots[...])
 
     def rows(i, carry):
         at = pl.multiple_of(i * 16, 16)
@@ -194,68 +244,86 @@
     lax.fori_loop(0, pre.shape[0] // 16, rows, 0)
 
 
-def weight_kernel(place_ref, feats_ref, cot_ref, w_in_t_ref, w_out_ref, out_ref, act, gpre,
-                  pre, slope):
+def weight_kernel(place_ref, feats, cots, w_in_t, w_out, part, act, gpre,
+                  pre, slope, own_in, own_out, sems):
     units = pre.shape[0]
-    full = feats_ref.shape[0]
     at = pl.multiple_of(place_ref[1] * units, units)
-    hidden_block(w_in_t_ref[pl.ds(at, units), :], w_out_ref[pl.ds(at, units), :],
-                 feats_ref, cot_ref, pre, slope, act, gpre)
-    part_in = dot_nt(feats_ref[...], gpre[...]).astype(BF16)
-    part_out = dot_nt(act[...], cot_ref[...]).astype(BF16)
+    own_in = Loaded(own_in, pltpu.make_async_copy(w_in_t.at[pl.ds(at, units)], own_in, sems.at[0]))
+    own_out = Loaded(own_out, pltpu.make_async_copy(w_out.at[pl.ds(at, units)], own_out, sems.at[1]))
+    feats, cots = feats.get(), cots.get()
+    full = feats.shape[0]
+    hidden_block(own_in.get()[...], own_out.get()[...], feats, cots, pre, slope, act.ref, gpre.ref)
+    act.send()
+    gpre.send()
+    part_in = dot_nt(feats[...], gpre.ref[...]).astype(BF16)
+    part_out = dot_nt(act.ref[...], cots[...]).astype(BF16)
     used = 0
     for column in range(0, units, LANES):
-        out_ref[used:used + full, :] = part_in[:, column:column + LANES]
+        part.ref[used:used + full, :] = part_in[:, column:column + LANES]
         used += full
     for column in range(0, full, LANES):
-        out_ref[used:used + units, :] = part_out[:, column:column + LANES]
+        part.ref[used:used + units, :] = part_out[:, column:column + LANES]
         used += units
-    if used < out_ref.shape[0]:
-        out_ref[used:, :] = jnp.zeros((out_ref.shape[0] - used, LANES), BF16)
-
-
-def point_kernel(groups, place_ref, feats_ref, cot_ref, w_in_t_ref, w_out_ref, w_in_own_ref,
-                 w_out_own_ref, act_own, gpre_own, x_ref, out_ref, grad_ref,
-                 pre, slope, act, gpre):
+    if used < part.ref.shape[0]:
+        part.ref[used:, :] = jnp.zeros((part.ref.shape[0] - used, LANES), BF16)
+
+
+def point_kernel(groups, place_ref, feats, cots, w_in_t, w_out, w_in_own, w_out_own, act_own,
+                 gpre_own, x, out, grad_ref, pre, slope, act, gpre):
     units = pre.shape[0]
+    feats, cots, w_in_t, w_out = feats.get(), cots.get(), w_in_t.get(), w_out.get()
 
     def start(k):
         return pl.multiple_of((place_ref[1] ^ k) * units, units)
 
-    mine = pl.ds(start(0), units)
-    branch = dot(w_out_own_ref[:, mine], act_own[...])
-    grad = dot(w_in_own_ref[:, mine], gpre_own[...])
+    branch = grad = None
     for k in range(1, groups):
         part = pl.ds(start(k), units)
-        hidden_block(w_in_t_ref[part, :], w_out_ref[part, :],
-                     feats_ref, cot_ref, pre, slope, act, gpre)
-        branch = branch + dot(w_out_own_ref[:, part], act[...])
-        grad = grad + dot(w_in_own_ref[:, part], gpre[...])
-    out_ref[...] = (x_ref[...].astype(F32) + branch.astype(BF16).astype(F32)).astype(BF16)
+        hidden_block(w_in_t[part, :], w_out[part, :], feats, cots, pre, slope, act, gpre)
+        more = dot(w_out_own.get()[:, part], act[...])
+        branch = more if branch is None else branch + more
+        more = dot(w_in_own.get()[:, part], gpre[...])
+        grad = more if grad is None else grad + more
+    mine = pl.ds(start(0), units)
+    branch = branch + dot(w_out_own.get()[:, mine], act_own.get()[...])
+    out.ref[...] = (x.get()[...].astype(F32) + branch.astype(BF16).astype(F32)).astype(BF16)
+    out.send()
+    grad = grad + dot(w_in_own.get()[:, mine], gpre_own.get()[...])
     grad_ref[...] = grad.astype(BF16)
 
 
-def prep_kernel(place_ref, w_in_ref, w_out_ref, w_in_t_ref, w_in_own_ref, w_out_own_ref):
-    channels = w_in_own_ref.shape[0]
+def prep_kernel(place_ref, w_in, w_out, w_in_t, w_in_own, w_out_own):
+    channels = w_in_own.ref.shape[0]
     start = place_ref[1] * channels
-    w_in_t_ref[...] = w_in_ref[...].astype(F32).T.astype(BF16)
-    w_in_own_ref[...] = w_in_ref[pl.ds(pl.multiple_of(start, channels), channels), :]
-    row = lax.broadcasted_iota(jnp.int32, (channels, w_out_ref.shape[1]), 0)
-    column = lax.broadcasted_iota(jnp.int32, (channels, w_out_ref.shape[1]), 1)
+    w_in, w_out = w_in.get(), w_out.get()
+    w_in_own.ref[...] = w_in[pl.ds(pl.multiple_of(start, channels), channels), :]
+    w_in_own.send()
+    w_in_t.ref[...] = w_in[...].astype(F32).T.astype(BF16)
+    w_in_t.send()
+    row = lax.broadcasted_iota(jnp.int32, (channels, w_out.shape[1]), 0)
+    column = lax.broadcasted_iota(jnp.int32, (channels, w_out.shape[1]), 1)
     pick = jnp.where(column == row + start, 1.0, 0.0).astype(BF16)
-    w_out_own_ref[...] = dot_nt(pick, w_out_ref[...]).astype(BF16)
+    w_out_own.ref[...] = dot_nt(pick, w_out[...]).astype(BF16)
 
 
 def join_kernel(place_ref, *refs):
-    pieces, out_ref = refs[:-1], refs[-1]
+    pieces, out_ref, sems = refs[:-2], refs[-2], refs[-1]
     channels = pieces[0].shape[0]
+    copies = []
     for k, piece in enumerate(pieces):
         start = pl.multiple_of((place_ref[1] ^ k) * channels, channels)
-        out_ref[pl.ds(start, channels), :] = piece[...]
-
-
-def back_kernel(edge, place_ref, nb_ref, rot_ref, grad_ref, cot_ref, padded_ref, side_ref, taps_ref,
-                accum_ref, send_ref, tap_ref, d_row, d_side, turned_all, moved_all, gathered):
+        copies.append(pltpu.make_async_copy(piece, out_ref.at[pl.ds(start, channels)], sems.at[k]))
+    for copy in copies:
+        copy.start()
+    for copy in copies:
+        copy.wait()
+
+
+def back_kernel(edge, place_ref, nb_ref, rot_ref, grad, cot, padded, side, taps,
+                accum, border, tap_ref, d_row, d_side, turned_all, moved_all, gathered):
+    accum_ref, send_ref = accum.ref, border.ref
+    grad_ref, taps_ref = grad.get(), taps.get()
+    padded_ref, side_ref, cot_ref = padded.get(), side.get(), cot.get()
     channels, pixels = grad_ref.shape
     wide = pixels + 2 * LANES
     tiles, _, rim = send_ref.shape
@@ -323,6 +391,7 @@
         slot = slice(block // 4 * 16, block // 4 * 16 + 16)
         tap_ref[slot, :] = (tap_ref[slot, :].astype(F32) + placed).astype(BF16)
 
+    accum.send()
     first = place_ref[0] * 8
     nb = [nb_ref[first + d] for d in range(8)]
     rot = [rot_ref[first + d] for d in range(8)]
@@ -342,13 +411,13 @@
     lax.fori_loop(0, tiles, store, 0)
 
 
-def border_kernel(edge, recv_ref, accum_ref, grad_ref):
-    pixels = accum_ref.shape[1]
-    rims = total_of(recv_ref)
+def border_kernel(edge, recv, accum, grad):
+    rims = total_of(recv.get())
     high = rims.astype(BF16)
     low = (rims - high.astype(F32)).astype(BF16)
-    pick = one_hot(rim_pixels(edge), pixels)
-    grad_ref[...] = (accum_ref[...] + dot_nt(high, pick) + dot_nt(low, pick)).astype(BF16)
+    pick = one_hot(rim_pixels(edge), edge * edge)
+    added = dot_nt(high, pick) + dot_nt(low, pick)
+    grad.ref[...] = (accum.get()[...] + added).astype(BF16)
 
 
 def total_of(ref):
@@ -356,43 +425,51 @@
                          ref[0].astype(F32))
 
 
-def sum_kernel(recv_ref, tap_ref, out_ref):
-    share = recv_ref.shape[1]
-    total = total_of(recv_ref).astype(BF16)
+def sum_kernel(recv, tap, out):
+    recv = recv.get()
+    share = recv.shape[1]
+    total, taps = total_of(recv).astype(BF16), tap.get()[...]
 
     def store(t, carry):
-        out_ref[t, :share, :] = total
-        out_ref[t, share:, :] = tap_ref[...]
+        out.ref[t, :share, :] = total
+        out.ref[t, share:, :] = taps
         return carry
 
-    lax.fori_loop(0, out_ref.shape[0], store, 0)
+    lax.fori_loop(0, out.ref.shape[0], store, 0)
 
 
 def final_kernel(groups, share, channels, scale, place_ref, *refs):
     pieces = refs[:groups]
-    g_in_ref, g_out_ref, g_tap_ref, all_taps = refs[groups:]
-    full, hidden = g_in_ref.shape
-    units = hidden // groups
-    tiles, rows, _ = pieces[0].shape
+    g_in, g_out, g_tap_ref, buf_in, buf_out, all_taps, sems = refs[groups:]
+    full, units = buf_in.shape[1:]
+    tiles, rows, _ = pieces[0].ref.shape
+    copies = []
     for k in range(groups):
+        piece = pieces[k].get()
         owner = place_ref[1] ^ k
         start = pl.multiple_of(owner * units, units)
         for tile in range(tiles):
             for row, count, column, at, into_in in chunks(tile, share, units, full):
-                values = pieces[k][tile, row:row + count, :].astype(F32) * scale
-                if into_in:
-                    g_in_ref[at:at + count, pl.ds(pl.multiple_of(start + column, LANES), LANES)] = values
-                else:
-                    g_out_ref[pl.ds(pl.multiple_of(start + at, 16), count), column:column + LANES] = values
-        taps = pieces[k][0, share:, :].astype(F32)
+                values = piece[tile, row:row + count, :].astype(F32) * scale
+                buffer = buf_in if into_in else buf_out
+                buffer[k, at:at + count, column:column + LANES] = values
+        copies.append(pltpu.make_async_copy(
+            buf_in.at[k], g_in.at[:, pl.ds(start, units)], sems.at[0, k]))
+        copies.append(pltpu.make_async_copy(
+            buf_out.at[k], g_out.at[pl.ds(start, units)], sems.at[1, k]))
+        for copy in copies[-2:]:
+            copy.start()
+        taps = piece[0, share:, :].astype(F32)
         for tile in range(1, tiles):
-            taps = taps + pieces[k][tile, share:, :].astype(F32)
+            taps = taps + piece[tile, share:, :].astype(F32)
         taps = taps * scale
         for block in range(channels // 16):
             values = taps[block // 4 * 16:block // 4 * 16 + 16, :]
             into = pl.ds(pl.multiple_of(owner * channels + block * 16, 16), 16)
             all_taps[into, :] = roll(values, -32 * (block % 4))
     g_tap_ref[...] = all_taps[...].T[:KSIZE * KSIZE, :]
+    for copy in copies:
+        copy.wait()
 
 
 def chunks(tile, share, units, full):
@@ -437,58 +514,70 @@
     nb, rot = neighbours.reshape(-1), rotations.reshape(-1)
     x, cot = inputs[0], grad_out[0]
 
-    [rims] = call(functools.partial(pack_kernel, edge), [((tiles, channels, rim), BF16)])(x)
+    [rims] = call(functools.partial(pack_kernel, edge), [(x, FAR)],
+                  [((tiles, channels, rim), BF16, FAR)])
     rims, kernel, w_in, w_out = lax.optimization_barrier((rims, kernel, w_in, w_out))
     rims = swap_rows(rims)
     cot_pieces = gather_pieces(cot, groups)
     taps = jnp.broadcast_to(kernel.astype(F32)[:, :, None], (KSIZE * KSIZE, channels, LANES))
     w_in_t, w_in_own, w_out_own = call(
-        prep_kernel, [((hidden, full), BF16)] + [((channels, hidden), BF16)] * 2
-    )(place, w_in, w_out)
-    [cots] = call(join_kernel, [((full, pixels), BF16)])(place, *cot_pieces)
+        prep_kernel, [(place, SCALAR), (w_in, FAR), (w_out, FAR)],
+        [((hidden, full), BF16, FAR)] + [((channels, hidden), BF16, FAR)] * 2)
+    [cots] = call(join_kernel, [(place, SCALAR)] + [(piece, RAW) for piece in cot_pieces],
+                  [((full, pixels), BF16, RAW)], [pltpu.SemaphoreType.DMA((groups,))])
     rims, cots, taps, w_in_t, w_in_own, w_out_own = lax.optimization_barrier(
         (rims, cots, taps, w_in_t, w_in_own, w_out_own))
 
+    here = [(place, SCALAR), (nb, SCALAR), (rot, SCALAR)]
     hid, padded, side = call(
-        functools.partial(conv_kernel, edge),
-        [((channels, pixels), BF16), ((channels, wide), BF16), ((channels, wide), BF16)],
-        [pltpu.VMEM((channels, len(SIDES) * rim), BF16)],
-    )(place, nb, rot, x, rims, taps)
+        functools.partial(conv_kernel, edge), here + [(x, FAR), (rims, NEAR), (taps, NEAR)],
+        [((channels, pixels), BF16, NEAR), ((channels, wide), BF16, FAR),
+         ((channels, wide), BF16, FAR)],
+        [pltpu.VMEM((channels, len(SIDES) * rim), BF16)])
     feats = lax.all_gather(hid, "chan", axis=0, tiled=True)
 
     used = 2 * full * units // LANES
     share = -(-used // (16 * tiles)) * 16
     tap_rows = -(-channels // 64) * 16
     values = [pltpu.VMEM((units, pixels), F32)] * 2
-    rounded = [((units, pixels), BF16)] * 2
-    part, act, gpre = call(weight_kernel, [((tiles * share, LANES), BF16)] + rounded, values)(
-        place, feats, cots, w_in_t, w_out)
+    part, act, gpre = call(
+        weight_kernel,
+        [(place, SCALAR), (feats, NEAR), (cots, FAR), (w_in_t, RAW), (w_out, RAW)],
+        [((tiles * share, LANES), BF16, FAR)] + [((units, pixels), BF16, FAR)] * 2,
+        values + [pltpu.VMEM((units, full), BF16)] * 2 + [pltpu.SemaphoreType.DMA((2,))])
     part = swap_rows(part.reshape(tiles, share, LANES))
 
     outputs, grad_hid = call(
-        functools.partial(point_kernel, groups), [((channels, pixels), BF16)] * 2,
-        values + [pltpu.VMEM(s, d) for s, d in rounded],
-    )(place, feats, cots, w_in_t, w_out, w_in_own, w_out_own, act, gpre, x)
+        functools.partial(point_kernel, groups),
+        [(place, SCALAR), (feats, NEAR), (cots, FAR), (w_in_t, FAR), (w_out, FAR), (w_in_own, FAR),
+         (w_out_own, FAR), (act, FAR), (gpre, FAR), (x, FAR)],
+        [((channels, pixels), BF16, FAR), ((channels, pixels), BF16, NEAR)],
+        values + [pltpu.VMEM((units, pixels), BF16)] * 2)
     accum, border, tap_part = call(
         functools.partial(back_kernel, edge),
-        [((channels, pixels), F32), ((tiles, channels, rim), BF16), ((tap_rows, LANES), BF16)],
+        here + [(grad_hid, NEAR), (cot, FAR), (padded, FAR), (side, FAR), (taps, NEAR)],
+        [((channels, pixels), F32, FAR), ((tiles, channels, rim), BF16, FAR),
+         ((tap_rows, LANES), BF16, NEAR)],
         [pltpu.VMEM((channels, 2 * LANES), BF16), pltpu.VMEM((channels, wide), BF16),
          pltpu.VMEM((KSIZE * 16, wide), BF16), pltpu.VMEM((LANES, wide), BF16),
-         pltpu.VMEM((tiles, channels, rim), F32)],
-    )(place, nb, rot, grad_hid, cot, padded, side, taps)
-
-    [mine] = call(sum_kernel, [((tiles, share + tap_rows, LANES), BF16)])(part, tap_part)
-    mine, border = lax.optimization_barrier((mine, border))
+         pltpu.VMEM((tiles, channels, rim), F32)])
+
+    [mine] = call(sum_kernel, [(part, NEAR), (tap_part, NEAR)],
+                  [((tiles, share + tap_rows, LANES), BF16, FAR)])
     weights = swap_rows(mine)
+    weights, border = lax.optimization_barrier((weights, border))
     border = swap_rows(border)
     pieces = gather_pieces(weights, groups)
-    [grad_in] = call(
-        functools.partial(border_kernel, edge), [((channels, pixels), BF16)])(border, accum)
     grads = call(
         functools.partial(final_kernel, groups, share, channels, scale),
-        [((full, hidden), F32), ((hidden, full), F32), ((KSIZE * KSIZE, full), F32)],
-        [pltpu.VMEM((full, LANES), F32)],
-    )(place, *pieces)
+        [(place, SCALAR)] + [(piece, NEAR) for piece in pieces],
+        [((full, hidden), F32, RAW), ((hidden, full), F32, RAW),
+         ((KSIZE * KSIZE, full), F32, NEAR)],
+        [pltpu.VMEM((groups, full, units), F32), pltpu.VMEM((groups, units, full), F32),
+         pltpu.VMEM((full, LANES), F32), pltpu.SemaphoreType.DMA((2, groups))])
+    border, *grads = lax.optimization_barrier((border, *grads))
+    [grad_in] = call(functools.partial(border_kernel, edge), [(border, NEAR), (accum, FAR)],
+                     [((channels, pixels), BF16, FAR)])
     return (outputs[None], grad_in[None], *grads)
 
 

time: 88.3 us -> 91 us (1.031)
  Pallas kernels: 19.1 us -> 24.5 us
  waiting for transfers between devices: 11.5 us -> 8.88 us
    pallas_call x10, Pallas kernels: 19.1 us -> 24.5 us  [call(): pl.pallas_call(run, out_shape=[jax.ShapeDtypeStruct(s, d) for s, d, _ in...]
    all_to_all x3, waiting for transfers between devices: 6.38 us -> 2.14 us  [swap_rows(): return lax.all_to_all(values, 'tile', 0, 0, tiled=True)]
    ppermute x6, waiting for transfers between devices: 5.16 us -> 6.74 us  [gather_pieces(): pieces[k ^ bit] = lax.ppermute(pieces[k], 'chan', swap)]
  transfers between devices with their start and end apart: 9 -> 9, of which waited for: 3 -> 4; matrix products, arithmetic and copies ran while one was open for 0% -> 0% of each run, Pallas kernels for 13% -> 18%
where the time goes in v2:
time: 91 us; the launch traced here: 90.3 us
  Pallas kernels  24.5 us (27%)
  blocking collectives  23.5 us (26%)
  starting transfers between devices  19.9 us (22%)
  local copies, waits for them, and re-layouts  12.6 us (14%)
  waiting for transfers between devices  8.88 us (10%)
    pallas_call x10, Pallas kernels, call(): pl.pallas_call(run, out_shape=[jax.ShapeDtypeStruct(s, d) for s, d, _ in...  24.5 us
    all_to_all x3, starting transfers between devices, swap_rows(): return lax.all_to_all(values, 'tile', 0, 0, tiled=True)  16.7 us
    all_to_all x1, blocking collectives, swap_rows(): return lax.all_to_all(values, 'tile', 0, 0, tiled=True)  16.1 us
    unnamed x42, local copies, waits for them, and re-layouts  12.1 us
    all_gather x1, blocking collectives, body(): feats = lax.all_gather(hid, 'chan', axis=0, tiled=True)  7.44 us
    ppermute x6, waiting for transfers between devices, gather_pieces(): pieces[k ^ bit] = lax.ppermute(pieces[k], 'chan', swap)  6.74 us
    ppermute x6, starting transfers between devices, gather_pieces(): pieces[k ^ bit] = lax.ppermute(pieces[k], 'chan', swap)  3.18 us
    all_to_all x3, waiting for transfers between devices, swap_rows(): return lax.all_to_all(values, 'tile', 0, 0, tiled=True)  2.14 us
  transfers between devices with their start and end apart: 9, of which 4 were waited for; matrix products, arithmetic and copies ran while one was open for 0% of the time, Pallas kernels for 18%

profile of v2, /device:TPU:0, one launch (start us, length us, event | category | flops | bytes accessed | tf_op | source)
XLA Modules:
  0.0 90.3 jit_solution(1140204107509511964)
XLA Ops:
  0.7 1.0 %copy-done.1 = bf16[1,64,1024]{2,1,0:T(8,128)(2,1)S(1)} copy-done((bf16[1,64,1024]{2,1,0:T(8,128)(2,1)S(1)}, bf16[1,64,1024]{2,1,0:T(8,128)(2,1)}, u32[]{:S(2)}) %copy-start.1) | copy-done | bytes 131096
  1.6 1.2 %shard_map.110 = bf16[8,64,256]{2,1,0:T(8,128)(2,1)} custom-call(bf16[64,1024]{1,0:T(8,128)(2,1)S(1)} %bitcast.7), custom_call_target="tpu_custom_call" | custom-call | tf_op jit(solution)/shard_map/pallas_call | solution.py:74
  2.8 7.4 %all-to-all-start = ((bf16[8,64,256]{2,1,0:T(8,128)(2,1)}), bf16[8,64,256]{2,1,0:T(8,128)(2,1)S(1)}, u32[]{:S(2)}, u32[]{:S(2)}) async-start(bf16[8,64,256]{2,1,0:T(8,128)(2,1)} %shard_map.110), calls=%async_computation | async-start | bytes 524288 | tf_op jit(solution)/shard_map/all_to_all | solution.py:500
  10.2 1.6 %collective-permute-start.1 = (bf16[64,1024]{1,0:T(8,128)(2,1)S(1)}, bf16[64,1024]{1,0:T(8,128)(2,1)S(1)}, u32[]{:S(2)}, u32[]{:S(2)}) collective-permute-start(bf16[64,1024]{1,0:T(8,128)(2,1)S(1)} %bitcast.10), channel_id=1, source_target_pairs={{0,2},{1,3},{2,0},{3,1},{4,6},{5,7},{6,4},{7,5},{8,10},{9,11},{10,... | collective-permute-start | bytes 393224 | tf_op jit(solution)/shard_map/ppermute | solution.py:494
  11.8 3.4 %collective-permute-done.1.refs_3_ = bf16[64,1024]{1,0:T(8,128)(2,1)S(1)} collective-permute-done((bf16[64,1024]{1,0:T(8,128)(2,1)S(1)}, bf16[64,1024]{1,0:T(8,128)(2,1)S(1)}, u32[]{:S(2)}, u32[]{:S(2)}) %collective-permute-start.1) | collective-permute-done | bytes 131104 | tf_op jit(solution)/shard_map/ppermute | solution.py:494
  16.2 1.0 %copy-done.3 = bf16[256,1024]{1,0:T(8,128)(2,1)S(1)} copy-done((bf16[256,1024]{1,0:T(8,128)(2,1)S(1)}, bf16[256,1024]{1,0:T(8,128)(2,1)}, u32[]{:S(2)}) %copy-start.3) | copy-done | bytes 524312
  17.3 1.5 %shard_map.112 = (bf16[1024,256]{1,0:T(8,128)(2,1)S(1)}, bf16[64,1024]{1,0:T(8,128)(2,1)S(1)}, bf16[64,1024]{1,0:T(8,128)(2,1)S(1)}) custom-call(s32[2]{0:T(128)S(1)} %pad_add_fusion.refs_0_, bf16[256,1024]{1,0:T(8,128)(2,1)S(1)} %copy-done.3, bf16[1024,256]{1,0:T(8,128)(2,1)S(1)} %copy-done), custom_call_target="tpu_custom_call" | custom-call | tf_op jit(solution)/shard_map/pallas_call | solution.py:74
  20.1 1.3 %shard_map.111.refs_2_ = bf16[256,1024]{1,0:T(8,128)(2,1)S(1)} custom-call(s32[2]{0:T(128)S(1)} %pad_add_fusion.refs_0_, bf16[64,1024]{1,0:T(8,128)(2,1)S(1)} %bitcast.12, bf16[64,1024]{1,0:T(8,128)(2,1)S(1)} %collective-permute-done.refs_2_, bf16[64,1024]{1,0:T(8,128)(2,1)S(1)} %collective-permute-done.1.refs_3_, ...), custom_call_target="tpu_custom_call" | custom-call | tf_op jit(solution)/shard_map/pallas_call | solution.py:74
  22.3 3.1 %shard_map.113 = (bf16[64,1024]{1,0:T(8,128)(2,1)S(1)}, bf16[64,1280]{1,0:T(8,128)(2,1)S(1)}, bf16[64,1280]{1,0:T(8,128)(2,1)S(1)}) custom-call(s32[2]{0:T(128)S(1)} %pad_add_fusion.refs_0_, s32[64]{0:T(128)S(1)} %reshape.20.refs_1_, s32[64]{0:T(128)S(1)} %reshape.21.refs_2_, bf16[64,1024]{1,0:T(8,128)(2,1)S(1)} %bitcast.8, ...), custom_call_target="tpu_custom_call" | custom-call | tf_op jit(solution)/shard_map/pallas_call | solution.py:74
  26.7 7.4 %all_gather.3.refs_1_ = bf16[256,1024]{1,0:T(8,128)(2,1)S(1)} all-gather(bf16[64,1024]{1,0:T(8,128)(2,1)S(1)} %get-tuple-element.47), channel_id=1, replica_groups=mesh['tile'=8,'chan'=4] {'chan'}, dimensions={0}, use_global_device_ids=true | all-gather | bytes 655360 | tf_op jit(solution)/shard_map/all_gather | solution.py:537
  34.1 2.5 %shard_map.114 = (bf16[1024,128]{1,0:T(8,128)(2,1)S(1)}, bf16[256,1024]{1,0:T(8,128)(2,1)S(1)}, bf16[256,1024]{1,0:T(8,128)(2,1)S(1)}) custom-call(s32[2]{0:T(128)S(1)} %pad_add_fusion.refs_0_, bf16[256,1024]{1,0:T(8,128)(2,1)S(1)} %all_gather.3.refs_1_, bf16[256,1024]{1,0:T(8,128)(2,1)S(1)} %shard_map.111.refs_2_, ...), custom_call_target="tpu_custom_call" | custom-call | tf_op jit(solution)/shard_map/pallas_call | solution.py:74
  39.0 5.9 %all-to-all-start.1 = ((bf16[8,128,128]{2,1,0:T(8,128)(2,1)}), bf16[8,128,128]{2,1,0:T(8,128)(2,1)S(1)}, u32[]{:S(2)}, u32[]{:S(2)}) async-start(bf16[8,128,128]{2,1,0:T(8,128)(2,1)} %bitcast.14), calls=%async_computation.1 | async-start | bytes 524288 | tf_op jit(solution)/shard_map/all_to_all | solution.py:500
  44.9 1.0 %copy-done.6 = bf16[256,1024]{1,0:T(8,128)(2,1)S(1)} copy-done((bf16[256,1024]{1,0:T(8,128)(2,1)S(1)}, bf16[256,1024]{1,0:T(8,128)(2,1)}, u32[]{:S(2)}) %copy-start.6) | copy-done | bytes 524312
  46.0 1.0 %copy-done.8 = bf16[256,1024]{1,0:T(8,128)(2,1)S(1)} copy-done((bf16[256,1024]{1,0:T(8,128)(2,1)S(1)}, bf16[256,1024]{1,0:T(8,128)(2,1)}, u32[]{:S(2)}) %copy-start.8) | copy-done | bytes 524312
  48.8 5.9 %shard_map.115 = (bf16[64,1024]{1,0:T(8,128)(2,1)}, bf16[64,1024]{1,0:T(8,128)(2,1)S(1)}) custom-call(s32[2]{0:T(128)S(1)} %pad_add_fusion.refs_0_, bf16[256,1024]{1,0:T(8,128)(2,1)S(1)} %all_gather.3.refs_1_, bf16[256,1024]{1,0:T(8,128)(2,1)S(1)} %shard_map.111.refs_2_, bf16[1024,256]{1,0:T(8,128)(2,1)S(1)} %get-tuple-element.49.refs_3_, ...), custom_call_target="tpu_custom_call" | custom-call | tf_op jit(solution)/shard_map/pallas_call | solution.py:74
  54.7 4.9 %shard_map.116 = (f32[64,1024]{1,0:T(8,128)S(1)}, bf16[8,64,256]{2,1,0:T(8,128)(2,1)}, bf16[16,128]{1,0:T(8,128)(2,1)S(1)}) custom-call(s32[2]{0:T(128)S(1)} %pad_add_fusion.refs_0_, s32[64]{0:T(128)S(1)} %reshape.20.refs_1_, s32[64]{0:T(128)S(1)} %reshape.21.refs_2_, bf16[64,1024]{1,0:T(8,128)(2,1)S(1)} %get-tuple-element.56.refs_3_, ...), custom_call_target="tpu_custom_call" | custom-call | tf_op jit(solution)/shard_map/pallas_call | solution.py:74
  59.9 16.1 %all_to_all.20.refs_1_ = bf16[8,144,128]{2,1,0:T(8,128)(2,1)S(1)} all-to-all(bf16[8,144,128]{2,1,0:T(8,128)(2,1)S(1)} %shard_map.117), channel_id=1, replica_groups=mesh['tile'=8,'chan'=4] {'tile'}, dimensions={0} | all-to-all | bytes 589824 | tf_op jit(solution)/shard_map/all_to_all | solution.py:500
  75.9 1.5 %collective-permute-start.4 = (bf16[8,144,128]{2,1,0:T(8,128)(2,1)S(1)}, bf16[8,144,128]{2,1,0:T(8,128)(2,1)S(1)}, u32[]{:S(2)}, u32[]{:S(2)}) collective-permute-start(bf16[8,144,128]{2,1,0:T(8,128)(2,1)S(1)} %all_to_all.20.refs_1_), channel_id=1, source_target_pairs={{0,2},{1,3},{2,0},{3,1},{4,6},{5,7},{6,4},{7,5},{8,10},{9,11},{10,... | collective-permute-start | bytes 884744 | tf_op jit(solution)/shard_map/ppermute | solution.py:494
  77.5 3.4 %all-to-all-start.3 = ((bf16[8,64,256]{2,1,0:T(8,128)(2,1)}), bf16[8,64,256]{2,1,0:T(8,128)(2,1)S(1)}, u32[]{:S(2)}, u32[]{:S(2)}) async-start(bf16[8,64,256]{2,1,0:T(8,128)(2,1)} %get-tuple-element.61), calls=%async_computation.3 | async-start | bytes 524288 | tf_op jit(solution)/shard_map/all_to_all | solution.py:500
  81.0 1.7 %collective-permute-done.4.refs_3_ = bf16[8,144,128]{2,1,0:T(8,128)(2,1)S(1)} collective-permute-done((bf16[8,144,128]{2,1,0:T(8,128)(2,1)S(1)}, bf16[8,144,128]{2,1,0:T(8,128)(2,1)S(1)}, u32[]{:S(2)}, u32[]{:S(2)}) %collective-permute-start.4) | collective-permute-done | bytes 294944 | tf_op jit(solution)/shard_map/ppermute | solution.py:494
  82.7 1.6 %collective-permute-done.5.refs_4_ = bf16[8,144,128]{2,1,0:T(8,128)(2,1)S(1)} collective-permute-done((bf16[8,144,128]{2,1,0:T(8,128)(2,1)S(1)}, bf16[8,144,128]{2,1,0:T(8,128)(2,1)S(1)}, u32[]{:S(2)}, u32[]{:S(2)}) %collective-permute-start.5) | collective-permute-done | bytes 294944 | tf_op jit(solution)/shard_map/ppermute | solution.py:494
  84.2 2.6 %shard_map.118 = (f32[256,1024]{1,0:T(8,128)}, f32[1024,256]{1,0:T(8,128)}, f32[25,256]{1,0:T(8,128)}) custom-call(s32[2]{0:T(128)S(1)} %pad_add_fusion.refs_0_, bf16[8,144,128]{2,1,0:T(8,128)(2,1)S(1)} %all_to_all.20.refs_1_, bf16[8,144,128]{2,1,0:T(8,128)(2,1)S(1)} %collective-permute-done.3.refs_2_, ...), custom_call_target="tpu_custom_call" | custom-call | tf_op jit(solution)/shard_map/pallas_call | solution.py:74
  86.9 2.1 %all-to-all-done.3.refs_0_ = bf16[8,64,256]{2,1,0:T(8,128)(2,1)S(1)} async-done(((bf16[8,64,256]{2,1,0:T(8,128)(2,1)}), bf16[8,64,256]{2,1,0:T(8,128)(2,1)S(1)}, u32[]{:S(2)}, u32[]{:S(2)}) %all-to-all-start.3) | async-done | bytes 262176 | tf_op jit(solution)/shard_map/all_to_all | solution.py:500
  89.0 1.2 %shard_map.119 = bf16[64,1024]{1,0:T(8,128)(2,1)} custom-call(bf16[8,64,256]{2,1,0:T(8,128)(2,1)S(1)} %all-to-all-done.3.refs_0_, f32[64,1024]{1,0:T(8,128)S(1)} %get-tuple-element.67.refs_1_), custom_call_target="tpu_custom_call" | custom-call | tf_op jit(solution)/shard_map/pallas_call | solution.py:74
  (52 shorter events, 8.8 us)
Async XLA Ops:
  0.6 15.6 %copy-start = (bf16[1024,256]{1,0:T(8,128)(2,1)S(1)}, bf16[1024,256]{1,0:T(8,128)(2,1)}, u32[]{:S(2)}) copy-start(bf16[1024,256]{1,0:T(8,128)(2,1)} %refs_4_.1) | copy-start | bytes 1572868
  0.6 1.0 %copy-start.1 = (bf16[1,64,1024]{2,1,0:T(8,128)(2,1)S(1)}, bf16[1,64,1024]{2,1,0:T(8,128)(2,1)}, u32[]{:S(2)}) copy-start(bf16[1,64,1024]{2,1,0:T(8,128)(2,1)} %param.7) | copy-start | bytes 393220
  2.8 7.4 %copy-start.4 = (bf16[1,64,1024]{2,1,0:T(8,128)(2,1)S(1)}, bf16[1,64,1024]{2,1,0:T(8,128)(2,1)}, u32[]{:S(2)}) copy-start(bf16[1,64,1024]{2,1,0:T(8,128)(2,1)} %param.8) | copy-start | bytes 393220
  2.8 18.5 %all-to-all-start = ((bf16[8,64,256]{2,1,0:T(8,128)(2,1)}), bf16[8,64,256]{2,1,0:T(8,128)(2,1)S(1)}, u32[]{:S(2)}, u32[]{:S(2)}) async-start(bf16[8,64,256]{2,1,0:T(8,128)(2,1)} %shard_map.110), calls=%async_computation | async-start | bytes 524288 | tf_op jit(solution)/shard_map/all_to_all | solution.py:500
  10.2 5.0 %collective-permute-start.1 = (bf16[64,1024]{1,0:T(8,128)(2,1)S(1)}, bf16[64,1024]{1,0:T(8,128)(2,1)S(1)}, u32[]{:S(2)}, u32[]{:S(2)}) collective-permute-start(bf16[64,1024]{1,0:T(8,128)(2,1)S(1)} %bitcast.10), channel_id=1, source_target_pairs={{0,2},{1,3},{2,0},{3,1},{4,6},{5,7},{6,4},{7,5},{8,10},{9,11},{10,... | collective-permute-start | bytes 393224 | tf_op jit(solution)/shard_map/ppermute | solution.py:494
  11.8 8.3 %collective-permute-start = (bf16[64,1024]{1,0:T(8,128)(2,1)S(1)}, bf16[64,1024]{1,0:T(8,128)(2,1)S(1)}, u32[]{:S(2)}, u32[]{:S(2)}) collective-permute-start(bf16[64,1024]{1,0:T(8,128)(2,1)S(1)} %bitcast.11), channel_id=1, source_target_pairs={{0,1},{1,0},{2,3},{3,2},{4,5},{5,4},{6,7},{7,6},{8,9},{9,8},{10,11... | collective-permute-start | bytes 393224 | tf_op jit(solution)/shard_map/ppermute | solution.py:494
  15.3 4.8 %collective-permute-start.2 = (bf16[64,1024]{1,0:T(8,128)(2,1)S(1)}, bf16[64,1024]{1,0:T(8,128)(2,1)S(1)}, u32[]{:S(2)}, u32[]{:S(2)}) collective-permute-start(bf16[64,1024]{1,0:T(8,128)(2,1)S(1)} %collective-permute-done.1.refs_3_), channel_id=1, source_target_pairs={{0,1},{1,0},{2,3},{3,2},{4,5},{5,4},{6,7},{7,6},{8,9},{9,8},{10,11... | collective-permute-start | bytes 393224 | tf_op jit(solution)/shard_map/ppermute | solution.py:494
  15.3 0.8 copy-start.20
  16.2 1.0 %copy-start.3 = (bf16[256,1024]{1,0:T(8,128)(2,1)S(1)}, bf16[256,1024]{1,0:T(8,128)(2,1)}, u32[]{:S(2)}) copy-start(bf16[256,1024]{1,0:T(8,128)(2,1)} %refs_1_) | copy-start | bytes 1572868
  20.1 1.3 %copy-start.18 = (bf16[25,64]{1,0:T(8,128)(2,1)S(1)}, bf16[25,64]{1,0:T(8,128)(2,1)}, u32[]{:S(2)}) copy-start(bf16[25,64]{1,0:T(8,128)(2,1)} %param.9) | copy-start | bytes 9604
  21.4 0.9 %copy-start.2 = (bf16[1,64,1024]{2,1,0:T(8,128)(2,1)S(1)}, bf16[1,64,1024]{2,1,0:T(8,128)(2,1)}, u32[]{:S(2)}) copy-start(bf16[1,64,1024]{2,1,0:T(8,128)(2,1)} %param.7) | copy-start | bytes 393220
  36.7 0.8 copy-start.5
  37.5 0.8 copy-start.7
  39.0 20.7 %all-to-all-start.1 = ((bf16[8,128,128]{2,1,0:T(8,128)(2,1)}), bf16[8,128,128]{2,1,0:T(8,128)(2,1)S(1)}, u32[]{:S(2)}, u32[]{:S(2)}) async-start(bf16[8,128,128]{2,1,0:T(8,128)(2,1)} %bitcast.14), calls=%async_computation.1 | async-start | bytes 524288 | tf_op jit(solution)/shard_map/all_to_all | solution.py:500
  44.9 1.0 %copy-start.6 = (bf16[256,1024]{1,0:T(8,128)(2,1)S(1)}, bf16[256,1024]{1,0:T(8,128)(2,1)}, u32[]{:S(2)}) copy-start(bf16[256,1024]{1,0:T(8,128)(2,1)} %copy-done.5) | copy-start | bytes 1572868
  46.0 1.0 %copy-start.8 = (bf16[256,1024]{1,0:T(8,128)(2,1)S(1)}, bf16[256,1024]{1,0:T(8,128)(2,1)}, u32[]{:S(2)}) copy-start(bf16[256,1024]{1,0:T(8,128)(2,1)} %copy-done.7) | copy-start | bytes 1572868
  47.0 0.9 %copy-start.15 = (bf16[64,1024]{1,0:T(8,128)(2,1)S(1)}, bf16[64,1024]{1,0:T(8,128)(2,1)}, u32[]{:S(2)}) copy-start(bf16[64,1024]{1,0:T(8,128)(2,1)} %copy-done.14) | copy-start | bytes 393220
  47.9 0.9 %copy-start.17 = (bf16[64,1024]{1,0:T(8,128)(2,1)S(1)}, bf16[64,1024]{1,0:T(8,128)(2,1)}, u32[]{:S(2)}) copy-start(bf16[64,1024]{1,0:T(8,128)(2,1)} %copy-done.16) | copy-start | bytes 393220
  48.8 5.9 %copy-start.11 = (bf16[64,1280]{1,0:T(8,128)(2,1)S(1)}, bf16[64,1280]{1,0:T(8,128)(2,1)}, u32[]{:S(2)}) copy-start(bf16[64,1280]{1,0:T(8,128)(2,1)} %copy-done.10) | copy-start | bytes 491524
  48.8 5.9 %copy-start.13 = (bf16[64,1280]{1,0:T(8,128)(2,1)S(1)}, bf16[64,1280]{1,0:T(8,128)(2,1)}, u32[]{:S(2)}) copy-start(bf16[64,1280]{1,0:T(8,128)(2,1)} %copy-done.12) | copy-start | bytes 491524
  75.9 6.7 %collective-permute-start.4 = (bf16[8,144,128]{2,1,0:T(8,128)(2,1)S(1)}, bf16[8,144,128]{2,1,0:T(8,128)(2,1)S(1)}, u32[]{:S(2)}, u32[]{:S(2)}) collective-permute-start(bf16[8,144,128]{2,1,0:T(8,128)(2,1)S(1)} %all_to_all.20.refs_1_), channel_id=1, source_target_pairs={{0,2},{1,3},{2,0},{3,1},{4,6},{5,7},{6,4},{7,5},{8,10},{9,11},{10,... | collective-permute-start | bytes 884744 | tf_op jit(solution)/shard_map/ppermute | solution.py:494
  77.5 11.6 %all-to-all-start.3 = ((bf16[8,64,256]{2,1,0:T(8,128)(2,1)}), bf16[8,64,256]{2,1,0:T(8,128)(2,1)S(1)}, u32[]{:S(2)}, u32[]{:S(2)}) async-start(bf16[8,64,256]{2,1,0:T(8,128)(2,1)} %get-tuple-element.61), calls=%async_computation.3 | async-start | bytes 524288 | tf_op jit(solution)/shard_map/all_to_all | solution.py:500
  80.9 1.8 %collective-permute-start.3 = (bf16[8,144,128]{2,1,0:T(8,128)(2,1)S(1)}, bf16[8,144,128]{2,1,0:T(8,128)(2,1)S(1)}, u32[]{:S(2)}, u32[]{:S(2)}) collective-permute-start(bf16[8,144,128]{2,1,0:T(8,128)(2,1)S(1)} %all_to_all.20.refs_1_), channel_id=1, source_target_pairs={{0,1},{1,0},{2,3},{3,2},{4,5},{5,4},{6,7},{7,6},{8,9},{9,8},{10,11... | collective-permute-start | bytes 884744 | tf_op jit(solution)/shard_map/ppermute | solution.py:494
  82.7 1.6 %collective-permute-start.5 = (bf16[8,144,128]{2,1,0:T(8,128)(2,1)S(1)}, bf16[8,144,128]{2,1,0:T(8,128)(2,1)S(1)}, u32[]{:S(2)}, u32[]{:S(2)}) collective-permute-start(bf16[8,144,128]{2,1,0:T(8,128)(2,1)S(1)} %collective-permute-done.4.refs_3_), channel_id=1, source_target_pairs={{0,1},{1,0},{2,3},{3,2},{4,5},{5,4},{6,7},{7,6},{8,9},{9,8},{10,11... | collective-permute-start | bytes 884744 | tf_op jit(solution)/shard_map/ppermute | solution.py:494
  (6 other events, 4.0 us)

commit v3 on v2

--- a/solution.py
+++ b/solution.py
@@ -42,7 +42,8 @@
             self.started = True
 
 
-def call(kernel, ins, outs, scratch=(), limit=16):
+def call(kernel, ins, outs, scratch=(), time=1.0, after=(), aliases=None, limit=16):
+    ins = list(ins) + [(a, RAW) for a in after]
     buffers = []
     for shape, dtype, place in [(a.shape, a.dtype, p) for a, p in ins] + list(outs):
         if place == FAR:
@@ -64,7 +65,7 @@
                 results.append(Stored(buffer, pltpu.make_async_copy(buffer, ref, sem)))
             else:
                 results.append(ref)
-        kernel(*operands, *results, *refs[ends[2]:])
+        kernel(*operands[:len(ins) - len(after)], *results, *refs[ends[2]:])
         far = [result for result in results if isinstance(result, Stored)]
         for result in far:
             result.send()
@@ -73,12 +74,17 @@
 
     return pl.pallas_call(
         run,
-        out_shape=[jax.ShapeDtypeStruct(s, d) for s, d, _ in outs],
+        out_shape=[pltpu.HBM(s, d) if p in (FAR, RAW) else jax.ShapeDtypeStruct(s, d)
+                   for s, d, p in outs],
         in_specs=[pl.BlockSpec(memory_space=SPACES[p]) for _, p in ins],
         out_specs=[pl.BlockSpec(memory_space=SPACES[p]) for _, _, p in outs],
         scratch_shapes=buffers + list(scratch),
+        input_output_aliases=aliases or {},
+        cost_estimate=pl.CostEstimate(
+            flops=int(time * 1e9), bytes_accessed=int(time * 3.5e6), transcendentals=0),
         compiler_params=pltpu.CompilerParams(vmem_limit_bytes=limit * 1024 * 1024),
-    )(*[a for a, _ in ins])
+    )(*[pltpu.with_memory_space_constraint(a, pltpu.HBM) if p in (FAR, RAW) else a
+        for a, p in ins])
 
 
 def dot(a, b):
@@ -189,13 +195,13 @@
     top, low = row_halo_maps(rot[1], rot[6], edge)
     padded_ref[:, :LANES] = dot(rims_ref[nb[1]], top).astype(BF16)
     padded_ref[:, LANES + pixels:] = dot(rims_ref[nb[6]], low).astype(BF16)
-    padded_ref[:, LANES:LANES + pixels] = x.get()[...]
-    padded.send()
     for position, d in enumerate(SIDES):
         gathered[:, position * rim:(position + 1) * rim] = rims_ref[nb[d]]
     packed = dot(gathered[...], side_map([rot[d] for d in SIDES], edge)).astype(BF16)
     side_ref[...] = dot(packed, spread_map(edge, wide)).astype(BF16)
     side.send()
+    padded_ref[:, LANES:LANES + pixels] = x.get()[...]
+    padded.send()
 
     def block(i, carry):
         at = pl.multiple_of(i * 16, 16)
@@ -244,62 +250,56 @@
     lax.fori_loop(0, pre.shape[0] // 16, rows, 0)
 
 
-def weight_kernel(place_ref, feats, cots, w_in_t, w_out, part, act, gpre,
-                  pre, slope, own_in, own_out, sems):
-    units = pre.shape[0]
-    at = pl.multiple_of(place_ref[1] * units, units)
-    own_in = Loaded(own_in, pltpu.make_async_copy(w_in_t.at[pl.ds(at, units)], own_in, sems.at[0]))
-    own_out = Loaded(own_out, pltpu.make_async_copy(w_out.at[pl.ds(at, units)], own_out, sems.at[1]))
+def weight_kernel(feats, cots, w_in_t, w_out, part, pre, slope, act, gpre, stack, sems):
     feats, cots = feats.get(), cots.get()
-    full = feats.shape[0]
-    hidden_block(own_in.get()[...], own_out.get()[...], feats, cots, pre, slope, act.ref, gpre.ref)
-    act.send()
-    gpre.send()
-    part_in = dot_nt(feats[...], gpre.ref[...]).astype(BF16)
-    part_out = dot_nt(act.ref[...], cots[...]).astype(BF16)
-    used = 0
-    for column in range(0, units, LANES):
-        part.ref[used:used + full, :] = part_in[:, column:column + LANES]
-        used += full
-    for column in range(0, full, LANES):
-        part.ref[used:used + units, :] = part_out[:, column:column + LANES]
-        used += units
-    if used < part.ref.shape[0]:
-        part.ref[used:, :] = jnp.zeros((part.ref.shape[0] - used, LANES), BF16)
-
-
-def point_kernel(groups, place_ref, feats, cots, w_in_t, w_out, w_in_own, w_out_own, act_own,
-                 gpre_own, x, out, grad_ref, pre, slope, act, gpre):
+    full, units = feats.shape[0], pre.shape[0]
+    hidden_block(w_in_t.get()[...], w_out.get()[...], feats, cots, pre, slope, act, gpre)
+    used, copies = 0, []
+    for values, height in ((dot_nt(feats[...], gpre[...]), full),
+                           (dot_nt(act[...], cots[...]), units)):
+        first = used
+        for column in range(0, values.shape[1], LANES):
+            stack[used:used + height, :] = values[:, column:column + LANES].astype(BF16)
+            used += height
+        copies.append(pltpu.make_async_copy(
+            stack.at[first:used], part.at[first:used], sems.at[len(copies)]))
+        copies[-1].start()
+    if used < part.shape[0]:
+        stack[used:, :] = jnp.zeros((part.shape[0] - used, LANES), BF16)
+        copies.append(pltpu.make_async_copy(stack.at[used:], part.at[used:], sems.at[2]))
+        copies[-1].start()
+    for copy in copies:
+        copy.wait()
+
+
+def point_kernel(feats, cots, w_in_t, w_out, w_in_own, w_out_own, x, out, grad_ref,
+                 pre, slope, act, gpre):
     units = pre.shape[0]
     feats, cots, w_in_t, w_out = feats.get(), cots.get(), w_in_t.get(), w_out.get()
-
-    def start(k):
-        return pl.multiple_of((place_ref[1] ^ k) * units, units)
-
     branch = grad = None
-    for k in range(1, groups):
-        part = pl.ds(start(k), units)
+    for at in range(0, w_out.shape[0], units):
+        part = slice(at, at + units)
         hidden_block(w_in_t[part, :], w_out[part, :], feats, cots, pre, slope, act, gpre)
         more = dot(w_out_own.get()[:, part], act[...])
         branch = more if branch is None else branch + more
         more = dot(w_in_own.get()[:, part], gpre[...])
         grad = more if grad is None else grad + more
-    mine = pl.ds(start(0), units)
-    branch = branch + dot(w_out_own.get()[:, mine], act_own.get()[...])
     out.ref[...] = (x.get()[...].astype(F32) + branch.astype(BF16).astype(F32)).astype(BF16)
     out.send()
-    grad = grad + dot(w_in_own.get()[:, mine], gpre_own.get()[...])
     grad_ref[...] = grad.astype(BF16)
 
 
-def prep_kernel(place_ref, w_in, w_out, w_in_t, w_in_own, w_out_own):
-    channels = w_in_own.ref.shape[0]
+def prep_kernel(place_ref, w_in, w_out, w_in_t, w_in_own, w_out_own, part_in_ref, part_out_ref):
+    channels, units = w_in_own.ref.shape[0], part_in_ref.shape[0]
     start = place_ref[1] * channels
+    share = pl.ds(pl.multiple_of(place_ref[1] * units, units), units)
     w_in, w_out = w_in.get(), w_out.get()
     w_in_own.ref[...] = w_in[pl.ds(pl.multiple_of(start, channels), channels), :]
     w_in_own.send()
     w_in_t.ref[...] = w_in[...].astype(F32).T.astype(BF16)
     w_in_t.send()
+    part_in_ref[...] = w_in_t.ref[share, :]
+    part_out_ref[...] = w_out[share, :]
     row = lax.broadcasted_iota(jnp.int32, (channels, w_out.shape[1]), 0)
     column = lax.broadcasted_iota(jnp.int32, (channels, w_out.shape[1]), 1)
     pick = jnp.where(column == row + start, 1.0, 0.0).astype(BF16)
@@ -307,46 +307,67 @@
 
 
 def join_kernel(place_ref, *refs):
-    pieces, out_ref, sems = refs[:-2], refs[-2], refs[-1]
-    channels = pieces[0].shape[0]
-    copies = []
+    pieces, out_ref = refs[:-1], refs[-1]
     for k, piece in enumerate(pieces):
+        piece = piece.get()
+        channels = piece.shape[0]
         start = pl.multiple_of((place_ref[1] ^ k) * channels, channels)
-        copies.append(pltpu.make_async_copy(piece, out_ref.at[pl.ds(start, channels)], sems.at[k]))
-    for copy in copies:
-        copy.start()
-    for copy in copies:
-        copy.wait()
-
-
-def back_kernel(edge, place_ref, nb_ref, rot_ref, grad, cot, padded, side, taps,
-                accum, border, tap_ref, d_row, d_side, turned_all, moved_all, gathered):
-    accum_ref, send_ref = accum.ref, border.ref
-    grad_ref, taps_ref = grad.get(), taps.get()
-    padded_ref, side_ref, cot_ref = padded.get(), side.get(), cot.get()
-    channels, pixels = grad_ref.shape
+        out_ref[pl.ds(start, channels), :] = piece[...]
+
+
+def tap_kernel(edge, grad, padded, side, tap_ref, turned_all, moved_all):
+    channels, pixels = grad.ref.shape
     wide = pixels + 2 * LANES
-    tiles, _, rim = send_ref.shape
-    slots = tap_ref.shape[0]
+    grad_ref = grad.get()
     moved_all[KSIZE * 16:, :] = jnp.zeros((LANES - KSIZE * 16, wide), BF16)
-    tap_ref[...] = jnp.zeros(tap_ref.shape, BF16)
     same = (lax.broadcasted_iota(jnp.int32, (16, KSIZE * LANES), 1) % 16
             == lax.broadcasted_iota(jnp.int32, (16, KSIZE * LANES), 0))
     line = lax.broadcasted_iota(jnp.int32, (KSIZE * LANES, LANES), 0)
     tap = lax.broadcasted_iota(jnp.int32, (KSIZE * LANES, LANES), 1)
     used = line % LANES < KSIZE * 16
     pick = jnp.where(used & (line // LANES * KSIZE + line % LANES // 16 == tap), 1.0, 0.0).astype(BF16)
-
-    for block in range(channels // 16):
-        at = block * 16
-        gs = grad_ref[at:at + 16, :].astype(F32)
-        xs = padded_ref[at:at + 16, :].astype(F32)
-        hs = side_ref[at:at + 16, :].astype(F32)
+    mask = {b: side_mask(b - HALO, (16, wide), edge) for b in range(KSIZE) if b != HALO}
+    lane = lax.broadcasted_iota(jnp.int32, (16, LANES), 1)
+    zeros = jnp.zeros((16, LANES), F32)
+    padded_ref, side_ref = padded.get(), side.get()
+    found = []
+    for at in range(0, channels, 16):
+        g = jnp.concatenate([zeros, grad_ref[at:at + 16, :].astype(F32), zeros], axis=1)
+        x = padded_ref[at:at + 16, :].astype(F32)
+        h = side_ref[at:at + 16, :].astype(F32)
+        for a in range(KSIZE):
+            shift = a - HALO
+            turned_all[a * 16:a * 16 + 16, :] = roll(g, shift * edge).astype(BF16)
+            moved = roll(jnp.where(mask[a], h, x), -shift) if shift else x
+            moved_all[a * 16:a * 16 + 16, :] = moved.astype(BF16)
+        products = dot_nt(turned_all[...], moved_all[...])
+        side_by_side = jnp.concatenate(
+            [products[a * 16:a * 16 + 16, :] for a in range(KSIZE)], axis=1)
+        taps = dot(jnp.where(same, side_by_side, 0.0).astype(BF16), pick)
+        place = at // 16 % 4
+        taps = jnp.where(lane // 32 == place, roll(taps, 32 * place), 0.0)
+        if place == 0:
+            found.append(taps)
+        else:
+            found[-1] = found[-1] + taps
+    tap_ref[...] = jnp.concatenate(found, axis=0).astype(BF16)
+
+
+def back_kernel(edge, place_ref, nb_ref, rot_ref, grad, cot, taps,
+                accum, border, d_row, d_side, gathered):
+    accum_ref, send_ref = accum.ref, border.ref
+    grad_ref, taps_ref = grad.get(), taps.get()
+    channels, pixels = grad_ref.shape
+    wide = pixels + 2 * LANES
+    tiles, _, rim = send_ref.shape
+    cot_ref = cot.get()
+
+    def block(i, carry):
+        at = pl.multiple_of(i * 16, 16)
+        gs = grad_ref[pl.ds(at, 16), :].astype(F32)
         zeros = jnp.zeros((8, LANES), F32)
-        turned_rows, moved_rows = [[] for _ in range(KSIZE)], [[] for _ in range(KSIZE)]
         rows, sides = [], []
         for half in (0, 8):
-            x, h = xs[half:half + 8], hs[half:half + 8]
             g = jnp.concatenate([zeros, gs[half:half + 8], zeros], axis=1)
             turned = [roll(g, (a - HALO) * edge) for a in range(KSIZE)]
             d_x = d_h = None
@@ -354,43 +375,29 @@
                 shift = b - HALO
                 back = None
                 for a in range(KSIZE):
-                    weight = taps_ref[a * KSIZE + b, at + half:at + half + 8, :]
+                    weight = taps_ref[a * KSIZE + b, pl.ds(at + half, 8), :]
                     term = jnp.tile(weight, (1, wide // LANES)) * turned[a]
                     back = term if back is None else back + term
                 back = roll(back, shift)
                 if shift:
-                    mask = side_mask(shift, x.shape, edge)
-                    moved_rows[b].append(roll(jnp.where(mask, h, x), -shift))
+                    mask = side_mask(shift, back.shape, edge)
                     inside = jnp.where(mask, 0.0, back)
                     outside = jnp.where(mask, back, 0.0)
                     d_h = outside if d_h is None else d_h + outside
                     d_x = inside if d_x is None else d_x + inside
                 else:
-                    moved_rows[b].append(x)
                     d_x = back if d_x is None else d_x + back
-            for a in range(KSIZE):
-                turned_rows[a].append(turned[a])
             rows.append(d_x)
             sides.append(d_h)
         d_x = jnp.concatenate(rows, axis=0)
-        accum_ref[at:at + 16, :] = (
-            d_x[:, LANES:LANES + pixels] + cot_ref[at:at + 16, :].astype(F32))
-        d_row[at:at + 16, :LANES] = d_x[:, :LANES].astype(BF16)
-        d_row[at:at + 16, LANES:] = d_x[:, LANES + pixels:].astype(BF16)
-        d_side[at:at + 16, :] = jnp.concatenate(sides, axis=0).astype(BF16)
-        for a in range(KSIZE):
-            turned_all[a * 16:a * 16 + 16, :] = jnp.concatenate(turned_rows[a], axis=0).astype(BF16)
-            moved_all[a * 16:a * 16 + 16, :] = jnp.concatenate(moved_rows[a], axis=0).astype(BF16)
-        products = dot_nt(turned_all[...], moved_all[...])
-        side_by_side = jnp.concatenate(
-            [products[a * 16:a * 16 + 16, :] for a in range(KSIZE)], axis=1)
-        found = dot(jnp.where(same, side_by_side, 0.0).astype(BF16), pick)
-        lane = lax.broadcasted_iota(jnp.int32, (16, LANES), 1)
-        place = block % 4
-        placed = jnp.where(lane // 32 == place, roll(found, 32 * place), 0.0)
-        slot = slice(block // 4 * 16, block // 4 * 16 + 16)
-        tap_ref[slot, :] = (tap_ref[slot, :].astype(F32) + placed).astype(BF16)
-
+        accum_ref[pl.ds(at, 16), :] = (
+            d_x[:, LANES:LANES + pixels] + cot_ref[pl.ds(at, 16), :].astype(F32))
+        d_row[pl.ds(at, 16), :LANES] = d_x[:, :LANES].astype(BF16)
+        d_row[pl.ds(at, 16), LANES:] = d_x[:, LANES + pixels:].astype(BF16)
+        d_side[pl.ds(at, 16), :] = jnp.concatenate(sides, axis=0).astype(BF16)
+        return carry
+
+    lax.fori_loop(0, channels // 16, block, 0)
     accum.send()
     first = place_ref[0] * 8
     nb = [nb_ref[first + d] for d in range(8)]
@@ -438,36 +445,43 @@
     lax.fori_loop(0, out.ref.shape[0], store, 0)
 
 
-def final_kernel(groups, share, channels, scale, place_ref, *refs):
-    pieces = refs[:groups]
-    g_in, g_out, g_tap_ref, buf_in, buf_out, all_taps, sems = refs[groups:]
+def final_kernel(which, last, share, channels, scale, place_ref, *refs):
+    count = len(which)
+    pieces, taps_in = refs[:count], refs[count]
+    g_in, g_out, g_tap_ref, buf_in, buf_out, sems = refs[-6:]
     full, units = buf_in.shape[1:]
     tiles, rows, _ = pieces[0].ref.shape
     copies = []
-    for k in range(groups):
-        piece = pieces[k].get()
+    all_taps = taps_in.get()[...] if last else jnp.zeros((full, LANES), F32)
+    row_of = lax.broadcasted_iota(jnp.int32, (full, LANES), 0)
+    for i, k in enumerate(which):
+        piece = pieces[i].get()
         owner = place_ref[1] ^ k
         start = pl.multiple_of(owner * units, units)
         for tile in range(tiles):
-            for row, count, column, at, into_in in chunks(tile, share, units, full):
-                values = piece[tile, row:row + count, :].astype(F32) * scale
+            for row, height, column, at, into_in in chunks(tile, share, units, full):
+                values = piece[tile, row:row + height, :].astype(F32) * scale
                 buffer = buf_in if into_in else buf_out
-                buffer[k, at:at + count, column:column + LANES] = values
+                buffer[i, at:at + height, column:column + LANES] = values
         copies.append(pltpu.make_async_copy(
-            buf_in.at[k], g_in.at[:, pl.ds(start, units)], sems.at[0, k]))
+            buf_in.at[i], g_in.at[:, pl.ds(start, units)], sems.at[0, i]))
         copies.append(pltpu.make_async_copy(
-            buf_out.at[k], g_out.at[pl.ds(start, units)], sems.at[1, k]))
+            buf_out.at[i], g_out.at[pl.ds(start, units)], sems.at[1, i]))
         for copy in copies[-2:]:
             copy.start()
         taps = piece[0, share:, :].astype(F32)
         for tile in range(1, tiles):
             taps = taps + piece[tile, share:, :].astype(F32)
-        taps = taps * scale
+        blocks = []
         for block in range(channels // 16):
             values = taps[block // 4 * 16:block // 4 * 16 + 16, :]
-            into = pl.ds(pl.multiple_of(owner * channels + block * 16, 16), 16)
-            all_taps[into, :] = roll(values, -32 * (block % 4))
-    g_tap_ref[...] = all_taps[...].T[:KSIZE * KSIZE, :]
+            blocks.append(roll(values, -32 * (block % 4)))
+        own = jnp.concatenate(blocks * (full // channels), axis=0)
+        all_taps = jnp.where(row_of // channels == owner, own, all_taps)
+    if last:
+        g_tap_ref[...] = all_taps.T[:KSIZE * KSIZE, :] * scale
+    else:
+        g_tap_ref[...] = all_taps
     for copy in copies:
         copy.wait()
 
@@ -516,66 +530,69 @@
 
     [rims] = call(functools.partial(pack_kernel, edge), [(x, FAR)],
                   [((tiles, channels, rim), BF16, FAR)])
-    rims, kernel, w_in, w_out = lax.optimization_barrier((rims, kernel, w_in, w_out))
+    _, kernel = lax.optimization_barrier((rims, kernel))
+    taps = jnp.broadcast_to(kernel.astype(F32)[:, :, None], (KSIZE * KSIZE, channels, LANES))
+    cot_pieces = gather_pieces(cot, groups)
+    w_in_t, w_in_own, w_out_own, part_in, part_out = call(
+        prep_kernel, [(place, SCALAR), (w_in, NEAR), (w_out, NEAR)],
+        [((hidden, full), BF16, FAR)] + [((channels, hidden), BF16, FAR)] * 2
+        + [((units, full), BF16, NEAR)] * 2, time=2.0, after=[rims])
+    [cots] = call(join_kernel, [(place, SCALAR)] + [(piece, NEAR) for piece in cot_pieces],
+                  [((full, pixels), BF16, NEAR)], time=0.6)
     rims = swap_rows(rims)
-    cot_pieces = gather_pieces(cot, groups)
-    taps = jnp.broadcast_to(kernel.astype(F32)[:, :, None], (KSIZE * KSIZE, channels, LANES))
-    w_in_t, w_in_own, w_out_own = call(
-        prep_kernel, [(place, SCALAR), (w_in, FAR), (w_out, FAR)],
-        [((hidden, full), BF16, FAR)] + [((channels, hidden), BF16, FAR)] * 2)
-    [cots] = call(join_kernel, [(place, SCALAR)] + [(piece, RAW) for piece in cot_pieces],
-                  [((full, pixels), BF16, RAW)], [pltpu.SemaphoreType.DMA((groups,))])
-    rims, cots, taps, w_in_t, w_in_own, w_out_own = lax.optimization_barrier(
-        (rims, cots, taps, w_in_t, w_in_own, w_out_own))
 
     here = [(place, SCALAR), (nb, SCALAR), (rot, SCALAR)]
     hid, padded, side = call(
         functools.partial(conv_kernel, edge), here + [(x, FAR), (rims, NEAR), (taps, NEAR)],
         [((channels, pixels), BF16, NEAR), ((channels, wide), BF16, FAR),
          ((channels, wide), BF16, FAR)],
-        [pltpu.VMEM((channels, len(SIDES) * rim), BF16)])
+        [pltpu.VMEM((channels, len(SIDES) * rim), BF16)], time=2.5)
     feats = lax.all_gather(hid, "chan", axis=0, tiled=True)
 
     used = 2 * full * units // LANES
     share = -(-used // (16 * tiles)) * 16
     tap_rows = -(-channels // 64) * 16
-    values = [pltpu.VMEM((units, pixels), F32)] * 2
-    part, act, gpre = call(
-        weight_kernel,
-        [(place, SCALAR), (feats, NEAR), (cots, FAR), (w_in_t, RAW), (w_out, RAW)],
-        [((tiles * share, LANES), BF16, FAR)] + [((units, pixels), BF16, FAR)] * 2,
-        values + [pltpu.VMEM((units, full), BF16)] * 2 + [pltpu.SemaphoreType.DMA((2,))])
+    values = [pltpu.VMEM((units, pixels), F32)] * 2 + [pltpu.VMEM((units, pixels), BF16)] * 2
+    [part] = call(
+        weight_kernel, [(feats, NEAR), (cots, NEAR), (part_in, NEAR), (part_out, NEAR)],
+        [((tiles * share, LANES), BF16, RAW)],
+        values + [pltpu.VMEM((tiles * share, LANES), BF16), pltpu.SemaphoreType.DMA((3,))],
+        time=2.2)
     part = swap_rows(part.reshape(tiles, share, LANES))
 
     outputs, grad_hid = call(
-        functools.partial(point_kernel, groups),
-        [(place, SCALAR), (feats, NEAR), (cots, FAR), (w_in_t, FAR), (w_out, FAR), (w_in_own, FAR),
-         (w_out_own, FAR), (act, FAR), (gpre, FAR), (x, FAR)],
-        [((channels, pixels), BF16, FAR), ((channels, pixels), BF16, NEAR)],
-        values + [pltpu.VMEM((units, pixels), BF16)] * 2)
-    accum, border, tap_part = call(
-        functools.partial(back_kernel, edge),
-        here + [(grad_hid, NEAR), (cot, FAR), (padded, FAR), (side, FAR), (taps, NEAR)],
-        [((channels, pixels), F32, FAR), ((tiles, channels, rim), BF16, FAR),
-         ((tap_rows, LANES), BF16, NEAR)],
-        [pltpu.VMEM((channels, 2 * LANES), BF16), pltpu.VMEM((channels, wide), BF16),
-         pltpu.VMEM((KSIZE * 16, wide), BF16), pltpu.VMEM((LANES, wide), BF16),
-         pltpu.VMEM((tiles, channels, rim), F32)])
-
+        point_kernel,
+        [(feats, NEAR), (cots, NEAR), (w_in_t, FAR), (w_out, FAR), (w_in_own, FAR),
+         (w_out_own, FAR), (x, FAR)],
+        [((channels, pixels), BF16, FAR), ((channels, pixels), BF16, NEAR)], values, time=5.5)
+    [tap_part] = call(
+        functools.partial(tap_kernel, edge), [(grad_hid, NEAR), (padded, FAR), (side, FAR)],
+        [((tap_rows, LANES), BF16, NEAR)],
+        [pltpu.VMEM((KSIZE * 16, wide), BF16), pltpu.VMEM((LANES, wide), BF16)], time=1.5)
     [mine] = call(sum_kernel, [(part, NEAR), (tap_part, NEAR)],
                   [((tiles, share + tap_rows, LANES), BF16, FAR)])
     weights = swap_rows(mine)
+
+    accum, border = call(
+        functools.partial(back_kernel, edge), here + [(grad_hid, NEAR), (cot, FAR), (taps, NEAR)],
+        [((channels, pixels), F32, FAR), ((tiles, channels, rim), BF16, FAR)],
+        [pltpu.VMEM((channels, 2 * LANES), BF16), pltpu.VMEM((channels, wide), BF16),
+         pltpu.VMEM((tiles, channels, rim), F32)], time=4.0, after=[mine])
     weights, border = lax.optimization_barrier((weights, border))
     border = swap_rows(border)
     pieces = gather_pieces(weights, groups)
-    grads = call(
-        functools.partial(final_kernel, groups, share, channels, scale),
-        [(place, SCALAR)] + [(piece, NEAR) for piece in pieces],
-        [((full, hidden), F32, RAW), ((hidden, full), F32, RAW),
-         ((KSIZE * KSIZE, full), F32, NEAR)],
-        [pltpu.VMEM((groups, full, units), F32), pltpu.VMEM((groups, units, full), F32),
-         pltpu.VMEM((full, LANES), F32), pltpu.SemaphoreType.DMA((2, groups))])
-    border, *grads = lax.optimization_barrier((border, *grads))
+    grads, ends = [], [(0, groups, 2), (1, groups, 2)]
+    for last, end in enumerate(ends):
+        which = list(range(*end))
+        tap_shape = (KSIZE * KSIZE, full) if last else (full, LANES)
+        grads = call(
+            functools.partial(final_kernel, which, last, share, channels, scale),
+            [(place, SCALAR)] + [(pieces[k], NEAR) for k in which]
+            + ([(grads[2], NEAR), (grads[0], RAW), (grads[1], RAW)] if last else []),
+            [((full, hidden), F32, RAW), ((hidden, full), F32, RAW), (tap_shape, F32, NEAR)],
+            [pltpu.VMEM((len(which), full, units), F32), pltpu.VMEM((len(which), units, full), F32),
+             pltpu.SemaphoreType.DMA((2, len(which)))],
+            time=1.3, aliases={2 + len(which): 0, 3 + len(which): 1} if last else None)
     [grad_in] = call(functools.partial(border_kernel, edge), [(border, NEAR), (accum, FAR)],
                      [((channels, pixels), BF16, FAR)])
     return (outputs[None], grad_in[None], *grads)

time: 91 us -> 80.1 us (0.88)
  blocking collectives: 23.5 us -> 7.2 us
  local copies, waits for them, and re-layouts: 12.6 us -> 1.14 us
  waiting for transfers between devices: 8.88 us -> 16.2 us
  starting transfers between devices: 19.9 us -> 24.8 us
  Pallas kernels: 24.5 us -> 29.2 us
    all_to_all x1 -> x0, blocking collectives: 16.1 us -> none  [swap_rows(): return lax.all_to_all(values, 'tile', 0, 0, tiled=True)]
    unnamed x42 -> x12, local copies, waits for them, and re-layouts: 12.1 us -> 0.71 us
    all_to_all x3 -> x4, waiting for transfers between devices: 2.14 us -> 12.1 us  [swap_rows(): return lax.all_to_all(values, 'tile', 0, 0, tiled=True)]
    all_to_all x3 -> x4, starting transfers between devices: 16.7 us -> 21.7 us  [swap_rows(): return lax.all_to_all(values, 'tile', 0, 0, tiled=True)]
    pallas_call x10 -> x12, Pallas kernels: 24.5 us -> 29.2 us  [call(): pl.pallas_call(run, out_shape=[pltpu.HBM(s, d) if p in (FAR, RAW) else ja...]
    ppermute x6, waiting for transfers between devices: 6.74 us -> 4.14 us  [gather_pieces(): pieces[k ^ bit] = lax.ppermute(pieces[k], 'chan', swap)]
  transfers between devices with their start and end apart: 9 -> 10, of which waited for: 4 -> 5; matrix products, arithmetic and copies ran while one was open for 0% -> 0% of each run, Pallas kernels for 18% -> 24%
where the time goes in v3:
time: 80.1 us; the launch traced here: 79.4 us
  Pallas kernels  29.2 us (36%)
  starting transfers between devices  24.8 us (31%)
  waiting for transfers between devices  16.2 us (20%)
  blocking collectives  7.2 us (9%)
  local copies, waits for them, and re-layouts  1.14 us (1%)
  between operations  0.82 us (1%)
    pallas_call x12, Pallas kernels, call(): pl.pallas_call(run, out_shape=[pltpu.HBM(s, d) if p in (FAR, RAW) else ja...  29.2 us
    all_to_all x4, starting transfers between devices, swap_rows(): return lax.all_to_all(values, 'tile', 0, 0, tiled=True)  21.7 us
    all_to_all x4, waiting for transfers between devices, swap_rows(): return lax.all_to_all(values, 'tile', 0, 0, tiled=True)  12.1 us
    all_gather x1, blocking collectives, body(): feats = lax.all_gather(hid, 'chan', axis=0, tiled=True)  7.2 us
    ppermute x6, waiting for transfers between devices, gather_pieces(): pieces[k ^ bit] = lax.ppermute(pieces[k], 'chan', swap)  4.14 us
    ppermute x6, starting transfers between devices, gather_pieces(): pieces[k ^ bit] = lax.ppermute(pieces[k], 'chan', swap)  3.11 us
  transfers between devices with their start and end apart: 10, of which 5 were waited for; matrix products, arithmetic and copies ran while one was open for 0% of the time, Pallas kernels for 24%

profile of v3, /device:TPU:0, one launch (start us, length us, event | category | flops | bytes accessed | tf_op | source)
XLA Modules:
  0.0 79.4 jit_solution(11969635228570198196)
XLA Ops:
  0.7 1.9 %shard_map.110.refs_3_ = bf16[8,64,256]{2,1,0:T(8,128)(2,1)} custom-call(bf16[64,1024]{1,0:T(8,128)(2,1)} %bitcast.12), custom_call_target="tpu_custom_call" | custom-call | flops 1000000000 | bytes 3500000 | tf_op jit(solution)/shard_map/pallas_call | solution.py:75
  2.6 7.4 %all-to-all-start = ((bf16[8,64,256]{2,1,0:T(8,128)(2,1)}), bf16[8,64,256]{2,1,0:T(8,128)(2,1)S(1)}, u32[]{:S(2)}, u32[]{:S(2)}) async-start(bf16[8,64,256]{2,1,0:T(8,128)(2,1)} %shard_map.110.refs_3_), calls=%async_computation | async-start | bytes 524288 | tf_op jit(solution)/shard_map/all_to_all | solution.py:514
  10.0 1.6 %collective-permute-start.1 = (bf16[64,1024]{1,0:T(8,128)(2,1)S(1)}, bf16[64,1024]{1,0:T(8,128)(2,1)S(1)}, u32[]{:S(2)}, u32[]{:S(2)}) collective-permute-start(bf16[64,1024]{1,0:T(8,128)(2,1)S(1)} %bitcast.8), channel_id=1, source_target_pairs={{0,2},{1,3},{2,0},{3,1},{4,6},{5,7},{6,4},{7,5},{8,10},{9,11},{10,... | collective-permute-start | bytes 393224 | tf_op jit(solution)/shard_map/ppermute | solution.py:508
  11.5 0.7 copy-done.4
  12.5 2.5 %collective-permute-done.1.refs_3_ = bf16[64,1024]{1,0:T(8,128)(2,1)S(1)} collective-permute-done((bf16[64,1024]{1,0:T(8,128)(2,1)S(1)}, bf16[64,1024]{1,0:T(8,128)(2,1)S(1)}, u32[]{:S(2)}, u32[]{:S(2)}) %collective-permute-start.1) | collective-permute-done | bytes 131104 | tf_op jit(solution)/shard_map/ppermute | solution.py:508
  15.0 1.7 %shard_map.113 = (bf16[1024,256]{1,0:T(8,128)(2,1)}, bf16[64,1024]{1,0:T(8,128)(2,1)}, bf16[64,1024]{1,0:T(8,128)(2,1)}, bf16[256,256]{1,0:T(8,128)(2,1)S(1)}, bf16[256,256]{1,0:T(8,128)(2,1)S(1)}) custom-call(s32[2]{0:T(128)S(1)} %pad_add_fusion.refs_0_, bf16[256,1024]{1,0:T(8,128)(2,1)S(1)} %copy-done, bf16[1024,256]{1,0:T(8,128)(2,1)S(1)} %copy-done.1, ...), custom_call_target="tpu_custom_call" | custom-call | flops 2000000000 | bytes 7000000 | tf_op jit(solution)/shard_map/pallas_call | solution.py:75
  17.3 1.6 %all-to-all-done.refs_4_ = bf16[8,64,256]{2,1,0:T(8,128)(2,1)S(1)} async-done(((bf16[8,64,256]{2,1,0:T(8,128)(2,1)}), bf16[8,64,256]{2,1,0:T(8,128)(2,1)S(1)}, u32[]{:S(2)}, u32[]{:S(2)}) %all-to-all-start) | async-done | bytes 262176 | tf_op jit(solution)/shard_map/all_to_all | solution.py:514
  19.1 2.8 %shard_map.111 = (bf16[64,1024]{1,0:T(8,128)(2,1)S(1)}, bf16[64,1280]{1,0:T(8,128)(2,1)}, bf16[64,1280]{1,0:T(8,128)(2,1)}) custom-call(s32[2]{0:T(128)S(1)} %pad_add_fusion.refs_0_, s32[64]{0:T(128)S(1)} %reshape.20.refs_1_, s32[64]{0:T(128)S(1)} %reshape.21.refs_2_, bf16[64,1024]{1,0:T(8,128)(2,1)} %bitcast.13, ...), custom_call_target="tpu_custom_call" | custom-call | flops 2500000000 | bytes 8750000 | tf_op jit(solution)/shard_map/pallas_call | solution.py:75
  21.9 7.2 %all_gather.3.refs_0_ = bf16[256,1024]{1,0:T(8,128)(2,1)S(1)} all-gather(bf16[64,1024]{1,0:T(8,128)(2,1)S(1)} %get-tuple-element.27), channel_id=1, replica_groups=mesh['tile'=8,'chan'=4] {'chan'}, dimensions={0}, use_global_device_ids=true | all-gather | bytes 655360 | tf_op jit(solution)/shard_map/all_gather | solution.py:550
  29.1 2.2 %shard_map.115 = bf16[1024,128]{1,0:T(8,128)(2,1)} custom-call(bf16[256,1024]{1,0:T(8,128)(2,1)S(1)} %all_gather.3.refs_0_, bf16[256,1024]{1,0:T(8,128)(2,1)S(1)} %shard_map.112.refs_1_, bf16[256,256]{1,0:T(8,128)(2,1)S(1)} %get-tuple-element.32.refs_2_, bf16[256,256]{1,0:T(8,128)(2,1)S(1)} %get-tuple-element.33.refs_3_), custom_call_target="tpu_custom_call" | custom-call | flops 2200000000 | bytes 7700000 | tf_op jit(solution)/shard_map/pallas_call | solution.py:75
  31.3 4.7 %all-to-all-start.1 = ((bf16[8,128,128]{2,1,0:T(8,128)(2,1)}), bf16[8,128,128]{2,1,0:T(8,128)(2,1)S(1)}, u32[]{:S(2)}, u32[]{:S(2)}) async-start(bf16[8,128,128]{2,1,0:T(8,128)(2,1)} %bitcast.11), calls=%async_computation.1 | async-start | bytes 524288 | tf_op jit(solution)/shard_map/all_to_all | solution.py:514
  36.0 6.9 %shard_map.114 = (bf16[64,1024]{1,0:T(8,128)(2,1)}, bf16[64,1024]{1,0:T(8,128)(2,1)S(1)}) custom-call(bf16[256,1024]{1,0:T(8,128)(2,1)S(1)} %all_gather.3.refs_0_, bf16[256,1024]{1,0:T(8,128)(2,1)S(1)} %shard_map.112.refs_1_, bf16[1024,256]{1,0:T(8,128)(2,1)} %get-tuple-element.28.refs_2_, bf16[1024,256]{1,0:T(8,128)(2,1)} %refs_3_.1, ...), custom_call_target="tpu_custom_call" | custom-call | flops 5500000256 | bytes 19250000 | tf_op jit(solution)/shard_map/pallas_call | solution.py:75
  42.9 2.6 %shard_map.116.refs_1_ = bf16[16,128]{1,0:T(8,128)(2,1)S(1)} custom-call(bf16[64,1024]{1,0:T(8,128)(2,1)S(1)} %get-tuple-element.34.refs_0_.refs_3_, bf16[64,1280]{1,0:T(8,128)(2,1)} %get-tuple-element.35.refs_1_, bf16[64,1280]{1,0:T(8,128)(2,1)} %get-tuple-element.36.refs_2_), custom_call_target="tpu_custom_call" | custom-call | flops 1500000000 | bytes 5250000 | tf_op jit(solution)/shard_map/pallas_call | solution.py:75
  45.6 0.8 %shard_map.117.refs_6_ = bf16[8,144,128]{2,1,0:T(8,128)(2,1)} custom-call(bf16[8,128,128]{2,1,0:T(8,128)(2,1)S(1)} %all-to-all-done.1.refs_0_, bf16[16,128]{1,0:T(8,128)(2,1)S(1)} %shard_map.116.refs_1_), custom_call_target="tpu_custom_call" | custom-call | flops 1000000000 | bytes 3500000 | tf_op jit(solution)/shard_map/pallas_call | solution.py:75
  46.4 6.0 %all-to-all-start.2 = ((bf16[8,144,128]{2,1,0:T(8,128)(2,1)}), bf16[8,144,128]{2,1,0:T(8,128)(2,1)S(1)}, u32[]{:S(2)}, u32[]{:S(2)}) async-start(bf16[8,144,128]{2,1,0:T(8,128)(2,1)} %shard_map.117.refs_6_), calls=%async_computation.2 | async-start | bytes 589824 | tf_op jit(solution)/shard_map/all_to_all | solution.py:514
  52.4 4.2 %shard_map.118 = (f32[64,1024]{1,0:T(8,128)}, bf16[8,64,256]{2,1,0:T(8,128)(2,1)}) custom-call(s32[2]{0:T(128)S(1)} %pad_add_fusion.refs_0_, s32[64]{0:T(128)S(1)} %reshape.20.refs_1_, s32[64]{0:T(128)S(1)} %reshape.21.refs_2_, bf16[64,1024]{1,0:T(8,128)(2,1)S(1)} %get-tuple-element.34.refs_0_.refs_3_, bf16[64,1024]{1,0:T(8,128)(2,1)} %bitcast.7, ...), custom_call_target="tpu_custom_call" | custom-call | flops 4000000000 | bytes 14000000 | tf_op jit(solution)/shard_map/pallas_call | solution.py:75
  56.7 5.3 %all-to-all-done.2.refs_1_ = bf16[8,144,128]{2,1,0:T(8,128)(2,1)S(1)} async-done(((bf16[8,144,128]{2,1,0:T(8,128)(2,1)}), bf16[8,144,128]{2,1,0:T(8,128)(2,1)S(1)}, u32[]{:S(2)}, u32[]{:S(2)}) %all-to-all-start.2) | async-done | bytes 294944 | tf_op jit(solution)/shard_map/all_to_all | solution.py:514
  62.0 1.5 %collective-permute-start.4 = (bf16[8,144,128]{2,1,0:T(8,128)(2,1)S(1)}, bf16[8,144,128]{2,1,0:T(8,128)(2,1)S(1)}, u32[]{:S(2)}, u32[]{:S(2)}) collective-permute-start(bf16[8,144,128]{2,1,0:T(8,128)(2,1)S(1)} %all-to-all-done.2.refs_1_), channel_id=1, source_target_pairs={{0,2},{1,3},{2,0},{3,1},{4,6},{5,7},{6,4},{7,5},{8,10},{9,11},{10,... | collective-permute-start | bytes 884744 | tf_op jit(solution)/shard_map/ppermute | solution.py:508
  63.5 3.6 %all-to-all-start.3 = ((bf16[8,64,256]{2,1,0:T(8,128)(2,1)}), bf16[8,64,256]{2,1,0:T(8,128)(2,1)S(1)}, u32[]{:S(2)}, u32[]{:S(2)}) async-start(bf16[8,64,256]{2,1,0:T(8,128)(2,1)} %get-tuple-element.38), calls=%async_computation.3 | async-start | bytes 524288 | tf_op jit(solution)/shard_map/all_to_all | solution.py:514
  67.1 1.6 %collective-permute-done.4.refs_2_ = bf16[8,144,128]{2,1,0:T(8,128)(2,1)S(1)} collective-permute-done((bf16[8,144,128]{2,1,0:T(8,128)(2,1)S(1)}, bf16[8,144,128]{2,1,0:T(8,128)(2,1)S(1)}, u32[]{:S(2)}, u32[]{:S(2)}) %collective-permute-start.4) | collective-permute-done | bytes 294944 | tf_op jit(solution)/shard_map/ppermute | solution.py:508
  68.7 1.6 %shard_map.120 = (f32[256,1024]{1,0:T(8,128)}, f32[1024,256]{1,0:T(8,128)}, f32[256,128]{1,0:T(8,128)S(1)}) custom-call(s32[2]{0:T(128)S(1)} %pad_add_fusion.refs_0_, bf16[8,144,128]{2,1,0:T(8,128)(2,1)S(1)} %all-to-all-done.2.refs_1_, bf16[8,144,128]{2,1,0:T(8,128)(2,1)S(1)} %collective-permute-done.4.refs_2_), custom_call_target="tpu_custom_call" | custom-call | flops 1300000000 | bytes 4550000 | tf_op jit(solution)/shard_map/pallas_call | solution.py:75
  70.3 5.2 %all-to-all-done.3.refs_0_ = bf16[8,64,256]{2,1,0:T(8,128)(2,1)S(1)} async-done(((bf16[8,64,256]{2,1,0:T(8,128)(2,1)}), bf16[8,64,256]{2,1,0:T(8,128)(2,1)S(1)}, u32[]{:S(2)}, u32[]{:S(2)}) %all-to-all-start.3) | async-done | bytes 262176 | tf_op jit(solution)/shard_map/all_to_all | solution.py:514
  75.5 1.6 %shard_map.119 = bf16[64,1024]{1,0:T(8,128)(2,1)} custom-call(bf16[8,64,256]{2,1,0:T(8,128)(2,1)S(1)} %all-to-all-done.3.refs_0_, f32[64,1024]{1,0:T(8,128)} %get-tuple-element.39.refs_1_), custom_call_target="tpu_custom_call" | custom-call | flops 1000000000 | bytes 3500000 | tf_op jit(solution)/shard_map/pallas_call | solution.py:75
  77.2 2.3 %shard_map.121 = (f32[256,1024]{1,0:T(8,128)}, f32[1024,256]{1,0:T(8,128)}, f32[25,256]{1,0:T(8,128)}) custom-call(s32[2]{0:T(128)S(1)} %pad_add_fusion.refs_0_, bf16[8,144,128]{2,1,0:T(8,128)(2,1)S(1)} %collective-permute-done.3.refs_1_, bf16[8,144,128]{2,1,0:T(8,128)(2,1)S(1)} %collective-permute-done.5.refs_2_, ...), custom_call_target="tpu_custom_call", output_to_operand_aliasing={{0}: (4, {}), {1}: (5, {})} | custom-call | flops 1300000000 | bytes 4550000 | tf_op jit(solution)/shard_map/pallas_call | solution.py:75
  (25 shorter events, 1.1 us)
Async XLA Ops:
  0.6 9.3 %copy-start.2 = (bf16[1,64,1024]{2,1,0:T(8,128)(2,1)S(1)}, bf16[1,64,1024]{2,1,0:T(8,128)(2,1)}, u32[]{:S(2)}) copy-start(bf16[1,64,1024]{2,1,0:T(8,128)(2,1)} %param.8) | copy-start | bytes 393220
  0.6 14.3 %copy-start.1 = (bf16[1024,256]{1,0:T(8,128)(2,1)S(1)}, bf16[1024,256]{1,0:T(8,128)(2,1)}, u32[]{:S(2)}) copy-start(bf16[1024,256]{1,0:T(8,128)(2,1)} %refs_3_.1) | copy-start | bytes 1572868
  2.5 12.5 %copy-start = (bf16[256,1024]{1,0:T(8,128)(2,1)S(1)}, bf16[256,1024]{1,0:T(8,128)(2,1)}, u32[]{:S(2)}) copy-start(bf16[256,1024]{1,0:T(8,128)(2,1)} %refs_1_.1) | copy-start | bytes 1572868
  2.6 16.3 %all-to-all-start = ((bf16[8,64,256]{2,1,0:T(8,128)(2,1)}), bf16[8,64,256]{2,1,0:T(8,128)(2,1)S(1)}, u32[]{:S(2)}, u32[]{:S(2)}) async-start(bf16[8,64,256]{2,1,0:T(8,128)(2,1)} %shard_map.110.refs_3_), calls=%async_computation | async-start | bytes 524288 | tf_op jit(solution)/shard_map/all_to_all | solution.py:514
  10.0 5.0 %collective-permute-start.1 = (bf16[64,1024]{1,0:T(8,128)(2,1)S(1)}, bf16[64,1024]{1,0:T(8,128)(2,1)S(1)}, u32[]{:S(2)}, u32[]{:S(2)}) collective-permute-start(bf16[64,1024]{1,0:T(8,128)(2,1)S(1)} %bitcast.8), channel_id=1, source_target_pairs={{0,2},{1,3},{2,0},{3,1},{4,6},{5,7},{6,4},{7,5},{8,10},{9,11},{10,... | collective-permute-start | bytes 393224 | tf_op jit(solution)/shard_map/ppermute | solution.py:508
  11.5 5.1 %collective-permute-start = (bf16[64,1024]{1,0:T(8,128)(2,1)S(1)}, bf16[64,1024]{1,0:T(8,128)(2,1)S(1)}, u32[]{:S(2)}, u32[]{:S(2)}) collective-permute-start(bf16[64,1024]{1,0:T(8,128)(2,1)S(1)} %bitcast.9), channel_id=1, source_target_pairs={{0,1},{1,0},{2,3},{3,2},{4,5},{5,4},{6,7},{7,6},{8,9},{9,8},{10,11... | collective-permute-start | bytes 393224 | tf_op jit(solution)/shard_map/ppermute | solution.py:508
  11.5 0.7 copy-start.4
  11.5 0.8 copy-start.5
  15.0 1.7 %collective-permute-start.2 = (bf16[64,1024]{1,0:T(8,128)(2,1)S(1)}, bf16[64,1024]{1,0:T(8,128)(2,1)S(1)}, u32[]{:S(2)}, u32[]{:S(2)}) collective-permute-start(bf16[64,1024]{1,0:T(8,128)(2,1)S(1)} %collective-permute-done.1.refs_3_), channel_id=1, source_target_pairs={{0,1},{1,0},{2,3},{3,2},{4,5},{5,4},{6,7},{7,6},{8,9},{9,8},{10,11... | collective-permute-start | bytes 393224 | tf_op jit(solution)/shard_map/ppermute | solution.py:508
  16.7 2.2 %copy-start.3 = (bf16[25,64]{1,0:T(8,128)(2,1)S(1)}, bf16[25,64]{1,0:T(8,128)(2,1)}, u32[]{:S(2)}) copy-start(bf16[25,64]{1,0:T(8,128)(2,1)} %param.9) | copy-start | bytes 9604
  31.3 14.2 %all-to-all-start.1 = ((bf16[8,128,128]{2,1,0:T(8,128)(2,1)}), bf16[8,128,128]{2,1,0:T(8,128)(2,1)S(1)}, u32[]{:S(2)}, u32[]{:S(2)}) async-start(bf16[8,128,128]{2,1,0:T(8,128)(2,1)} %bitcast.11), calls=%async_computation.1 | async-start | bytes 524288 | tf_op jit(solution)/shard_map/all_to_all | solution.py:514
  46.4 15.6 %all-to-all-start.2 = ((bf16[8,144,128]{2,1,0:T(8,128)(2,1)}), bf16[8,144,128]{2,1,0:T(8,128)(2,1)S(1)}, u32[]{:S(2)}, u32[]{:S(2)}) async-start(bf16[8,144,128]{2,1,0:T(8,128)(2,1)} %shard_map.117.refs_6_), calls=%async_computation.2 | async-start | bytes 589824 | tf_op jit(solution)/shard_map/all_to_all | solution.py:514
  62.0 6.7 %collective-permute-start.4 = (bf16[8,144,128]{2,1,0:T(8,128)(2,1)S(1)}, bf16[8,144,128]{2,1,0:T(8,128)(2,1)S(1)}, u32[]{:S(2)}, u32[]{:S(2)}) collective-permute-start(bf16[8,144,128]{2,1,0:T(8,128)(2,1)S(1)} %all-to-all-done.2.refs_1_), channel_id=1, source_target_pairs={{0,2},{1,3},{2,0},{3,1},{4,6},{5,7},{6,4},{7,5},{8,10},{9,11},{10,... | collective-permute-start | bytes 884744 | tf_op jit(solution)/shard_map/ppermute | solution.py:508
  63.5 12.0 %all-to-all-start.3 = ((bf16[8,64,256]{2,1,0:T(8,128)(2,1)}), bf16[8,64,256]{2,1,0:T(8,128)(2,1)S(1)}, u32[]{:S(2)}, u32[]{:S(2)}) async-start(bf16[8,64,256]{2,1,0:T(8,128)(2,1)} %get-tuple-element.38), calls=%async_computation.3 | async-start | bytes 524288 | tf_op jit(solution)/shard_map/all_to_all | solution.py:514
  67.1 10.0 %collective-permute-start.3 = (bf16[8,144,128]{2,1,0:T(8,128)(2,1)S(1)}, bf16[8,144,128]{2,1,0:T(8,128)(2,1)S(1)}, u32[]{:S(2)}, u32[]{:S(2)}) collective-permute-start(bf16[8,144,128]{2,1,0:T(8,128)(2,1)S(1)} %all-to-all-done.2.refs_1_), channel_id=1, source_target_pairs={{0,1},{1,0},{2,3},{3,2},{4,5},{5,4},{6,7},{7,6},{8,9},{9,8},{10,11... | collective-permute-start | bytes 884744 | tf_op jit(solution)/shard_map/ppermute | solution.py:508
  68.7 8.4 %collective-permute-start.5 = (bf16[8,144,128]{2,1,0:T(8,128)(2,1)S(1)}, bf16[8,144,128]{2,1,0:T(8,128)(2,1)S(1)}, u32[]{:S(2)}, u32[]{:S(2)}) collective-permute-start(bf16[8,144,128]{2,1,0:T(8,128)(2,1)S(1)} %collective-permute-done.4.refs_2_), channel_id=1, source_target_pairs={{0,1},{1,0},{2,3},{3,2},{4,5},{5,4},{6,7},{7,6},{8,9},{9,8},{10,11... | collective-permute-start | bytes 884744 | tf_op jit(solution)/shard_map/ppermute | solution.py:508

commit v4 on v3

--- a/solution.py
+++ b/solution.py
@@ -43,7 +43,7 @@
 
 
 def call(kernel, ins, outs, scratch=(), time=1.0, after=(), aliases=None, limit=16):
-    ins = list(ins) + [(a, RAW) for a in after]
+    ins = list(ins) + list(after)
     buffers = []
     for shape, dtype, place in [(a.shape, a.dtype, p) for a, p in ins] + list(outs):
         if place == FAR:
@@ -176,10 +176,14 @@
     return values if shift % size == 0 else pltpu.roll(values, shift % size, axis=1)
 
 
-def pack_kernel(edge, x, rims):
+def pack_kernel(edge, x, rims, rim, sems):
     pick = one_hot(rim_pixels(edge), edge * edge)
-    rim = dot(x.get()[...], pick).astype(BF16)
-    rims.ref[...] = jnp.broadcast_to(rim[None], rims.ref.shape)
+    rim[...] = dot(x.get()[...], pick).astype(BF16)
+    copies = [pltpu.make_async_copy(rim, rims.at[t], sems.at[t]) for t in range(rims.shape[0])]
+    for copy in copies:
+        copy.start()
+    for copy in copies:
+        copy.wait()
 
 
 def conv_kernel(edge, place_ref, nb_ref, rot_ref, x, rims, taps,
@@ -189,9 +193,8 @@
     channels, pixels = hidden_ref.shape
     wide = pixels + 2 * LANES
     rim = rims_ref.shape[2]
-    first = place_ref[0] * 8
-    nb = [nb_ref[first + d] for d in range(8)]
-    rot = [rot_ref[first + d] for d in range(8)]
+    nb = [nb_ref[place_ref[0], d] for d in range(8)]
+    rot = [rot_ref[place_ref[0], d] for d in range(8)]
     top, low = row_halo_maps(rot[1], rot[6], edge)
     padded_ref[:, :LANES] = dot(rims_ref[nb[1]], top).astype(BF16)
     padded_ref[:, LANES + pixels:] = dot(rims_ref[nb[6]], low).astype(BF16)
@@ -272,38 +275,35 @@
         copy.wait()
 
 
-def point_kernel(feats, cots, w_in_t, w_out, w_in_own, w_out_own, x, out, grad_ref,
-                 pre, slope, act, gpre):
-    units = pre.shape[0]
+def point_kernel(edge, place_ref, feats, cots, w_in, w_in_t, w_out, x, padded, side,
+                 out, grad_ref, tap_ref, pre, slope, act, gpre, turned_all, moved_all):
+    units, channels = pre.shape[0], grad_ref.shape[0]
     feats, cots, w_in_t, w_out = feats.get(), cots.get(), w_in_t.get(), w_out.get()
+    start = place_ref[1] * channels
+    own = pl.ds(pl.multiple_of(start, channels), channels)
+    row = lax.broadcasted_iota(jnp.int32, (channels, w_out.shape[1]), 0)
+    column = lax.broadcasted_iota(jnp.int32, (channels, w_out.shape[1]), 1)
+    pick = jnp.where(column == row + start, 1.0, 0.0).astype(BF16)
     branch = grad = None
     for at in range(0, w_out.shape[0], units):
         part = slice(at, at + units)
         hidden_block(w_in_t[part, :], w_out[part, :], feats, cots, pre, slope, act, gpre)
-        more = dot(w_out_own.get()[:, part], act[...])
+        more = dot(dot_nt(pick, w_out[part, :]).astype(BF16), act[...])
         branch = more if branch is None else branch + more
-        more = dot(w_in_own.get()[:, part], gpre[...])
+        more = dot(w_in.get()[own, part], gpre[...])
         grad = more if grad is None else grad + more
     out.ref[...] = (x.get()[...].astype(F32) + branch.astype(BF16).astype(F32)).astype(BF16)
     out.send()
     grad_ref[...] = grad.astype(BF16)
-
-
-def prep_kernel(place_ref, w_in, w_out, w_in_t, w_in_own, w_out_own, part_in_ref, part_out_ref):
-    channels, units = w_in_own.ref.shape[0], part_in_ref.shape[0]
-    start = place_ref[1] * channels
-    share = pl.ds(pl.multiple_of(place_ref[1] * units, units), units)
-    w_in, w_out = w_in.get(), w_out.get()
-    w_in_own.ref[...] = w_in[pl.ds(pl.multiple_of(start, channels), channels), :]
-    w_in_own.send()
-    w_in_t.ref[...] = w_in[...].astype(F32).T.astype(BF16)
-    w_in_t.send()
-    part_in_ref[...] = w_in_t.ref[share, :]
-    part_out_ref[...] = w_out[share, :]
-    row = lax.broadcasted_iota(jnp.int32, (channels, w_out.shape[1]), 0)
-    column = lax.broadcasted_iota(jnp.int32, (channels, w_out.shape[1]), 1)
-    pick = jnp.where(column == row + start, 1.0, 0.0).astype(BF16)
-    w_out_own.ref[...] = dot_nt(pick, w_out[...]).astype(BF16)
+    tap_terms(edge, grad_ref, padded.get(), side.get(), tap_ref, turned_all, moved_all)
+
+
+def prep_kernel(place_ref, w_in, w_out, w_in_t_ref, part_in_ref, part_out_ref):
+    w_in_t_ref[...] = w_in.get()[...].astype(F32).T.astype(BF16)
+    units = part_in_ref.shape[0]
+    mine = pl.ds(pl.multiple_of(place_ref[1] * units, units), units)
+    part_in_ref[...] = w_in_t_ref[mine, :]
+    part_out_ref[...] = w_out.get()[mine, :]
 
 
 def join_kernel(place_ref, *refs):
@@ -315,10 +315,9 @@
         out_ref[pl.ds(start, channels), :] = piece[...]
 
 
-def tap_kernel(edge, grad, padded, side, tap_ref, turned_all, moved_all):
-    channels, pixels = grad.ref.shape
+def tap_terms(edge, grad_ref, padded_ref, side_ref, tap_ref, turned_all, moved_all):
+    channels, pixels = grad_ref.shape
     wide = pixels + 2 * LANES
-    grad_ref = grad.get()
     moved_all[KSIZE * 16:, :] = jnp.zeros((LANES - KSIZE * 16, wide), BF16)
     same = (lax.broadcasted_iota(jnp.int32, (16, KSIZE * LANES), 1) % 16
             == lax.broadcasted_iota(jnp.int32, (16, KSIZE * LANES), 0))
@@ -329,7 +328,6 @@
     mask = {b: side_mask(b - HALO, (16, wide), edge) for b in range(KSIZE) if b != HALO}
     lane = lax.broadcasted_iota(jnp.int32, (16, LANES), 1)
     zeros = jnp.zeros((16, LANES), F32)
-    padded_ref, side_ref = padded.get(), side.get()
     found = []
     for at in range(0, channels, 16):
         g = jnp.concatenate([zeros, grad_ref[at:at + 16, :].astype(F32), zeros], axis=1)
@@ -353,14 +351,13 @@
     tap_ref[...] = jnp.concatenate(found, axis=0).astype(BF16)
 
 
-def back_kernel(edge, place_ref, nb_ref, rot_ref, grad, cot, taps,
+def back_kernel(edge, place_ref, nb_ref, rot_ref, grad, taps,
                 accum, border, d_row, d_side, gathered):
     accum_ref, send_ref = accum.ref, border.ref
     grad_ref, taps_ref = grad.get(), taps.get()
     channels, pixels = grad_ref.shape
     wide = pixels + 2 * LANES
     tiles, _, rim = send_ref.shape
-    cot_ref = cot.get()
 
     def block(i, carry):
         at = pl.multiple_of(i * 16, 16)
@@ -390,8 +387,7 @@
             rows.append(d_x)
             sides.append(d_h)
         d_x = jnp.concatenate(rows, axis=0)
-        accum_ref[pl.ds(at, 16), :] = (
-            d_x[:, LANES:LANES + pixels] + cot_ref[pl.ds(at, 16), :].astype(F32))
+        accum_ref[pl.ds(at, 16), :] = d_x[:, LANES:LANES + pixels]
         d_row[pl.ds(at, 16), :LANES] = d_x[:, :LANES].astype(BF16)
         d_row[pl.ds(at, 16), LANES:] = d_x[:, LANES + pixels:].astype(BF16)
         d_side[pl.ds(at, 16), :] = jnp.concatenate(sides, axis=0).astype(BF16)
@@ -399,9 +395,8 @@
 
     lax.fori_loop(0, channels // 16, block, 0)
     accum.send()
-    first = place_ref[0] * 8
-    nb = [nb_ref[first + d] for d in range(8)]
-    rot = [rot_ref[first + d] for d in range(8)]
+    nb = [nb_ref[place_ref[0], d] for d in range(8)]
+    rot = [rot_ref[place_ref[0], d] for d in range(8)]
     gathered[...] = jnp.zeros(gathered.shape, F32)
     top, low = row_halo_maps(rot[1], rot[6], edge)
     gathered[nb[1]] += dot_nt(d_row[:, :LANES], top)
@@ -418,12 +413,13 @@
     lax.fori_loop(0, tiles, store, 0)
 
 
-def border_kernel(edge, recv, accum, grad):
+def border_kernel(edge, recv, accum, cot, grad):
     rims = total_of(recv.get())
     high = rims.astype(BF16)
     low = (rims - high.astype(F32)).astype(BF16)
     pick = one_hot(rim_pixels(edge), edge * edge)
     added = dot_nt(high, pick) + dot_nt(low, pick)
+    added = added + cot.get()[...].astype(F32)
     grad.ref[...] = (accum.get()[...] + added).astype(BF16)
 
 
@@ -458,17 +454,15 @@
         piece = pieces[i].get()
         owner = place_ref[1] ^ k
         start = pl.multiple_of(owner * units, units)
-        for tile in range(tiles):
-            for row, height, column, at, into_in in chunks(tile, share, units, full):
-                values = piece[tile, row:row + height, :].astype(F32) * scale
-                buffer = buf_in if into_in else buf_out
-                buffer[i, at:at + height, column:column + LANES] = values
-        copies.append(pltpu.make_async_copy(
-            buf_in.at[i], g_in.at[:, pl.ds(start, units)], sems.at[0, i]))
-        copies.append(pltpu.make_async_copy(
-            buf_out.at[i], g_out.at[pl.ds(start, units)], sems.at[1, i]))
-        for copy in copies[-2:]:
-            copy.start()
+        for in_in, buffer, target in ((True, buf_in, g_in.at[:, pl.ds(start, units)]),
+                                      (False, buf_out, g_out.at[pl.ds(start, units)])):
+            for tile in range(tiles):
+                for row, height, column, at, into_in in chunks(tile, share, units, full):
+                    if into_in == in_in:
+                        values = piece[tile, row:row + height, :].astype(F32) * scale
+                        buffer[i, at:at + height, column:column + LANES] = values
+            copies.append(pltpu.make_async_copy(buffer.at[i], target, sems.at[int(in_in), i]))
+            copies[-1].start()
         taps = piece[0, share:, :].astype(F32)
         for tile in range(1, tiles):
             taps = taps + piece[tile, share:, :].astype(F32)
@@ -525,59 +519,59 @@
     units = hidden // groups
     scale = (tiles * pixels) ** -0.5
     place = jnp.stack([lax.axis_index("tile"), lax.axis_index("chan")]).astype(jnp.int32)
-    nb, rot = neighbours.reshape(-1), rotations.reshape(-1)
     x, cot = inputs[0], grad_out[0]
 
     [rims] = call(functools.partial(pack_kernel, edge), [(x, FAR)],
-                  [((tiles, channels, rim), BF16, FAR)])
+                  [((tiles, channels, rim), BF16, RAW)],
+                  [pltpu.VMEM((channels, rim), BF16), pltpu.SemaphoreType.DMA((tiles,))])
     _, kernel = lax.optimization_barrier((rims, kernel))
     taps = jnp.broadcast_to(kernel.astype(F32)[:, :, None], (KSIZE * KSIZE, channels, LANES))
     cot_pieces = gather_pieces(cot, groups)
-    w_in_t, w_in_own, w_out_own, part_in, part_out = call(
+    w_in_t, part_in, part_out = call(
         prep_kernel, [(place, SCALAR), (w_in, NEAR), (w_out, NEAR)],
-        [((hidden, full), BF16, FAR)] + [((channels, hidden), BF16, FAR)] * 2
-        + [((units, full), BF16, NEAR)] * 2, time=2.0, after=[rims])
-    [cots] = call(join_kernel, [(place, SCALAR)] + [(piece, NEAR) for piece in cot_pieces],
-                  [((full, pixels), BF16, NEAR)], time=0.6)
+        [((hidden, full), BF16, NEAR)] + [((units, full), BF16, NEAR)] * 2, time=0.7,
+        after=[(rims, RAW), (taps, NEAR)])
     rims = swap_rows(rims)
 
-    here = [(place, SCALAR), (nb, SCALAR), (rot, SCALAR)]
+    here = [(place, SCALAR), (neighbours, SCALAR), (rotations, SCALAR)]
     hid, padded, side = call(
         functools.partial(conv_kernel, edge), here + [(x, FAR), (rims, NEAR), (taps, NEAR)],
         [((channels, pixels), BF16, NEAR), ((channels, wide), BF16, FAR),
          ((channels, wide), BF16, FAR)],
-        [pltpu.VMEM((channels, len(SIDES) * rim), BF16)], time=2.5)
+        [pltpu.VMEM((channels, len(SIDES) * rim), BF16)], time=2.5, after=[(part_in, NEAR)])
     feats = lax.all_gather(hid, "chan", axis=0, tiled=True)
+    [cots] = call(join_kernel, [(place, SCALAR)] + [(piece, NEAR) for piece in cot_pieces],
+                  [((full, pixels), BF16, NEAR)], time=0.6, after=[(feats, NEAR)])
 
     used = 2 * full * units // LANES
     share = -(-used // (16 * tiles)) * 16
     tap_rows = -(-channels // 64) * 16
     values = [pltpu.VMEM((units, pixels), F32)] * 2 + [pltpu.VMEM((units, pixels), BF16)] * 2
     [part] = call(
-        weight_kernel, [(feats, NEAR), (cots, NEAR), (part_in, NEAR), (part_out, NEAR)],
+        weight_kernel,
+        [(feats, NEAR), (cots, NEAR), (part_in, NEAR), (part_out, NEAR)],
         [((tiles * share, LANES), BF16, RAW)],
         values + [pltpu.VMEM((tiles * share, LANES), BF16), pltpu.SemaphoreType.DMA((3,))],
         time=2.2)
     part = swap_rows(part.reshape(tiles, share, LANES))
 
-    outputs, grad_hid = call(
-        point_kernel,
-        [(feats, NEAR), (cots, NEAR), (w_in_t, FAR), (w_out, FAR), (w_in_own, FAR),
-         (w_out_own, FAR), (x, FAR)],
-        [((channels, pixels), BF16, FAR), ((channels, pixels), BF16, NEAR)], values, time=5.5)
-    [tap_part] = call(
-        functools.partial(tap_kernel, edge), [(grad_hid, NEAR), (padded, FAR), (side, FAR)],
-        [((tap_rows, LANES), BF16, NEAR)],
-        [pltpu.VMEM((KSIZE * 16, wide), BF16), pltpu.VMEM((LANES, wide), BF16)], time=1.5)
+    outputs, grad_hid, tap_part = call(
+        functools.partial(point_kernel, edge),
+        [(place, SCALAR), (feats, NEAR), (cots, NEAR), (w_in, FAR), (w_in_t, NEAR), (w_out, NEAR),
+         (x, FAR), (padded, FAR), (side, FAR)],
+        [((channels, pixels), BF16, FAR), ((channels, pixels), BF16, NEAR),
+         ((tap_rows, LANES), BF16, NEAR)],
+        values + [pltpu.VMEM((KSIZE * 16, wide), BF16), pltpu.VMEM((LANES, wide), BF16)],
+        time=7.0)
     [mine] = call(sum_kernel, [(part, NEAR), (tap_part, NEAR)],
                   [((tiles, share + tap_rows, LANES), BF16, FAR)])
     weights = swap_rows(mine)
 
     accum, border = call(
-        functools.partial(back_kernel, edge), here + [(grad_hid, NEAR), (cot, FAR), (taps, NEAR)],
+        functools.partial(back_kernel, edge), here + [(grad_hid, NEAR), (taps, NEAR)],
         [((channels, pixels), F32, FAR), ((tiles, channels, rim), BF16, FAR)],
         [pltpu.VMEM((channels, 2 * LANES), BF16), pltpu.VMEM((channels, wide), BF16),
-         pltpu.VMEM((tiles, channels, rim), F32)], time=4.0, after=[mine])
+         pltpu.VMEM((tiles, channels, rim), F32)], time=4.0, after=[(mine, RAW)])
     weights, border = lax.optimization_barrier((weights, border))
     border = swap_rows(border)
     pieces = gather_pieces(weights, groups)
@@ -593,8 +587,8 @@
             [pltpu.VMEM((len(which), full, units), F32), pltpu.VMEM((len(which), units, full), F32),
              pltpu.SemaphoreType.DMA((2, len(which)))],
             time=1.3, aliases={2 + len(which): 0, 3 + len(which): 1} if last else None)
-    [grad_in] = call(functools.partial(border_kernel, edge), [(border, NEAR), (accum, FAR)],
-                     [((channels, pixels), BF16, FAR)])
+    [grad_in] = call(functools.partial(border_kernel, edge), [(border, NEAR), (accum, FAR), (cot, FAR)],
+                     [((channels, pixels), BF16, FAR)], after=[(grads[0], RAW)])
     return (outputs[None], grad_in[None], *grads)
 
 

time: 80.1 us -> 75.3 us (0.940)
  Pallas kernels: 29.2 us -> 25.9 us
  starting transfers between devices: 24.8 us -> 21.5 us
  waiting for transfers between devices: 16.2 us -> 18.5 us
    pallas_call x12 -> x11, Pallas kernels: 29.2 us -> 25.9 us  [call(): pl.pallas_call(run, out_shape=[pltpu.HBM(s, d) if p in (FAR, RAW) else ja...]
    all_to_all x4, starting transfers between devices: 21.7 us -> 19.1 us  [swap_rows(): return lax.all_to_all(values, 'tile', 0, 0, tiled=True)]
    all_to_all x4, waiting for transfers between devices: 12.1 us -> 13.9 us  [swap_rows(): return lax.all_to_all(values, 'tile', 0, 0, tiled=True)]
  transfers between devices with their start and end apart: 10 -> 10, of which waited for: 5 -> 6; matrix products, arithmetic and copies ran while one was open for 0% -> 0% of each run, Pallas kernels for 24% -> 25%
where the time goes in v4:
time: 75.3 us; the launch traced here: 74.7 us
  Pallas kernels  25.9 us (34%)
  starting transfers between devices  21.5 us (29%)
  waiting for transfers between devices  18.5 us (25%)
  blocking collectives  7.2 us (10%)
  between operations  0.86 us (1%)
    pallas_call x11, Pallas kernels, call(): pl.pallas_call(run, out_shape=[pltpu.HBM(s, d) if p in (FAR, RAW) else ja...  25.9 us
    all_to_all x4, starting transfers between devices, swap_rows(): return lax.all_to_all(values, 'tile', 0, 0, tiled=True)  19.1 us
    all_to_all x4, waiting for transfers between devices, swap_rows(): return lax.all_to_all(values, 'tile', 0, 0, tiled=True)  13.9 us
    all_gather x1, blocking collectives, body(): feats = lax.all_gather(hid, 'chan', axis=0, tiled=True)  7.2 us
    ppermute x6, waiting for transfers between devices, gather_pieces(): pieces[k ^ bit] = lax.ppermute(pieces[k], 'chan', swap)  4.58 us
    ppermute x6, starting transfers between devices, gather_pieces(): pieces[k ^ bit] = lax.ppermute(pieces[k], 'chan', swap)  2.42 us
  transfers between devices with their start and end apart: 10, of which 6 were waited for; matrix products, arithmetic and copies ran while one was open for 0% of the time, Pallas kernels for 25%

profile of v4, /device:TPU:0, one launch (start us, length us, event | category | flops | bytes accessed | tf_op | source)
XLA Modules:
  0.0 74.7 jit_solution(8032978677333085484)
XLA Ops:
  0.6 1.9 %shard_map.110.refs_3_ = bf16[8,64,256]{2,1,0:T(8,128)(2,1)} custom-call(bf16[64,1024]{1,0:T(8,128)(2,1)} %bitcast.12), custom_call_target="tpu_custom_call" | custom-call | flops 1000000000 | bytes 3500000 | tf_op jit(solution)/shard_map/pallas_call | solution.py:75
  2.6 7.4 %all-to-all-start = ((bf16[8,64,256]{2,1,0:T(8,128)(2,1)}), bf16[8,64,256]{2,1,0:T(8,128)(2,1)S(1)}, u32[]{:S(2)}, u32[]{:S(2)}) async-start(bf16[8,64,256]{2,1,0:T(8,128)(2,1)} %shard_map.110.refs_3_), calls=%async_computation | async-start | bytes 524288 | tf_op jit(solution)/shard_map/all_to_all | solution.py:508
  10.0 1.6 %collective-permute-start.1 = (bf16[64,1024]{1,0:T(8,128)(2,1)S(1)}, bf16[64,1024]{1,0:T(8,128)(2,1)S(1)}, u32[]{:S(2)}, u32[]{:S(2)}) collective-permute-start(bf16[64,1024]{1,0:T(8,128)(2,1)S(1)} %bitcast.8), channel_id=1, source_target_pairs={{0,2},{1,3},{2,0},{3,1},{4,6},{5,7},{6,4},{7,5},{8,10},{9,11},{10,... | collective-permute-start | bytes 393224 | tf_op jit(solution)/shard_map/ppermute | solution.py:502
  12.0 0.8 %shard_map.111 = (bf16[1024,256]{1,0:T(8,128)(2,1)S(1)}, bf16[256,256]{1,0:T(8,128)(2,1)S(1)}, bf16[256,256]{1,0:T(8,128)(2,1)S(1)}) custom-call(s32[2]{0:T(128)S(1)} %pad_add_fusion.refs_0_, bf16[256,1024]{1,0:T(8,128)(2,1)S(1)} %copy-done, bf16[1024,256]{1,0:T(8,128)(2,1)S(1)} %copy-done.1, bf16[8,64,256]{2,1,0:T(8,128)(2,1)} %shard_map.110.refs_3_, ...), custom_call_target="tpu_custom_call" | custom-call | flops 700000000 | bytes 2450000 | tf_op jit(solution)/shard_map/pallas_call | solution.py:75
  12.7 2.3 %collective-permute-done.1.refs_3_ = bf16[64,1024]{1,0:T(8,128)(2,1)S(1)} collective-permute-done((bf16[64,1024]{1,0:T(8,128)(2,1)S(1)}, bf16[64,1024]{1,0:T(8,128)(2,1)S(1)}, u32[]{:S(2)}, u32[]{:S(2)}) %collective-permute-start.1) | collective-permute-done | bytes 131104 | tf_op jit(solution)/shard_map/ppermute | solution.py:502
  15.0 3.9 %all-to-all-done.refs_4_ = bf16[8,64,256]{2,1,0:T(8,128)(2,1)S(1)} async-done(((bf16[8,64,256]{2,1,0:T(8,128)(2,1)}), bf16[8,64,256]{2,1,0:T(8,128)(2,1)S(1)}, u32[]{:S(2)}, u32[]{:S(2)}) %all-to-all-start) | async-done | bytes 262176 | tf_op jit(solution)/shard_map/all_to_all | solution.py:508
  18.9 2.9 %shard_map.112 = (bf16[64,1024]{1,0:T(8,128)(2,1)S(1)}, bf16[64,1280]{1,0:T(8,128)(2,1)}, bf16[64,1280]{1,0:T(8,128)(2,1)}) custom-call(s32[2]{0:T(128)S(1)} %pad_add_fusion.refs_0_, s32[8,8]{1,0:T(8,128)S(1)} %copy-done.3, s32[8,8]{1,0:T(8,128)S(1)} %copy-done.4, bf16[64,1024]{1,0:T(8,128)(2,1)} %bitcast.13, bf16[8,64,256]{2,1,0:T(8,128)(2,1)S(1)} %all-to-all-done.refs_4_, ...), custom_call_target="tpu_custom_call" | custom-call | flops 2500000000 | bytes 8750000 | tf_op jit(solution)/shard_map/pallas_call | solution.py:75
  21.8 7.2 %all_gather.3.refs_5_.refs_1_.refs_0_ = bf16[256,1024]{1,0:T(8,128)(2,1)S(1)} all-gather(bf16[64,1024]{1,0:T(8,128)(2,1)S(1)} %get-tuple-element.27), channel_id=1, replica_groups=mesh['tile'=8,'chan'=4] {'chan'}, dimensions={0}, use_global_device_ids=true | all-gather | bytes 655360 | tf_op jit(solution)/shard_map/all_gather | solution.py:542
  29.0 0.6 shard_map.113.refs_2_.refs_1_
  29.9 2.2 %shard_map.115 = bf16[1024,128]{1,0:T(8,128)(2,1)} custom-call(bf16[256,1024]{1,0:T(8,128)(2,1)S(1)} %all_gather.3.refs_5_.refs_1_.refs_0_, bf16[256,1024]{1,0:T(8,128)(2,1)S(1)} %shard_map.113.refs_2_.refs_1_, bf16[256,256]{1,0:T(8,128)(2,1)S(1)} %get-tuple-element.26.refs_6_.refs_2_, bf16[256,256]{1,0:T(8,128)(2,1)S(1)} %copy-done.8), custom_call_target="tpu_custom_call" | custom-call | flops 2200000000 | bytes 7700000 | tf_op jit(solution)/shard_map/pallas_call | solution.py:75
  32.1 3.7 %all-to-all-start.1 = ((bf16[8,128,128]{2,1,0:T(8,128)(2,1)}), bf16[8,128,128]{2,1,0:T(8,128)(2,1)S(1)}, u32[]{:S(2)}, u32[]{:S(2)}) async-start(bf16[8,128,128]{2,1,0:T(8,128)(2,1)} %bitcast.11), calls=%async_computation.1 | async-start | bytes 524288 | tf_op jit(solution)/shard_map/all_to_all | solution.py:508
  35.9 7.8 %shard_map.114 = (bf16[64,1024]{1,0:T(8,128)(2,1)}, bf16[64,1024]{1,0:T(8,128)(2,1)S(1)}, bf16[16,128]{1,0:T(8,128)(2,1)S(1)}) custom-call(s32[2]{0:T(128)S(1)} %pad_add_fusion.refs_0_, bf16[256,1024]{1,0:T(8,128)(2,1)S(1)} %all_gather.3.refs_5_.refs_1_.refs_0_, bf16[256,1024]{1,0:T(8,128)(2,1)S(1)} %copy-done.6, bf16[256,1024]{1,0:T(8,128)(2,1)} %refs_3_.1, ...), custom_call_target="tpu_custom_call" | custom-call | flops 7000000000 | bytes 24500000 | tf_op jit(solution)/shard_map/pallas_call | solution.py:75
  43.7 1.7 %all-to-all-done.1.refs_0_ = bf16[8,128,128]{2,1,0:T(8,128)(2,1)S(1)} async-done(((bf16[8,128,128]{2,1,0:T(8,128)(2,1)}), bf16[8,128,128]{2,1,0:T(8,128)(2,1)S(1)}, u32[]{:S(2)}, u32[]{:S(2)}) %all-to-all-start.1) | async-done | bytes 262176 | tf_op jit(solution)/shard_map/all_to_all | solution.py:508
  45.3 0.8 %shard_map.116.refs_5_ = bf16[8,144,128]{2,1,0:T(8,128)(2,1)} custom-call(bf16[8,128,128]{2,1,0:T(8,128)(2,1)S(1)} %all-to-all-done.1.refs_0_, bf16[16,128]{1,0:T(8,128)(2,1)S(1)} %get-tuple-element.33.refs_1_), custom_call_target="tpu_custom_call" | custom-call | flops 1000000000 | bytes 3500000 | tf_op jit(solution)/shard_map/pallas_call | solution.py:75
  46.2 4.4 %all-to-all-start.2 = ((bf16[8,144,128]{2,1,0:T(8,128)(2,1)}), bf16[8,144,128]{2,1,0:T(8,128)(2,1)S(1)}, u32[]{:S(2)}, u32[]{:S(2)}) async-start(bf16[8,144,128]{2,1,0:T(8,128)(2,1)} %shard_map.116.refs_5_), calls=%async_computation.2 | async-start | bytes 589824 | tf_op jit(solution)/shard_map/all_to_all | solution.py:508
  50.5 3.4 %shard_map.117 = (f32[64,1024]{1,0:T(8,128)}, bf16[8,64,256]{2,1,0:T(8,128)(2,1)}) custom-call(s32[2]{0:T(128)S(1)} %pad_add_fusion.refs_0_, s32[8,8]{1,0:T(8,128)S(1)} %copy-done.3, s32[8,8]{1,0:T(8,128)S(1)} %copy-done.4, bf16[64,1024]{1,0:T(8,128)(2,1)S(1)} %get-tuple-element.34.refs_3_, f32[25,64,128]{2,1,0:T(8,128)S(1)} %broadcast_in_dim.12.refs_4_.refs_5_, ...), custom_call_target="tpu_custom_call" | custom-call | flops 4000000000 | bytes 14000000 | tf_op jit(solution)/shard_map/pallas_call | solution.py:75
  54.0 6.2 %all-to-all-done.2.refs_1_ = bf16[8,144,128]{2,1,0:T(8,128)(2,1)S(1)} async-done(((bf16[8,144,128]{2,1,0:T(8,128)(2,1)}), bf16[8,144,128]{2,1,0:T(8,128)(2,1)S(1)}, u32[]{:S(2)}, u32[]{:S(2)}) %all-to-all-start.2) | async-done | bytes 294944 | tf_op jit(solution)/shard_map/all_to_all | solution.py:508
  60.2 0.8 %collective-permute-start.4 = (bf16[8,144,128]{2,1,0:T(8,128)(2,1)S(1)}, bf16[8,144,128]{2,1,0:T(8,128)(2,1)S(1)}, u32[]{:S(2)}, u32[]{:S(2)}) collective-permute-start(bf16[8,144,128]{2,1,0:T(8,128)(2,1)S(1)} %all-to-all-done.2.refs_1_), channel_id=1, source_target_pairs={{0,2},{1,3},{2,0},{3,1},{4,6},{5,7},{6,4},{7,5},{8,10},{9,11},{10,... | collective-permute-start | bytes 884744 | tf_op jit(solution)/shard_map/ppermute | solution.py:502
  61.0 3.6 %all-to-all-start.3 = ((bf16[8,64,256]{2,1,0:T(8,128)(2,1)}), bf16[8,64,256]{2,1,0:T(8,128)(2,1)S(1)}, u32[]{:S(2)}, u32[]{:S(2)}) async-start(bf16[8,64,256]{2,1,0:T(8,128)(2,1)} %get-tuple-element.36), calls=%async_computation.3 | async-start | bytes 524288 | tf_op jit(solution)/shard_map/all_to_all | solution.py:508
  64.6 2.3 %collective-permute-done.4.refs_2_ = bf16[8,144,128]{2,1,0:T(8,128)(2,1)S(1)} collective-permute-done((bf16[8,144,128]{2,1,0:T(8,128)(2,1)S(1)}, bf16[8,144,128]{2,1,0:T(8,128)(2,1)S(1)}, u32[]{:S(2)}, u32[]{:S(2)}) %collective-permute-start.4) | collective-permute-done | bytes 294944 | tf_op jit(solution)/shard_map/ppermute | solution.py:502
  66.9 1.6 %shard_map.118 = (f32[256,1024]{1,0:T(8,128)}, f32[1024,256]{1,0:T(8,128)}, f32[256,128]{1,0:T(8,128)S(1)}) custom-call(s32[2]{0:T(128)S(1)} %pad_add_fusion.refs_0_, bf16[8,144,128]{2,1,0:T(8,128)(2,1)S(1)} %all-to-all-done.2.refs_1_, bf16[8,144,128]{2,1,0:T(8,128)(2,1)S(1)} %collective-permute-done.4.refs_2_), custom_call_target="tpu_custom_call" | custom-call | flops 1300000000 | bytes 4550000 | tf_op jit(solution)/shard_map/pallas_call | solution.py:75
  68.5 2.3 %shard_map.119 = (f32[256,1024]{1,0:T(8,128)}, f32[1024,256]{1,0:T(8,128)}, f32[25,256]{1,0:T(8,128)}) custom-call(s32[2]{0:T(128)S(1)} %pad_add_fusion.refs_0_, bf16[8,144,128]{2,1,0:T(8,128)(2,1)S(1)} %collective-permute-done.3.refs_1_, bf16[8,144,128]{2,1,0:T(8,128)(2,1)S(1)} %collective-permute-done.5.refs_2_, ...), custom_call_target="tpu_custom_call", output_to_operand_aliasing={{0}: (4, {}), {1}: (5, {})} | custom-call | flops 1300000000 | bytes 4550000 | tf_op jit(solution)/shard_map/pallas_call | solution.py:75
  70.8 2.2 %all-to-all-done.3.refs_0_ = bf16[8,64,256]{2,1,0:T(8,128)(2,1)S(1)} async-done(((bf16[8,64,256]{2,1,0:T(8,128)(2,1)}), bf16[8,64,256]{2,1,0:T(8,128)(2,1)S(1)}, u32[]{:S(2)}, u32[]{:S(2)}) %all-to-all-start.3) | async-done | bytes 262176 | tf_op jit(solution)/shard_map/all_to_all | solution.py:508
  73.0 1.7 %shard_map.120 = bf16[64,1024]{1,0:T(8,128)(2,1)} custom-call(bf16[8,64,256]{2,1,0:T(8,128)(2,1)S(1)} %all-to-all-done.3.refs_0_, f32[64,1024]{1,0:T(8,128)} %get-tuple-element.37.refs_1_, bf16[64,1024]{1,0:T(8,128)(2,1)} %bitcast.7, f32[256,1024]{1,0:T(8,128)} %get-tuple-element.22.refs_3_), custom_call_target="tpu_custom_call" | custom-call | flops 1000000000 | bytes 3500000 | tf_op jit(solution)/shard_map/pallas_call | solution.py:75
  (30 shorter events, 0.7 us)
Async XLA Ops:
  0.6 9.3 %copy-start.2 = (bf16[1,64,1024]{2,1,0:T(8,128)(2,1)S(1)}, bf16[1,64,1024]{2,1,0:T(8,128)(2,1)}, u32[]{:S(2)}) copy-start(bf16[1,64,1024]{2,1,0:T(8,128)(2,1)} %param.8) | copy-start | bytes 393220
  2.5 9.1 %copy-start.9 = (bf16[25,64]{1,0:T(8,128)(2,1)S(1)}, bf16[25,64]{1,0:T(8,128)(2,1)}, u32[]{:S(2)}) copy-start(bf16[25,64]{1,0:T(8,128)(2,1)} %param.9) | copy-start | bytes 9604
  2.6 9.4 %copy-start.1 = (bf16[1024,256]{1,0:T(8,128)(2,1)S(1)}, bf16[1024,256]{1,0:T(8,128)(2,1)}, u32[]{:S(2)}) copy-start(bf16[1024,256]{1,0:T(8,128)(2,1)} %refs_5_.1) | copy-start | bytes 1572868
  2.6 16.3 %all-to-all-start = ((bf16[8,64,256]{2,1,0:T(8,128)(2,1)}), bf16[8,64,256]{2,1,0:T(8,128)(2,1)S(1)}, u32[]{:S(2)}, u32[]{:S(2)}) async-start(bf16[8,64,256]{2,1,0:T(8,128)(2,1)} %shard_map.110.refs_3_), calls=%async_computation | async-start | bytes 524288 | tf_op jit(solution)/shard_map/all_to_all | solution.py:508
  10.0 2.0 %copy-start = (bf16[256,1024]{1,0:T(8,128)(2,1)S(1)}, bf16[256,1024]{1,0:T(8,128)(2,1)}, u32[]{:S(2)}) copy-start(bf16[256,1024]{1,0:T(8,128)(2,1)} %refs_3_.1) | copy-start | bytes 1572868
  10.0 5.0 %collective-permute-start.1 = (bf16[64,1024]{1,0:T(8,128)(2,1)S(1)}, bf16[64,1024]{1,0:T(8,128)(2,1)S(1)}, u32[]{:S(2)}, u32[]{:S(2)}) collective-permute-start(bf16[64,1024]{1,0:T(8,128)(2,1)S(1)} %bitcast.8), channel_id=1, source_target_pairs={{0,2},{1,3},{2,0},{3,1},{4,6},{5,7},{6,4},{7,5},{8,10},{9,11},{10,... | collective-permute-start | bytes 393224 | tf_op jit(solution)/shard_map/ppermute | solution.py:502
  11.6 17.4 %collective-permute-start = (bf16[64,1024]{1,0:T(8,128)(2,1)S(1)}, bf16[64,1024]{1,0:T(8,128)(2,1)S(1)}, u32[]{:S(2)}, u32[]{:S(2)}) collective-permute-start(bf16[64,1024]{1,0:T(8,128)(2,1)S(1)} %bitcast.9), channel_id=1, source_target_pairs={{0,1},{1,0},{2,3},{3,2},{4,5},{5,4},{6,7},{7,6},{8,9},{9,8},{10,11... | collective-permute-start | bytes 393224 | tf_op jit(solution)/shard_map/ppermute | solution.py:502
  11.9 6.9 %copy-start.3 = (s32[8,8]{1,0:T(8,128)S(1)}, s32[8,8]{1,0:T(8,128)}, u32[]{:S(2)}) copy-start(s32[8,8]{1,0:T(8,128)} %refs_1_.5) | copy-start | bytes 772
  12.0 6.9 %copy-start.4 = (s32[8,8]{1,0:T(8,128)S(1)}, s32[8,8]{1,0:T(8,128)}, u32[]{:S(2)}) copy-start(s32[8,8]{1,0:T(8,128)} %refs_2_.5) | copy-start | bytes 772
  12.7 9.1 %copy-start.7 = (bf16[256,256]{1,0:T(8,128)(2,1)}, bf16[256,256]{1,0:T(8,128)(2,1)S(1)}, u32[]{:S(2)}) copy-start(bf16[256,256]{1,0:T(8,128)(2,1)S(1)} %get-tuple-element.32.refs_3_) | copy-start | bytes 393220
  15.0 14.0 %collective-permute-start.2 = (bf16[64,1024]{1,0:T(8,128)(2,1)S(1)}, bf16[64,1024]{1,0:T(8,128)(2,1)S(1)}, u32[]{:S(2)}, u32[]{:S(2)}) collective-permute-start(bf16[64,1024]{1,0:T(8,128)(2,1)S(1)} %collective-permute-done.1.refs_3_), channel_id=1, source_target_pairs={{0,1},{1,0},{2,3},{3,2},{4,5},{5,4},{6,7},{7,6},{8,9},{9,8},{10,11... | collective-permute-start | bytes 393224 | tf_op jit(solution)/shard_map/ppermute | solution.py:502
  29.0 0.9 %copy-start.8 = (bf16[256,256]{1,0:T(8,128)(2,1)S(1)}, bf16[256,256]{1,0:T(8,128)(2,1)}, u32[]{:S(2)}) copy-start(bf16[256,256]{1,0:T(8,128)(2,1)} %copy-done.7) | copy-start | bytes 393220
  29.6 2.5 %copy-start.5 = (bf16[256,1024]{1,0:T(8,128)(2,1)}, bf16[256,1024]{1,0:T(8,128)(2,1)S(1)}, u32[]{:S(2)}) copy-start(bf16[256,1024]{1,0:T(8,128)(2,1)S(1)} %shard_map.113.refs_2_.refs_1_) | copy-start | bytes 1572868
  32.1 3.7 %copy-start.6 = (bf16[256,1024]{1,0:T(8,128)(2,1)S(1)}, bf16[256,1024]{1,0:T(8,128)(2,1)}, u32[]{:S(2)}) copy-start(bf16[256,1024]{1,0:T(8,128)(2,1)} %copy-done.5) | copy-start | bytes 1572868
  32.1 13.2 %all-to-all-start.1 = ((bf16[8,128,128]{2,1,0:T(8,128)(2,1)}), bf16[8,128,128]{2,1,0:T(8,128)(2,1)S(1)}, u32[]{:S(2)}, u32[]{:S(2)}) async-start(bf16[8,128,128]{2,1,0:T(8,128)(2,1)} %bitcast.11), calls=%async_computation.1 | async-start | bytes 524288 | tf_op jit(solution)/shard_map/all_to_all | solution.py:508
  46.2 14.0 %all-to-all-start.2 = ((bf16[8,144,128]{2,1,0:T(8,128)(2,1)}), bf16[8,144,128]{2,1,0:T(8,128)(2,1)S(1)}, u32[]{:S(2)}, u32[]{:S(2)}) async-start(bf16[8,144,128]{2,1,0:T(8,128)(2,1)} %shard_map.116.refs_5_), calls=%async_computation.2 | async-start | bytes 589824 | tf_op jit(solution)/shard_map/all_to_all | solution.py:508
  60.2 6.7 %collective-permute-start.4 = (bf16[8,144,128]{2,1,0:T(8,128)(2,1)S(1)}, bf16[8,144,128]{2,1,0:T(8,128)(2,1)S(1)}, u32[]{:S(2)}, u32[]{:S(2)}) collective-permute-start(bf16[8,144,128]{2,1,0:T(8,128)(2,1)S(1)} %all-to-all-done.2.refs_1_), channel_id=1, source_target_pairs={{0,2},{1,3},{2,0},{3,1},{4,6},{5,7},{6,4},{7,5},{8,10},{9,11},{10,... | collective-permute-start | bytes 884744 | tf_op jit(solution)/shard_map/ppermute | solution.py:502
  61.0 12.0 %all-to-all-start.3 = ((bf16[8,64,256]{2,1,0:T(8,128)(2,1)}), bf16[8,64,256]{2,1,0:T(8,128)(2,1)S(1)}, u32[]{:S(2)}, u32[]{:S(2)}) async-start(bf16[8,64,256]{2,1,0:T(8,128)(2,1)} %get-tuple-element.36), calls=%async_computation.3 | async-start | bytes 524288 | tf_op jit(solution)/shard_map/all_to_all | solution.py:508
  64.6 3.9 %collective-permute-start.3 = (bf16[8,144,128]{2,1,0:T(8,128)(2,1)S(1)}, bf16[8,144,128]{2,1,0:T(8,128)(2,1)S(1)}, u32[]{:S(2)}, u32[]{:S(2)}) collective-permute-start(bf16[8,144,128]{2,1,0:T(8,128)(2,1)S(1)} %all-to-all-done.2.refs_1_), channel_id=1, source_target_pairs={{0,1},{1,0},{2,3},{3,2},{4,5},{5,4},{6,7},{7,6},{8,9},{9,8},{10,11... | collective-permute-start | bytes 884744 | tf_op jit(solution)/shard_map/ppermute | solution.py:502
  66.9 1.6 %collective-permute-start.5 = (bf16[8,144,128]{2,1,0:T(8,128)(2,1)S(1)}, bf16[8,144,128]{2,1,0:T(8,128)(2,1)S(1)}, u32[]{:S(2)}, u32[]{:S(2)}) collective-permute-start(bf16[8,144,128]{2,1,0:T(8,128)(2,1)S(1)} %collective-permute-done.4.refs_2_), channel_id=1, source_target_pairs={{0,1},{1,0},{2,3},{3,2},{4,5},{5,4},{6,7},{7,6},{8,9},{9,8},{10,11... | collective-permute-start | bytes 884744 | tf_op jit(solution)/shard_map/ppermute | solution.py:502

commit v5 on v4

--- a/solution.py
+++ b/solution.py
@@ -15,8 +15,8 @@
 BF16 = jnp.bfloat16
 F32 = jnp.float32
 
-SCALAR, NEAR, FAR, RAW = "scalar", "near", "far", "raw"
-SPACES = {SCALAR: pltpu.SMEM, NEAR: pltpu.VMEM, FAR: pltpu.HBM, RAW: pltpu.HBM}
+NEAR, FAR, RAW = "near", "far", "raw"
+SPACES = {NEAR: pltpu.VMEM, FAR: pltpu.HBM, RAW: pltpu.HBM}
 
 
 class Loaded:
@@ -87,6 +87,11 @@
         for a, p in ins])
 
 
+def tile_row(table):
+    row = table.get()[pl.ds(lax.axis_index("tile"), 1), :]
+    return [row[0, d] for d in range(8)]
+
+
 def dot(a, b):
     return lax.dot_general(a, b, (((1,), (0,)), ((), ())), preferred_element_type=F32)
 
@@ -186,15 +191,14 @@
         copy.wait()
 
 
-def conv_kernel(edge, place_ref, nb_ref, rot_ref, x, rims, taps,
+def conv_kernel(edge, neighbours, rotations, x, rims, taps,
                 hidden_ref, padded, side, gathered):
     padded_ref, side_ref = padded.ref, side.ref
     rims_ref, taps_ref = rims.get(), taps.get()
     channels, pixels = hidden_ref.shape
     wide = pixels + 2 * LANES
     rim = rims_ref.shape[2]
-    nb = [nb_ref[place_ref[0], d] for d in range(8)]
-    rot = [rot_ref[place_ref[0], d] for d in range(8)]
+    nb, rot = tile_row(neighbours), tile_row(rotations)
     top, low = row_halo_maps(rot[1], rot[6], edge)
     padded_ref[:, :LANES] = dot(rims_ref[nb[1]], top).astype(BF16)
     padded_ref[:, LANES + pixels:] = dot(rims_ref[nb[6]], low).astype(BF16)
@@ -210,6 +214,7 @@
         at = pl.multiple_of(i * 16, 16)
         xs = padded_ref[pl.ds(at, 16), :].astype(F32)
         hs = side_ref[pl.ds(at, 16), :].astype(F32)
+        taps = [taps_ref[tap, pl.ds(at, 16), :].astype(F32) for tap in range(KSIZE * KSIZE)]
         halves = []
         for half in (0, 8):
             x, h = xs[half:half + 8], hs[half:half + 8]
@@ -220,8 +225,7 @@
                 if shift:
                     moved = roll(jnp.where(side_mask(shift, x.shape, edge), h, x), -shift)
                 for a in range(KSIZE):
-                    tap = taps_ref[a * KSIZE + b, pl.ds(at + half, 8), :]
-                    term = jnp.tile(tap, (1, wide // LANES)) * moved
+                    term = jnp.tile(taps[a * KSIZE + b][half:half + 8], (1, wide // LANES)) * moved
                     sums[a] = term if sums[a] is None else sums[a] + term
             total = None
             for a in range(KSIZE):
@@ -275,44 +279,40 @@
         copy.wait()
 
 
-def point_kernel(edge, place_ref, feats, cots, w_in, w_in_t, w_out, x, padded, side,
+def point_kernel(edge, feats, cots, w_in, w_in_t, w_out, x, padded, side,
                  out, grad_ref, tap_ref, pre, slope, act, gpre, turned_all, moved_all):
-    units, channels = pre.shape[0], grad_ref.shape[0]
-    feats, cots, w_in_t, w_out = feats.get(), cots.get(), w_in_t.get(), w_out.get()
-    start = place_ref[1] * channels
-    own = pl.ds(pl.multiple_of(start, channels), channels)
+    channels = grad_ref.shape[0]
+    start = pl.multiple_of(lax.axis_index("chan") * channels, channels)
+    w_out = w_out.get()
+    hidden_block(w_in_t.get()[...], w_out[...], feats.get(), cots.get(), pre, slope, act, gpre)
+    grad_ref[...] = dot(w_in.get()[pl.ds(start, channels), :], gpre[...]).astype(BF16)
     row = lax.broadcasted_iota(jnp.int32, (channels, w_out.shape[1]), 0)
     column = lax.broadcasted_iota(jnp.int32, (channels, w_out.shape[1]), 1)
     pick = jnp.where(column == row + start, 1.0, 0.0).astype(BF16)
-    branch = grad = None
-    for at in range(0, w_out.shape[0], units):
-        part = slice(at, at + units)
-        hidden_block(w_in_t[part, :], w_out[part, :], feats, cots, pre, slope, act, gpre)
-        more = dot(dot_nt(pick, w_out[part, :]).astype(BF16), act[...])
-        branch = more if branch is None else branch + more
-        more = dot(w_in.get()[own, part], gpre[...])
-        grad = more if grad is None else grad + more
+    branch = dot(dot_nt(pick, w_out[...]).astype(BF16), act[...])
     out.ref[...] = (x.get()[...].astype(F32) + branch.astype(BF16).astype(F32)).astype(BF16)
     out.send()
-    grad_ref[...] = grad.astype(BF16)
     tap_terms(edge, grad_ref, padded.get(), side.get(), tap_ref, turned_all, moved_all)
 
 
-def prep_kernel(place_ref, w_in, w_out, w_in_t_ref, part_in_ref, part_out_ref):
+def prep_kernel(w_in, x, neighbours, rotations, w_in_t_ref, x_ref, nb_ref, rot_ref):
+    nb_ref[...], rot_ref[...] = neighbours.get()[...], rotations.get()[...]
     w_in_t_ref[...] = w_in.get()[...].astype(F32).T.astype(BF16)
-    units = part_in_ref.shape[0]
-    mine = pl.ds(pl.multiple_of(place_ref[1] * units, units), units)
-    part_in_ref[...] = w_in_t_ref[mine, :]
-    part_out_ref[...] = w_out.get()[mine, :]
-
-
-def join_kernel(place_ref, *refs):
-    pieces, out_ref = refs[:-1], refs[-1]
+    x_ref[...] = x.get()[...]
+
+
+def join_kernel(w_in_t, w_out, *refs):
+    pieces, (out_ref, part_in_ref, part_out_ref) = refs[:-3], refs[-3:]
+    chan = lax.axis_index("chan")
     for k, piece in enumerate(pieces):
         piece = piece.get()
         channels = piece.shape[0]
-        start = pl.multiple_of((place_ref[1] ^ k) * channels, channels)
+        start = pl.multiple_of((chan ^ k) * channels, channels)
         out_ref[pl.ds(start, channels), :] = piece[...]
+    units = part_in_ref.shape[0]
+    mine = pl.ds(pl.multiple_of(chan * units, units), units)
+    part_in_ref[...] = w_in_t.get()[mine, :]
+    part_out_ref[...] = w_out.get()[mine, :]
 
 
 def tap_terms(edge, grad_ref, padded_ref, side_ref, tap_ref, turned_all, moved_all):
@@ -351,9 +351,9 @@
     tap_ref[...] = jnp.concatenate(found, axis=0).astype(BF16)
 
 
-def back_kernel(edge, place_ref, nb_ref, rot_ref, grad, taps,
-                accum, border, d_row, d_side, gathered):
-    accum_ref, send_ref = accum.ref, border.ref
+def back_kernel(edge, neighbours, rotations, grad, taps, cot,
+                accum_ref, border, d_row, d_side, gathered):
+    send_ref = border.ref
     grad_ref, taps_ref = grad.get(), taps.get()
     channels, pixels = grad_ref.shape
     wide = pixels + 2 * LANES
@@ -362,6 +362,7 @@
     def block(i, carry):
         at = pl.multiple_of(i * 16, 16)
         gs = grad_ref[pl.ds(at, 16), :].astype(F32)
+        taps_of = [taps_ref[tap, pl.ds(at, 16), :].astype(F32) for tap in range(KSIZE * KSIZE)]
         zeros = jnp.zeros((8, LANES), F32)
         rows, sides = [], []
         for half in (0, 8):
@@ -372,7 +373,7 @@
                 shift = b - HALO
                 back = None
                 for a in range(KSIZE):
-                    weight = taps_ref[a * KSIZE + b, pl.ds(at + half, 8), :]
+                    weight = taps_of[a * KSIZE + b][half:half + 8]
                     term = jnp.tile(weight, (1, wide // LANES)) * turned[a]
                     back = term if back is None else back + term
                 back = roll(back, shift)
@@ -394,9 +395,8 @@
         return carry
 
     lax.fori_loop(0, channels // 16, block, 0)
-    accum.send()
-    nb = [nb_ref[place_ref[0], d] for d in range(8)]
-    rot = [rot_ref[place_ref[0], d] for d in range(8)]
+    accum_ref[...] += cot.get()[...].astype(F32)
+    nb, rot = tile_row(neighbours), tile_row(rotations)
     gathered[...] = jnp.zeros(gathered.shape, F32)
     top, low = row_halo_maps(rot[1], rot[6], edge)
     gathered[nb[1]] += dot_nt(d_row[:, :LANES], top)
@@ -413,13 +413,12 @@
     lax.fori_loop(0, tiles, store, 0)
 
 
-def border_kernel(edge, recv, accum, cot, grad):
+def border_kernel(edge, recv, accum, grad):
     rims = total_of(recv.get())
     high = rims.astype(BF16)
     low = (rims - high.astype(F32)).astype(BF16)
     pick = one_hot(rim_pixels(edge), edge * edge)
     added = dot_nt(high, pick) + dot_nt(low, pick)
-    added = added + cot.get()[...].astype(F32)
     grad.ref[...] = (accum.get()[...] + added).astype(BF16)
 
 
@@ -428,20 +427,19 @@
                          ref[0].astype(F32))
 
 
-def sum_kernel(recv, tap, out):
+def sum_kernel(recv, tap, out, total, sems):
     recv = recv.get()
     share = recv.shape[1]
-    total, taps = total_of(recv).astype(BF16), tap.get()[...]
-
-    def store(t, carry):
-        out.ref[t, :share, :] = total
-        out.ref[t, share:, :] = taps
-        return carry
-
-    lax.fori_loop(0, out.ref.shape[0], store, 0)
-
-
-def final_kernel(which, last, share, channels, scale, place_ref, *refs):
+    total[:share, :] = total_of(recv).astype(BF16)
+    total[share:, :] = tap.get()[...]
+    copies = [pltpu.make_async_copy(total, out.at[t], sems.at[t]) for t in range(out.shape[0])]
+    for copy in copies:
+        copy.start()
+    for copy in copies:
+        copy.wait()
+
+
+def final_kernel(which, last, share, channels, scale, *refs):
     count = len(which)
     pieces, taps_in = refs[:count], refs[count]
     g_in, g_out, g_tap_ref, buf_in, buf_out, sems = refs[-6:]
@@ -452,7 +450,7 @@
     row_of = lax.broadcasted_iota(jnp.int32, (full, LANES), 0)
     for i, k in enumerate(which):
         piece = pieces[i].get()
-        owner = place_ref[1] ^ k
+        owner = lax.axis_index("chan") ^ k
         start = pl.multiple_of(owner * units, units)
         for in_in, buffer, target in ((True, buf_in, g_in.at[:, pl.ds(start, units)]),
                                       (False, buf_out, g_out.at[pl.ds(start, units)])):
@@ -518,30 +516,33 @@
     rim = 4 * HALO * edge
     units = hidden // groups
     scale = (tiles * pixels) ** -0.5
-    place = jnp.stack([lax.axis_index("tile"), lax.axis_index("chan")]).astype(jnp.int32)
     x, cot = inputs[0], grad_out[0]
 
     [rims] = call(functools.partial(pack_kernel, edge), [(x, FAR)],
                   [((tiles, channels, rim), BF16, RAW)],
                   [pltpu.VMEM((channels, rim), BF16), pltpu.SemaphoreType.DMA((tiles,))])
     _, kernel = lax.optimization_barrier((rims, kernel))
-    taps = jnp.broadcast_to(kernel.astype(F32)[:, :, None], (KSIZE * KSIZE, channels, LANES))
+    taps = jnp.broadcast_to(kernel[:, :, None], (KSIZE * KSIZE, channels, LANES))
     cot_pieces = gather_pieces(cot, groups)
-    w_in_t, part_in, part_out = call(
-        prep_kernel, [(place, SCALAR), (w_in, NEAR), (w_out, NEAR)],
-        [((hidden, full), BF16, NEAR)] + [((units, full), BF16, NEAR)] * 2, time=0.7,
+    table = neighbours.shape
+    w_in_t, x_near, nb_near, rot_near = call(
+        prep_kernel, [(w_in, NEAR), (x, FAR), (neighbours, NEAR), (rotations, NEAR)],
+        [((hidden, full), BF16, NEAR), ((channels, pixels), BF16, NEAR)]
+        + [(neighbours.shape, jnp.int32, NEAR)] * 2, time=1.2,
         after=[(rims, RAW), (taps, NEAR)])
     rims = swap_rows(rims)
 
-    here = [(place, SCALAR), (neighbours, SCALAR), (rotations, SCALAR)]
     hid, padded, side = call(
-        functools.partial(conv_kernel, edge), here + [(x, FAR), (rims, NEAR), (taps, NEAR)],
-        [((channels, pixels), BF16, NEAR), ((channels, wide), BF16, FAR),
-         ((channels, wide), BF16, FAR)],
-        [pltpu.VMEM((channels, len(SIDES) * rim), BF16)], time=2.5, after=[(part_in, NEAR)])
+        functools.partial(conv_kernel, edge),
+        [(nb_near, NEAR), (rot_near, NEAR), (x_near, NEAR), (rims, NEAR), (taps, NEAR)],
+        [((channels, pixels), BF16, NEAR)] + [((channels, wide), BF16, FAR)] * 2,
+        [pltpu.VMEM((channels, len(SIDES) * rim), BF16)], time=2.5,
+        after=[(w_in_t, NEAR)])
     feats = lax.all_gather(hid, "chan", axis=0, tiled=True)
-    [cots] = call(join_kernel, [(place, SCALAR)] + [(piece, NEAR) for piece in cot_pieces],
-                  [((full, pixels), BF16, NEAR)], time=0.6, after=[(feats, NEAR)])
+    cots, part_in, part_out = call(
+        join_kernel, [(w_in_t, NEAR), (w_out, NEAR)] + [(piece, NEAR) for piece in cot_pieces],
+        [((full, pixels), BF16, NEAR)] + [((units, full), BF16, NEAR)] * 2, time=0.6,
+        after=[(feats, NEAR)])
 
     used = 2 * full * units // LANES
     share = -(-used // (16 * tiles)) * 16
@@ -557,19 +558,22 @@
 
     outputs, grad_hid, tap_part = call(
         functools.partial(point_kernel, edge),
-        [(place, SCALAR), (feats, NEAR), (cots, NEAR), (w_in, FAR), (w_in_t, NEAR), (w_out, NEAR),
+        [(feats, NEAR), (cots, NEAR), (w_in, FAR), (w_in_t, NEAR), (w_out, NEAR),
          (x, FAR), (padded, FAR), (side, FAR)],
         [((channels, pixels), BF16, FAR), ((channels, pixels), BF16, NEAR),
          ((tap_rows, LANES), BF16, NEAR)],
-        values + [pltpu.VMEM((KSIZE * 16, wide), BF16), pltpu.VMEM((LANES, wide), BF16)],
-        time=7.0)
+        [pltpu.VMEM((hidden, pixels), F32)] * 2 + [pltpu.VMEM((hidden, pixels), BF16)] * 2
+        + [pltpu.VMEM((KSIZE * 16, wide), BF16), pltpu.VMEM((LANES, wide), BF16)],
+        time=5.5, limit=32)
     [mine] = call(sum_kernel, [(part, NEAR), (tap_part, NEAR)],
-                  [((tiles, share + tap_rows, LANES), BF16, FAR)])
+                  [((tiles, share + tap_rows, LANES), BF16, RAW)],
+                  [pltpu.VMEM((share + tap_rows, LANES), BF16), pltpu.SemaphoreType.DMA((tiles,))])
     weights = swap_rows(mine)
 
     accum, border = call(
-        functools.partial(back_kernel, edge), here + [(grad_hid, NEAR), (taps, NEAR)],
-        [((channels, pixels), F32, FAR), ((tiles, channels, rim), BF16, FAR)],
+        functools.partial(back_kernel, edge),
+        [(neighbours, NEAR), (rotations, NEAR), (grad_hid, NEAR), (taps, NEAR), (cot, FAR)],
+        [((channels, pixels), F32, NEAR), ((tiles, channels, rim), BF16, FAR)],
         [pltpu.VMEM((channels, 2 * LANES), BF16), pltpu.VMEM((channels, wide), BF16),
          pltpu.VMEM((tiles, channels, rim), F32)], time=4.0, after=[(mine, RAW)])
     weights, border = lax.optimization_barrier((weights, border))
@@ -581,13 +585,13 @@
         tap_shape = (KSIZE * KSIZE, full) if last else (full, LANES)
         grads = call(
             functools.partial(final_kernel, which, last, share, channels, scale),
-            [(place, SCALAR)] + [(pieces[k], NEAR) for k in which]
+            [(pieces[k], NEAR) for k in which]
             + ([(grads[2], NEAR), (grads[0], RAW), (grads[1], RAW)] if last else []),
             [((full, hidden), F32, RAW), ((hidden, full), F32, RAW), (tap_shape, F32, NEAR)],
             [pltpu.VMEM((len(which), full, units), F32), pltpu.VMEM((len(which), units, full), F32),
              pltpu.SemaphoreType.DMA((2, len(which)))],
-            time=1.3, aliases={2 + len(which): 0, 3 + len(which): 1} if last else None)
-    [grad_in] = call(functools.partial(border_kernel, edge), [(border, NEAR), (accum, FAR), (cot, FAR)],
+            time=1.3, aliases={1 + len(which): 0, 2 + len(which): 1} if last else None)
+    [grad_in] = call(functools.partial(border_kernel, edge), [(border, NEAR), (accum, NEAR)],
                      [((channels, pixels), BF16, FAR)], after=[(grads[0], RAW)])
     return (outputs[None], grad_in[None], *grads)
 

time: 75.3 us -> 72.2 us (0.959)
  Pallas kernels: 25.9 us -> 21 us
  waiting for transfers between devices: 18.5 us -> 21.5 us
  starting transfers between devices: 21.5 us -> 20.6 us
    pallas_call x11, Pallas kernels: 25.9 us -> 21 us  [call(): pl.pallas_call(run, out_shape=[pltpu.HBM(s, d) if p in (FAR, RAW) else ja...]
    all_to_all x4, waiting for transfers between devices: 13.9 us -> 16.6 us  [swap_rows(): return lax.all_to_all(values, 'tile', 0, 0, tiled=True)]
    all_to_all x4, starting transfers between devices: 19.1 us -> 18.2 us  [swap_rows(): return lax.all_to_all(values, 'tile', 0, 0, tiled=True)]
  transfers between devices with their start and end apart: 10 -> 10, of which waited for: 6 -> 7; matrix products, arithmetic and copies ran while one was open for 0% -> 0% of each run, Pallas kernels for 25% -> 21%
where the time goes in v5:
time: 72.2 us; the launch traced here: 71.6 us
  waiting for transfers between devices  21.5 us (30%)
  Pallas kernels  21 us (29%)
  starting transfers between devices  20.6 us (29%)
  blocking collectives  7.33 us (10%)
  between operations  0.82 us (1%)
    pallas_call x11, Pallas kernels, call(): pl.pallas_call(run, out_shape=[pltpu.HBM(s, d) if p in (FAR, RAW) else ja...  21 us
    all_to_all x4, starting transfers between devices, swap_rows(): return lax.all_to_all(values, 'tile', 0, 0, tiled=True)  18.2 us
    all_to_all x4, waiting for transfers between devices, swap_rows(): return lax.all_to_all(values, 'tile', 0, 0, tiled=True)  16.6 us
    all_gather x1, blocking collectives, body(): feats = lax.all_gather(hid, 'chan', axis=0, tiled=True)  7.33 us
    ppermute x6, waiting for transfers between devices, gather_pieces(): pieces[k ^ bit] = lax.ppermute(pieces[k], 'chan', swap)  4.92 us
    ppermute x6, starting transfers between devices, gather_pieces(): pieces[k ^ bit] = lax.ppermute(pieces[k], 'chan', swap)  2.43 us
  transfers between devices with their start and end apart: 10, of which 7 were waited for; matrix products, arithmetic and copies ran while one was open for 0% of the time, Pallas kernels for 21%

profile of v5, /device:TPU:0, one launch (start us, length us, event | category | flops | bytes accessed | tf_op | source)
XLA Modules:
  0.0 71.6 jit_solution(12244140987669048908)
XLA Ops:
  0.7 1.9 %shard_map.110.refs_4_ = bf16[8,64,256]{2,1,0:T(8,128)(2,1)} custom-call(bf16[64,1024]{1,0:T(8,128)(2,1)} %bitcast.10), custom_call_target="tpu_custom_call" | custom-call | flops 1000000000 | bytes 3500000 | tf_op jit(solution)/shard_map/pallas_call | solution.py:75
  2.6 7.4 %all-to-all-start = ((bf16[8,64,256]{2,1,0:T(8,128)(2,1)}), bf16[8,64,256]{2,1,0:T(8,128)(2,1)S(1)}, u32[]{:S(2)}, u32[]{:S(2)}) async-start(bf16[8,64,256]{2,1,0:T(8,128)(2,1)} %shard_map.110.refs_4_), calls=%async_computation | async-start | bytes 524288 | tf_op jit(solution)/shard_map/all_to_all | solution.py:506
  10.0 1.6 %collective-permute-start.1 = (bf16[64,1024]{1,0:T(8,128)(2,1)S(1)}, bf16[64,1024]{1,0:T(8,128)(2,1)S(1)}, u32[]{:S(2)}, u32[]{:S(2)}) collective-permute-start(bf16[64,1024]{1,0:T(8,128)(2,1)S(1)} %bitcast.6), channel_id=1, source_target_pairs={{0,2},{1,3},{2,0},{3,1},{4,6},{5,7},{6,4},{7,5},{8,10},{9,11},{10,... | collective-permute-start | bytes 393224 | tf_op jit(solution)/shard_map/ppermute | solution.py:500
  11.9 1.1 %shard_map.111 = (bf16[1024,256]{1,0:T(8,128)(2,1)S(1)}, bf16[64,1024]{1,0:T(8,128)(2,1)S(1)}, s32[8,8]{1,0:T(8,128)S(1)}, s32[8,8]{1,0:T(8,128)S(1)}) custom-call(bf16[256,1024]{1,0:T(8,128)(2,1)S(1)} %copy-done, bf16[64,1024]{1,0:T(8,128)(2,1)} %bitcast.11, s32[8,8]{1,0:T(8,128)S(1)} %copy-done.3, s32[8,8]{1,0:T(8,128)S(1)} %copy-done.4, ...), custom_call_target="tpu_custom_call" | custom-call | flops 1200000000 | bytes 4200000 | tf_op jit(solution)/shard_map/pallas_call | solution.py:75
  13.0 2.1 %collective-permute-done.1.refs_4_ = bf16[64,1024]{1,0:T(8,128)(2,1)S(1)} collective-permute-done((bf16[64,1024]{1,0:T(8,128)(2,1)S(1)}, bf16[64,1024]{1,0:T(8,128)(2,1)S(1)}, u32[]{:S(2)}, u32[]{:S(2)}) %collective-permute-start.1) | collective-permute-done | bytes 131104 | tf_op jit(solution)/shard_map/ppermute | solution.py:500
  15.0 3.9 %all-to-all-done.refs_3_ = bf16[8,64,256]{2,1,0:T(8,128)(2,1)S(1)} async-done(((bf16[8,64,256]{2,1,0:T(8,128)(2,1)}), bf16[8,64,256]{2,1,0:T(8,128)(2,1)S(1)}, u32[]{:S(2)}, u32[]{:S(2)}) %all-to-all-start) | async-done | bytes 262176 | tf_op jit(solution)/shard_map/all_to_all | solution.py:506
  18.9 1.8 %shard_map.112 = (bf16[64,1024]{1,0:T(8,128)(2,1)S(1)}, bf16[64,1280]{1,0:T(8,128)(2,1)}, bf16[64,1280]{1,0:T(8,128)(2,1)}) custom-call(s32[8,8]{1,0:T(8,128)S(1)} %get-tuple-element.30.refs_0_, s32[8,8]{1,0:T(8,128)S(1)} %get-tuple-element.31.refs_1_, bf16[64,1024]{1,0:T(8,128)(2,1)S(1)} %get-tuple-element.32.refs_2_, ...), custom_call_target="tpu_custom_call" | custom-call | flops 2500000000 | bytes 8750000 | tf_op jit(solution)/shard_map/pallas_call | solution.py:75
  20.7 7.3 %all_gather.3.refs_6_.refs_0_ = bf16[256,1024]{1,0:T(8,128)(2,1)S(1)} all-gather(bf16[64,1024]{1,0:T(8,128)(2,1)S(1)} %get-tuple-element.34), channel_id=1, replica_groups=mesh['tile'=8,'chan'=4] {'chan'}, dimensions={0}, use_global_device_ids=true | all-gather | bytes 655360 | tf_op jit(solution)/shard_map/all_gather | solution.py:541
  28.2 2.2 %shard_map.115 = bf16[1024,128]{1,0:T(8,128)(2,1)} custom-call(bf16[256,1024]{1,0:T(8,128)(2,1)S(1)} %all_gather.3.refs_6_.refs_0_, bf16[256,1024]{1,0:T(8,128)(2,1)S(1)} %get-tuple-element.35.refs_1_, bf16[256,256]{1,0:T(8,128)(2,1)S(1)} %get-tuple-element.39.refs_2_, bf16[256,256]{1,0:T(8,128)(2,1)S(1)} %get-tuple-element.40.refs_3_), custom_call_target="tpu_custom_call" | custom-call | flops 2200000000 | bytes 7700000 | tf_op jit(solution)/shard_map/pallas_call | solution.py:75
  30.4 3.6 %all-to-all-start.1 = ((bf16[8,128,128]{2,1,0:T(8,128)(2,1)}), bf16[8,128,128]{2,1,0:T(8,128)(2,1)S(1)}, u32[]{:S(2)}, u32[]{:S(2)}) async-start(bf16[8,128,128]{2,1,0:T(8,128)(2,1)} %bitcast.9), calls=%async_computation.1 | async-start | bytes 524288 | tf_op jit(solution)/shard_map/all_to_all | solution.py:506
  34.0 6.3 %shard_map.114 = (bf16[64,1024]{1,0:T(8,128)(2,1)}, bf16[64,1024]{1,0:T(8,128)(2,1)S(1)}, bf16[16,128]{1,0:T(8,128)(2,1)S(1)}) custom-call(bf16[256,1024]{1,0:T(8,128)(2,1)S(1)} %all_gather.3.refs_6_.refs_0_, bf16[256,1024]{1,0:T(8,128)(2,1)S(1)} %get-tuple-element.35.refs_1_, bf16[256,1024]{1,0:T(8,128)(2,1)} %refs_2_.3, ...), custom_call_target="tpu_custom_call" | custom-call | flops 5500000256 | bytes 19250000 | tf_op jit(solution)/shard_map/pallas_call | solution.py:75
  40.3 3.2 %all-to-all-done.1.refs_0_ = bf16[8,128,128]{2,1,0:T(8,128)(2,1)S(1)} async-done(((bf16[8,128,128]{2,1,0:T(8,128)(2,1)}), bf16[8,128,128]{2,1,0:T(8,128)(2,1)S(1)}, u32[]{:S(2)}, u32[]{:S(2)}) %all-to-all-start.1) | async-done | bytes 262176 | tf_op jit(solution)/shard_map/all_to_all | solution.py:506
  43.5 0.8 %shard_map.116.refs_5_ = bf16[8,144,128]{2,1,0:T(8,128)(2,1)} custom-call(bf16[8,128,128]{2,1,0:T(8,128)(2,1)S(1)} %all-to-all-done.1.refs_0_, bf16[16,128]{1,0:T(8,128)(2,1)S(1)} %get-tuple-element.41.refs_1_), custom_call_target="tpu_custom_call" | custom-call | flops 1000000000 | bytes 3500000 | tf_op jit(solution)/shard_map/pallas_call | solution.py:75
  44.3 3.6 %all-to-all-start.2 = ((bf16[8,144,128]{2,1,0:T(8,128)(2,1)}), bf16[8,144,128]{2,1,0:T(8,128)(2,1)S(1)}, u32[]{:S(2)}, u32[]{:S(2)}) async-start(bf16[8,144,128]{2,1,0:T(8,128)(2,1)} %shard_map.116.refs_5_), calls=%async_computation.2 | async-start | bytes 589824 | tf_op jit(solution)/shard_map/all_to_all | solution.py:506
  47.9 2.9 %shard_map.117 = (f32[64,1024]{1,0:T(8,128)S(1)}, bf16[8,64,256]{2,1,0:T(8,128)(2,1)}) custom-call(s32[8,8]{1,0:T(8,128)S(1)} %copy-done.3, s32[8,8]{1,0:T(8,128)S(1)} %copy-done.4, bf16[64,1024]{1,0:T(8,128)(2,1)S(1)} %get-tuple-element.42.refs_2_, bf16[25,64,128]{2,1,0:T(8,128)(2,1)S(1)} %broadcast_in_dim.12.refs_5_.refs_4_.refs_3_, ...), custom_call_target="tpu_custom_call" | custom-call | flops 4000000000 | bytes 14000000 | tf_op jit(solution)/shard_map/pallas_call | solution.py:75
  50.7 6.8 %all-to-all-done.2.refs_0_ = bf16[8,144,128]{2,1,0:T(8,128)(2,1)S(1)} async-done(((bf16[8,144,128]{2,1,0:T(8,128)(2,1)}), bf16[8,144,128]{2,1,0:T(8,128)(2,1)S(1)}, u32[]{:S(2)}, u32[]{:S(2)}) %all-to-all-start.2) | async-done | bytes 294944 | tf_op jit(solution)/shard_map/all_to_all | solution.py:506
  57.5 0.8 %collective-permute-start.4 = (bf16[8,144,128]{2,1,0:T(8,128)(2,1)S(1)}, bf16[8,144,128]{2,1,0:T(8,128)(2,1)S(1)}, u32[]{:S(2)}, u32[]{:S(2)}) collective-permute-start(bf16[8,144,128]{2,1,0:T(8,128)(2,1)S(1)} %all-to-all-done.2.refs_0_), channel_id=1, source_target_pairs={{0,2},{1,3},{2,0},{3,1},{4,6},{5,7},{6,4},{7,5},{8,10},{9,11},{10,... | collective-permute-start | bytes 884744 | tf_op jit(solution)/shard_map/ppermute | solution.py:500
  58.4 3.6 %all-to-all-start.3 = ((bf16[8,64,256]{2,1,0:T(8,128)(2,1)}), bf16[8,64,256]{2,1,0:T(8,128)(2,1)S(1)}, u32[]{:S(2)}, u32[]{:S(2)}) async-start(bf16[8,64,256]{2,1,0:T(8,128)(2,1)} %get-tuple-element.44), calls=%async_computation.3 | async-start | bytes 524288 | tf_op jit(solution)/shard_map/all_to_all | solution.py:506
  62.0 2.3 %collective-permute-done.4.refs_1_ = bf16[8,144,128]{2,1,0:T(8,128)(2,1)S(1)} collective-permute-done((bf16[8,144,128]{2,1,0:T(8,128)(2,1)S(1)}, bf16[8,144,128]{2,1,0:T(8,128)(2,1)S(1)}, u32[]{:S(2)}, u32[]{:S(2)}) %collective-permute-start.4) | collective-permute-done | bytes 294944 | tf_op jit(solution)/shard_map/ppermute | solution.py:500
  64.3 1.0 %shard_map.118 = (f32[256,1024]{1,0:T(8,128)}, f32[1024,256]{1,0:T(8,128)}, f32[256,128]{1,0:T(8,128)S(1)}) custom-call(bf16[8,144,128]{2,1,0:T(8,128)(2,1)S(1)} %all-to-all-done.2.refs_0_, bf16[8,144,128]{2,1,0:T(8,128)(2,1)S(1)} %collective-permute-done.4.refs_1_), custom_call_target="tpu_custom_call" | custom-call | flops 1300000000 | bytes 4550000 | tf_op jit(solution)/shard_map/pallas_call | solution.py:75
  65.4 0.5 collective-permute-done.5.refs_1_
  65.9 1.7 %shard_map.119 = (f32[256,1024]{1,0:T(8,128)}, f32[1024,256]{1,0:T(8,128)}, f32[25,256]{1,0:T(8,128)}) custom-call(bf16[8,144,128]{2,1,0:T(8,128)(2,1)S(1)} %collective-permute-done.3.refs_0_, bf16[8,144,128]{2,1,0:T(8,128)(2,1)S(1)} %collective-permute-done.5.refs_1_, ...), custom_call_target="tpu_custom_call", output_to_operand_aliasing={{0}: (3, {}), {1}: (4, {})} | custom-call | flops 1300000000 | bytes 4550000 | tf_op jit(solution)/shard_map/pallas_call | solution.py:75
  67.6 2.8 %all-to-all-done.3.refs_0_ = bf16[8,64,256]{2,1,0:T(8,128)(2,1)S(1)} async-done(((bf16[8,64,256]{2,1,0:T(8,128)(2,1)}), bf16[8,64,256]{2,1,0:T(8,128)(2,1)S(1)}, u32[]{:S(2)}, u32[]{:S(2)}) %all-to-all-start.3) | async-done | bytes 262176 | tf_op jit(solution)/shard_map/all_to_all | solution.py:506
  70.4 1.2 %shard_map.120 = bf16[64,1024]{1,0:T(8,128)(2,1)} custom-call(bf16[8,64,256]{2,1,0:T(8,128)(2,1)S(1)} %all-to-all-done.3.refs_0_, f32[64,1024]{1,0:T(8,128)S(1)} %get-tuple-element.45.refs_1_, f32[256,1024]{1,0:T(8,128)} %get-tuple-element.26.refs_2_), custom_call_target="tpu_custom_call" | custom-call | flops 1000000000 | bytes 3500000 | tf_op jit(solution)/shard_map/pallas_call | solution.py:75
  (21 shorter events, 0.4 us)
Async XLA Ops:
  0.6 9.3 %copy-start.2 = (bf16[1,64,1024]{2,1,0:T(8,128)(2,1)S(1)}, bf16[1,64,1024]{2,1,0:T(8,128)(2,1)}, u32[]{:S(2)}) copy-start(bf16[1,64,1024]{2,1,0:T(8,128)(2,1)} %param.8) | copy-start | bytes 393220
  0.6 10.9 %copy-start.5 = (bf16[25,64]{1,0:T(8,128)(2,1)S(1)}, bf16[25,64]{1,0:T(8,128)(2,1)}, u32[]{:S(2)}) copy-start(bf16[25,64]{1,0:T(8,128)(2,1)} %param.9) | copy-start | bytes 9604
  2.6 9.3 %copy-start = (bf16[256,1024]{1,0:T(8,128)(2,1)S(1)}, bf16[256,1024]{1,0:T(8,128)(2,1)}, u32[]{:S(2)}) copy-start(bf16[256,1024]{1,0:T(8,128)(2,1)} %refs_2_.3) | copy-start | bytes 1572868
  2.6 16.3 %all-to-all-start = ((bf16[8,64,256]{2,1,0:T(8,128)(2,1)}), bf16[8,64,256]{2,1,0:T(8,128)(2,1)S(1)}, u32[]{:S(2)}, u32[]{:S(2)}) async-start(bf16[8,64,256]{2,1,0:T(8,128)(2,1)} %shard_map.110.refs_4_), calls=%async_computation | async-start | bytes 524288 | tf_op jit(solution)/shard_map/all_to_all | solution.py:506
  10.0 1.9 %copy-start.3 = (s32[8,8]{1,0:T(8,128)S(1)}, s32[8,8]{1,0:T(8,128)}, u32[]{:S(2)}) copy-start(s32[8,8]{1,0:T(8,128)} %refs_0_.3) | copy-start | bytes 772
  10.0 1.9 %copy-start.4 = (s32[8,8]{1,0:T(8,128)S(1)}, s32[8,8]{1,0:T(8,128)}, u32[]{:S(2)}) copy-start(s32[8,8]{1,0:T(8,128)} %refs_1_.3) | copy-start | bytes 772
  10.0 5.0 %collective-permute-start.1 = (bf16[64,1024]{1,0:T(8,128)(2,1)S(1)}, bf16[64,1024]{1,0:T(8,128)(2,1)S(1)}, u32[]{:S(2)}, u32[]{:S(2)}) collective-permute-start(bf16[64,1024]{1,0:T(8,128)(2,1)S(1)} %bitcast.6), channel_id=1, source_target_pairs={{0,2},{1,3},{2,0},{3,1},{4,6},{5,7},{6,4},{7,5},{8,10},{9,11},{10,... | collective-permute-start | bytes 393224 | tf_op jit(solution)/shard_map/ppermute | solution.py:500
  11.6 16.5 %collective-permute-start = (bf16[64,1024]{1,0:T(8,128)(2,1)S(1)}, bf16[64,1024]{1,0:T(8,128)(2,1)S(1)}, u32[]{:S(2)}, u32[]{:S(2)}) collective-permute-start(bf16[64,1024]{1,0:T(8,128)(2,1)S(1)} %bitcast.7), channel_id=1, source_target_pairs={{0,1},{1,0},{2,3},{3,2},{4,5},{5,4},{6,7},{7,6},{8,9},{9,8},{10,11... | collective-permute-start | bytes 393224 | tf_op jit(solution)/shard_map/ppermute | solution.py:500
  15.0 13.1 %collective-permute-start.2 = (bf16[64,1024]{1,0:T(8,128)(2,1)S(1)}, bf16[64,1024]{1,0:T(8,128)(2,1)S(1)}, u32[]{:S(2)}, u32[]{:S(2)}) collective-permute-start(bf16[64,1024]{1,0:T(8,128)(2,1)S(1)} %collective-permute-done.1.refs_4_), channel_id=1, source_target_pairs={{0,1},{1,0},{2,3},{3,2},{4,5},{5,4},{6,7},{7,6},{8,9},{9,8},{10,11... | collective-permute-start | bytes 393224 | tf_op jit(solution)/shard_map/ppermute | solution.py:500
  20.7 7.4 %copy-start.1 = (bf16[1024,256]{1,0:T(8,128)(2,1)S(1)}, bf16[1024,256]{1,0:T(8,128)(2,1)}, u32[]{:S(2)}) copy-start(bf16[1024,256]{1,0:T(8,128)(2,1)} %refs_4_.1) | copy-start | bytes 1572868
  30.4 13.1 %all-to-all-start.1 = ((bf16[8,128,128]{2,1,0:T(8,128)(2,1)}), bf16[8,128,128]{2,1,0:T(8,128)(2,1)S(1)}, u32[]{:S(2)}, u32[]{:S(2)}) async-start(bf16[8,128,128]{2,1,0:T(8,128)(2,1)} %bitcast.9), calls=%async_computation.1 | async-start | bytes 524288 | tf_op jit(solution)/shard_map/all_to_all | solution.py:506
  44.3 13.2 %all-to-all-start.2 = ((bf16[8,144,128]{2,1,0:T(8,128)(2,1)}), bf16[8,144,128]{2,1,0:T(8,128)(2,1)S(1)}, u32[]{:S(2)}, u32[]{:S(2)}) async-start(bf16[8,144,128]{2,1,0:T(8,128)(2,1)} %shard_map.116.refs_5_), calls=%async_computation.2 | async-start | bytes 589824 | tf_op jit(solution)/shard_map/all_to_all | solution.py:506
  57.5 6.8 %collective-permute-start.4 = (bf16[8,144,128]{2,1,0:T(8,128)(2,1)S(1)}, bf16[8,144,128]{2,1,0:T(8,128)(2,1)S(1)}, u32[]{:S(2)}, u32[]{:S(2)}) collective-permute-start(bf16[8,144,128]{2,1,0:T(8,128)(2,1)S(1)} %all-to-all-done.2.refs_0_), channel_id=1, source_target_pairs={{0,2},{1,3},{2,0},{3,1},{4,6},{5,7},{6,4},{7,5},{8,10},{9,11},{10,... | collective-permute-start | bytes 884744 | tf_op jit(solution)/shard_map/ppermute | solution.py:500
  58.4 12.0 %all-to-all-start.3 = ((bf16[8,64,256]{2,1,0:T(8,128)(2,1)}), bf16[8,64,256]{2,1,0:T(8,128)(2,1)S(1)}, u32[]{:S(2)}, u32[]{:S(2)}) async-start(bf16[8,64,256]{2,1,0:T(8,128)(2,1)} %get-tuple-element.44), calls=%async_computation.3 | async-start | bytes 524288 | tf_op jit(solution)/shard_map/all_to_all | solution.py:506
  62.0 3.4 %collective-permute-start.3 = (bf16[8,144,128]{2,1,0:T(8,128)(2,1)S(1)}, bf16[8,144,128]{2,1,0:T(8,128)(2,1)S(1)}, u32[]{:S(2)}, u32[]{:S(2)}) collective-permute-start(bf16[8,144,128]{2,1,0:T(8,128)(2,1)S(1)} %all-to-all-done.2.refs_0_), channel_id=1, source_target_pairs={{0,1},{1,0},{2,3},{3,2},{4,5},{5,4},{6,7},{7,6},{8,9},{9,8},{10,11... | collective-permute-start | bytes 884744 | tf_op jit(solution)/shard_map/ppermute | solution.py:500
  64.3 1.6 %collective-permute-start.5 = (bf16[8,144,128]{2,1,0:T(8,128)(2,1)S(1)}, bf16[8,144,128]{2,1,0:T(8,128)(2,1)S(1)}, u32[]{:S(2)}, u32[]{:S(2)}) collective-permute-start(bf16[8,144,128]{2,1,0:T(8,128)(2,1)S(1)} %collective-permute-done.4.refs_1_), channel_id=1, source_target_pairs={{0,1},{1,0},{2,3},{3,2},{4,5},{5,4},{6,7},{7,6},{8,9},{9,8},{10,11... | collective-permute-start | bytes 884744 | tf_op jit(solution)/shard_map/ppermute | solution.py:500

commit v6 on v5

--- a/solution.py
+++ b/solution.py
@@ -153,9 +153,9 @@
     quarter = jnp.zeros_like(slot)
     for position in range(len(SIDES)):
         quarter = jnp.where(slot == position, turns[position], quarter)
-    index = slot * rim + turned_lane(b_row, b_col, quarter, edge)
+    index = turned_lane(b_row, b_col, quarter, edge)
     index = jnp.where(row < edge + 2 * HALO, index, -1)
-    return one_hot(index, len(SIDES) * rim)
+    return one_hot(index, rim), slot
 
 
 def spread_map(edge, wide):
@@ -197,14 +197,19 @@
     rims_ref, taps_ref = rims.get(), taps.get()
     channels, pixels = hidden_ref.shape
     wide = pixels + 2 * LANES
-    rim = rims_ref.shape[2]
     nb, rot = tile_row(neighbours), tile_row(rotations)
     top, low = row_halo_maps(rot[1], rot[6], edge)
     padded_ref[:, :LANES] = dot(rims_ref[nb[1]], top).astype(BF16)
     padded_ref[:, LANES + pixels:] = dot(rims_ref[nb[6]], low).astype(BF16)
     for position, d in enumerate(SIDES):
-        gathered[:, position * rim:(position + 1) * rim] = rims_ref[nb[d]]
-    packed = dot(gathered[...], side_map([rot[d] for d in SIDES], edge)).astype(BF16)
+        gathered[position * channels:(position + 1) * channels, :] = rims_ref[nb[d]]
+    pick, slot = side_map([rot[d] for d in SIDES], edge)
+    candidates = dot(gathered[...], pick)
+    packed = candidates[:channels, :]
+    for position in range(1, len(SIDES)):
+        packed = jnp.where(slot == position,
+                           candidates[position * channels:(position + 1) * channels, :], packed)
+    packed = packed.astype(BF16)
     side_ref[...] = dot(packed, spread_map(edge, wide)).astype(BF16)
     side.send()
     padded_ref[:, LANES:LANES + pixels] = x.get()[...]
@@ -238,29 +243,36 @@
     lax.fori_loop(0, channels // 16, block, 0)
 
 
-def gelu_parts(pre, grad_act):
-    cumul = 0.5 * (1.0 + lax.erf(pre * 0.7071067811865476))
-    slope = cumul + pre * jnp.exp(-0.5 * pre * pre) * 0.3989422804014327
-    return (pre * cumul).astype(BF16), (grad_act * slope).astype(BF16)
-
-
-def hidden_block(w_in_t, w_out, feats, cots, pre, slope, act, gpre):
-    pre[...] = dot(w_in_t, feats[...])
-    slope[...] = dot(w_out, cots[...])
-
-    def rows(i, carry):
-        at = pl.multiple_of(i * 16, 16)
-        act[pl.ds(at, 16), :], gpre[pl.ds(at, 16), :] = gelu_parts(
-            pre[pl.ds(at, 16), :], slope[pl.ds(at, 16), :])
+def normal_below(values):
+    return 0.5 * (1.0 + lax.erf(values * 0.7071067811865476))
+
+
+def gelu_slope(values, below):
+    return below + values * jnp.exp(-0.5 * values * values) * 0.3989422804014327
+
+
+def column_steps(ref):
+    return [slice(at, at + 2 * LANES) for at in range(0, ref.shape[1], 2 * LANES)]
+
+
+def over_units(units, block, body):
+    def step(i, carry):
+        body(pl.ds(pl.multiple_of(i * block, block), block))
         return carry
 
-    lax.fori_loop(0, pre.shape[0] // 16, rows, 0)
-
-
-def weight_kernel(feats, cots, w_in_t, w_out, part, pre, slope, act, gpre, stack, sems):
+    lax.fori_loop(0, units // block, step, 0)
+
+
+def weight_kernel(feats, cots, w_in_t, w_out, part, act, gpre, stack, sems):
     feats, cots = feats.get(), cots.get()
-    full, units = feats.shape[0], pre.shape[0]
-    hidden_block(w_in_t.get()[...], w_out.get()[...], feats, cots, pre, slope, act, gpre)
+    full, units = feats.shape[0], act.shape[0]
+    w_in_t, w_out = w_in_t.get()[...], w_out.get()[...]
+    for part_of in column_steps(feats):
+        pre = dot(w_in_t, feats[:, part_of])
+        below = normal_below(pre)
+        act[:, part_of] = (pre * below).astype(BF16)
+        slope = gelu_slope(pre, below)
+        gpre[:, part_of] = (dot(w_out, cots[:, part_of]) * slope).astype(BF16)
     used, copies = 0, []
     for values, height in ((dot_nt(feats[...], gpre[...]), full),
                            (dot_nt(act[...], cots[...]), units)):
@@ -279,20 +291,41 @@
         copy.wait()
 
 
-def point_kernel(edge, feats, cots, w_in, w_in_t, w_out, x, padded, side,
-                 out, grad_ref, tap_ref, pre, slope, act, gpre, turned_all, moved_all):
-    channels = grad_ref.shape[0]
-    start = pl.multiple_of(lax.axis_index("chan") * channels, channels)
-    w_out = w_out.get()
-    hidden_block(w_in_t.get()[...], w_out[...], feats.get(), cots.get(), pre, slope, act, gpre)
-    grad_ref[...] = dot(w_in.get()[pl.ds(start, channels), :], gpre[...]).astype(BF16)
+def out_kernel(block, feats, w_in_t, w_out, x, out, act):
+    feats, w_in_t, w_out = feats.get(), w_in_t.get(), w_out.get()
+
+    def units(rows):
+        for part_of in column_steps(feats):
+            pre = dot(w_in_t[rows, :], feats[:, part_of])
+            act[rows, part_of] = (pre * normal_below(pre)).astype(BF16)
+
+    over_units(w_out.shape[0], block, units)
+    channels = out.ref.shape[0]
     row = lax.broadcasted_iota(jnp.int32, (channels, w_out.shape[1]), 0)
     column = lax.broadcasted_iota(jnp.int32, (channels, w_out.shape[1]), 1)
-    pick = jnp.where(column == row + start, 1.0, 0.0).astype(BF16)
+    pick = jnp.where(column == row + lax.axis_index("chan") * channels, 1.0, 0.0).astype(BF16)
     branch = dot(dot_nt(pick, w_out[...]).astype(BF16), act[...])
     out.ref[...] = (x.get()[...].astype(F32) + branch.astype(BF16).astype(F32)).astype(BF16)
-    out.send()
+
+
+def back_kernel(edge, block, tiles, feats, cots, w_in, w_in_t, w_out, padded, side, cot, neighbours,
+                rotations, taps, accum_ref, tap_ref, *refs):
+    outs, (gpre, grad_ref, turned_all, moved_all, d_row, d_side, gathered) = refs[:-7], refs[-7:]
+    channels = grad_ref.shape[0]
+    feats, cots, w_in_t, w_out = feats.get(), cots.get(), w_in_t.get(), w_out.get()
+
+    def units(rows):
+        for part_of in column_steps(feats):
+            pre = dot(w_in_t[rows, :], feats[:, part_of])
+            slope = gelu_slope(pre, normal_below(pre))
+            gpre[rows, part_of] = (dot(w_out[rows, :], cots[:, part_of]) * slope).astype(BF16)
+
+    over_units(w_out.shape[0], block, units)
+    own = pl.ds(pl.multiple_of(lax.axis_index("chan") * channels, channels), channels)
+    grad_ref[...] = dot(w_in.get()[own, :], gpre[...]).astype(BF16)
     tap_terms(edge, grad_ref, padded.get(), side.get(), tap_ref, turned_all, moved_all)
+    halo_adjoint(edge, neighbours, rotations, grad_ref, taps.get(), cot.get(), accum_ref, outs,
+                 d_row, d_side, gathered)
 
 
 def prep_kernel(w_in, x, neighbours, rotations, w_in_t_ref, x_ref, nb_ref, rot_ref):
@@ -351,13 +384,11 @@
     tap_ref[...] = jnp.concatenate(found, axis=0).astype(BF16)
 
 
-def back_kernel(edge, neighbours, rotations, grad, taps, cot,
-                accum_ref, border, d_row, d_side, gathered):
-    send_ref = border.ref
-    grad_ref, taps_ref = grad.get(), taps.get()
+def halo_adjoint(edge, neighbours, rotations, grad_ref, taps_ref, cot_ref, accum_ref, outs,
+                 d_row, d_side, gathered):
     channels, pixels = grad_ref.shape
     wide = pixels + 2 * LANES
-    tiles, _, rim = send_ref.shape
+    tiles = gathered.shape[0]
 
     def block(i, carry):
         at = pl.multiple_of(i * 16, 16)
@@ -395,26 +426,57 @@
         return carry
 
     lax.fori_loop(0, channels // 16, block, 0)
-    accum_ref[...] += cot.get()[...].astype(F32)
+    accum_ref[...] += cot_ref[...].astype(F32)
     nb, rot = tile_row(neighbours), tile_row(rotations)
     gathered[...] = jnp.zeros(gathered.shape, F32)
     top, low = row_halo_maps(rot[1], rot[6], edge)
-    gathered[nb[1]] += dot_nt(d_row[:, :LANES], top)
-    gathered[nb[6]] += dot_nt(d_row[:, LANES:], low)
-    packed = dot_nt(d_side[...], spread_map(edge, wide)).astype(BF16)
-    picks = side_map([rot[d] for d in SIDES], edge)
+    gathered[slot_of(nb[1], tiles)] += dot_nt(d_row[:, :LANES], top)
+    gathered[slot_of(nb[6], tiles)] += dot_nt(d_row[:, LANES:], low)
+    packed = dot_nt(d_side[...], spread_map(edge, wide))
+    pick, slot = side_map([rot[d] for d in SIDES], edge)
     for position, d in enumerate(SIDES):
-        gathered[nb[d]] += dot_nt(packed, picks[position * rim:(position + 1) * rim, :])
-
-    def store(t, carry):
-        send_ref[t] = gathered[t].astype(BF16)
-        return carry
-
-    lax.fori_loop(0, tiles, store, 0)
-
-
-def border_kernel(edge, recv, accum, grad):
-    rims = total_of(recv.get())
+        own = jnp.where(slot == position, packed, 0.0).astype(BF16)
+        gathered[slot_of(nb[d], tiles)] += dot_nt(own, pick)
+    store_parts(gathered, outs)
+
+
+def store_parts(values, outs):
+    for part, out in enumerate(outs):
+        out = out.ref if isinstance(out, Stored) else out
+        rows = out.shape[0]
+
+        def store(t, carry, out=out, first=part * rows):
+            out[t] = values[first + t].astype(BF16)
+            return carry
+
+        lax.fori_loop(0, rows, store, 0)
+
+
+def halves(tiles):
+    return tiles & (tiles - 1) == 0
+
+
+def slot_of(tile, tiles):
+    if not halves(tiles):
+        return tile
+    apart, slot = tile ^ lax.axis_index("tile"), 0
+    for bit in range(tiles.bit_length() - 1):
+        slot = slot * 2 + ((apart >> bit) & 1)
+    return slot
+
+
+def pair_kernel(kept, other, *refs):
+    outs, total = refs[:-1], refs[-1]
+    total[...] = kept.get()[...].astype(F32) + other.get()[...].astype(F32)
+    store_parts(total, outs)
+
+
+def border_kernel(edge, accum, *refs):
+    parts, grad = refs[:-1], refs[-1]
+    rims = None
+    for part in parts:
+        more = total_of(part.get())
+        rims = more if rims is None else rims + more
     high = rims.astype(BF16)
     low = (rims - high.astype(F32)).astype(BF16)
     pick = one_hot(rim_pixels(edge), edge * edge)
@@ -491,19 +553,32 @@
     return found
 
 
-def gather_pieces(own, groups):
+def gather_pieces(own, groups, beside=()):
     pieces = {0: own}
     bit = groups // 2
     while bit:
         swap = [(i, i ^ bit) for i in range(groups)]
         for k in list(pieces):
             pieces[k ^ bit] = lax.ppermute(pieces[k], "chan", swap)
+        if len(pieces) == 2 and beside:
+            pieces[bit], *beside = lax.optimization_barrier((pieces[bit], *beside))
         bit //= 2
-    return [pieces[k] for k in range(groups)]
+    return [pieces[k] for k in range(groups)], beside
 
 
 def swap_rows(values):
     return lax.all_to_all(values, "tile", 0, 0, tiled=True)
+
+
+def halve(parts, bit, after):
+    kept, given = parts
+    half = ((kept.shape[0] // 2, *kept.shape[1:]), BF16, NEAR)
+    return call(pair_kernel, [(kept, NEAR), (swap_bit(given, bit), NEAR)], [half] * 2,
+                [pltpu.VMEM(kept.shape, F32)], time=0.3, after=after)
+
+
+def swap_bit(values, bit):
+    return lax.ppermute(values, "tile", [(t, t ^ bit) for t in range(lax.axis_size("tile"))])
 
 
 def body(inputs, grad_out, kernel, w_in, w_out, neighbours, rotations):
@@ -523,7 +598,7 @@
                   [pltpu.VMEM((channels, rim), BF16), pltpu.SemaphoreType.DMA((tiles,))])
     _, kernel = lax.optimization_barrier((rims, kernel))
     taps = jnp.broadcast_to(kernel[:, :, None], (KSIZE * KSIZE, channels, LANES))
-    cot_pieces = gather_pieces(cot, groups)
+    cot_pieces, _ = gather_pieces(cot, groups)
     table = neighbours.shape
     w_in_t, x_near, nb_near, rot_near = call(
         prep_kernel, [(w_in, NEAR), (x, FAR), (neighbours, NEAR), (rotations, NEAR)],
@@ -536,7 +611,7 @@
         functools.partial(conv_kernel, edge),
         [(nb_near, NEAR), (rot_near, NEAR), (x_near, NEAR), (rims, NEAR), (taps, NEAR)],
         [((channels, pixels), BF16, NEAR)] + [((channels, wide), BF16, FAR)] * 2,
-        [pltpu.VMEM((channels, len(SIDES) * rim), BF16)], time=2.5,
+        [pltpu.VMEM((len(SIDES) * channels, rim), BF16)], time=2.0,
         after=[(w_in_t, NEAR)])
     feats = lax.all_gather(hid, "chan", axis=0, tiled=True)
     cots, part_in, part_out = call(
@@ -547,38 +622,45 @@
     used = 2 * full * units // LANES
     share = -(-used // (16 * tiles)) * 16
     tap_rows = -(-channels // 64) * 16
-    values = [pltpu.VMEM((units, pixels), F32)] * 2 + [pltpu.VMEM((units, pixels), BF16)] * 2
+    block = 2 * LANES
     [part] = call(
         weight_kernel,
         [(feats, NEAR), (cots, NEAR), (part_in, NEAR), (part_out, NEAR)],
         [((tiles * share, LANES), BF16, RAW)],
-        values + [pltpu.VMEM((tiles * share, LANES), BF16), pltpu.SemaphoreType.DMA((3,))],
+        [pltpu.VMEM((units, pixels), BF16)] * 2
+        + [pltpu.VMEM((tiles * share, LANES), BF16), pltpu.SemaphoreType.DMA((3,))],
         time=2.2)
     part = swap_rows(part.reshape(tiles, share, LANES))
 
-    outputs, grad_hid, tap_part = call(
-        functools.partial(point_kernel, edge),
-        [(feats, NEAR), (cots, NEAR), (w_in, FAR), (w_in_t, NEAR), (w_out, NEAR),
-         (x, FAR), (padded, FAR), (side, FAR)],
-        [((channels, pixels), BF16, FAR), ((channels, pixels), BF16, NEAR),
-         ((tap_rows, LANES), BF16, NEAR)],
-        [pltpu.VMEM((hidden, pixels), F32)] * 2 + [pltpu.VMEM((hidden, pixels), BF16)] * 2
-        + [pltpu.VMEM((KSIZE * 16, wide), BF16), pltpu.VMEM((LANES, wide), BF16)],
-        time=5.5, limit=32)
+    parts = 2 if halves(tiles) else 1
+    placed = ((tiles // parts, channels, rim), BF16, NEAR if parts > 1 else FAR)
+    accum, tap_part, *border = call(
+        functools.partial(back_kernel, edge, block, tiles),
+        [(feats, NEAR), (cots, NEAR), (w_in, FAR), (w_in_t, NEAR), (w_out, NEAR), (padded, FAR),
+         (side, FAR), (cot, FAR), (neighbours, NEAR), (rotations, NEAR), (taps, NEAR)],
+        [((channels, pixels), F32, NEAR), ((tap_rows, LANES), BF16, NEAR)] + [placed] * parts,
+        [pltpu.VMEM((hidden, pixels), BF16), pltpu.VMEM((channels, pixels), BF16),
+         pltpu.VMEM((KSIZE * 16, wide), BF16), pltpu.VMEM((LANES, wide), BF16),
+         pltpu.VMEM((channels, 2 * LANES), BF16), pltpu.VMEM((channels, wide), BF16),
+         pltpu.VMEM((tiles, channels, rim), F32)], time=7.5, limit=32)
     [mine] = call(sum_kernel, [(part, NEAR), (tap_part, NEAR)],
                   [((tiles, share + tap_rows, LANES), BF16, RAW)],
                   [pltpu.VMEM((share + tap_rows, LANES), BF16), pltpu.SemaphoreType.DMA((tiles,))])
     weights = swap_rows(mine)
 
-    accum, border = call(
-        functools.partial(back_kernel, edge),
-        [(neighbours, NEAR), (rotations, NEAR), (grad_hid, NEAR), (taps, NEAR), (cot, FAR)],
-        [((channels, pixels), F32, NEAR), ((tiles, channels, rim), BF16, FAR)],
-        [pltpu.VMEM((channels, 2 * LANES), BF16), pltpu.VMEM((channels, wide), BF16),
-         pltpu.VMEM((tiles, channels, rim), F32)], time=4.0, after=[(mine, RAW)])
-    weights, border = lax.optimization_barrier((weights, border))
-    border = swap_rows(border)
-    pieces = gather_pieces(weights, groups)
+    [outputs] = call(
+        functools.partial(out_kernel, block),
+        [(feats, NEAR), (w_in_t, NEAR), (w_out, NEAR), (x, FAR)], [((channels, pixels), BF16, FAR)],
+        [pltpu.VMEM((hidden, pixels), BF16)], time=4.0, limit=32, after=[(mine, RAW)])
+    bit = 1
+    while bit * 2 < tiles and parts > 1:
+        border, bit = halve(border, bit, [(outputs, RAW)] if bit > 1 else []), bit * 2
+    weights, outputs, *border = lax.optimization_barrier((weights, outputs, *border))
+    border = [border[0], swap_bit(border[1], bit)] if parts > 1 else [swap_rows(border[0])]
+    [grad_in] = call(functools.partial(border_kernel, edge),
+                     [(accum, NEAR)] + [(part, NEAR) for part in border],
+                     [((channels, pixels), BF16, FAR)])
+    pieces, [grad_in] = gather_pieces(weights, groups, [grad_in])
     grads, ends = [], [(0, groups, 2), (1, groups, 2)]
     for last, end in enumerate(ends):
         which = list(range(*end))
@@ -591,8 +673,6 @@
             [pltpu.VMEM((len(which), full, units), F32), pltpu.VMEM((len(which), units, full), F32),
              pltpu.SemaphoreType.DMA((2, len(which)))],
             time=1.3, aliases={1 + len(which): 0, 2 + len(which): 1} if last else None)
-    [grad_in] = call(functools.partial(border_kernel, edge), [(border, NEAR), (accum, NEAR)],
-                     [((channels, pixels), BF16, FAR)], after=[(grads[0], RAW)])
     return (outputs[None], grad_in[None], *grads)
 
 

time: 72.2 us -> 68.3 us (0.946)
  waiting for transfers between devices: 21.5 us -> 15.7 us
  starting transfers between devices: 20.6 us -> 22.6 us
    all_to_all x4 -> x3, waiting for transfers between devices: 16.6 us -> 6.88 us  [swap_rows(): return lax.all_to_all(values, 'tile', 0, 0, tiled=True)]
    ppermute x0 -> x3, waiting for transfers between devices: none -> 6.17 us  [swap_bit(): lax.ppermute(values, 'tile', [(t, t ^ bit) for t in range(lax.axis_size('...]
    ppermute x0 -> x3, starting transfers between devices: none -> 4.98 us  [swap_bit(): lax.ppermute(values, 'tile', [(t, t ^ bit) for t in range(lax.axis_size('...]
    all_to_all x4 -> x3, starting transfers between devices: 18.2 us -> 15.1 us  [swap_rows(): return lax.all_to_all(values, 'tile', 0, 0, tiled=True)]
    ppermute x6, waiting for transfers between devices: 4.92 us -> 2.59 us  [gather_pieces(): pieces[k ^ bit] = lax.ppermute(pieces[k], 'chan', swap)]
    pallas_call x11 -> x13, Pallas kernels: 21 us -> 21 us  [call(): pl.pallas_call(run, out_shape=[pltpu.HBM(s, d) if p in (FAR, RAW) else ja...]
  transfers between devices with their start and end apart: 10 -> 12, of which waited for: 7 -> 7; matrix products, arithmetic and copies ran while one was open for 0% -> 0% of each run, Pallas kernels for 21% -> 23%
where the time goes in v6:
time: 68.3 us; the launch traced here: 67.8 us
  starting transfers between devices  22.6 us (33%)
  Pallas kernels  21 us (31%)
  waiting for transfers between devices  15.7 us (23%)
  blocking collectives  7.33 us (11%)
  between operations  0.84 us (1%)
    pallas_call x13, Pallas kernels, call(): pl.pallas_call(run, out_shape=[pltpu.HBM(s, d) if p in (FAR, RAW) else ja...  21 us
    all_to_all x3, starting transfers between devices, swap_rows(): return lax.all_to_all(values, 'tile', 0, 0, tiled=True)  15.1 us
    all_gather x1, blocking collectives, body(): feats = lax.all_gather(hid, 'chan', axis=0, tiled=True)  7.33 us
    all_to_all x3, waiting for transfers between devices, swap_rows(): return lax.all_to_all(values, 'tile', 0, 0, tiled=True)  6.88 us
    ppermute x3, waiting for transfers between devices, swap_bit(): lax.ppermute(values, 'tile', [(t, t ^ bit) for t in range(lax.axis_size('...  6.17 us
    ppermute x3, starting transfers between devices, swap_bit(): lax.ppermute(values, 'tile', [(t, t ^ bit) for t in range(lax.axis_size('...  4.98 us
    ppermute x6, waiting for transfers between devices, gather_pieces(): pieces[k ^ bit] = lax.ppermute(pieces[k], 'chan', swap)  2.59 us
    ppermute x6, starting transfers between devices, gather_pieces(): pieces[k ^ bit] = lax.ppermute(pieces[k], 'chan', swap)  2.5 us
  transfers between devices with their start and end apart: 12, of which 7 were waited for; matrix products, arithmetic and copies ran while one was open for 0% of the time, Pallas kernels for 23%

profile of v6, /device:TPU:0, one launch (start us, length us, event | category | flops | bytes accessed | tf_op | source)
XLA Modules:
  0.0 67.8 jit_solution(11295115511023748768)
XLA Ops:
  0.7 1.9 %shard_map.110.refs_4_ = bf16[8,64,256]{2,1,0:T(8,128)(2,1)} custom-call(bf16[64,1024]{1,0:T(8,128)(2,1)} %bitcast.10), custom_call_target="tpu_custom_call" | custom-call | flops 1000000000 | bytes 3500000 | tf_op jit(solution)/shard_map/pallas_call | solution.py:75
  2.6 7.4 %all-to-all-start = ((bf16[8,64,256]{2,1,0:T(8,128)(2,1)}), bf16[8,64,256]{2,1,0:T(8,128)(2,1)S(1)}, u32[]{:S(2)}, u32[]{:S(2)}) async-start(bf16[8,64,256]{2,1,0:T(8,128)(2,1)} %shard_map.110.refs_4_), calls=%async_computation | async-start | bytes 524288 | tf_op jit(solution)/shard_map/all_to_all | solution.py:570
  10.0 1.6 %collective-permute-start.1 = (bf16[64,1024]{1,0:T(8,128)(2,1)S(1)}, bf16[64,1024]{1,0:T(8,128)(2,1)S(1)}, u32[]{:S(2)}, u32[]{:S(2)}) collective-permute-start(bf16[64,1024]{1,0:T(8,128)(2,1)S(1)} %bitcast.6), channel_id=1, source_target_pairs={{0,2},{1,3},{2,0},{3,1},{4,6},{5,7},{6,4},{7,5},{8,10},{9,11},{10,... | collective-permute-start | bytes 393224 | tf_op jit(solution)/shard_map/ppermute | solution.py:562
  11.9 1.1 %shard_map.111 = (bf16[1024,256]{1,0:T(8,128)(2,1)S(1)}, bf16[64,1024]{1,0:T(8,128)(2,1)S(1)}, s32[8,8]{1,0:T(8,128)S(1)}, s32[8,8]{1,0:T(8,128)S(1)}) custom-call(bf16[256,1024]{1,0:T(8,128)(2,1)S(1)} %copy-done, bf16[64,1024]{1,0:T(8,128)(2,1)} %bitcast.11, s32[8,8]{1,0:T(8,128)S(1)} %copy-done.3, s32[8,8]{1,0:T(8,128)S(1)} %copy-done.4, ...), custom_call_target="tpu_custom_call" | custom-call | flops 1200000000 | bytes 4200000 | tf_op jit(solution)/shard_map/pallas_call | solution.py:75
  13.0 2.1 %collective-permute-done.1.refs_4_ = bf16[64,1024]{1,0:T(8,128)(2,1)S(1)} collective-permute-done((bf16[64,1024]{1,0:T(8,128)(2,1)S(1)}, bf16[64,1024]{1,0:T(8,128)(2,1)S(1)}, u32[]{:S(2)}, u32[]{:S(2)}) %collective-permute-start.1) | collective-permute-done | bytes 131104 | tf_op jit(solution)/shard_map/ppermute | solution.py:562
  15.0 3.9 %all-to-all-done.refs_3_ = bf16[8,64,256]{2,1,0:T(8,128)(2,1)S(1)} async-done(((bf16[8,64,256]{2,1,0:T(8,128)(2,1)}), bf16[8,64,256]{2,1,0:T(8,128)(2,1)S(1)}, u32[]{:S(2)}, u32[]{:S(2)}) %all-to-all-start) | async-done | bytes 262176 | tf_op jit(solution)/shard_map/all_to_all | solution.py:570
  18.9 1.7 %shard_map.112 = (bf16[64,1024]{1,0:T(8,128)(2,1)S(1)}, bf16[64,1280]{1,0:T(8,128)(2,1)}, bf16[64,1280]{1,0:T(8,128)(2,1)}) custom-call(s32[8,8]{1,0:T(8,128)S(1)} %get-tuple-element.37.refs_0_, s32[8,8]{1,0:T(8,128)S(1)} %get-tuple-element.38.refs_1_, bf16[64,1024]{1,0:T(8,128)(2,1)S(1)} %get-tuple-element.39.refs_2_, ...), custom_call_target="tpu_custom_call" | custom-call | flops 2000000000 | bytes 7000000 | tf_op jit(solution)/shard_map/pallas_call | solution.py:75
  20.6 7.3 %all_gather.3.refs_6_.refs_0_ = bf16[256,1024]{1,0:T(8,128)(2,1)S(1)} all-gather(bf16[64,1024]{1,0:T(8,128)(2,1)S(1)} %get-tuple-element.41), channel_id=1, replica_groups=mesh['tile'=8,'chan'=4] {'chan'}, dimensions={0}, use_global_device_ids=true | all-gather | bytes 655360 | tf_op jit(solution)/shard_map/all_gather | solution.py:616
  28.0 1.7 %shard_map.114 = bf16[1024,128]{1,0:T(8,128)(2,1)} custom-call(bf16[256,1024]{1,0:T(8,128)(2,1)S(1)} %all_gather.3.refs_6_.refs_0_, bf16[256,1024]{1,0:T(8,128)(2,1)S(1)} %get-tuple-element.42.refs_1_, bf16[256,256]{1,0:T(8,128)(2,1)S(1)} %get-tuple-element.43.refs_2_, bf16[256,256]{1,0:T(8,128)(2,1)S(1)} %get-tuple-element.44.refs_3_), custom_call_target="tpu_custom_call" | custom-call | flops 2200000000 | bytes 7700000 | tf_op jit(solution)/shard_map/pallas_call | solution.py:75
  29.8 3.6 %all-to-all-start.1 = ((bf16[8,128,128]{2,1,0:T(8,128)(2,1)}), bf16[8,128,128]{2,1,0:T(8,128)(2,1)S(1)}, u32[]{:S(2)}, u32[]{:S(2)}) async-start(bf16[8,128,128]{2,1,0:T(8,128)(2,1)} %bitcast.9), calls=%async_computation.1 | async-start | bytes 524288 | tf_op jit(solution)/shard_map/all_to_all | solution.py:570
  33.4 7.0 %shard_map.115 = (f32[64,1024]{1,0:T(8,128)S(1)}, bf16[16,128]{1,0:T(8,128)(2,1)S(1)}, bf16[4,64,256]{2,1,0:T(8,128)(2,1)S(1)}, bf16[4,64,256]{2,1,0:T(8,128)(2,1)S(1)}) custom-call(bf16[256,1024]{1,0:T(8,128)(2,1)S(1)} %all_gather.3.refs_6_.refs_0_, bf16[256,1024]{1,0:T(8,128)(2,1)S(1)} %get-tuple-element.42.refs_1_, bf16[256,1024]{1,0:T(8,128)(2,1)} %refs_2_.4, ...), custom_call_target="tpu_custom_call" | custom-call | flops 7500000256 | bytes 26250000 | tf_op jit(solution)/shard_map/pallas_call | solution.py:75
  40.3 2.1 %collective-permute-start.3 = (bf16[4,64,256]{2,1,0:T(8,128)(2,1)S(1)}, bf16[4,64,256]{2,1,0:T(8,128)(2,1)S(1)}, u32[]{:S(2)}, u32[]{:S(2)}) collective-permute-start(bf16[4,64,256]{2,1,0:T(8,128)(2,1)S(1)} %get-tuple-element.49), channel_id=1, source_target_pairs={{0,4},{4,0},{8,12},{12,8},{16,20},{20,16},{24,28},{28,24},{1,5},{5... | collective-permute-start | bytes 393224 | tf_op jit(solution)/shard_map/ppermute | solution.py:581
  42.8 0.8 %shard_map.116.refs_4_ = bf16[8,144,128]{2,1,0:T(8,128)(2,1)} custom-call(bf16[8,128,128]{2,1,0:T(8,128)(2,1)S(1)} %all-to-all-done.1.refs_0_, bf16[16,128]{1,0:T(8,128)(2,1)S(1)} %get-tuple-element.47.refs_1_), custom_call_target="tpu_custom_call" | custom-call | flops 1000000000 | bytes 3500000 | tf_op jit(solution)/shard_map/pallas_call | solution.py:75
  43.7 4.1 %all-to-all-start.2 = ((bf16[8,144,128]{2,1,0:T(8,128)(2,1)}), bf16[8,144,128]{2,1,0:T(8,128)(2,1)S(1)}, u32[]{:S(2)}, u32[]{:S(2)}) async-start(bf16[8,144,128]{2,1,0:T(8,128)(2,1)} %shard_map.116.refs_4_), calls=%async_computation.2 | async-start | bytes 589824 | tf_op jit(solution)/shard_map/all_to_all | solution.py:570
  47.9 2.1 %collective-permute-start.4 = (bf16[2,64,256]{2,1,0:T(8,128)(2,1)S(1)}, bf16[2,64,256]{2,1,0:T(8,128)(2,1)S(1)}, u32[]{:S(2)}, u32[]{:S(2)}) collective-permute-start(bf16[2,64,256]{2,1,0:T(8,128)(2,1)S(1)} %get-tuple-element.51), channel_id=1, source_target_pairs={{0,8},{4,12},{8,0},{12,4},{16,24},{20,28},{24,16},{28,20},{1,9},{5... | collective-permute-start | bytes 196616 | tf_op jit(solution)/shard_map/ppermute | solution.py:581
  50.0 2.9 %shard_map.117.refs_2_ = bf16[64,1024]{1,0:T(8,128)(2,1)} custom-call(bf16[256,1024]{1,0:T(8,128)(2,1)S(1)} %all_gather.3.refs_6_.refs_0_, bf16[1024,256]{1,0:T(8,128)(2,1)S(1)} %get-tuple-element.40.refs_5_.refs_0_.refs_3_.refs_1_, bf16[1024,256]{1,0:T(8,128)(2,1)S(1)} %copy-done.1, bf16[64,1024]{1,0:T(8,128)(2,1)} %bitcast.12, ...), custom_call_target="tpu_custom_call" | custom-call | flops 4000000000 | bytes 14000000 | tf_op jit(solution)/shard_map/pallas_call | solution.py:75
  52.8 2.2 %collective-permute-done.4.refs_1_ = bf16[2,64,256]{2,1,0:T(8,128)(2,1)S(1)} collective-permute-done((bf16[2,64,256]{2,1,0:T(8,128)(2,1)S(1)}, bf16[2,64,256]{2,1,0:T(8,128)(2,1)S(1)}, u32[]{:S(2)}, u32[]{:S(2)}) %collective-permute-start.4) | collective-permute-done | bytes 65568 | tf_op jit(solution)/shard_map/ppermute | solution.py:581
  55.0 2.6 %all-to-all-done.2.refs_0_ = bf16[8,144,128]{2,1,0:T(8,128)(2,1)S(1)} async-done(((bf16[8,144,128]{2,1,0:T(8,128)(2,1)}), bf16[8,144,128]{2,1,0:T(8,128)(2,1)S(1)}, u32[]{:S(2)}, u32[]{:S(2)}) %all-to-all-start.2) | async-done | bytes 294944 | tf_op jit(solution)/shard_map/all_to_all | solution.py:570
  57.6 0.8 %collective-permute-start.5 = (bf16[8,144,128]{2,1,0:T(8,128)(2,1)S(1)}, bf16[8,144,128]{2,1,0:T(8,128)(2,1)S(1)}, u32[]{:S(2)}, u32[]{:S(2)}) collective-permute-start(bf16[8,144,128]{2,1,0:T(8,128)(2,1)S(1)} %all-to-all-done.2.refs_0_), channel_id=1, source_target_pairs={{0,2},{1,3},{2,0},{3,1},{4,6},{5,7},{6,4},{7,5},{8,10},{9,11},{10,... | collective-permute-start | bytes 884744 | tf_op jit(solution)/shard_map/ppermute | solution.py:562
  58.5 0.8 %collective-permute-start.6 = (bf16[1,64,256]{2,1,0:T(8,128)(2,1)S(1)}, bf16[1,64,256]{2,1,0:T(8,128)(2,1)S(1)}, u32[]{:S(2)}, u32[]{:S(2)}) collective-permute-start(bf16[1,64,256]{2,1,0:T(8,128)(2,1)S(1)} %get-tuple-element.58), channel_id=1, source_target_pairs={{0,16},{4,20},{8,24},{12,28},{16,0},{20,4},{24,8},{28,12},{1,17},{... | collective-permute-start | bytes 98312 | tf_op jit(solution)/shard_map/ppermute | solution.py:581
  59.3 4.0 %collective-permute-done.6.refs_2_ = bf16[1,64,256]{2,1,0:T(8,128)(2,1)S(1)} collective-permute-done((bf16[1,64,256]{2,1,0:T(8,128)(2,1)S(1)}, bf16[1,64,256]{2,1,0:T(8,128)(2,1)S(1)}, u32[]{:S(2)}, u32[]{:S(2)}) %collective-permute-start.6) | collective-permute-done | bytes 32800 | tf_op jit(solution)/shard_map/ppermute | solution.py:581
  63.3 1.1 %shard_map.120 = bf16[64,1024]{1,0:T(8,128)(2,1)} custom-call(f32[64,1024]{1,0:T(8,128)S(1)} %get-tuple-element.56.refs_0_, bf16[1,64,256]{2,1,0:T(8,128)(2,1)S(1)} %get-tuple-element.57.refs_1_, bf16[1,64,256]{2,1,0:T(8,128)(2,1)S(1)} %collective-permute-done.6.refs_2_), custom_call_target="tpu_custom_call" | custom-call | flops 1000000000 | bytes 3500000 | tf_op jit(solution)/shard_map/pallas_call | solution.py:75
  64.5 1.0 %shard_map.121 = (f32[256,1024]{1,0:T(8,128)}, f32[1024,256]{1,0:T(8,128)}, f32[256,128]{1,0:T(8,128)S(1)}) custom-call(bf16[8,144,128]{2,1,0:T(8,128)(2,1)S(1)} %all-to-all-done.2.refs_0_, bf16[8,144,128]{2,1,0:T(8,128)(2,1)S(1)} %collective-permute-done.5.refs_1_), custom_call_target="tpu_custom_call" | custom-call | flops 1300000000 | bytes 4550000 | tf_op jit(solution)/shard_map/pallas_call | solution.py:75
  66.1 1.7 %shard_map.122 = (f32[256,1024]{1,0:T(8,128)}, f32[1024,256]{1,0:T(8,128)}, f32[25,256]{1,0:T(8,128)}) custom-call(bf16[8,144,128]{2,1,0:T(8,128)(2,1)S(1)} %collective-permute-done.7.refs_0_, bf16[8,144,128]{2,1,0:T(8,128)(2,1)S(1)} %collective-permute-done.8.refs_1_, ...), custom_call_target="tpu_custom_call", output_to_operand_aliasing={{0}: (3, {}), {1}: (4, {})} | custom-call | flops 1300000000 | bytes 4550000 | tf_op jit(solution)/shard_map/pallas_call | solution.py:75
  (27 shorter events, 1.5 us)
Async XLA Ops:
  0.6 9.3 %copy-start.2 = (bf16[1,64,1024]{2,1,0:T(8,128)(2,1)S(1)}, bf16[1,64,1024]{2,1,0:T(8,128)(2,1)}, u32[]{:S(2)}) copy-start(bf16[1,64,1024]{2,1,0:T(8,128)(2,1)} %param.8) | copy-start | bytes 393220
  0.6 10.9 %copy-start.5 = (bf16[25,64]{1,0:T(8,128)(2,1)S(1)}, bf16[25,64]{1,0:T(8,128)(2,1)}, u32[]{:S(2)}) copy-start(bf16[25,64]{1,0:T(8,128)(2,1)} %param.9) | copy-start | bytes 9604
  2.6 9.3 %copy-start = (bf16[256,1024]{1,0:T(8,128)(2,1)S(1)}, bf16[256,1024]{1,0:T(8,128)(2,1)}, u32[]{:S(2)}) copy-start(bf16[256,1024]{1,0:T(8,128)(2,1)} %refs_2_.4) | copy-start | bytes 1572868
  2.6 16.3 %all-to-all-start = ((bf16[8,64,256]{2,1,0:T(8,128)(2,1)}), bf16[8,64,256]{2,1,0:T(8,128)(2,1)S(1)}, u32[]{:S(2)}, u32[]{:S(2)}) async-start(bf16[8,64,256]{2,1,0:T(8,128)(2,1)} %shard_map.110.refs_4_), calls=%async_computation | async-start | bytes 524288 | tf_op jit(solution)/shard_map/all_to_all | solution.py:570
  10.0 1.9 %copy-start.3 = (s32[8,8]{1,0:T(8,128)S(1)}, s32[8,8]{1,0:T(8,128)}, u32[]{:S(2)}) copy-start(s32[8,8]{1,0:T(8,128)} %refs_8_.1) | copy-start | bytes 772
  10.0 1.9 %copy-start.4 = (s32[8,8]{1,0:T(8,128)S(1)}, s32[8,8]{1,0:T(8,128)}, u32[]{:S(2)}) copy-start(s32[8,8]{1,0:T(8,128)} %refs_9_.1) | copy-start | bytes 772
  10.0 5.0 %collective-permute-start.1 = (bf16[64,1024]{1,0:T(8,128)(2,1)S(1)}, bf16[64,1024]{1,0:T(8,128)(2,1)S(1)}, u32[]{:S(2)}, u32[]{:S(2)}) collective-permute-start(bf16[64,1024]{1,0:T(8,128)(2,1)S(1)} %bitcast.6), channel_id=1, source_target_pairs={{0,2},{1,3},{2,0},{3,1},{4,6},{5,7},{6,4},{7,5},{8,10},{9,11},{10,... | collective-permute-start | bytes 393224 | tf_op jit(solution)/shard_map/ppermute | solution.py:562
  11.6 16.4 %collective-permute-start = (bf16[64,1024]{1,0:T(8,128)(2,1)S(1)}, bf16[64,1024]{1,0:T(8,128)(2,1)S(1)}, u32[]{:S(2)}, u32[]{:S(2)}) collective-permute-start(bf16[64,1024]{1,0:T(8,128)(2,1)S(1)} %bitcast.7), channel_id=1, source_target_pairs={{0,1},{1,0},{2,3},{3,2},{4,5},{5,4},{6,7},{7,6},{8,9},{9,8},{10,11... | collective-permute-start | bytes 393224 | tf_op jit(solution)/shard_map/ppermute | solution.py:562
  15.0 12.9 %collective-permute-start.2 = (bf16[64,1024]{1,0:T(8,128)(2,1)S(1)}, bf16[64,1024]{1,0:T(8,128)(2,1)S(1)}, u32[]{:S(2)}, u32[]{:S(2)}) collective-permute-start(bf16[64,1024]{1,0:T(8,128)(2,1)S(1)} %collective-permute-done.1.refs_4_), channel_id=1, source_target_pairs={{0,1},{1,0},{2,3},{3,2},{4,5},{5,4},{6,7},{7,6},{8,9},{9,8},{10,11... | collective-permute-start | bytes 393224 | tf_op jit(solution)/shard_map/ppermute | solution.py:562
  20.6 7.4 %copy-start.1 = (bf16[1024,256]{1,0:T(8,128)(2,1)S(1)}, bf16[1024,256]{1,0:T(8,128)(2,1)}, u32[]{:S(2)}) copy-start(bf16[1024,256]{1,0:T(8,128)(2,1)} %refs_2_.5) | copy-start | bytes 1572868
  29.8 13.1 %all-to-all-start.1 = ((bf16[8,128,128]{2,1,0:T(8,128)(2,1)}), bf16[8,128,128]{2,1,0:T(8,128)(2,1)S(1)}, u32[]{:S(2)}, u32[]{:S(2)}) async-start(bf16[8,128,128]{2,1,0:T(8,128)(2,1)} %bitcast.9), calls=%async_computation.1 | async-start | bytes 524288 | tf_op jit(solution)/shard_map/all_to_all | solution.py:570
  40.3 7.5 %collective-permute-start.3 = (bf16[4,64,256]{2,1,0:T(8,128)(2,1)S(1)}, bf16[4,64,256]{2,1,0:T(8,128)(2,1)S(1)}, u32[]{:S(2)}, u32[]{:S(2)}) collective-permute-start(bf16[4,64,256]{2,1,0:T(8,128)(2,1)S(1)} %get-tuple-element.49), channel_id=1, source_target_pairs={{0,4},{4,0},{8,12},{12,8},{16,20},{20,16},{24,28},{28,24},{1,5},{5... | collective-permute-start | bytes 393224 | tf_op jit(solution)/shard_map/ppermute | solution.py:581
  43.7 14.0 %all-to-all-start.2 = ((bf16[8,144,128]{2,1,0:T(8,128)(2,1)}), bf16[8,144,128]{2,1,0:T(8,128)(2,1)S(1)}, u32[]{:S(2)}, u32[]{:S(2)}) async-start(bf16[8,144,128]{2,1,0:T(8,128)(2,1)} %shard_map.116.refs_4_), calls=%async_computation.2 | async-start | bytes 589824 | tf_op jit(solution)/shard_map/all_to_all | solution.py:570
  47.9 7.1 %collective-permute-start.4 = (bf16[2,64,256]{2,1,0:T(8,128)(2,1)S(1)}, bf16[2,64,256]{2,1,0:T(8,128)(2,1)S(1)}, u32[]{:S(2)}, u32[]{:S(2)}) collective-permute-start(bf16[2,64,256]{2,1,0:T(8,128)(2,1)S(1)} %get-tuple-element.51), channel_id=1, source_target_pairs={{0,8},{4,12},{8,0},{12,4},{16,24},{20,28},{24,16},{28,20},{1,9},{5... | collective-permute-start | bytes 196616 | tf_op jit(solution)/shard_map/ppermute | solution.py:581
  57.6 6.8 %collective-permute-start.5 = (bf16[8,144,128]{2,1,0:T(8,128)(2,1)S(1)}, bf16[8,144,128]{2,1,0:T(8,128)(2,1)S(1)}, u32[]{:S(2)}, u32[]{:S(2)}) collective-permute-start(bf16[8,144,128]{2,1,0:T(8,128)(2,1)S(1)} %all-to-all-done.2.refs_0_), channel_id=1, source_target_pairs={{0,2},{1,3},{2,0},{3,1},{4,6},{5,7},{6,4},{7,5},{8,10},{9,11},{10,... | collective-permute-start | bytes 884744 | tf_op jit(solution)/shard_map/ppermute | solution.py:562
  58.5 4.8 %collective-permute-start.6 = (bf16[1,64,256]{2,1,0:T(8,128)(2,1)S(1)}, bf16[1,64,256]{2,1,0:T(8,128)(2,1)S(1)}, u32[]{:S(2)}, u32[]{:S(2)}) collective-permute-start(bf16[1,64,256]{2,1,0:T(8,128)(2,1)S(1)} %get-tuple-element.58), channel_id=1, source_target_pairs={{0,16},{4,20},{8,24},{12,28},{16,0},{20,4},{24,8},{28,12},{1,17},{... | collective-permute-start | bytes 98312 | tf_op jit(solution)/shard_map/ppermute | solution.py:581
  59.3 6.2 %collective-permute-start.7 = (bf16[8,144,128]{2,1,0:T(8,128)(2,1)S(1)}, bf16[8,144,128]{2,1,0:T(8,128)(2,1)S(1)}, u32[]{:S(2)}, u32[]{:S(2)}) collective-permute-start(bf16[8,144,128]{2,1,0:T(8,128)(2,1)S(1)} %all-to-all-done.2.refs_0_), channel_id=1, source_target_pairs={{0,1},{1,0},{2,3},{3,2},{4,5},{5,4},{6,7},{7,6},{8,9},{9,8},{10,11... | collective-permute-start | bytes 884744 | tf_op jit(solution)/shard_map/ppermute | solution.py:562
  64.4 1.6 %collective-permute-start.8 = (bf16[8,144,128]{2,1,0:T(8,128)(2,1)S(1)}, bf16[8,144,128]{2,1,0:T(8,128)(2,1)S(1)}, u32[]{:S(2)}, u32[]{:S(2)}) collective-permute-start(bf16[8,144,128]{2,1,0:T(8,128)(2,1)S(1)} %collective-permute-done.5.refs_1_), channel_id=1, source_target_pairs={{0,1},{1,0},{2,3},{3,2},{4,5},{5,4},{6,7},{7,6},{8,9},{9,8},{10,11... | collective-permute-start | bytes 884744 | tf_op jit(solution)/shard_map/ppermute | solution.py:562

commit v7 on v6

--- a/solution.py
+++ b/solution.py
@@ -191,26 +191,24 @@
         copy.wait()
 
 
-def conv_kernel(edge, neighbours, rotations, x, rims, taps,
+def conv_kernel(edge, neighbours, top, low, pick, slot, spread, x, rims, taps,
                 hidden_ref, padded, side, gathered):
     padded_ref, side_ref = padded.ref, side.ref
     rims_ref, taps_ref = rims.get(), taps.get()
     channels, pixels = hidden_ref.shape
     wide = pixels + 2 * LANES
-    nb, rot = tile_row(neighbours), tile_row(rotations)
-    top, low = row_halo_maps(rot[1], rot[6], edge)
-    padded_ref[:, :LANES] = dot(rims_ref[nb[1]], top).astype(BF16)
-    padded_ref[:, LANES + pixels:] = dot(rims_ref[nb[6]], low).astype(BF16)
+    nb = tile_row(neighbours)
+    padded_ref[:, :LANES] = dot(rims_ref[nb[1]], top.get()[...]).astype(BF16)
+    padded_ref[:, LANES + pixels:] = dot(rims_ref[nb[6]], low.get()[...]).astype(BF16)
     for position, d in enumerate(SIDES):
         gathered[position * channels:(position + 1) * channels, :] = rims_ref[nb[d]]
-    pick, slot = side_map([rot[d] for d in SIDES], edge)
-    candidates = dot(gathered[...], pick)
+    candidates, slot = dot(gathered[...], pick.get()[...]), slot.get()[...]
     packed = candidates[:channels, :]
     for position in range(1, len(SIDES)):
         packed = jnp.where(slot == position,
                            candidates[position * channels:(position + 1) * channels, :], packed)
     packed = packed.astype(BF16)
-    side_ref[...] = dot(packed, spread_map(edge, wide)).astype(BF16)
+    side_ref[...] = dot(packed, spread.get()[...]).astype(BF16)
     side.send()
     padded_ref[:, LANES:LANES + pixels] = x.get()[...]
     padded.send()
@@ -328,8 +326,14 @@
                  d_row, d_side, gathered)
 
 
-def prep_kernel(w_in, x, neighbours, rotations, w_in_t_ref, x_ref, nb_ref, rot_ref):
-    nb_ref[...], rot_ref[...] = neighbours.get()[...], rotations.get()[...]
+def prep_kernel(edge, w_in, x, neighbours, rotations, w_in_t_ref, x_ref, nb_ref, *map_refs):
+    nb_ref[...] = neighbours.get()[...]
+    rot = tile_row(rotations)
+    pick, slot = side_map([rot[d] for d in SIDES], edge)
+    wide = x_ref.shape[1] + 2 * LANES
+    maps = (*row_halo_maps(rot[1], rot[6], edge), pick, slot, spread_map(edge, wide))
+    for ref, values in zip(map_refs, maps):
+        ref[...] = values
     w_in_t_ref[...] = w_in.get()[...].astype(F32).T.astype(BF16)
     x_ref[...] = x.get()[...]
 
@@ -460,9 +464,13 @@
     if not halves(tiles):
         return tile
     apart, slot = tile ^ lax.axis_index("tile"), 0
-    for bit in range(tiles.bit_length() - 1):
-        slot = slot * 2 + ((apart >> bit) & 1)
+    for bit in halving_bits(tiles):
+        slot = slot * 2 + jnp.where(apart & bit != 0, 1, 0)
     return slot
+
+
+def halving_bits(tiles):
+    return [1 << i for i in range(tiles.bit_length() - 2, 0, -2)] + [1, 2][:tiles.bit_length() - 2]
 
 
 def pair_kernel(kept, other, *refs):
@@ -501,31 +509,38 @@
         copy.wait()
 
 
-def final_kernel(which, last, share, channels, scale, *refs):
-    count = len(which)
-    pieces, taps_in = refs[:count], refs[count]
+def compact_kernel(share, values, out):
+    values = values.get()
+    tiles, rows, _ = values.shape
+    for tile in range(tiles):
+        out[tile * share:(tile + 1) * share, :] = values[tile, :share, :]
+    taps = values[0, share:, :].astype(F32)
+    for tile in range(1, tiles):
+        taps = taps + values[tile, share:, :].astype(F32)
+    out[tiles * share:, :] = taps.astype(BF16)
+
+
+def final_kernel(which, channels, tap_rows, scale, last, *refs):
+    pieces, taps_in = refs[:len(which)], refs[len(which)]
     g_in, g_out, g_tap_ref, buf_in, buf_out, sems = refs[-6:]
     full, units = buf_in.shape[1:]
-    tiles, rows, _ = pieces[0].ref.shape
     copies = []
-    all_taps = taps_in.get()[...] if last else jnp.zeros((full, LANES), F32)
+    all_taps = taps_in.get()[...]
     row_of = lax.broadcasted_iota(jnp.int32, (full, LANES), 0)
     for i, k in enumerate(which):
         piece = pieces[i].get()
         owner = lax.axis_index("chan") ^ k
         start = pl.multiple_of(owner * units, units)
-        for in_in, buffer, target in ((True, buf_in, g_in.at[:, pl.ds(start, units)]),
-                                      (False, buf_out, g_out.at[pl.ds(start, units)])):
-            for tile in range(tiles):
-                for row, height, column, at, into_in in chunks(tile, share, units, full):
-                    if into_in == in_in:
-                        values = piece[tile, row:row + height, :].astype(F32) * scale
-                        buffer[i, at:at + height, column:column + LANES] = values
-            copies.append(pltpu.make_async_copy(buffer.at[i], target, sems.at[int(in_in), i]))
+        used = 0
+        for buffer, target in ((buf_in, g_in.at[:, pl.ds(start, units)]),
+                               (buf_out, g_out.at[pl.ds(start, units)])):
+            height, width = buffer.shape[1:]
+            for column in range(0, width, LANES):
+                buffer[i, :, column:column + LANES] = piece[used:used + height, :].astype(F32) * scale
+                used += height
+            copies.append(pltpu.make_async_copy(buffer.at[i], target, sems.at[len(copies)]))
             copies[-1].start()
-        taps = piece[0, share:, :].astype(F32)
-        for tile in range(1, tiles):
-            taps = taps + piece[tile, share:, :].astype(F32)
+        taps = piece[piece.shape[0] - tap_rows:, :].astype(F32)
         blocks = []
         for block in range(channels // 16):
             values = taps[block // 4 * 16:block // 4 * 16 + 16, :]
@@ -540,30 +555,18 @@
         copy.wait()
 
 
-def chunks(tile, share, units, full):
-    inside, found = units // LANES * full, []
-    row, end = tile * share, min((tile + 1) * share, 2 * units * full // LANES)
-    while row < end:
-        height = full if row < inside else units
-        offset = row if row < inside else row - inside
-        column, at = offset // height * LANES, offset % height
-        count = min(end - row, height - at)
-        found.append((row - tile * share, count, column, at, row < inside))
-        row += count
-    return found
-
-
-def gather_pieces(own, groups, beside=()):
+def swap_chan(values, bit):
+    return lax.ppermute(values, "chan", [(i, i ^ bit) for i in range(lax.axis_size("chan"))])
+
+
+def gather_pieces(own, groups):
     pieces = {0: own}
     bit = groups // 2
     while bit:
-        swap = [(i, i ^ bit) for i in range(groups)]
         for k in list(pieces):
-            pieces[k ^ bit] = lax.ppermute(pieces[k], "chan", swap)
-        if len(pieces) == 2 and beside:
-            pieces[bit], *beside = lax.optimization_barrier((pieces[bit], *beside))
+            pieces[k ^ bit] = swap_chan(pieces[k], bit)
         bit //= 2
-    return [pieces[k] for k in range(groups)], beside
+    return [pieces[k] for k in range(groups)]
 
 
 def swap_rows(values):
@@ -598,18 +601,21 @@
                   [pltpu.VMEM((channels, rim), BF16), pltpu.SemaphoreType.DMA((tiles,))])
     _, kernel = lax.optimization_barrier((rims, kernel))
     taps = jnp.broadcast_to(kernel[:, :, None], (KSIZE * KSIZE, channels, LANES))
-    cot_pieces, _ = gather_pieces(cot, groups)
+    cot_pieces = gather_pieces(cot, groups)
     table = neighbours.shape
-    w_in_t, x_near, nb_near, rot_near = call(
-        prep_kernel, [(w_in, NEAR), (x, FAR), (neighbours, NEAR), (rotations, NEAR)],
-        [((hidden, full), BF16, NEAR), ((channels, pixels), BF16, NEAR)]
-        + [(neighbours.shape, jnp.int32, NEAR)] * 2, time=1.2,
+    w_in_t, x_near, nb_near, *maps = call(
+        functools.partial(prep_kernel, edge),
+        [(w_in, NEAR), (x, FAR), (neighbours, NEAR), (rotations, NEAR)],
+        [((hidden, full), BF16, NEAR), ((channels, pixels), BF16, NEAR),
+         (neighbours.shape, jnp.int32, NEAR), ((rim, LANES), BF16, NEAR), ((rim, LANES), BF16, NEAR),
+         ((rim, 2 * LANES), BF16, NEAR), ((1, 2 * LANES), jnp.int32, NEAR),
+         ((2 * LANES, wide), BF16, NEAR)], time=1.2,
         after=[(rims, RAW), (taps, NEAR)])
     rims = swap_rows(rims)
 
     hid, padded, side = call(
         functools.partial(conv_kernel, edge),
-        [(nb_near, NEAR), (rot_near, NEAR), (x_near, NEAR), (rims, NEAR), (taps, NEAR)],
+        [(a, NEAR) for a in (nb_near, *maps, x_near, rims, taps)],
         [((channels, pixels), BF16, NEAR)] + [((channels, wide), BF16, FAR)] * 2,
         [pltpu.VMEM((len(SIDES) * channels, rim), BF16)], time=2.0,
         after=[(w_in_t, NEAR)])
@@ -646,33 +652,47 @@
     [mine] = call(sum_kernel, [(part, NEAR), (tap_part, NEAR)],
                   [((tiles, share + tap_rows, LANES), BF16, RAW)],
                   [pltpu.VMEM((share + tap_rows, LANES), BF16), pltpu.SemaphoreType.DMA((tiles,))])
-    weights = swap_rows(mine)
+    [weights] = call(functools.partial(compact_kernel, share), [(swap_rows(mine), NEAR)],
+                     [((tiles * share + tap_rows, LANES), BF16, NEAR)], time=0.1)
 
     [outputs] = call(
         functools.partial(out_kernel, block),
         [(feats, NEAR), (w_in_t, NEAR), (w_out, NEAR), (x, FAR)], [((channels, pixels), BF16, FAR)],
         [pltpu.VMEM((hidden, pixels), BF16)], time=4.0, limit=32, after=[(mine, RAW)])
-    bit = 1
-    while bit * 2 < tiles and parts > 1:
-        border, bit = halve(border, bit, [(outputs, RAW)] if bit > 1 else []), bit * 2
+    bits = halving_bits(tiles) if parts > 1 else [0]
+    for step, bit in enumerate(bits[:-1]):
+        border = halve(border, bit, [(outputs, RAW)] if step else [])
     weights, outputs, *border = lax.optimization_barrier((weights, outputs, *border))
-    border = [border[0], swap_bit(border[1], bit)] if parts > 1 else [swap_rows(border[0])]
+    border = [border[0], swap_bit(border[1], bits[-1])] if parts > 1 else [swap_rows(border[0])]
     [grad_in] = call(functools.partial(border_kernel, edge),
                      [(accum, NEAR)] + [(part, NEAR) for part in border],
                      [((channels, pixels), BF16, FAR)])
-    pieces, [grad_in] = gather_pieces(weights, groups, [grad_in])
-    grads, ends = [], [(0, groups, 2), (1, groups, 2)]
-    for last, end in enumerate(ends):
-        which = list(range(*end))
+
+    def place(which, grads, last):
         tap_shape = (KSIZE * KSIZE, full) if last else (full, LANES)
-        grads = call(
-            functools.partial(final_kernel, which, last, share, channels, scale),
-            [(pieces[k], NEAR) for k in which]
-            + ([(grads[2], NEAR), (grads[0], RAW), (grads[1], RAW)] if last else []),
+        more = [(grads[0], RAW), (grads[1], RAW)] if grads[0] is not None else []
+        return call(
+            functools.partial(final_kernel, which, channels, tap_rows, scale, last),
+            [(pieces[k], NEAR) for k in which] + [(grads[2], NEAR)] + more,
             [((full, hidden), F32, RAW), ((hidden, full), F32, RAW), (tap_shape, F32, NEAR)],
             [pltpu.VMEM((len(which), full, units), F32), pltpu.VMEM((len(which), units, full), F32),
-             pltpu.SemaphoreType.DMA((2, len(which)))],
-            time=1.3, aliases={1 + len(which): 0, 2 + len(which): 1} if last else None)
+             pltpu.SemaphoreType.DMA((2 * len(which),))],
+            time=1.2, aliases={1 + len(which): 0, 2 + len(which): 1} if more else None)
+
+    pieces = {0: weights}
+    bit = groups // 2
+    while bit > 1:
+        for k in [k for k in pieces if k % 2 == 0]:
+            pieces[k ^ bit] = swap_chan(pieces[k], bit)
+        bit //= 2
+    pieces[1] = swap_chan(weights, 1)
+    even, odd = list(range(2, groups, 2)), list(range(3, groups, 2))
+    for k in even:
+        pieces[k], grad_in = lax.optimization_barrier((pieces[k], grad_in))
+    for k in odd:
+        pieces[k] = swap_chan(pieces[k ^ 1], 1)
+    grads = place([0, 1, *even], [None, None, jnp.zeros((full, LANES), F32)], False)
+    grads = place(odd, grads, True)
     return (outputs[None], grad_in[None], *grads)
 
 

time: 68.3 us -> 67.1 us (0.982)
  waiting for transfers between devices: 15.7 us -> 14.1 us
    ppermute x3, waiting for transfers between devices: 6.17 us -> 5.09 us  [swap_bit(): lax.ppermute(values, 'tile', [(t, t ^ bit) for t in range(lax.axis_size('...]
    ppermute x3, starting transfers between devices: 4.98 us -> 5.75 us  [swap_bit(): lax.ppermute(values, 'tile', [(t, t ^ bit) for t in range(lax.axis_size('...]
    pallas_call x13 -> x14, Pallas kernels: 21 us -> 21.2 us  [call(): pl.pallas_call(run, out_shape=[pltpu.HBM(s, d) if p in (FAR, RAW) else ja...]
  transfers between devices with their start and end apart: 12 -> 12, of which waited for: 7 -> 8; matrix products, arithmetic and copies ran while one was open for 0% -> 0% of each run, Pallas kernels for 23% -> 24%
where the time goes in v7:
time: 67.1 us; the launch traced here: 66.6 us
  starting transfers between devices  22.8 us (34%)
  Pallas kernels  21.2 us (32%)
  waiting for transfers between devices  14.1 us (21%)
  blocking collectives  7.33 us (11%)
  between operations  0.82 us (1%)
    pallas_call x14, Pallas kernels, call(): pl.pallas_call(run, out_shape=[pltpu.HBM(s, d) if p in (FAR, RAW) else ja...  21.2 us
    all_to_all x3, starting transfers between devices, swap_rows(): return lax.all_to_all(values, 'tile', 0, 0, tiled=True)  14.6 us
    all_gather x1, blocking collectives, body(): feats = lax.all_gather(hid, 'chan', axis=0, tiled=True)  7.33 us
    all_to_all x3, waiting for transfers between devices, swap_rows(): return lax.all_to_all(values, 'tile', 0, 0, tiled=True)  6.31 us
    ppermute x3, starting transfers between devices, swap_bit(): lax.ppermute(values, 'tile', [(t, t ^ bit) for t in range(lax.axis_size('...  5.75 us
    ppermute x3, waiting for transfers between devices, swap_bit(): lax.ppermute(values, 'tile', [(t, t ^ bit) for t in range(lax.axis_size('...  5.09 us
    ppermute x6, waiting for transfers between devices, swap_chan(): lax.ppermute(values, 'chan', [(i, i ^ bit) for i in range(lax.axis_size('...  2.72 us
    ppermute x6, starting transfers between devices, swap_chan(): lax.ppermute(values, 'chan', [(i, i ^ bit) for i in range(lax.axis_size('...  2.44 us
  transfers between devices with their start and end apart: 12, of which 8 were waited for; matrix products, arithmetic and copies ran while one was open for 0% of the time, Pallas kernels for 24%

profile of v7, /device:TPU:0, one launch (start us, length us, event | category | flops | bytes accessed | tf_op | source)
XLA Modules:
  0.0 66.6 jit_solution(2966240589132196287)
XLA Ops:
  0.7 1.9 %shard_map.110.refs_4_ = bf16[8,64,256]{2,1,0:T(8,128)(2,1)} custom-call(bf16[64,1024]{1,0:T(8,128)(2,1)} %bitcast.10), custom_call_target="tpu_custom_call" | custom-call | flops 1000000000 | bytes 3500000 | tf_op jit(solution)/shard_map/pallas_call | solution.py:75
  2.6 7.4 %all-to-all-start = ((bf16[8,64,256]{2,1,0:T(8,128)(2,1)}), bf16[8,64,256]{2,1,0:T(8,128)(2,1)S(1)}, u32[]{:S(2)}, u32[]{:S(2)}) async-start(bf16[8,64,256]{2,1,0:T(8,128)(2,1)} %shard_map.110.refs_4_), calls=%async_computation | async-start | bytes 524288 | tf_op jit(solution)/shard_map/all_to_all | solution.py:573
  10.0 1.6 %collective-permute-start.1 = (bf16[64,1024]{1,0:T(8,128)(2,1)S(1)}, bf16[64,1024]{1,0:T(8,128)(2,1)S(1)}, u32[]{:S(2)}, u32[]{:S(2)}) collective-permute-start(bf16[64,1024]{1,0:T(8,128)(2,1)S(1)} %bitcast.6), channel_id=1, source_target_pairs={{0,2},{1,3},{2,0},{3,1},{4,6},{5,7},{6,4},{7,5},{8,10},{9,11},{10,... | collective-permute-start | bytes 393224 | tf_op jit(solution)/shard_map/ppermute | solution.py:559
  11.9 1.3 %shard_map.111 = (bf16[1024,256]{1,0:T(8,128)(2,1)S(1)}, bf16[64,1024]{1,0:T(8,128)(2,1)S(1)}, s32[8,8]{1,0:T(8,128)S(1)}, bf16[256,128]{1,0:T(8,128)(2,1)S(1)},...) custom-call(bf16[256,1024]{1,0:T(8,128)(2,1)S(1)} %copy-done, ...), custom_call_target="tpu_custom_call" | custom-call | flops 1200000000 | bytes 4200000 | tf_op jit(solution)/shard_map/pallas_call | solution.py:75
  13.2 1.8 %collective-permute-done.1.refs_4_ = bf16[64,1024]{1,0:T(8,128)(2,1)S(1)} collective-permute-done((bf16[64,1024]{1,0:T(8,128)(2,1)S(1)}, bf16[64,1024]{1,0:T(8,128)(2,1)S(1)}, u32[]{:S(2)}, u32[]{:S(2)}) %collective-permute-start.1) | collective-permute-done | bytes 131104 | tf_op jit(solution)/shard_map/ppermute | solution.py:559
  15.0 3.9 %all-to-all-done.refs_7_ = bf16[8,64,256]{2,1,0:T(8,128)(2,1)S(1)} async-done(((bf16[8,64,256]{2,1,0:T(8,128)(2,1)}), bf16[8,64,256]{2,1,0:T(8,128)(2,1)S(1)}, u32[]{:S(2)}, u32[]{:S(2)}) %all-to-all-start) | async-done | bytes 262176 | tf_op jit(solution)/shard_map/all_to_all | solution.py:573
  18.9 1.7 %shard_map.112 = (bf16[64,1024]{1,0:T(8,128)(2,1)S(1)}, bf16[64,1280]{1,0:T(8,128)(2,1)}, bf16[64,1280]{1,0:T(8,128)(2,1)}) custom-call(s32[8,8]{1,0:T(8,128)S(1)} %get-tuple-element.41.refs_0_, bf16[256,128]{1,0:T(8,128)(2,1)S(1)} %get-tuple-element.42.refs_1_, bf16[256,128]{1,0:T(8,128)(2,1)S(1)} %get-tuple-element.43.refs_2_, ...), custom_call_target="tpu_custom_call" | custom-call | flops 2000000000 | bytes 7000000 | tf_op jit(solution)/shard_map/pallas_call | solution.py:75
  20.6 7.3 %all_gather.3.refs_6_.refs_0_ = bf16[256,1024]{1,0:T(8,128)(2,1)S(1)} all-gather(bf16[64,1024]{1,0:T(8,128)(2,1)S(1)} %get-tuple-element.49), channel_id=1, replica_groups=mesh['tile'=8,'chan'=4] {'chan'}, dimensions={0}, use_global_device_ids=true | all-gather | bytes 655360 | tf_op jit(solution)/shard_map/all_gather | solution.py:622
  28.0 1.7 %shard_map.114 = bf16[1024,128]{1,0:T(8,128)(2,1)} custom-call(bf16[256,1024]{1,0:T(8,128)(2,1)S(1)} %all_gather.3.refs_6_.refs_0_, bf16[256,1024]{1,0:T(8,128)(2,1)S(1)} %get-tuple-element.50.refs_1_, bf16[256,256]{1,0:T(8,128)(2,1)S(1)} %get-tuple-element.51.refs_2_, bf16[256,256]{1,0:T(8,128)(2,1)S(1)} %get-tuple-element.52.refs_3_), custom_call_target="tpu_custom_call" | custom-call | flops 2200000000 | bytes 7700000 | tf_op jit(solution)/shard_map/pallas_call | solution.py:75
  29.7 3.6 %all-to-all-start.1 = ((bf16[8,128,128]{2,1,0:T(8,128)(2,1)}), bf16[8,128,128]{2,1,0:T(8,128)(2,1)S(1)}, u32[]{:S(2)}, u32[]{:S(2)}) async-start(bf16[8,128,128]{2,1,0:T(8,128)(2,1)} %bitcast.9), calls=%async_computation.1 | async-start | bytes 524288 | tf_op jit(solution)/shard_map/all_to_all | solution.py:573
  33.3 6.9 %shard_map.115 = (f32[64,1024]{1,0:T(8,128)S(1)}, bf16[16,128]{1,0:T(8,128)(2,1)S(1)}, bf16[4,64,256]{2,1,0:T(8,128)(2,1)S(1)}, bf16[4,64,256]{2,1,0:T(8,128)(2,1)S(1)}) custom-call(bf16[256,1024]{1,0:T(8,128)(2,1)S(1)} %all_gather.3.refs_6_.refs_0_, bf16[256,1024]{1,0:T(8,128)(2,1)S(1)} %get-tuple-element.50.refs_1_, bf16[256,1024]{1,0:T(8,128)(2,1)} %refs_2_.4, ...), custom_call_target="tpu_custom_call" | custom-call | flops 7500000256 | bytes 26250000 | tf_op jit(solution)/shard_map/pallas_call | solution.py:75
  40.2 3.0 %collective-permute-start.3 = (bf16[4,64,256]{2,1,0:T(8,128)(2,1)S(1)}, bf16[4,64,256]{2,1,0:T(8,128)(2,1)S(1)}, u32[]{:S(2)}, u32[]{:S(2)}) collective-permute-start(bf16[4,64,256]{2,1,0:T(8,128)(2,1)S(1)} %get-tuple-element.57), channel_id=1, source_target_pairs={{0,16},{4,20},{8,24},{12,28},{16,0},{20,4},{24,8},{28,12},{1,17},{... | collective-permute-start | bytes 393224 | tf_op jit(solution)/shard_map/ppermute | solution.py:584
  43.2 0.8 %shard_map.116.refs_4_ = bf16[8,144,128]{2,1,0:T(8,128)(2,1)} custom-call(bf16[8,128,128]{2,1,0:T(8,128)(2,1)S(1)} %all-to-all-done.1.refs_0_, bf16[16,128]{1,0:T(8,128)(2,1)S(1)} %get-tuple-element.55.refs_1_), custom_call_target="tpu_custom_call" | custom-call | flops 1000000000 | bytes 3500000 | tf_op jit(solution)/shard_map/pallas_call | solution.py:75
  44.0 3.7 %all-to-all-start.2 = ((bf16[8,144,128]{2,1,0:T(8,128)(2,1)}), bf16[8,144,128]{2,1,0:T(8,128)(2,1)S(1)}, u32[]{:S(2)}, u32[]{:S(2)}) async-start(bf16[8,144,128]{2,1,0:T(8,128)(2,1)} %shard_map.116.refs_4_), calls=%async_computation.2 | async-start | bytes 589824 | tf_op jit(solution)/shard_map/all_to_all | solution.py:573
  47.7 1.9 %collective-permute-done.3.refs_1_ = bf16[4,64,256]{2,1,0:T(8,128)(2,1)S(1)} collective-permute-done((bf16[4,64,256]{2,1,0:T(8,128)(2,1)S(1)}, bf16[4,64,256]{2,1,0:T(8,128)(2,1)S(1)}, u32[]{:S(2)}, u32[]{:S(2)}) %collective-permute-start.3) | collective-permute-done | bytes 131104 | tf_op jit(solution)/shard_map/ppermute | solution.py:584
  49.6 1.7 %collective-permute-start.4 = (bf16[2,64,256]{2,1,0:T(8,128)(2,1)S(1)}, bf16[2,64,256]{2,1,0:T(8,128)(2,1)S(1)}, u32[]{:S(2)}, u32[]{:S(2)}) collective-permute-start(bf16[2,64,256]{2,1,0:T(8,128)(2,1)S(1)} %get-tuple-element.59), channel_id=1, source_target_pairs={{0,4},{4,0},{8,12},{12,8},{16,20},{20,16},{24,28},{28,24},{1,5},{5... | collective-permute-start | bytes 196616 | tf_op jit(solution)/shard_map/ppermute | solution.py:584
  51.3 2.9 %shard_map.118.refs_2_ = bf16[64,1024]{1,0:T(8,128)(2,1)} custom-call(bf16[256,1024]{1,0:T(8,128)(2,1)S(1)} %all_gather.3.refs_6_.refs_0_, bf16[1024,256]{1,0:T(8,128)(2,1)S(1)} %get-tuple-element.48.refs_9_.refs_0_.refs_3_.refs_1_, bf16[1024,256]{1,0:T(8,128)(2,1)S(1)} %copy-done.1, bf16[64,1024]{1,0:T(8,128)(2,1)} %bitcast.12, ...), custom_call_target="tpu_custom_call" | custom-call | flops 4000000000 | bytes 14000000 | tf_op jit(solution)/shard_map/pallas_call | solution.py:75
  54.6 2.5 %all-to-all-done.2.refs_0_ = bf16[8,144,128]{2,1,0:T(8,128)(2,1)S(1)} async-done(((bf16[8,144,128]{2,1,0:T(8,128)(2,1)}), bf16[8,144,128]{2,1,0:T(8,128)(2,1)S(1)}, u32[]{:S(2)}, u32[]{:S(2)}) %all-to-all-start.2) | async-done | bytes 294944 | tf_op jit(solution)/shard_map/all_to_all | solution.py:573
  57.1 0.8 %collective-permute-start.5 = (bf16[1040,128]{1,0:T(8,128)(2,1)S(1)}, bf16[1040,128]{1,0:T(8,128)(2,1)S(1)}, u32[]{:S(2)}, u32[]{:S(2)}) collective-permute-start(bf16[1040,128]{1,0:T(8,128)(2,1)S(1)} %shard_map.117.refs_0_), channel_id=1, source_target_pairs={{0,2},{1,3},{2,0},{3,1},{4,6},{5,7},{6,4},{7,5},{8,10},{9,11},{10,... | collective-permute-start | bytes 798728 | tf_op jit(solution)/shard_map/ppermute | solution.py:559
  57.9 1.1 %collective-permute-start.6 = (bf16[1,64,256]{2,1,0:T(8,128)(2,1)S(1)}, bf16[1,64,256]{2,1,0:T(8,128)(2,1)S(1)}, u32[]{:S(2)}, u32[]{:S(2)}) collective-permute-start(bf16[1,64,256]{2,1,0:T(8,128)(2,1)S(1)} %get-tuple-element.66), channel_id=1, source_target_pairs={{0,8},{4,12},{8,0},{12,4},{16,24},{20,28},{24,16},{28,20},{1,9},{5... | collective-permute-start | bytes 98312 | tf_op jit(solution)/shard_map/ppermute | solution.py:584
  59.0 2.8 %collective-permute-done.6.refs_2_ = bf16[1,64,256]{2,1,0:T(8,128)(2,1)S(1)} collective-permute-done((bf16[1,64,256]{2,1,0:T(8,128)(2,1)S(1)}, bf16[1,64,256]{2,1,0:T(8,128)(2,1)S(1)}, u32[]{:S(2)}, u32[]{:S(2)}) %collective-permute-start.6) | collective-permute-done | bytes 32800 | tf_op jit(solution)/shard_map/ppermute | solution.py:584
  61.8 1.1 %shard_map.121 = bf16[64,1024]{1,0:T(8,128)(2,1)} custom-call(f32[64,1024]{1,0:T(8,128)S(1)} %get-tuple-element.64.refs_0_, bf16[1,64,256]{2,1,0:T(8,128)(2,1)S(1)} %get-tuple-element.65.refs_1_, bf16[1,64,256]{2,1,0:T(8,128)(2,1)S(1)} %collective-permute-done.6.refs_2_), custom_call_target="tpu_custom_call" | custom-call | flops 1000000000 | bytes 3500000 | tf_op jit(solution)/shard_map/pallas_call | solution.py:75
  63.6 1.2 %shard_map.122 = (f32[256,1024]{1,0:T(8,128)}, f32[1024,256]{1,0:T(8,128)}, f32[256,128]{1,0:T(8,128)S(1)}) custom-call(bf16[1040,128]{1,0:T(8,128)(2,1)S(1)} %shard_map.117.refs_0_, bf16[1040,128]{1,0:T(8,128)(2,1)S(1)} %collective-permute-done.8.refs_1_, bf16[1040,128]{1,0:T(8,128)(2,1)S(1)} %collective-permute-done.5.refs_2_, ...), custom_call_target="tpu_custom_call" | custom-call | flops 1200000000 | bytes 4200000 | tf_op jit(solution)/shard_map/pallas_call | solution.py:75
  65.1 1.5 %shard_map.123 = (f32[256,1024]{1,0:T(8,128)}, f32[1024,256]{1,0:T(8,128)}, f32[25,256]{1,0:T(8,128)}) custom-call(bf16[1040,128]{1,0:T(8,128)(2,1)S(1)} %collective-permute-done.7.refs_0_, f32[256,128]{1,0:T(8,128)S(1)} %get-tuple-element.69.refs_1_, f32[256,1024]{1,0:T(8,128)} %get-tuple-element.70.refs_2_, ...), custom_call_target="tpu_custom_call", output_to_operand_aliasing={{0}: (2, {}), {1}: (3, {})} | custom-call | flops 1200000000 | bytes 4200000 | tf_op jit(solution)/shard_map/pallas_call | solution.py:75
  (29 shorter events, 1.7 us)
Async XLA Ops:
  0.6 9.3 %copy-start.2 = (bf16[1,64,1024]{2,1,0:T(8,128)(2,1)S(1)}, bf16[1,64,1024]{2,1,0:T(8,128)(2,1)}, u32[]{:S(2)}) copy-start(bf16[1,64,1024]{2,1,0:T(8,128)(2,1)} %param.8) | copy-start | bytes 393220
  0.6 10.9 %copy-start.5 = (bf16[25,64]{1,0:T(8,128)(2,1)S(1)}, bf16[25,64]{1,0:T(8,128)(2,1)}, u32[]{:S(2)}) copy-start(bf16[25,64]{1,0:T(8,128)(2,1)} %param.9) | copy-start | bytes 9604
  2.6 9.3 %copy-start = (bf16[256,1024]{1,0:T(8,128)(2,1)S(1)}, bf16[256,1024]{1,0:T(8,128)(2,1)}, u32[]{:S(2)}) copy-start(bf16[256,1024]{1,0:T(8,128)(2,1)} %refs_2_.4) | copy-start | bytes 1572868
  2.6 16.3 %all-to-all-start = ((bf16[8,64,256]{2,1,0:T(8,128)(2,1)}), bf16[8,64,256]{2,1,0:T(8,128)(2,1)S(1)}, u32[]{:S(2)}, u32[]{:S(2)}) async-start(bf16[8,64,256]{2,1,0:T(8,128)(2,1)} %shard_map.110.refs_4_), calls=%async_computation | async-start | bytes 524288 | tf_op jit(solution)/shard_map/all_to_all | solution.py:573
  10.0 1.9 %copy-start.3 = (s32[8,8]{1,0:T(8,128)S(1)}, s32[8,8]{1,0:T(8,128)}, u32[]{:S(2)}) copy-start(s32[8,8]{1,0:T(8,128)} %refs_8_.1) | copy-start | bytes 772
  10.0 1.9 %copy-start.4 = (s32[8,8]{1,0:T(8,128)S(1)}, s32[8,8]{1,0:T(8,128)}, u32[]{:S(2)}) copy-start(s32[8,8]{1,0:T(8,128)} %refs_9_.1) | copy-start | bytes 772
  10.0 5.0 %collective-permute-start.1 = (bf16[64,1024]{1,0:T(8,128)(2,1)S(1)}, bf16[64,1024]{1,0:T(8,128)(2,1)S(1)}, u32[]{:S(2)}, u32[]{:S(2)}) collective-permute-start(bf16[64,1024]{1,0:T(8,128)(2,1)S(1)} %bitcast.6), channel_id=1, source_target_pairs={{0,2},{1,3},{2,0},{3,1},{4,6},{5,7},{6,4},{7,5},{8,10},{9,11},{10,... | collective-permute-start | bytes 393224 | tf_op jit(solution)/shard_map/ppermute | solution.py:559
  11.6 16.3 %collective-permute-start = (bf16[64,1024]{1,0:T(8,128)(2,1)S(1)}, bf16[64,1024]{1,0:T(8,128)(2,1)S(1)}, u32[]{:S(2)}, u32[]{:S(2)}) collective-permute-start(bf16[64,1024]{1,0:T(8,128)(2,1)S(1)} %bitcast.7), channel_id=1, source_target_pairs={{0,1},{1,0},{2,3},{3,2},{4,5},{5,4},{6,7},{7,6},{8,9},{9,8},{10,11... | collective-permute-start | bytes 393224 | tf_op jit(solution)/shard_map/ppermute | solution.py:559
  15.0 12.9 %collective-permute-start.2 = (bf16[64,1024]{1,0:T(8,128)(2,1)S(1)}, bf16[64,1024]{1,0:T(8,128)(2,1)S(1)}, u32[]{:S(2)}, u32[]{:S(2)}) collective-permute-start(bf16[64,1024]{1,0:T(8,128)(2,1)S(1)} %collective-permute-done.1.refs_4_), channel_id=1, source_target_pairs={{0,1},{1,0},{2,3},{3,2},{4,5},{5,4},{6,7},{7,6},{8,9},{9,8},{10,11... | collective-permute-start | bytes 393224 | tf_op jit(solution)/shard_map/ppermute | solution.py:559
  20.6 7.4 %copy-start.1 = (bf16[1024,256]{1,0:T(8,128)(2,1)S(1)}, bf16[1024,256]{1,0:T(8,128)(2,1)}, u32[]{:S(2)}) copy-start(bf16[1024,256]{1,0:T(8,128)(2,1)} %refs_2_.5) | copy-start | bytes 1572868
  29.7 13.5 %all-to-all-start.1 = ((bf16[8,128,128]{2,1,0:T(8,128)(2,1)}), bf16[8,128,128]{2,1,0:T(8,128)(2,1)S(1)}, u32[]{:S(2)}, u32[]{:S(2)}) async-start(bf16[8,128,128]{2,1,0:T(8,128)(2,1)} %bitcast.9), calls=%async_computation.1 | async-start | bytes 524288 | tf_op jit(solution)/shard_map/all_to_all | solution.py:573
  40.2 9.4 %collective-permute-start.3 = (bf16[4,64,256]{2,1,0:T(8,128)(2,1)S(1)}, bf16[4,64,256]{2,1,0:T(8,128)(2,1)S(1)}, u32[]{:S(2)}, u32[]{:S(2)}) collective-permute-start(bf16[4,64,256]{2,1,0:T(8,128)(2,1)S(1)} %get-tuple-element.57), channel_id=1, source_target_pairs={{0,16},{4,20},{8,24},{12,28},{16,0},{20,4},{24,8},{28,12},{1,17},{... | collective-permute-start | bytes 393224 | tf_op jit(solution)/shard_map/ppermute | solution.py:584
  44.0 13.0 %all-to-all-start.2 = ((bf16[8,144,128]{2,1,0:T(8,128)(2,1)}), bf16[8,144,128]{2,1,0:T(8,128)(2,1)S(1)}, u32[]{:S(2)}, u32[]{:S(2)}) async-start(bf16[8,144,128]{2,1,0:T(8,128)(2,1)} %shard_map.116.refs_4_), calls=%async_computation.2 | async-start | bytes 589824 | tf_op jit(solution)/shard_map/all_to_all | solution.py:573
  49.6 4.9 %collective-permute-start.4 = (bf16[2,64,256]{2,1,0:T(8,128)(2,1)S(1)}, bf16[2,64,256]{2,1,0:T(8,128)(2,1)S(1)}, u32[]{:S(2)}, u32[]{:S(2)}) collective-permute-start(bf16[2,64,256]{2,1,0:T(8,128)(2,1)S(1)} %get-tuple-element.59), channel_id=1, source_target_pairs={{0,4},{4,0},{8,12},{12,8},{16,20},{20,16},{24,28},{28,24},{1,5},{5... | collective-permute-start | bytes 196616 | tf_op jit(solution)/shard_map/ppermute | solution.py:584
  57.1 6.5 %collective-permute-start.5 = (bf16[1040,128]{1,0:T(8,128)(2,1)S(1)}, bf16[1040,128]{1,0:T(8,128)(2,1)S(1)}, u32[]{:S(2)}, u32[]{:S(2)}) collective-permute-start(bf16[1040,128]{1,0:T(8,128)(2,1)S(1)} %shard_map.117.refs_0_), channel_id=1, source_target_pairs={{0,2},{1,3},{2,0},{3,1},{4,6},{5,7},{6,4},{7,5},{8,10},{9,11},{10,... | collective-permute-start | bytes 798728 | tf_op jit(solution)/shard_map/ppermute | solution.py:559
  57.9 3.9 %collective-permute-start.6 = (bf16[1,64,256]{2,1,0:T(8,128)(2,1)S(1)}, bf16[1,64,256]{2,1,0:T(8,128)(2,1)S(1)}, u32[]{:S(2)}, u32[]{:S(2)}) collective-permute-start(bf16[1,64,256]{2,1,0:T(8,128)(2,1)S(1)} %get-tuple-element.66), channel_id=1, source_target_pairs={{0,8},{4,12},{8,0},{12,4},{16,24},{20,28},{24,16},{28,20},{1,9},{5... | collective-permute-start | bytes 98312 | tf_op jit(solution)/shard_map/ppermute | solution.py:584
  59.0 4.6 %collective-permute-start.8 = (bf16[1040,128]{1,0:T(8,128)(2,1)S(1)}, bf16[1040,128]{1,0:T(8,128)(2,1)S(1)}, u32[]{:S(2)}, u32[]{:S(2)}) collective-permute-start(bf16[1040,128]{1,0:T(8,128)(2,1)S(1)} %shard_map.117.refs_0_), channel_id=1, source_target_pairs={{0,1},{1,0},{2,3},{3,2},{4,5},{5,4},{6,7},{7,6},{8,9},{9,8},{10,11... | collective-permute-start | bytes 798728 | tf_op jit(solution)/shard_map/ppermute | solution.py:559
  63.5 1.5 %collective-permute-start.7 = (bf16[1040,128]{1,0:T(8,128)(2,1)S(1)}, bf16[1040,128]{1,0:T(8,128)(2,1)S(1)}, u32[]{:S(2)}, u32[]{:S(2)}) collective-permute-start(bf16[1040,128]{1,0:T(8,128)(2,1)S(1)} %collective-permute-done.5.refs_2_), channel_id=1, source_target_pairs={{0,1},{1,0},{2,3},{3,2},{4,5},{5,4},{6,7},{7,6},{8,9},{9,8},{10,11... | collective-permute-start | bytes 798728 | tf_op jit(solution)/shard_map/ppermute | solution.py:559

commit v8 on v7

--- a/solution.py
+++ b/solution.py
@@ -15,8 +15,8 @@
 BF16 = jnp.bfloat16
 F32 = jnp.float32
 
-NEAR, FAR, RAW = "near", "far", "raw"
-SPACES = {NEAR: pltpu.VMEM, FAR: pltpu.HBM, RAW: pltpu.HBM}
+NEAR, FAR, RAW, PINNED = "near", "far", "raw", "pinned"
+SPACES = {NEAR: pltpu.VMEM, FAR: pltpu.HBM, RAW: pltpu.HBM, PINNED: pltpu.VMEM}
 
 
 class Loaded:
@@ -74,7 +74,7 @@
 
     return pl.pallas_call(
         run,
-        out_shape=[pltpu.HBM(s, d) if p in (FAR, RAW) else jax.ShapeDtypeStruct(s, d)
+        out_shape=[SPACES[p](s, d) if p != NEAR else jax.ShapeDtypeStruct(s, d)
                    for s, d, p in outs],
         in_specs=[pl.BlockSpec(memory_space=SPACES[p]) for _, p in ins],
         out_specs=[pl.BlockSpec(memory_space=SPACES[p]) for _, _, p in outs],
@@ -191,42 +191,31 @@
         copy.wait()
 
 
-def conv_kernel(edge, neighbours, top, low, pick, slot, spread, x, rims, taps,
-                hidden_ref, padded, side, gathered):
-    padded_ref, side_ref = padded.ref, side.ref
-    rims_ref, taps_ref = rims.get(), taps.get()
-    channels, pixels = hidden_ref.shape
+def shifted(values, shift, edge):
+    if not shift:
+        return values
+    return roll(jnp.where(side_mask(shift, values.shape, edge), 0.0, values), -shift)
+
+
+def tap_rows_of(taps_ref, at):
+    return [taps_ref[tap, pl.ds(at, 16), :].astype(F32) for tap in range(KSIZE * KSIZE)]
+
+
+def center_conv(edge, x_ref, taps_ref, out_ref):
+    channels, pixels = x_ref.shape
     wide = pixels + 2 * LANES
-    nb = tile_row(neighbours)
-    padded_ref[:, :LANES] = dot(rims_ref[nb[1]], top.get()[...]).astype(BF16)
-    padded_ref[:, LANES + pixels:] = dot(rims_ref[nb[6]], low.get()[...]).astype(BF16)
-    for position, d in enumerate(SIDES):
-        gathered[position * channels:(position + 1) * channels, :] = rims_ref[nb[d]]
-    candidates, slot = dot(gathered[...], pick.get()[...]), slot.get()[...]
-    packed = candidates[:channels, :]
-    for position in range(1, len(SIDES)):
-        packed = jnp.where(slot == position,
-                           candidates[position * channels:(position + 1) * channels, :], packed)
-    packed = packed.astype(BF16)
-    side_ref[...] = dot(packed, spread.get()[...]).astype(BF16)
-    side.send()
-    padded_ref[:, LANES:LANES + pixels] = x.get()[...]
-    padded.send()
 
     def block(i, carry):
         at = pl.multiple_of(i * 16, 16)
-        xs = padded_ref[pl.ds(at, 16), :].astype(F32)
-        hs = side_ref[pl.ds(at, 16), :].astype(F32)
-        taps = [taps_ref[tap, pl.ds(at, 16), :].astype(F32) for tap in range(KSIZE * KSIZE)]
+        xs = x_ref[pl.ds(at, 16), :].astype(F32)
+        taps = tap_rows_of(taps_ref, at)
+        zeros = jnp.zeros((8, LANES), F32)
         halves = []
         for half in (0, 8):
-            x, h = xs[half:half + 8], hs[half:half + 8]
+            x = jnp.concatenate([zeros, xs[half:half + 8], zeros], axis=1)
             sums = [None] * KSIZE
             for b in range(KSIZE):
-                shift = b - HALO
-                moved = x
-                if shift:
-                    moved = roll(jnp.where(side_mask(shift, x.shape, edge), h, x), -shift)
+                moved = shifted(x, b - HALO, edge)
                 for a in range(KSIZE):
                     term = jnp.tile(taps[a * KSIZE + b][half:half + 8], (1, wide // LANES)) * moved
                     sums[a] = term if sums[a] is None else sums[a] + term
@@ -235,10 +224,86 @@
                 part = roll(sums[a], -(a - HALO) * edge)[:, LANES:LANES + pixels]
                 total = part if total is None else total + part
             halves.append(total)
-        hidden_ref[pl.ds(at, 16), :] = jnp.concatenate(halves, axis=0).astype(BF16)
+        out_ref[pl.ds(at, 16), :] = jnp.concatenate(halves, axis=0)
         return carry
 
     lax.fori_loop(0, channels // 16, block, 0)
+
+
+def row_terms(rows, taps, edge, below):
+    lane = lax.broadcasted_iota(jnp.int32, rows.shape, 1)
+    total = None
+    for a in range(KSIZE):
+        far = a - HALO if below else HALO - a
+        if far <= 0:
+            continue
+        sums = None
+        for b in range(KSIZE):
+            term = taps[a * KSIZE + b] * shifted(rows, b - HALO, edge)
+            sums = term if sums is None else sums + term
+        if below:
+            part = jnp.where(lane >= LANES - far * edge, roll(sums, LANES - far * edge), 0.0)
+        else:
+            part = jnp.where(lane < far * edge, roll(sums, far * edge - LANES), 0.0)
+        total = part if total is None else total + part
+    return total
+
+
+def side_terms(packed, taps, edge):
+    place = lax.broadcasted_iota(jnp.int32, packed.shape, 1) % (2 * HALO)
+    beside = jnp.where(place == 0, roll(packed, -1), jnp.where(place == 3, roll(packed, 1), 0.0))
+    total = None
+    for a in range(KSIZE):
+        def tap(b):
+            return jnp.tile(taps[a * KSIZE + b], (1, packed.shape[1] // LANES))
+
+        terms = (jnp.where(place < HALO, tap(0), tap(4)) * packed
+                 + jnp.where(place == 0, tap(1), tap(3)) * beside)
+        part = roll(terms, -a * 2 * HALO)[:, :2 * HALO * edge]
+        total = part if total is None else total + part
+    return total
+
+
+def column_map(edge):
+    pixel = lax.broadcasted_iota(jnp.int32, (1, edge * edge), 1)
+    row, col = pixel // edge, pixel % edge
+    index = jnp.where(col < HALO, row * 2 * HALO + col, row * 2 * HALO + col - (edge - 2 * HALO))
+    return one_hot(jnp.where((col < HALO) | (col >= edge - HALO), index, -1), 2 * HALO * edge)
+
+
+def conv_kernel(edge, neighbours, top, low, pick, slot, columns, center, rims, taps,
+                hidden_ref, halo, gathered, sides):
+    rims_ref, taps_ref, halo_ref = rims.get(), taps.get(), halo.ref
+    channels, pixels = hidden_ref.shape
+    nb = tile_row(neighbours)
+    halo_ref[:, :LANES] = dot(rims_ref[nb[1]], top.get()[...]).astype(BF16)
+    halo_ref[:, LANES:2 * LANES] = dot(rims_ref[nb[6]], low.get()[...]).astype(BF16)
+    for position, d in enumerate(SIDES):
+        gathered[position * channels:(position + 1) * channels, :] = rims_ref[nb[d]]
+    candidates, slot = dot(gathered[...], pick.get()[...]), slot.get()[...]
+    packed = candidates[:channels, :]
+    for position in range(1, len(SIDES)):
+        packed = jnp.where(slot == position,
+                           candidates[position * channels:(position + 1) * channels, :], packed)
+    halo_ref[:, 2 * LANES:] = packed.astype(BF16)
+    halo.send()
+    center = center.get()
+    ends = []
+    for at in range(0, channels, 16):
+        halos = halo_ref[at:at + 16, :].astype(F32)
+        taps_of = tap_rows_of(taps_ref, at)
+        ends.append((row_terms(halos[:, :LANES], taps_of, edge, False),
+                     row_terms(halos[:, LANES:2 * LANES], taps_of, edge, True)))
+        sides[at:at + 16, :] = side_terms(halos[:, 2 * LANES:], taps_of, edge)
+    high = sides[...].astype(BF16)
+    low = (sides[...] - high.astype(F32)).astype(BF16)
+    columns = columns.get()[...]
+    hidden = center[...] + dot(high, columns) + dot(low, columns)
+    hidden_ref[:, LANES:pixels - LANES] = hidden[:, LANES:pixels - LANES].astype(BF16)
+    first = jnp.concatenate([end[0] for end in ends], axis=0)
+    last = jnp.concatenate([end[1] for end in ends], axis=0)
+    hidden_ref[:, :LANES] = (hidden[:, :LANES] + first).astype(BF16)
+    hidden_ref[:, pixels - LANES:] = (hidden[:, pixels - LANES:] + last).astype(BF16)
 
 
 def normal_below(values):
@@ -261,7 +326,7 @@
     lax.fori_loop(0, units // block, step, 0)
 
 
-def weight_kernel(feats, cots, w_in_t, w_out, part, act, gpre, stack, sems):
+def weight_kernel(feats, cots, w_in_t, w_out, part, gpre, act, stack, sems):
     feats, cots = feats.get(), cots.get()
     full, units = feats.shape[0], act.shape[0]
     w_in_t, w_out = w_in_t.get()[...], w_out.get()[...]
@@ -306,36 +371,48 @@
     out.ref[...] = (x.get()[...].astype(F32) + branch.astype(BF16).astype(F32)).astype(BF16)
 
 
-def back_kernel(edge, block, tiles, feats, cots, w_in, w_in_t, w_out, padded, side, cot, neighbours,
-                rotations, taps, accum_ref, tap_ref, *refs):
-    outs, (gpre, grad_ref, turned_all, moved_all, d_row, d_side, gathered) = refs[:-7], refs[-7:]
-    channels = grad_ref.shape[0]
+def back_kernel(edge, groups, tiles, feats, cots, w_in, w_in_t, w_out, gpre_own, x, halo, cot,
+                neighbours, rotations, taps, accum_ref, tap_ref, *refs):
+    outs, (gpre, grad_ref, padded_ref, side_ref, turned_all, moved_all, d_row, d_side, gathered) = (
+        refs[:-9], refs[-9:])
+    channels, pixels = grad_ref.shape
     feats, cots, w_in_t, w_out = feats.get(), cots.get(), w_in_t.get(), w_out.get()
 
-    def units(rows):
+    chan, units = lax.axis_index("chan"), gpre_own.ref.shape[0]
+
+    def others(k, carry):
+        rows = pl.ds(pl.multiple_of((chan ^ k) * units, units), units)
         for part_of in column_steps(feats):
             pre = dot(w_in_t[rows, :], feats[:, part_of])
             slope = gelu_slope(pre, normal_below(pre))
             gpre[rows, part_of] = (dot(w_out[rows, :], cots[:, part_of]) * slope).astype(BF16)
-
-    over_units(w_out.shape[0], block, units)
+        return carry
+
+    lax.fori_loop(1, groups, others, 0)
+    gpre[pl.ds(pl.multiple_of(chan * units, units), units), :] = gpre_own.get()[...]
     own = pl.ds(pl.multiple_of(lax.axis_index("chan") * channels, channels), channels)
     grad_ref[...] = dot(w_in.get()[own, :], gpre[...]).astype(BF16)
-    tap_terms(edge, grad_ref, padded.get(), side.get(), tap_ref, turned_all, moved_all)
-    halo_adjoint(edge, neighbours, rotations, grad_ref, taps.get(), cot.get(), accum_ref, outs,
-                 d_row, d_side, gathered)
-
-
-def prep_kernel(edge, w_in, x, neighbours, rotations, w_in_t_ref, x_ref, nb_ref, *map_refs):
+    halo = halo.get()
+    padded_ref[:, :LANES] = halo[:, :LANES]
+    padded_ref[:, LANES:LANES + pixels] = x.get()[...]
+    padded_ref[:, LANES + pixels:] = halo[:, LANES:2 * LANES]
+    spread = spread_map(edge, padded_ref.shape[1])
+    side_ref[...] = dot(halo[:, 2 * LANES:], spread).astype(BF16)
+    tap_terms(edge, grad_ref, padded_ref, side_ref, tap_ref, turned_all, moved_all)
+    halo_adjoint(edge, neighbours, rotations, spread, grad_ref, taps.get(), cot.get(), accum_ref,
+                 outs, d_row, d_side, gathered)
+
+
+def prep_kernel(edge, w_in, x, neighbours, rotations, taps, w_in_t_ref, center_ref, nb_ref,
+                *map_refs):
     nb_ref[...] = neighbours.get()[...]
     rot = tile_row(rotations)
     pick, slot = side_map([rot[d] for d in SIDES], edge)
-    wide = x_ref.shape[1] + 2 * LANES
-    maps = (*row_halo_maps(rot[1], rot[6], edge), pick, slot, spread_map(edge, wide))
+    maps = (*row_halo_maps(rot[1], rot[6], edge), pick, slot, column_map(edge))
     for ref, values in zip(map_refs, maps):
         ref[...] = values
     w_in_t_ref[...] = w_in.get()[...].astype(F32).T.astype(BF16)
-    x_ref[...] = x.get()[...]
+    center_conv(edge, x.get(), taps.get(), center_ref)
 
 
 def join_kernel(w_in_t, w_out, *refs):
@@ -388,7 +465,7 @@
     tap_ref[...] = jnp.concatenate(found, axis=0).astype(BF16)
 
 
-def halo_adjoint(edge, neighbours, rotations, grad_ref, taps_ref, cot_ref, accum_ref, outs,
+def halo_adjoint(edge, neighbours, rotations, spread, grad_ref, taps_ref, cot_ref, accum_ref, outs,
                  d_row, d_side, gathered):
     channels, pixels = grad_ref.shape
     wide = pixels + 2 * LANES
@@ -436,7 +513,7 @@
     top, low = row_halo_maps(rot[1], rot[6], edge)
     gathered[slot_of(nb[1], tiles)] += dot_nt(d_row[:, :LANES], top)
     gathered[slot_of(nb[6], tiles)] += dot_nt(d_row[:, LANES:], low)
-    packed = dot_nt(d_side[...], spread_map(edge, wide))
+    packed = dot_nt(d_side[...], spread)
     pick, slot = side_map([rot[d] for d in SIDES], edge)
     for position, d in enumerate(SIDES):
         own = jnp.where(slot == position, packed, 0.0).astype(BF16)
@@ -457,7 +534,7 @@
 
 
 def halves(tiles):
-    return tiles & (tiles - 1) == 0
+    return tiles > 1 and tiles & (tiles - 1) == 0
 
 
 def slot_of(tile, tiles):
@@ -470,7 +547,8 @@
 
 
 def halving_bits(tiles):
-    return [1 << i for i in range(tiles.bit_length() - 2, 0, -2)] + [1, 2][:tiles.bit_length() - 2]
+    bits = [1 << i for i in range(tiles.bit_length() - 1)]
+    return bits[1:2] + bits[:1] + bits[2:]
 
 
 def pair_kernel(kept, other, *refs):
@@ -480,7 +558,7 @@
 
 
 def border_kernel(edge, accum, *refs):
-    parts, grad = refs[:-1], refs[-1]
+    parts, grad_ref = refs[:-1], refs[-1]
     rims = None
     for part in parts:
         more = total_of(part.get())
@@ -489,7 +567,7 @@
     low = (rims - high.astype(F32)).astype(BF16)
     pick = one_hot(rim_pixels(edge), edge * edge)
     added = dot_nt(high, pick) + dot_nt(low, pick)
-    grad.ref[...] = (accum.get()[...] + added).astype(BF16)
+    grad_ref[...] = (accum.get()[...] + added).astype(BF16)
 
 
 def total_of(ref):
@@ -522,9 +600,14 @@
 
 def final_kernel(which, channels, tap_rows, scale, last, *refs):
     pieces, taps_in = refs[:len(which)], refs[len(which)]
-    g_in, g_out, g_tap_ref, buf_in, buf_out, sems = refs[-6:]
+    copies = []
+    if last:
+        g_in, g_out, g_tap_ref, buf_in, buf_out, sems = refs[-6:]
+    else:
+        g_in, g_out, g_tap_ref, copied, buf_in, buf_out, sems = refs[-7:]
+        copies.append(pltpu.make_async_copy(refs[len(which) + 1].get(), copied, sems.at[0]))
+        copies[0].start()
     full, units = buf_in.shape[1:]
-    copies = []
     all_taps = taps_in.get()[...]
     row_of = lax.broadcasted_iota(jnp.int32, (full, LANES), 0)
     for i, k in enumerate(which):
@@ -603,22 +686,21 @@
     taps = jnp.broadcast_to(kernel[:, :, None], (KSIZE * KSIZE, channels, LANES))
     cot_pieces = gather_pieces(cot, groups)
     table = neighbours.shape
-    w_in_t, x_near, nb_near, *maps = call(
+    w_in_t, center, nb_near, *maps = call(
         functools.partial(prep_kernel, edge),
-        [(w_in, NEAR), (x, FAR), (neighbours, NEAR), (rotations, NEAR)],
-        [((hidden, full), BF16, NEAR), ((channels, pixels), BF16, NEAR),
+        [(w_in, NEAR), (x, FAR), (neighbours, NEAR), (rotations, NEAR), (taps, NEAR)],
+        [((hidden, full), BF16, NEAR), ((channels, pixels), F32, NEAR),
          (neighbours.shape, jnp.int32, NEAR), ((rim, LANES), BF16, NEAR), ((rim, LANES), BF16, NEAR),
          ((rim, 2 * LANES), BF16, NEAR), ((1, 2 * LANES), jnp.int32, NEAR),
-         ((2 * LANES, wide), BF16, NEAR)], time=1.2,
-        after=[(rims, RAW), (taps, NEAR)])
+         ((2 * HALO * edge, pixels), BF16, NEAR)], time=2.0, after=[(rims, RAW)])
     rims = swap_rows(rims)
 
-    hid, padded, side = call(
+    hid, halo = call(
         functools.partial(conv_kernel, edge),
-        [(a, NEAR) for a in (nb_near, *maps, x_near, rims, taps)],
-        [((channels, pixels), BF16, NEAR)] + [((channels, wide), BF16, FAR)] * 2,
-        [pltpu.VMEM((len(SIDES) * channels, rim), BF16)], time=2.0,
-        after=[(w_in_t, NEAR)])
+        [(a, NEAR) for a in (nb_near, *maps, center, rims, taps)],
+        [((channels, pixels), BF16, NEAR), ((channels, 4 * LANES), BF16, FAR)],
+        [pltpu.VMEM((len(SIDES) * channels, rim), BF16),
+         pltpu.VMEM((channels, 2 * HALO * edge), F32)], time=1.0, after=[(w_in_t, NEAR)])
     feats = lax.all_gather(hid, "chan", axis=0, tiled=True)
     cots, part_in, part_out = call(
         join_kernel, [(w_in_t, NEAR), (w_out, NEAR)] + [(piece, NEAR) for piece in cot_pieces],
@@ -629,11 +711,11 @@
     share = -(-used // (16 * tiles)) * 16
     tap_rows = -(-channels // 64) * 16
     block = 2 * LANES
-    [part] = call(
+    part, gpre = call(
         weight_kernel,
         [(feats, NEAR), (cots, NEAR), (part_in, NEAR), (part_out, NEAR)],
-        [((tiles * share, LANES), BF16, RAW)],
-        [pltpu.VMEM((units, pixels), BF16)] * 2
+        [((tiles * share, LANES), BF16, RAW), ((units, pixels), BF16, NEAR)],
+        [pltpu.VMEM((units, pixels), BF16)]
         + [pltpu.VMEM((tiles * share, LANES), BF16), pltpu.SemaphoreType.DMA((3,))],
         time=2.2)
     part = swap_rows(part.reshape(tiles, share, LANES))
@@ -641,11 +723,12 @@
     parts = 2 if halves(tiles) else 1
     placed = ((tiles // parts, channels, rim), BF16, NEAR if parts > 1 else FAR)
     accum, tap_part, *border = call(
-        functools.partial(back_kernel, edge, block, tiles),
-        [(feats, NEAR), (cots, NEAR), (w_in, FAR), (w_in_t, NEAR), (w_out, NEAR), (padded, FAR),
-         (side, FAR), (cot, FAR), (neighbours, NEAR), (rotations, NEAR), (taps, NEAR)],
+        functools.partial(back_kernel, edge, groups, tiles),
+        [(feats, NEAR), (cots, NEAR), (w_in, FAR), (w_in_t, NEAR), (w_out, NEAR), (gpre, FAR), (x, FAR),
+         (halo, FAR), (cot, FAR), (neighbours, NEAR), (rotations, NEAR), (taps, NEAR)],
         [((channels, pixels), F32, NEAR), ((tap_rows, LANES), BF16, NEAR)] + [placed] * parts,
         [pltpu.VMEM((hidden, pixels), BF16), pltpu.VMEM((channels, pixels), BF16),
+         pltpu.VMEM((channels, wide), BF16), pltpu.VMEM((channels, wide), BF16),
          pltpu.VMEM((KSIZE * 16, wide), BF16), pltpu.VMEM((LANES, wide), BF16),
          pltpu.VMEM((channels, 2 * LANES), BF16), pltpu.VMEM((channels, wide), BF16),
          pltpu.VMEM((tiles, channels, rim), F32)], time=7.5, limit=32)
@@ -666,18 +749,18 @@
     border = [border[0], swap_bit(border[1], bits[-1])] if parts > 1 else [swap_rows(border[0])]
     [grad_in] = call(functools.partial(border_kernel, edge),
                      [(accum, NEAR)] + [(part, NEAR) for part in border],
-                     [((channels, pixels), BF16, FAR)])
-
-    def place(which, grads, last):
+                     [((channels, pixels), BF16, PINNED)])
+
+    def place(which, taps_so_far, more, last):
         tap_shape = (KSIZE * KSIZE, full) if last else (full, LANES)
-        more = [(grads[0], RAW), (grads[1], RAW)] if grads[0] is not None else []
+        copied = [] if last else [(more[0][0].shape, more[0][0].dtype, RAW)]
         return call(
             functools.partial(final_kernel, which, channels, tap_rows, scale, last),
-            [(pieces[k], NEAR) for k in which] + [(grads[2], NEAR)] + more,
-            [((full, hidden), F32, RAW), ((hidden, full), F32, RAW), (tap_shape, F32, NEAR)],
+            [(pieces[k], NEAR) for k in which] + [(taps_so_far, NEAR)] + more,
+            [((full, hidden), F32, RAW), ((hidden, full), F32, RAW), (tap_shape, F32, NEAR)] + copied,
             [pltpu.VMEM((len(which), full, units), F32), pltpu.VMEM((len(which), units, full), F32),
-             pltpu.SemaphoreType.DMA((2 * len(which),))],
-            time=1.2, aliases={1 + len(which): 0, 2 + len(which): 1} if more else None)
+             pltpu.SemaphoreType.DMA((2 * len(which) + 1,))],
+            time=1.2, aliases={1 + len(which): 0, 2 + len(which): 1} if last else None)
 
     pieces = {0: weights}
     bit = groups // 2
@@ -691,8 +774,9 @@
         pieces[k], grad_in = lax.optimization_barrier((pieces[k], grad_in))
     for k in odd:
         pieces[k] = swap_chan(pieces[k ^ 1], 1)
-    grads = place([0, 1, *even], [None, None, jnp.zeros((full, LANES), F32)], False)
-    grads = place(odd, grads, True)
+    g_in, g_out, taps_so_far, grad_in = place(
+        [0, 1, *even], jnp.zeros((full, LANES), F32), [(grad_in, NEAR)], False)
+    grads = place(odd, taps_so_far, [(g_in, RAW), (g_out, RAW)], True)
     return (outputs[None], grad_in[None], *grads)
 
 

time: 67.1 us -> 66.6 us (level)
    all_to_all x3, waiting for transfers between devices: 6.31 us -> 8.24 us  [swap_rows(): return lax.all_to_all(values, 'tile', 0, 0, tiled=True)]
    ppermute x6, waiting for transfers between devices: 2.72 us -> 1.61 us  [swap_chan(): lax.ppermute(values, 'chan', [(i, i ^ bit) for i in range(lax.axis_size('...]
where the time goes in v8:
time: 66.6 us; the launch traced here: 66.1 us
  starting transfers between devices  22.4 us (34%)
  Pallas kernels  20.7 us (31%)
  waiting for transfers between devices  14.5 us (22%)
  blocking collectives  7.33 us (11%)
  between operations  0.83 us (1%)
    pallas_call x14, Pallas kernels, call(): pl.pallas_call(run, out_shape=[SPACES[p](s, d) if p != NEAR else jax.Shap...  20.7 us
    all_to_all x3, starting transfers between devices, swap_rows(): return lax.all_to_all(values, 'tile', 0, 0, tiled=True)  14.8 us
    all_to_all x3, waiting for transfers between devices, swap_rows(): return lax.all_to_all(values, 'tile', 0, 0, tiled=True)  8.24 us
    all_gather x1, blocking collectives, body(): feats = lax.all_gather(hid, 'chan', axis=0, tiled=True)  7.33 us
    ppermute x3, starting transfers between devices, swap_bit(): lax.ppermute(values, 'tile', [(t, t ^ bit) for t in range(lax.axis_size('...  5.17 us
    ppermute x3, waiting for transfers between devices, swap_bit(): lax.ppermute(values, 'tile', [(t, t ^ bit) for t in range(lax.axis_size('...  4.61 us
    ppermute x6, starting transfers between devices, swap_chan(): lax.ppermute(values, 'chan', [(i, i ^ bit) for i in range(lax.axis_size('...  2.48 us
    ppermute x6, waiting for transfers between devices, swap_chan(): lax.ppermute(values, 'chan', [(i, i ^ bit) for i in range(lax.axis_size('...  1.61 us
  transfers between devices with their start and end apart: 12, of which 8 were waited for; matrix products, arithmetic and copies ran while one was open for 0% of the time, Pallas kernels for 24%

profile of v8, /device:TPU:0, one launch (start us, length us, event | category | flops | bytes accessed | tf_op | source)
XLA Modules:
  0.0 66.1 jit_solution(9122378644118881229)
XLA Ops:
  0.7 1.9 %shard_map.110.refs_5_ = bf16[8,64,256]{2,1,0:T(8,128)(2,1)} custom-call(bf16[64,1024]{1,0:T(8,128)(2,1)} %bitcast.10), custom_call_target="tpu_custom_call" | custom-call | flops 1000000000 | bytes 3500000 | tf_op jit(solution)/shard_map/pallas_call | solution.py:75
  2.6 7.4 %all-to-all-start = ((bf16[8,64,256]{2,1,0:T(8,128)(2,1)}), bf16[8,64,256]{2,1,0:T(8,128)(2,1)S(1)}, u32[]{:S(2)}, u32[]{:S(2)}) async-start(bf16[8,64,256]{2,1,0:T(8,128)(2,1)} %shard_map.110.refs_5_), calls=%async_computation | async-start | bytes 524288 | tf_op jit(solution)/shard_map/all_to_all | solution.py:656
  10.0 1.6 %collective-permute-start.1 = (bf16[64,1024]{1,0:T(8,128)(2,1)S(1)}, bf16[64,1024]{1,0:T(8,128)(2,1)S(1)}, u32[]{:S(2)}, u32[]{:S(2)}) collective-permute-start(bf16[64,1024]{1,0:T(8,128)(2,1)S(1)} %bitcast.6), channel_id=1, source_target_pairs={{0,2},{1,3},{2,0},{3,1},{4,6},{5,7},{6,4},{7,5},{8,10},{9,11},{10,... | collective-permute-start | bytes 393224 | tf_op jit(solution)/shard_map/ppermute | solution.py:642
  11.9 2.1 %shard_map.111 = (bf16[1024,256]{1,0:T(8,128)(2,1)S(1)}, f32[64,1024]{1,0:T(8,128)S(1)}, s32[8,8]{1,0:T(8,128)S(1)}, bf16[256,128]{1,0:T(8,128)(2,1)S(1)}, bf16[...) custom-call(bf16[256,1024]{1,0:T(8,128)(2,1)S(1)} %copy-done, ...), custom_call_target="tpu_custom_call" | custom-call | flops 2000000000 | bytes 7000000 | tf_op jit(solution)/shard_map/pallas_call | solution.py:75
  14.0 1.0 %collective-permute-done.1.refs_4_ = bf16[64,1024]{1,0:T(8,128)(2,1)S(1)} collective-permute-done((bf16[64,1024]{1,0:T(8,128)(2,1)S(1)}, bf16[64,1024]{1,0:T(8,128)(2,1)S(1)}, u32[]{:S(2)}, u32[]{:S(2)}) %collective-permute-start.1) | collective-permute-done | bytes 131104 | tf_op jit(solution)/shard_map/ppermute | solution.py:642
  15.0 3.9 %all-to-all-done.refs_7_ = bf16[8,64,256]{2,1,0:T(8,128)(2,1)S(1)} async-done(((bf16[8,64,256]{2,1,0:T(8,128)(2,1)}), bf16[8,64,256]{2,1,0:T(8,128)(2,1)S(1)}, u32[]{:S(2)}, u32[]{:S(2)}) %all-to-all-start) | async-done | bytes 262176 | tf_op jit(solution)/shard_map/all_to_all | solution.py:656
  18.9 1.3 %shard_map.112 = (bf16[64,1024]{1,0:T(8,128)(2,1)S(1)}, bf16[64,512]{1,0:T(8,128)(2,1)}) custom-call(s32[8,8]{1,0:T(8,128)S(1)} %get-tuple-element.43.refs_0_, bf16[256,128]{1,0:T(8,128)(2,1)S(1)} %get-tuple-element.44.refs_1_, bf16[256,128]{1,0:T(8,128)(2,1)S(1)} %get-tuple-element.45.refs_2_, bf16[256,256]{1,0:T(8,128)(2,1)S(1)} %get-tuple-element.46.refs_3_, ...), custom_call_target="tpu_custom_call" | custom-call | flops 1000000000 | bytes 3500000 | tf_op jit(solution)/shard_map/pallas_call | solution.py:75
  20.2 7.3 %all_gather.3.refs_6_.refs_0_ = bf16[256,1024]{1,0:T(8,128)(2,1)S(1)} all-gather(bf16[64,1024]{1,0:T(8,128)(2,1)S(1)} %get-tuple-element.51), channel_id=1, replica_groups=mesh['tile'=8,'chan'=4] {'chan'}, dimensions={0}, use_global_device_ids=true | all-gather | bytes 655360 | tf_op jit(solution)/shard_map/all_gather | solution.py:704
  27.6 1.7 %shard_map.114 = (bf16[1024,128]{1,0:T(8,128)(2,1)}, bf16[256,1024]{1,0:T(8,128)(2,1)S(1)}) custom-call(bf16[256,1024]{1,0:T(8,128)(2,1)S(1)} %all_gather.3.refs_6_.refs_0_, bf16[256,1024]{1,0:T(8,128)(2,1)S(1)} %get-tuple-element.52.refs_1_, bf16[256,256]{1,0:T(8,128)(2,1)S(1)} %get-tuple-element.53.refs_2_, bf16[256,256]{1,0:T(8,128)(2,1)S(1)} %get-tuple-element.54.refs_3_), custom_call_target="tpu_custom_call" | custom-call | flops 2200000000 | bytes 7700000 | tf_op jit(solution)/shard_map/pallas_call | solution.py:75
  29.3 3.6 %all-to-all-start.1 = ((bf16[8,128,128]{2,1,0:T(8,128)(2,1)}), bf16[8,128,128]{2,1,0:T(8,128)(2,1)S(1)}, u32[]{:S(2)}, u32[]{:S(2)}) async-start(bf16[8,128,128]{2,1,0:T(8,128)(2,1)} %bitcast.9), calls=%async_computation.1 | async-start | bytes 524288 | tf_op jit(solution)/shard_map/all_to_all | solution.py:656
  32.9 6.6 %shard_map.115 = (f32[64,1024]{1,0:T(8,128)S(1)}, bf16[16,128]{1,0:T(8,128)(2,1)S(1)}, bf16[4,64,256]{2,1,0:T(8,128)(2,1)S(1)}, bf16[4,64,256]{2,1,0:T(8,128)(2,1)S(1)}) custom-call(bf16[256,1024]{1,0:T(8,128)(2,1)S(1)} %all_gather.3.refs_6_.refs_0_, bf16[256,1024]{1,0:T(8,128)(2,1)S(1)} %get-tuple-element.52.refs_1_, bf16[256,1024]{1,0:T(8,128)(2,1)} %refs_2_.4, ...), custom_call_target="tpu_custom_call" | custom-call | flops 7500000256 | bytes 26250000 | tf_op jit(solution)/shard_map/pallas_call | solution.py:75
  39.6 2.1 %collective-permute-start.3 = (bf16[4,64,256]{2,1,0:T(8,128)(2,1)S(1)}, bf16[4,64,256]{2,1,0:T(8,128)(2,1)S(1)}, u32[]{:S(2)}, u32[]{:S(2)}) collective-permute-start(bf16[4,64,256]{2,1,0:T(8,128)(2,1)S(1)} %get-tuple-element.60), channel_id=1, source_target_pairs={{0,8},{4,12},{8,0},{12,4},{16,24},{20,28},{24,16},{28,20},{1,9},{5... | collective-permute-start | bytes 393224 | tf_op jit(solution)/shard_map/ppermute | solution.py:667
  41.7 0.8 %all-to-all-done.1.refs_0_ = bf16[8,128,128]{2,1,0:T(8,128)(2,1)S(1)} async-done(((bf16[8,128,128]{2,1,0:T(8,128)(2,1)}), bf16[8,128,128]{2,1,0:T(8,128)(2,1)S(1)}, u32[]{:S(2)}, u32[]{:S(2)}) %all-to-all-start.1) | async-done | bytes 262176 | tf_op jit(solution)/shard_map/all_to_all | solution.py:656
  42.4 0.8 %shard_map.116.refs_4_ = bf16[8,144,128]{2,1,0:T(8,128)(2,1)} custom-call(bf16[8,128,128]{2,1,0:T(8,128)(2,1)S(1)} %all-to-all-done.1.refs_0_, bf16[16,128]{1,0:T(8,128)(2,1)S(1)} %get-tuple-element.58.refs_1_), custom_call_target="tpu_custom_call" | custom-call | flops 1000000000 | bytes 3500000 | tf_op jit(solution)/shard_map/pallas_call | solution.py:75
  43.3 3.8 %all-to-all-start.2 = ((bf16[8,144,128]{2,1,0:T(8,128)(2,1)}), bf16[8,144,128]{2,1,0:T(8,128)(2,1)S(1)}, u32[]{:S(2)}, u32[]{:S(2)}) async-start(bf16[8,144,128]{2,1,0:T(8,128)(2,1)} %shard_map.116.refs_4_), calls=%async_computation.2 | async-start | bytes 589824 | tf_op jit(solution)/shard_map/all_to_all | solution.py:656
  47.1 2.1 %collective-permute-start.4 = (bf16[2,64,256]{2,1,0:T(8,128)(2,1)S(1)}, bf16[2,64,256]{2,1,0:T(8,128)(2,1)S(1)}, u32[]{:S(2)}, u32[]{:S(2)}) collective-permute-start(bf16[2,64,256]{2,1,0:T(8,128)(2,1)S(1)} %get-tuple-element.62), channel_id=1, source_target_pairs={{0,4},{4,0},{8,12},{12,8},{16,20},{20,16},{24,28},{28,24},{1,5},{5... | collective-permute-start | bytes 196616 | tf_op jit(solution)/shard_map/ppermute | solution.py:667
  49.2 2.9 %shard_map.118.refs_2_ = bf16[64,1024]{1,0:T(8,128)(2,1)} custom-call(bf16[256,1024]{1,0:T(8,128)(2,1)S(1)} %all_gather.3.refs_6_.refs_0_, bf16[1024,256]{1,0:T(8,128)(2,1)S(1)} %get-tuple-element.50.refs_9_.refs_0_.refs_3_.refs_1_, bf16[1024,256]{1,0:T(8,128)(2,1)S(1)} %copy-done.1, bf16[64,1024]{1,0:T(8,128)(2,1)} %bitcast.13, ...), custom_call_target="tpu_custom_call" | custom-call | flops 4000000000 | bytes 14000000 | tf_op jit(solution)/shard_map/pallas_call | solution.py:75
  52.1 0.8 %collective-permute-done.4.refs_1_ = bf16[2,64,256]{2,1,0:T(8,128)(2,1)S(1)} collective-permute-done((bf16[2,64,256]{2,1,0:T(8,128)(2,1)S(1)}, bf16[2,64,256]{2,1,0:T(8,128)(2,1)S(1)}, u32[]{:S(2)}, u32[]{:S(2)}) %collective-permute-start.4) | collective-permute-done | bytes 65568 | tf_op jit(solution)/shard_map/ppermute | solution.py:667
  52.9 3.6 %all-to-all-done.2.refs_0_ = bf16[8,144,128]{2,1,0:T(8,128)(2,1)S(1)} async-done(((bf16[8,144,128]{2,1,0:T(8,128)(2,1)}), bf16[8,144,128]{2,1,0:T(8,128)(2,1)S(1)}, u32[]{:S(2)}, u32[]{:S(2)}) %all-to-all-start.2) | async-done | bytes 294944 | tf_op jit(solution)/shard_map/all_to_all | solution.py:656
  56.6 0.9 %collective-permute-start.6 = (bf16[1040,128]{1,0:T(8,128)(2,1)S(1)}, bf16[1040,128]{1,0:T(8,128)(2,1)S(1)}, u32[]{:S(2)}, u32[]{:S(2)}) collective-permute-start(bf16[1040,128]{1,0:T(8,128)(2,1)S(1)} %shard_map.117.refs_0_), channel_id=1, source_target_pairs={{0,2},{1,3},{2,0},{3,1},{4,6},{5,7},{6,4},{7,5},{8,10},{9,11},{10,... | collective-permute-start | bytes 798728 | tf_op jit(solution)/shard_map/ppermute | solution.py:642
  57.4 1.0 %collective-permute-start.7 = (bf16[1,64,256]{2,1,0:T(8,128)(2,1)S(1)}, bf16[1,64,256]{2,1,0:T(8,128)(2,1)S(1)}, u32[]{:S(2)}, u32[]{:S(2)}) collective-permute-start(bf16[1,64,256]{2,1,0:T(8,128)(2,1)S(1)} %get-tuple-element.69), channel_id=1, source_target_pairs={{0,16},{4,20},{8,24},{12,28},{16,0},{20,4},{24,8},{28,12},{1,17},{... | collective-permute-start | bytes 98312 | tf_op jit(solution)/shard_map/ppermute | solution.py:667
  58.5 3.8 %collective-permute-done.7.refs_2_ = bf16[1,64,256]{2,1,0:T(8,128)(2,1)S(1)} collective-permute-done((bf16[1,64,256]{2,1,0:T(8,128)(2,1)S(1)}, bf16[1,64,256]{2,1,0:T(8,128)(2,1)S(1)}, u32[]{:S(2)}, u32[]{:S(2)}) %collective-permute-start.7) | collective-permute-done | bytes 32800 | tf_op jit(solution)/shard_map/ppermute | solution.py:667
  63.1 1.2 %shard_map.122 = (f32[256,1024]{1,0:T(8,128)}, f32[1024,256]{1,0:T(8,128)}, f32[256,128]{1,0:T(8,128)S(1)}, bf16[64,1024]{1,0:T(8,128)(2,1)}) custom-call(bf16[1040,128]{1,0:T(8,128)(2,1)S(1)} %shard_map.117.refs_0_, bf16[1040,128]{1,0:T(8,128)(2,1)S(1)} %collective-permute-done.5.refs_1_, bf16[1040,128]{1,0:T(8,128)(2,1)S(1)} %collective-permute-done.6.refs_2_, ...), custom_call_target="tpu_custom_call" | custom-call | flops 1200000000 | bytes 4200000 | tf_op jit(solution)/shard_map/pallas_call | solution.py:75
  64.6 1.5 %shard_map.123 = (f32[256,1024]{1,0:T(8,128)}, f32[1024,256]{1,0:T(8,128)}, f32[25,256]{1,0:T(8,128)}) custom-call(bf16[1040,128]{1,0:T(8,128)(2,1)S(1)} %collective-permute-done.8.refs_0_, f32[256,128]{1,0:T(8,128)S(1)} %get-tuple-element.73.refs_1_, f32[256,1024]{1,0:T(8,128)} %get-tuple-element.74.refs_2_, ...), custom_call_target="tpu_custom_call", output_to_operand_aliasing={{0}: (2, {}), {1}: (3, {})} | custom-call | flops 1200000000 | bytes 4200000 | tf_op jit(solution)/shard_map/pallas_call | solution.py:75
  (31 shorter events, 1.6 us)
Async XLA Ops:
  0.6 9.3 %copy-start.2 = (bf16[1,64,1024]{2,1,0:T(8,128)(2,1)S(1)}, bf16[1,64,1024]{2,1,0:T(8,128)(2,1)}, u32[]{:S(2)}) copy-start(bf16[1,64,1024]{2,1,0:T(8,128)(2,1)} %param.8) | copy-start | bytes 393220
  0.6 10.9 %copy-start.6 = (bf16[25,64]{1,0:T(8,128)(2,1)S(1)}, bf16[25,64]{1,0:T(8,128)(2,1)}, u32[]{:S(2)}) copy-start(bf16[25,64]{1,0:T(8,128)(2,1)} %param.9) | copy-start | bytes 9604
  2.6 9.3 %copy-start = (bf16[256,1024]{1,0:T(8,128)(2,1)S(1)}, bf16[256,1024]{1,0:T(8,128)(2,1)}, u32[]{:S(2)}) copy-start(bf16[256,1024]{1,0:T(8,128)(2,1)} %refs_2_.4) | copy-start | bytes 1572868
  2.6 16.3 %all-to-all-start = ((bf16[8,64,256]{2,1,0:T(8,128)(2,1)}), bf16[8,64,256]{2,1,0:T(8,128)(2,1)S(1)}, u32[]{:S(2)}, u32[]{:S(2)}) async-start(bf16[8,64,256]{2,1,0:T(8,128)(2,1)} %shard_map.110.refs_5_), calls=%async_computation | async-start | bytes 524288 | tf_op jit(solution)/shard_map/all_to_all | solution.py:656
  10.0 1.9 %copy-start.3 = (s32[8,8]{1,0:T(8,128)S(1)}, s32[8,8]{1,0:T(8,128)}, u32[]{:S(2)}) copy-start(s32[8,8]{1,0:T(8,128)} %refs_9_.1) | copy-start | bytes 772
  10.0 1.9 %copy-start.4 = (s32[8,8]{1,0:T(8,128)S(1)}, s32[8,8]{1,0:T(8,128)}, u32[]{:S(2)}) copy-start(s32[8,8]{1,0:T(8,128)} %refs_10_.1) | copy-start | bytes 772
  10.0 5.0 %collective-permute-start.1 = (bf16[64,1024]{1,0:T(8,128)(2,1)S(1)}, bf16[64,1024]{1,0:T(8,128)(2,1)S(1)}, u32[]{:S(2)}, u32[]{:S(2)}) collective-permute-start(bf16[64,1024]{1,0:T(8,128)(2,1)S(1)} %bitcast.6), channel_id=1, source_target_pairs={{0,2},{1,3},{2,0},{3,1},{4,6},{5,7},{6,4},{7,5},{8,10},{9,11},{10,... | collective-permute-start | bytes 393224 | tf_op jit(solution)/shard_map/ppermute | solution.py:642
  11.6 16.0 %collective-permute-start = (bf16[64,1024]{1,0:T(8,128)(2,1)S(1)}, bf16[64,1024]{1,0:T(8,128)(2,1)S(1)}, u32[]{:S(2)}, u32[]{:S(2)}) collective-permute-start(bf16[64,1024]{1,0:T(8,128)(2,1)S(1)} %bitcast.7), channel_id=1, source_target_pairs={{0,1},{1,0},{2,3},{3,2},{4,5},{5,4},{6,7},{7,6},{8,9},{9,8},{10,11... | collective-permute-start | bytes 393224 | tf_op jit(solution)/shard_map/ppermute | solution.py:642
  15.0 12.5 %collective-permute-start.2 = (bf16[64,1024]{1,0:T(8,128)(2,1)S(1)}, bf16[64,1024]{1,0:T(8,128)(2,1)S(1)}, u32[]{:S(2)}, u32[]{:S(2)}) collective-permute-start(bf16[64,1024]{1,0:T(8,128)(2,1)S(1)} %collective-permute-done.1.refs_4_), channel_id=1, source_target_pairs={{0,1},{1,0},{2,3},{3,2},{4,5},{5,4},{6,7},{7,6},{8,9},{9,8},{10,11... | collective-permute-start | bytes 393224 | tf_op jit(solution)/shard_map/ppermute | solution.py:642
  20.2 7.4 %copy-start.1 = (bf16[1024,256]{1,0:T(8,128)(2,1)S(1)}, bf16[1024,256]{1,0:T(8,128)(2,1)}, u32[]{:S(2)}) copy-start(bf16[1024,256]{1,0:T(8,128)(2,1)} %refs_2_.5) | copy-start | bytes 1572868
  29.3 3.6 %copy-start.5 = (bf16[256,1024]{1,0:T(8,128)(2,1)}, bf16[256,1024]{1,0:T(8,128)(2,1)S(1)}, u32[]{:S(2)}) copy-start(bf16[256,1024]{1,0:T(8,128)(2,1)S(1)} %get-tuple-element.56.refs_5_) | copy-start | bytes 1572868
  29.3 13.1 %all-to-all-start.1 = ((bf16[8,128,128]{2,1,0:T(8,128)(2,1)}), bf16[8,128,128]{2,1,0:T(8,128)(2,1)S(1)}, u32[]{:S(2)}, u32[]{:S(2)}) async-start(bf16[8,128,128]{2,1,0:T(8,128)(2,1)} %bitcast.9), calls=%async_computation.1 | async-start | bytes 524288 | tf_op jit(solution)/shard_map/all_to_all | solution.py:656
  39.6 7.5 %collective-permute-start.3 = (bf16[4,64,256]{2,1,0:T(8,128)(2,1)S(1)}, bf16[4,64,256]{2,1,0:T(8,128)(2,1)S(1)}, u32[]{:S(2)}, u32[]{:S(2)}) collective-permute-start(bf16[4,64,256]{2,1,0:T(8,128)(2,1)S(1)} %get-tuple-element.60), channel_id=1, source_target_pairs={{0,8},{4,12},{8,0},{12,4},{16,24},{20,28},{24,16},{28,20},{1,9},{5... | collective-permute-start | bytes 393224 | tf_op jit(solution)/shard_map/ppermute | solution.py:667
  43.3 13.3 %all-to-all-start.2 = ((bf16[8,144,128]{2,1,0:T(8,128)(2,1)}), bf16[8,144,128]{2,1,0:T(8,128)(2,1)S(1)}, u32[]{:S(2)}, u32[]{:S(2)}) async-start(bf16[8,144,128]{2,1,0:T(8,128)(2,1)} %shard_map.116.refs_4_), calls=%async_computation.2 | async-start | bytes 589824 | tf_op jit(solution)/shard_map/all_to_all | solution.py:656
  47.1 5.8 %collective-permute-start.4 = (bf16[2,64,256]{2,1,0:T(8,128)(2,1)S(1)}, bf16[2,64,256]{2,1,0:T(8,128)(2,1)S(1)}, u32[]{:S(2)}, u32[]{:S(2)}) collective-permute-start(bf16[2,64,256]{2,1,0:T(8,128)(2,1)S(1)} %get-tuple-element.62), channel_id=1, source_target_pairs={{0,4},{4,0},{8,12},{12,8},{16,20},{20,16},{24,28},{28,24},{1,5},{5... | collective-permute-start | bytes 196616 | tf_op jit(solution)/shard_map/ppermute | solution.py:667
  56.6 6.5 %collective-permute-start.6 = (bf16[1040,128]{1,0:T(8,128)(2,1)S(1)}, bf16[1040,128]{1,0:T(8,128)(2,1)S(1)}, u32[]{:S(2)}, u32[]{:S(2)}) collective-permute-start(bf16[1040,128]{1,0:T(8,128)(2,1)S(1)} %shard_map.117.refs_0_), channel_id=1, source_target_pairs={{0,2},{1,3},{2,0},{3,1},{4,6},{5,7},{6,4},{7,5},{8,10},{9,11},{10,... | collective-permute-start | bytes 798728 | tf_op jit(solution)/shard_map/ppermute | solution.py:642
  57.4 4.8 %collective-permute-start.7 = (bf16[1,64,256]{2,1,0:T(8,128)(2,1)S(1)}, bf16[1,64,256]{2,1,0:T(8,128)(2,1)S(1)}, u32[]{:S(2)}, u32[]{:S(2)}) collective-permute-start(bf16[1,64,256]{2,1,0:T(8,128)(2,1)S(1)} %get-tuple-element.69), channel_id=1, source_target_pairs={{0,16},{4,20},{8,24},{12,28},{16,0},{20,4},{24,8},{28,12},{1,17},{... | collective-permute-start | bytes 98312 | tf_op jit(solution)/shard_map/ppermute | solution.py:667
  58.5 4.6 %collective-permute-start.5 = (bf16[1040,128]{1,0:T(8,128)(2,1)S(1)}, bf16[1040,128]{1,0:T(8,128)(2,1)S(1)}, u32[]{:S(2)}, u32[]{:S(2)}) collective-permute-start(bf16[1040,128]{1,0:T(8,128)(2,1)S(1)} %shard_map.117.refs_0_), channel_id=1, source_target_pairs={{0,1},{1,0},{2,3},{3,2},{4,5},{5,4},{6,7},{7,6},{8,9},{9,8},{10,11... | collective-permute-start | bytes 798728 | tf_op jit(solution)/shard_map/ppermute | solution.py:642
  63.0 1.5 %collective-permute-start.8 = (bf16[1040,128]{1,0:T(8,128)(2,1)S(1)}, bf16[1040,128]{1,0:T(8,128)(2,1)S(1)}, u32[]{:S(2)}, u32[]{:S(2)}) collective-permute-start(bf16[1040,128]{1,0:T(8,128)(2,1)S(1)} %collective-permute-done.6.refs_2_), channel_id=1, source_target_pairs={{0,1},{1,0},{2,3},{3,2},{4,5},{5,4},{6,7},{7,6},{8,9},{9,8},{10,11... | collective-permute-start | bytes 798728 | tf_op jit(solution)/shard_map/ppermute | solution.py:642

commit v9 on v8

--- a/solution.py
+++ b/solution.py
@@ -275,7 +275,8 @@
                 hidden_ref, halo, gathered, sides):
     rims_ref, taps_ref, halo_ref = rims.get(), taps.get(), halo.ref
     channels, pixels = hidden_ref.shape
-    nb = tile_row(neighbours)
+    tiles = rims_ref.shape[0]
+    nb = [lax.rem(tile + tiles - first_tile(tiles), tiles) for tile in tile_row(neighbours)]
     halo_ref[:, :LANES] = dot(rims_ref[nb[1]], top.get()[...]).astype(BF16)
     halo_ref[:, LANES:2 * LANES] = dot(rims_ref[nb[6]], low.get()[...]).astype(BF16)
     for position, d in enumerate(SIDES):
@@ -652,8 +653,14 @@
     return [pieces[k] for k in range(groups)]
 
 
+def first_tile(tiles):
+    return tiles // 2
+
+
 def swap_rows(values):
-    return lax.all_to_all(values, "tile", 0, 0, tiled=True)
+    tiles = lax.axis_size("tile")
+    group = [(first_tile(tiles) + i) % tiles for i in range(tiles)]
+    return lax.all_to_all(values, "tile", 0, 0, tiled=True, axis_index_groups=[group])
 
 
 def halve(parts, bit, after):
@@ -746,7 +753,8 @@
     for step, bit in enumerate(bits[:-1]):
         border = halve(border, bit, [(outputs, RAW)] if step else [])
     weights, outputs, *border = lax.optimization_barrier((weights, outputs, *border))
-    border = [border[0], swap_bit(border[1], bits[-1])] if parts > 1 else [swap_rows(border[0])]
+    border = [border[0], swap_bit(border[1], bits[-1])] if parts > 1 else [
+        lax.all_to_all(border[0], "tile", 0, 0, tiled=True)]
     [grad_in] = call(functools.partial(border_kernel, edge),
                      [(accum, NEAR)] + [(part, NEAR) for part in border],
                      [((channels, pixels), BF16, PINNED)])

time: 66.6 us -> 63.2 us (0.949)
  waiting for transfers between devices: 14.5 us -> 8.06 us
  starting transfers between devices: 22.4 us -> 25.4 us
    all_to_all x3, waiting for transfers between devices: 8.24 us -> 2.62 us  [swap_rows(): lax.all_to_all(values, 'tile', 0, 0, tiled=True, axis_index_groups=[group])]
    all_to_all x3, starting transfers between devices: 14.8 us -> 18.6 us  [swap_rows(): lax.all_to_all(values, 'tile', 0, 0, tiled=True, axis_index_groups=[group])]
    ppermute x3, starting transfers between devices: 5.17 us -> 4.32 us  [swap_bit(): lax.ppermute(values, 'tile', [(t, t ^ bit) for t in range(lax.axis_size('...]
    ppermute x3, waiting for transfers between devices: 4.61 us -> 3.84 us  [swap_bit(): lax.ppermute(values, 'tile', [(t, t ^ bit) for t in range(lax.axis_size('...]
  transfers between devices with their start and end apart: 12 -> 12, of which waited for: 8 -> 8; matrix products, arithmetic and copies ran while one was open for 0% -> 0% of each run, Pallas kernels for 24% -> 25%
where the time goes in v9:
time: 63.2 us; the launch traced here: 62.7 us
  starting transfers between devices  25.4 us (40%)
  Pallas kernels  20.7 us (33%)
  waiting for transfers between devices  8.06 us (13%)
  blocking collectives  7.33 us (12%)
  between operations  0.81 us (1%)
    pallas_call x14, Pallas kernels, call(): pl.pallas_call(run, out_shape=[SPACES[p](s, d) if p != NEAR else jax.Shap...  20.7 us
    all_to_all x3, starting transfers between devices, swap_rows(): lax.all_to_all(values, 'tile', 0, 0, tiled=True, axis_index_groups=[group])  18.6 us
    all_gather x1, blocking collectives, body(): feats = lax.all_gather(hid, 'chan', axis=0, tiled=True)  7.33 us
    ppermute x3, starting transfers between devices, swap_bit(): lax.ppermute(values, 'tile', [(t, t ^ bit) for t in range(lax.axis_size('...  4.32 us
    ppermute x3, waiting for transfers between devices, swap_bit(): lax.ppermute(values, 'tile', [(t, t ^ bit) for t in range(lax.axis_size('...  3.84 us
    all_to_all x3, waiting for transfers between devices, swap_rows(): lax.all_to_all(values, 'tile', 0, 0, tiled=True, axis_index_groups=[group])  2.62 us
    ppermute x6, starting transfers between devices, swap_chan(): lax.ppermute(values, 'chan', [(i, i ^ bit) for i in range(lax.axis_size('...  2.49 us
    ppermute x6, waiting for transfers between devices, swap_chan(): lax.ppermute(values, 'chan', [(i, i ^ bit) for i in range(lax.axis_size('...  1.6 us
  transfers between devices with their start and end apart: 12, of which 8 were waited for; matrix products, arithmetic and copies ran while one was open for 0% of the time, Pallas kernels for 25%

profile of v9, /device:TPU:0, one launch (start us, length us, event | category | flops | bytes accessed | tf_op | source)
XLA Modules:
  0.0 62.7 jit_solution(5679785182078782150)
XLA Ops:
  0.7 1.9 %shard_map.110.refs_5_ = bf16[8,64,256]{2,1,0:T(8,128)(2,1)} custom-call(bf16[64,1024]{1,0:T(8,128)(2,1)} %bitcast.10), custom_call_target="tpu_custom_call" | custom-call | flops 1000000000 | bytes 3500000 | tf_op jit(solution)/shard_map/pallas_call | solution.py:75
  2.6 8.0 %all-to-all-start = ((bf16[8,64,256]{2,1,0:T(8,128)(2,1)}), bf16[8,64,256]{2,1,0:T(8,128)(2,1)S(1)}, u32[]{:S(2)}, u32[]{:S(2)}) async-start(bf16[8,64,256]{2,1,0:T(8,128)(2,1)} %shard_map.110.refs_5_), calls=%async_computation | async-start | bytes 524288 | tf_op jit(solution)/shard_map/all_to_all | solution.py:663
  10.5 1.6 %collective-permute-start.1 = (bf16[64,1024]{1,0:T(8,128)(2,1)S(1)}, bf16[64,1024]{1,0:T(8,128)(2,1)S(1)}, u32[]{:S(2)}, u32[]{:S(2)}) collective-permute-start(bf16[64,1024]{1,0:T(8,128)(2,1)S(1)} %bitcast.6), channel_id=1, source_target_pairs={{0,2},{1,3},{2,0},{3,1},{4,6},{5,7},{6,4},{7,5},{8,10},{9,11},{10,... | collective-permute-start | bytes 393224 | tf_op jit(solution)/shard_map/ppermute | solution.py:643
  12.4 2.1 %shard_map.111 = (bf16[1024,256]{1,0:T(8,128)(2,1)S(1)}, f32[64,1024]{1,0:T(8,128)S(1)}, s32[8,8]{1,0:T(8,128)S(1)}, bf16[256,128]{1,0:T(8,128)(2,1)S(1)}, bf16[...) custom-call(bf16[256,1024]{1,0:T(8,128)(2,1)S(1)} %copy-done, ...), custom_call_target="tpu_custom_call" | custom-call | flops 2000000000 | bytes 7000000 | tf_op jit(solution)/shard_map/pallas_call | solution.py:75
  14.6 1.0 %collective-permute-done.1.refs_4_ = bf16[64,1024]{1,0:T(8,128)(2,1)S(1)} collective-permute-done((bf16[64,1024]{1,0:T(8,128)(2,1)S(1)}, bf16[64,1024]{1,0:T(8,128)(2,1)S(1)}, u32[]{:S(2)}, u32[]{:S(2)}) %collective-permute-start.1) | collective-permute-done | bytes 131104 | tf_op jit(solution)/shard_map/ppermute | solution.py:643
  15.6 1.5 %all-to-all-done.refs_7_ = bf16[8,64,256]{2,1,0:T(8,128)(2,1)S(1)} async-done(((bf16[8,64,256]{2,1,0:T(8,128)(2,1)}), bf16[8,64,256]{2,1,0:T(8,128)(2,1)S(1)}, u32[]{:S(2)}, u32[]{:S(2)}) %all-to-all-start) | async-done | bytes 262176 | tf_op jit(solution)/shard_map/all_to_all | solution.py:663
  17.1 1.3 %shard_map.112 = (bf16[64,1024]{1,0:T(8,128)(2,1)S(1)}, bf16[64,512]{1,0:T(8,128)(2,1)}) custom-call(s32[8,8]{1,0:T(8,128)S(1)} %get-tuple-element.43.refs_0_, bf16[256,128]{1,0:T(8,128)(2,1)S(1)} %get-tuple-element.44.refs_1_, bf16[256,128]{1,0:T(8,128)(2,1)S(1)} %get-tuple-element.45.refs_2_, bf16[256,256]{1,0:T(8,128)(2,1)S(1)} %get-tuple-element.46.refs_3_, ...), custom_call_target="tpu_custom_call" | custom-call | flops 1000000000 | bytes 3500000 | tf_op jit(solution)/shard_map/pallas_call | solution.py:75
  18.4 7.3 %all_gather.3.refs_6_.refs_0_ = bf16[256,1024]{1,0:T(8,128)(2,1)S(1)} all-gather(bf16[64,1024]{1,0:T(8,128)(2,1)S(1)} %get-tuple-element.51), channel_id=1, replica_groups=mesh['tile'=8,'chan'=4] {'chan'}, dimensions={0}, use_global_device_ids=true | all-gather | bytes 655360 | tf_op jit(solution)/shard_map/all_gather | solution.py:711
  25.8 1.7 %shard_map.114 = (bf16[1024,128]{1,0:T(8,128)(2,1)}, bf16[256,1024]{1,0:T(8,128)(2,1)S(1)}) custom-call(bf16[256,1024]{1,0:T(8,128)(2,1)S(1)} %all_gather.3.refs_6_.refs_0_, bf16[256,1024]{1,0:T(8,128)(2,1)S(1)} %get-tuple-element.52.refs_1_, bf16[256,256]{1,0:T(8,128)(2,1)S(1)} %get-tuple-element.53.refs_2_, bf16[256,256]{1,0:T(8,128)(2,1)S(1)} %get-tuple-element.54.refs_3_), custom_call_target="tpu_custom_call" | custom-call | flops 2200000000 | bytes 7700000 | tf_op jit(solution)/shard_map/pallas_call | solution.py:75
  27.5 5.3 %all-to-all-start.1 = ((bf16[8,128,128]{2,1,0:T(8,128)(2,1)}), bf16[8,128,128]{2,1,0:T(8,128)(2,1)S(1)}, u32[]{:S(2)}, u32[]{:S(2)}) async-start(bf16[8,128,128]{2,1,0:T(8,128)(2,1)} %bitcast.9), calls=%async_computation.1 | async-start | bytes 524288 | tf_op jit(solution)/shard_map/all_to_all | solution.py:663
  32.9 6.6 %shard_map.115 = (f32[64,1024]{1,0:T(8,128)S(1)}, bf16[16,128]{1,0:T(8,128)(2,1)S(1)}, bf16[4,64,256]{2,1,0:T(8,128)(2,1)S(1)}, bf16[4,64,256]{2,1,0:T(8,128)(2,1)S(1)}) custom-call(bf16[256,1024]{1,0:T(8,128)(2,1)S(1)} %all_gather.3.refs_6_.refs_0_, bf16[256,1024]{1,0:T(8,128)(2,1)S(1)} %get-tuple-element.52.refs_1_, bf16[256,1024]{1,0:T(8,128)(2,1)} %refs_2_.4, ...), custom_call_target="tpu_custom_call" | custom-call | flops 7500000256 | bytes 26250000 | tf_op jit(solution)/shard_map/pallas_call | solution.py:75
  39.5 0.6 %collective-permute-start.3 = (bf16[4,64,256]{2,1,0:T(8,128)(2,1)S(1)}, bf16[4,64,256]{2,1,0:T(8,128)(2,1)S(1)}, u32[]{:S(2)}, u32[]{:S(2)}) collective-permute-start(bf16[4,64,256]{2,1,0:T(8,128)(2,1)S(1)} %get-tuple-element.60), channel_id=1, source_target_pairs={{0,8},{4,12},{8,0},{12,4},{16,24},{20,28},{24,16},{28,20},{1,9},{5... | collective-permute-start | bytes 393224 | tf_op jit(solution)/shard_map/ppermute | solution.py:674
  40.2 0.8 %shard_map.116.refs_4_ = bf16[8,144,128]{2,1,0:T(8,128)(2,1)} custom-call(bf16[8,128,128]{2,1,0:T(8,128)(2,1)S(1)} %all-to-all-done.1.refs_0_, bf16[16,128]{1,0:T(8,128)(2,1)S(1)} %get-tuple-element.58.refs_1_), custom_call_target="tpu_custom_call" | custom-call | flops 1000000000 | bytes 3500000 | tf_op jit(solution)/shard_map/pallas_call | solution.py:75
  41.0 5.3 %all-to-all-start.2 = ((bf16[8,144,128]{2,1,0:T(8,128)(2,1)}), bf16[8,144,128]{2,1,0:T(8,128)(2,1)S(1)}, u32[]{:S(2)}, u32[]{:S(2)}) async-start(bf16[8,144,128]{2,1,0:T(8,128)(2,1)} %shard_map.116.refs_4_), calls=%async_computation.2 | async-start | bytes 589824 | tf_op jit(solution)/shard_map/all_to_all | solution.py:663
  46.4 1.5 %collective-permute-start.4 = (bf16[2,64,256]{2,1,0:T(8,128)(2,1)S(1)}, bf16[2,64,256]{2,1,0:T(8,128)(2,1)S(1)}, u32[]{:S(2)}, u32[]{:S(2)}) collective-permute-start(bf16[2,64,256]{2,1,0:T(8,128)(2,1)S(1)} %get-tuple-element.62), channel_id=1, source_target_pairs={{0,4},{4,0},{8,12},{12,8},{16,20},{20,16},{24,28},{28,24},{1,5},{5... | collective-permute-start | bytes 196616 | tf_op jit(solution)/shard_map/ppermute | solution.py:674
  48.0 2.9 %shard_map.118.refs_2_ = bf16[64,1024]{1,0:T(8,128)(2,1)} custom-call(bf16[256,1024]{1,0:T(8,128)(2,1)S(1)} %all_gather.3.refs_6_.refs_0_, bf16[1024,256]{1,0:T(8,128)(2,1)S(1)} %get-tuple-element.50.refs_9_.refs_0_.refs_3_.refs_1_, bf16[1024,256]{1,0:T(8,128)(2,1)S(1)} %copy-done.1, bf16[64,1024]{1,0:T(8,128)(2,1)} %bitcast.13, ...), custom_call_target="tpu_custom_call" | custom-call | flops 4000000000 | bytes 14000000 | tf_op jit(solution)/shard_map/pallas_call | solution.py:75
  50.8 1.2 %collective-permute-done.4.refs_1_ = bf16[2,64,256]{2,1,0:T(8,128)(2,1)S(1)} collective-permute-done((bf16[2,64,256]{2,1,0:T(8,128)(2,1)S(1)}, bf16[2,64,256]{2,1,0:T(8,128)(2,1)S(1)}, u32[]{:S(2)}, u32[]{:S(2)}) %collective-permute-start.4) | collective-permute-done | bytes 65568 | tf_op jit(solution)/shard_map/ppermute | solution.py:674
  52.0 1.1 %all-to-all-done.2.refs_0_ = bf16[8,144,128]{2,1,0:T(8,128)(2,1)S(1)} async-done(((bf16[8,144,128]{2,1,0:T(8,128)(2,1)}), bf16[8,144,128]{2,1,0:T(8,128)(2,1)S(1)}, u32[]{:S(2)}, u32[]{:S(2)}) %all-to-all-start.2) | async-done | bytes 294944 | tf_op jit(solution)/shard_map/all_to_all | solution.py:663
  53.1 0.9 %collective-permute-start.6 = (bf16[1040,128]{1,0:T(8,128)(2,1)S(1)}, bf16[1040,128]{1,0:T(8,128)(2,1)S(1)}, u32[]{:S(2)}, u32[]{:S(2)}) collective-permute-start(bf16[1040,128]{1,0:T(8,128)(2,1)S(1)} %shard_map.117.refs_0_), channel_id=1, source_target_pairs={{0,2},{1,3},{2,0},{3,1},{4,6},{5,7},{6,4},{7,5},{8,10},{9,11},{10,... | collective-permute-start | bytes 798728 | tf_op jit(solution)/shard_map/ppermute | solution.py:643
  54.0 2.1 %collective-permute-start.7 = (bf16[1,64,256]{2,1,0:T(8,128)(2,1)S(1)}, bf16[1,64,256]{2,1,0:T(8,128)(2,1)S(1)}, u32[]{:S(2)}, u32[]{:S(2)}) collective-permute-start(bf16[1,64,256]{2,1,0:T(8,128)(2,1)S(1)} %get-tuple-element.69), channel_id=1, source_target_pairs={{0,16},{4,20},{8,24},{12,28},{16,0},{20,4},{24,8},{28,12},{1,17},{... | collective-permute-start | bytes 98312 | tf_op jit(solution)/shard_map/ppermute | solution.py:674
  56.2 2.7 %collective-permute-done.7.refs_2_ = bf16[1,64,256]{2,1,0:T(8,128)(2,1)S(1)} collective-permute-done((bf16[1,64,256]{2,1,0:T(8,128)(2,1)S(1)}, bf16[1,64,256]{2,1,0:T(8,128)(2,1)S(1)}, u32[]{:S(2)}, u32[]{:S(2)}) %collective-permute-start.7) | collective-permute-done | bytes 32800 | tf_op jit(solution)/shard_map/ppermute | solution.py:674
  58.8 0.5 shard_map.121.refs_4_
  59.6 1.2 %shard_map.122 = (f32[256,1024]{1,0:T(8,128)}, f32[1024,256]{1,0:T(8,128)}, f32[256,128]{1,0:T(8,128)S(1)}, bf16[64,1024]{1,0:T(8,128)(2,1)}) custom-call(bf16[1040,128]{1,0:T(8,128)(2,1)S(1)} %shard_map.117.refs_0_, bf16[1040,128]{1,0:T(8,128)(2,1)S(1)} %collective-permute-done.5.refs_1_, bf16[1040,128]{1,0:T(8,128)(2,1)S(1)} %collective-permute-done.6.refs_2_, ...), custom_call_target="tpu_custom_call" | custom-call | flops 1200000000 | bytes 4200000 | tf_op jit(solution)/shard_map/pallas_call | solution.py:75
  61.1 1.5 %shard_map.123 = (f32[256,1024]{1,0:T(8,128)}, f32[1024,256]{1,0:T(8,128)}, f32[25,256]{1,0:T(8,128)}) custom-call(bf16[1040,128]{1,0:T(8,128)(2,1)S(1)} %collective-permute-done.8.refs_0_, f32[256,128]{1,0:T(8,128)S(1)} %get-tuple-element.73.refs_1_, f32[256,1024]{1,0:T(8,128)} %get-tuple-element.74.refs_2_, ...), custom_call_target="tpu_custom_call", output_to_operand_aliasing={{0}: (2, {}), {1}: (3, {})} | custom-call | flops 1200000000 | bytes 4200000 | tf_op jit(solution)/shard_map/pallas_call | solution.py:75
  (31 shorter events, 1.2 us)
Async XLA Ops:
  0.6 9.9 %copy-start.2 = (bf16[1,64,1024]{2,1,0:T(8,128)(2,1)S(1)}, bf16[1,64,1024]{2,1,0:T(8,128)(2,1)}, u32[]{:S(2)}) copy-start(bf16[1,64,1024]{2,1,0:T(8,128)(2,1)} %param.8) | copy-start | bytes 393220
  0.6 11.5 %copy-start.6 = (bf16[25,64]{1,0:T(8,128)(2,1)S(1)}, bf16[25,64]{1,0:T(8,128)(2,1)}, u32[]{:S(2)}) copy-start(bf16[25,64]{1,0:T(8,128)(2,1)} %param.9) | copy-start | bytes 9604
  2.6 9.9 %copy-start = (bf16[256,1024]{1,0:T(8,128)(2,1)S(1)}, bf16[256,1024]{1,0:T(8,128)(2,1)}, u32[]{:S(2)}) copy-start(bf16[256,1024]{1,0:T(8,128)(2,1)} %refs_2_.4) | copy-start | bytes 1572868
  2.6 14.5 %all-to-all-start = ((bf16[8,64,256]{2,1,0:T(8,128)(2,1)}), bf16[8,64,256]{2,1,0:T(8,128)(2,1)S(1)}, u32[]{:S(2)}, u32[]{:S(2)}) async-start(bf16[8,64,256]{2,1,0:T(8,128)(2,1)} %shard_map.110.refs_5_), calls=%async_computation | async-start | bytes 524288 | tf_op jit(solution)/shard_map/all_to_all | solution.py:663
  10.5 1.9 %copy-start.3 = (s32[8,8]{1,0:T(8,128)S(1)}, s32[8,8]{1,0:T(8,128)}, u32[]{:S(2)}) copy-start(s32[8,8]{1,0:T(8,128)} %refs_9_.1) | copy-start | bytes 772
  10.5 1.9 %copy-start.4 = (s32[8,8]{1,0:T(8,128)S(1)}, s32[8,8]{1,0:T(8,128)}, u32[]{:S(2)}) copy-start(s32[8,8]{1,0:T(8,128)} %refs_10_.1) | copy-start | bytes 772
  10.5 5.0 %collective-permute-start.1 = (bf16[64,1024]{1,0:T(8,128)(2,1)S(1)}, bf16[64,1024]{1,0:T(8,128)(2,1)S(1)}, u32[]{:S(2)}, u32[]{:S(2)}) collective-permute-start(bf16[64,1024]{1,0:T(8,128)(2,1)S(1)} %bitcast.6), channel_id=1, source_target_pairs={{0,2},{1,3},{2,0},{3,1},{4,6},{5,7},{6,4},{7,5},{8,10},{9,11},{10,... | collective-permute-start | bytes 393224 | tf_op jit(solution)/shard_map/ppermute | solution.py:643
  12.1 13.6 %collective-permute-start = (bf16[64,1024]{1,0:T(8,128)(2,1)S(1)}, bf16[64,1024]{1,0:T(8,128)(2,1)S(1)}, u32[]{:S(2)}, u32[]{:S(2)}) collective-permute-start(bf16[64,1024]{1,0:T(8,128)(2,1)S(1)} %bitcast.7), channel_id=1, source_target_pairs={{0,1},{1,0},{2,3},{3,2},{4,5},{5,4},{6,7},{7,6},{8,9},{9,8},{10,11... | collective-permute-start | bytes 393224 | tf_op jit(solution)/shard_map/ppermute | solution.py:643
  15.6 10.2 %collective-permute-start.2 = (bf16[64,1024]{1,0:T(8,128)(2,1)S(1)}, bf16[64,1024]{1,0:T(8,128)(2,1)S(1)}, u32[]{:S(2)}, u32[]{:S(2)}) collective-permute-start(bf16[64,1024]{1,0:T(8,128)(2,1)S(1)} %collective-permute-done.1.refs_4_), channel_id=1, source_target_pairs={{0,1},{1,0},{2,3},{3,2},{4,5},{5,4},{6,7},{7,6},{8,9},{9,8},{10,11... | collective-permute-start | bytes 393224 | tf_op jit(solution)/shard_map/ppermute | solution.py:643
  18.4 7.4 %copy-start.1 = (bf16[1024,256]{1,0:T(8,128)(2,1)S(1)}, bf16[1024,256]{1,0:T(8,128)(2,1)}, u32[]{:S(2)}) copy-start(bf16[1024,256]{1,0:T(8,128)(2,1)} %refs_2_.5) | copy-start | bytes 1572868
  27.5 5.3 %copy-start.5 = (bf16[256,1024]{1,0:T(8,128)(2,1)}, bf16[256,1024]{1,0:T(8,128)(2,1)S(1)}, u32[]{:S(2)}) copy-start(bf16[256,1024]{1,0:T(8,128)(2,1)S(1)} %get-tuple-element.56.refs_5_) | copy-start | bytes 1572868
  27.5 12.7 %all-to-all-start.1 = ((bf16[8,128,128]{2,1,0:T(8,128)(2,1)}), bf16[8,128,128]{2,1,0:T(8,128)(2,1)S(1)}, u32[]{:S(2)}, u32[]{:S(2)}) async-start(bf16[8,128,128]{2,1,0:T(8,128)(2,1)} %bitcast.9), calls=%async_computation.1 | async-start | bytes 524288 | tf_op jit(solution)/shard_map/all_to_all | solution.py:663
  39.5 6.9 %collective-permute-start.3 = (bf16[4,64,256]{2,1,0:T(8,128)(2,1)S(1)}, bf16[4,64,256]{2,1,0:T(8,128)(2,1)S(1)}, u32[]{:S(2)}, u32[]{:S(2)}) collective-permute-start(bf16[4,64,256]{2,1,0:T(8,128)(2,1)S(1)} %get-tuple-element.60), channel_id=1, source_target_pairs={{0,8},{4,12},{8,0},{12,4},{16,24},{20,28},{24,16},{28,20},{1,9},{5... | collective-permute-start | bytes 393224 | tf_op jit(solution)/shard_map/ppermute | solution.py:674
  41.0 12.1 %all-to-all-start.2 = ((bf16[8,144,128]{2,1,0:T(8,128)(2,1)}), bf16[8,144,128]{2,1,0:T(8,128)(2,1)S(1)}, u32[]{:S(2)}, u32[]{:S(2)}) async-start(bf16[8,144,128]{2,1,0:T(8,128)(2,1)} %shard_map.116.refs_4_), calls=%async_computation.2 | async-start | bytes 589824 | tf_op jit(solution)/shard_map/all_to_all | solution.py:663
  46.4 5.6 %collective-permute-start.4 = (bf16[2,64,256]{2,1,0:T(8,128)(2,1)S(1)}, bf16[2,64,256]{2,1,0:T(8,128)(2,1)S(1)}, u32[]{:S(2)}, u32[]{:S(2)}) collective-permute-start(bf16[2,64,256]{2,1,0:T(8,128)(2,1)S(1)} %get-tuple-element.62), channel_id=1, source_target_pairs={{0,4},{4,0},{8,12},{12,8},{16,20},{20,16},{24,28},{28,24},{1,5},{5... | collective-permute-start | bytes 196616 | tf_op jit(solution)/shard_map/ppermute | solution.py:674
  53.1 6.5 %collective-permute-start.6 = (bf16[1040,128]{1,0:T(8,128)(2,1)S(1)}, bf16[1040,128]{1,0:T(8,128)(2,1)S(1)}, u32[]{:S(2)}, u32[]{:S(2)}) collective-permute-start(bf16[1040,128]{1,0:T(8,128)(2,1)S(1)} %shard_map.117.refs_0_), channel_id=1, source_target_pairs={{0,2},{1,3},{2,0},{3,1},{4,6},{5,7},{6,4},{7,5},{8,10},{9,11},{10,... | collective-permute-start | bytes 798728 | tf_op jit(solution)/shard_map/ppermute | solution.py:643
  54.0 4.8 %collective-permute-start.7 = (bf16[1,64,256]{2,1,0:T(8,128)(2,1)S(1)}, bf16[1,64,256]{2,1,0:T(8,128)(2,1)S(1)}, u32[]{:S(2)}, u32[]{:S(2)}) collective-permute-start(bf16[1,64,256]{2,1,0:T(8,128)(2,1)S(1)} %get-tuple-element.69), channel_id=1, source_target_pairs={{0,16},{4,20},{8,24},{12,28},{16,0},{20,4},{24,8},{28,12},{1,17},{... | collective-permute-start | bytes 98312 | tf_op jit(solution)/shard_map/ppermute | solution.py:674
  56.2 3.5 %collective-permute-start.5 = (bf16[1040,128]{1,0:T(8,128)(2,1)S(1)}, bf16[1040,128]{1,0:T(8,128)(2,1)S(1)}, u32[]{:S(2)}, u32[]{:S(2)}) collective-permute-start(bf16[1040,128]{1,0:T(8,128)(2,1)S(1)} %shard_map.117.refs_0_), channel_id=1, source_target_pairs={{0,1},{1,0},{2,3},{3,2},{4,5},{5,4},{6,7},{7,6},{8,9},{9,8},{10,11... | collective-permute-start | bytes 798728 | tf_op jit(solution)/shard_map/ppermute | solution.py:643
  59.6 1.5 %collective-permute-start.8 = (bf16[1040,128]{1,0:T(8,128)(2,1)S(1)}, bf16[1040,128]{1,0:T(8,128)(2,1)S(1)}, u32[]{:S(2)}, u32[]{:S(2)}) collective-permute-start(bf16[1040,128]{1,0:T(8,128)(2,1)S(1)} %collective-permute-done.6.refs_2_), channel_id=1, source_target_pairs={{0,1},{1,0},{2,3},{3,2},{4,5},{5,4},{6,7},{7,6},{8,9},{9,8},{10,11... | collective-permute-start | bytes 798728 | tf_op jit(solution)/shard_map/ppermute | solution.py:643

commit v10 on v9

--- a/solution.py
+++ b/solution.py
@@ -632,7 +632,8 @@
         own = jnp.concatenate(blocks * (full // channels), axis=0)
         all_taps = jnp.where(row_of // channels == owner, own, all_taps)
     if last:
-        g_tap_ref[...] = all_taps.T[:KSIZE * KSIZE, :] * scale
+        g_tap_ref.ref[...] = all_taps.T[:KSIZE * KSIZE, :] * scale
+        g_tap_ref.send()
     else:
         g_tap_ref[...] = all_taps
     for copy in copies:
@@ -765,7 +766,8 @@
         return call(
             functools.partial(final_kernel, which, channels, tap_rows, scale, last),
             [(pieces[k], NEAR) for k in which] + [(taps_so_far, NEAR)] + more,
-            [((full, hidden), F32, RAW), ((hidden, full), F32, RAW), (tap_shape, F32, NEAR)] + copied,
+            [((full, hidden), F32, RAW), ((hidden, full), F32, RAW), (tap_shape, F32, FAR if last else NEAR)]
+            + copied,
             [pltpu.VMEM((len(which), full, units), F32), pltpu.VMEM((len(which), units, full), F32),
              pltpu.SemaphoreType.DMA((2 * len(which) + 1,))],
             time=1.2, aliases={1 + len(which): 0, 2 + len(which): 1} if last else None)

time: 63.2 us -> 62.6 us (level)
  no operation moved by 1% of the time
where the time goes in v10:
time: 62.6 us; the launch traced here: 62.1 us
  starting transfers between devices  25.4 us (41%)
  Pallas kernels  20.1 us (32%)
  waiting for transfers between devices  8.06 us (13%)
  blocking collectives  7.33 us (12%)
  between operations  0.81 us (1%)
    pallas_call x14, Pallas kernels, call(): pl.pallas_call(run, out_shape=[SPACES[p](s, d) if p != NEAR else jax.Shap...  20.1 us
    all_to_all x3, starting transfers between devices, swap_rows(): lax.all_to_all(values, 'tile', 0, 0, tiled=True, axis_index_groups=[group])  18.6 us
    all_gather x1, blocking collectives, body(): feats = lax.all_gather(hid, 'chan', axis=0, tiled=True)  7.33 us
    ppermute x3, starting transfers between devices, swap_bit(): lax.ppermute(values, 'tile', [(t, t ^ bit) for t in range(lax.axis_size('...  4.32 us
    ppermute x3, waiting for transfers between devices, swap_bit(): lax.ppermute(values, 'tile', [(t, t ^ bit) for t in range(lax.axis_size('...  3.84 us
    all_to_all x3, waiting for transfers between devices, swap_rows(): lax.all_to_all(values, 'tile', 0, 0, tiled=True, axis_index_groups=[group])  2.62 us
    ppermute x6, starting transfers between devices, swap_chan(): lax.ppermute(values, 'chan', [(i, i ^ bit) for i in range(lax.axis_size('...  2.49 us
    ppermute x6, waiting for transfers between devices, swap_chan(): lax.ppermute(values, 'chan', [(i, i ^ bit) for i in range(lax.axis_size('...  1.6 us
  transfers between devices with their start and end apart: 12, of which 8 were waited for; matrix products, arithmetic and copies ran while one was open for 0% of the time, Pallas kernels for 25%

profile of v10, /device:TPU:0, one launch (start us, length us, event | category | flops | bytes accessed | tf_op | source)
XLA Modules:
  0.0 62.1 jit_solution(10442592217961349042)
XLA Ops:
  0.7 1.9 %shard_map.110.refs_5_ = bf16[8,64,256]{2,1,0:T(8,128)(2,1)} custom-call(bf16[64,1024]{1,0:T(8,128)(2,1)} %bitcast.10), custom_call_target="tpu_custom_call" | custom-call | flops 1000000000 | bytes 3500000 | tf_op jit(solution)/shard_map/pallas_call | solution.py:75
  2.6 8.0 %all-to-all-start = ((bf16[8,64,256]{2,1,0:T(8,128)(2,1)}), bf16[8,64,256]{2,1,0:T(8,128)(2,1)S(1)}, u32[]{:S(2)}, u32[]{:S(2)}) async-start(bf16[8,64,256]{2,1,0:T(8,128)(2,1)} %shard_map.110.refs_5_), calls=%async_computation | async-start | bytes 524288 | tf_op jit(solution)/shard_map/all_to_all | solution.py:664
  10.5 1.6 %collective-permute-start.1 = (bf16[64,1024]{1,0:T(8,128)(2,1)S(1)}, bf16[64,1024]{1,0:T(8,128)(2,1)S(1)}, u32[]{:S(2)}, u32[]{:S(2)}) collective-permute-start(bf16[64,1024]{1,0:T(8,128)(2,1)S(1)} %bitcast.6), channel_id=1, source_target_pairs={{0,2},{1,3},{2,0},{3,1},{4,6},{5,7},{6,4},{7,5},{8,10},{9,11},{10,... | collective-permute-start | bytes 393224 | tf_op jit(solution)/shard_map/ppermute | solution.py:644
  12.4 2.1 %shard_map.111 = (bf16[1024,256]{1,0:T(8,128)(2,1)S(1)}, f32[64,1024]{1,0:T(8,128)S(1)}, s32[8,8]{1,0:T(8,128)S(1)}, bf16[256,128]{1,0:T(8,128)(2,1)S(1)}, bf16[...) custom-call(bf16[256,1024]{1,0:T(8,128)(2,1)S(1)} %copy-done, ...), custom_call_target="tpu_custom_call" | custom-call | flops 2000000000 | bytes 7000000 | tf_op jit(solution)/shard_map/pallas_call | solution.py:75
  14.6 1.0 %collective-permute-done.1.refs_4_ = bf16[64,1024]{1,0:T(8,128)(2,1)S(1)} collective-permute-done((bf16[64,1024]{1,0:T(8,128)(2,1)S(1)}, bf16[64,1024]{1,0:T(8,128)(2,1)S(1)}, u32[]{:S(2)}, u32[]{:S(2)}) %collective-permute-start.1) | collective-permute-done | bytes 131104 | tf_op jit(solution)/shard_map/ppermute | solution.py:644
  15.6 1.5 %all-to-all-done.refs_7_ = bf16[8,64,256]{2,1,0:T(8,128)(2,1)S(1)} async-done(((bf16[8,64,256]{2,1,0:T(8,128)(2,1)}), bf16[8,64,256]{2,1,0:T(8,128)(2,1)S(1)}, u32[]{:S(2)}, u32[]{:S(2)}) %all-to-all-start) | async-done | bytes 262176 | tf_op jit(solution)/shard_map/all_to_all | solution.py:664
  17.1 1.3 %shard_map.112 = (bf16[64,1024]{1,0:T(8,128)(2,1)S(1)}, bf16[64,512]{1,0:T(8,128)(2,1)}) custom-call(s32[8,8]{1,0:T(8,128)S(1)} %get-tuple-element.43.refs_0_, bf16[256,128]{1,0:T(8,128)(2,1)S(1)} %get-tuple-element.44.refs_1_, bf16[256,128]{1,0:T(8,128)(2,1)S(1)} %get-tuple-element.45.refs_2_, bf16[256,256]{1,0:T(8,128)(2,1)S(1)} %get-tuple-element.46.refs_3_, ...), custom_call_target="tpu_custom_call" | custom-call | flops 1000000000 | bytes 3500000 | tf_op jit(solution)/shard_map/pallas_call | solution.py:75
  18.4 7.3 %all_gather.3.refs_6_.refs_0_ = bf16[256,1024]{1,0:T(8,128)(2,1)S(1)} all-gather(bf16[64,1024]{1,0:T(8,128)(2,1)S(1)} %get-tuple-element.51), channel_id=1, replica_groups=mesh['tile'=8,'chan'=4] {'chan'}, dimensions={0}, use_global_device_ids=true | all-gather | bytes 655360 | tf_op jit(solution)/shard_map/all_gather | solution.py:712
  25.8 1.7 %shard_map.114 = (bf16[1024,128]{1,0:T(8,128)(2,1)}, bf16[256,1024]{1,0:T(8,128)(2,1)S(1)}) custom-call(bf16[256,1024]{1,0:T(8,128)(2,1)S(1)} %all_gather.3.refs_6_.refs_0_, bf16[256,1024]{1,0:T(8,128)(2,1)S(1)} %get-tuple-element.52.refs_1_, bf16[256,256]{1,0:T(8,128)(2,1)S(1)} %get-tuple-element.53.refs_2_, bf16[256,256]{1,0:T(8,128)(2,1)S(1)} %get-tuple-element.54.refs_3_), custom_call_target="tpu_custom_call" | custom-call | flops 2200000000 | bytes 7700000 | tf_op jit(solution)/shard_map/pallas_call | solution.py:75
  27.5 5.3 %all-to-all-start.1 = ((bf16[8,128,128]{2,1,0:T(8,128)(2,1)}), bf16[8,128,128]{2,1,0:T(8,128)(2,1)S(1)}, u32[]{:S(2)}, u32[]{:S(2)}) async-start(bf16[8,128,128]{2,1,0:T(8,128)(2,1)} %bitcast.9), calls=%async_computation.1 | async-start | bytes 524288 | tf_op jit(solution)/shard_map/all_to_all | solution.py:664
  32.9 6.6 %shard_map.115 = (f32[64,1024]{1,0:T(8,128)S(1)}, bf16[16,128]{1,0:T(8,128)(2,1)S(1)}, bf16[4,64,256]{2,1,0:T(8,128)(2,1)S(1)}, bf16[4,64,256]{2,1,0:T(8,128)(2,1)S(1)}) custom-call(bf16[256,1024]{1,0:T(8,128)(2,1)S(1)} %all_gather.3.refs_6_.refs_0_, bf16[256,1024]{1,0:T(8,128)(2,1)S(1)} %get-tuple-element.52.refs_1_, bf16[256,1024]{1,0:T(8,128)(2,1)} %refs_2_.4, ...), custom_call_target="tpu_custom_call" | custom-call | flops 7500000256 | bytes 26250000 | tf_op jit(solution)/shard_map/pallas_call | solution.py:75
  39.5 0.6 %collective-permute-start.3 = (bf16[4,64,256]{2,1,0:T(8,128)(2,1)S(1)}, bf16[4,64,256]{2,1,0:T(8,128)(2,1)S(1)}, u32[]{:S(2)}, u32[]{:S(2)}) collective-permute-start(bf16[4,64,256]{2,1,0:T(8,128)(2,1)S(1)} %get-tuple-element.60), channel_id=1, source_target_pairs={{0,8},{4,12},{8,0},{12,4},{16,24},{20,28},{24,16},{28,20},{1,9},{5... | collective-permute-start | bytes 393224 | tf_op jit(solution)/shard_map/ppermute | solution.py:675
  40.2 0.8 %shard_map.116.refs_4_ = bf16[8,144,128]{2,1,0:T(8,128)(2,1)} custom-call(bf16[8,128,128]{2,1,0:T(8,128)(2,1)S(1)} %all-to-all-done.1.refs_0_, bf16[16,128]{1,0:T(8,128)(2,1)S(1)} %get-tuple-element.58.refs_1_), custom_call_target="tpu_custom_call" | custom-call | flops 1000000000 | bytes 3500000 | tf_op jit(solution)/shard_map/pallas_call | solution.py:75
  41.0 5.3 %all-to-all-start.2 = ((bf16[8,144,128]{2,1,0:T(8,128)(2,1)}), bf16[8,144,128]{2,1,0:T(8,128)(2,1)S(1)}, u32[]{:S(2)}, u32[]{:S(2)}) async-start(bf16[8,144,128]{2,1,0:T(8,128)(2,1)} %shard_map.116.refs_4_), calls=%async_computation.2 | async-start | bytes 589824 | tf_op jit(solution)/shard_map/all_to_all | solution.py:664
  46.4 1.5 %collective-permute-start.4 = (bf16[2,64,256]{2,1,0:T(8,128)(2,1)S(1)}, bf16[2,64,256]{2,1,0:T(8,128)(2,1)S(1)}, u32[]{:S(2)}, u32[]{:S(2)}) collective-permute-start(bf16[2,64,256]{2,1,0:T(8,128)(2,1)S(1)} %get-tuple-element.62), channel_id=1, source_target_pairs={{0,4},{4,0},{8,12},{12,8},{16,20},{20,16},{24,28},{28,24},{1,5},{5... | collective-permute-start | bytes 196616 | tf_op jit(solution)/shard_map/ppermute | solution.py:675
  48.0 2.9 %shard_map.118.refs_2_ = bf16[64,1024]{1,0:T(8,128)(2,1)} custom-call(bf16[256,1024]{1,0:T(8,128)(2,1)S(1)} %all_gather.3.refs_6_.refs_0_, bf16[1024,256]{1,0:T(8,128)(2,1)S(1)} %get-tuple-element.50.refs_9_.refs_0_.refs_3_.refs_1_, bf16[1024,256]{1,0:T(8,128)(2,1)S(1)} %copy-done.1, bf16[64,1024]{1,0:T(8,128)(2,1)} %bitcast.13, ...), custom_call_target="tpu_custom_call" | custom-call | flops 4000000000 | bytes 14000000 | tf_op jit(solution)/shard_map/pallas_call | solution.py:75
  50.8 1.2 %collective-permute-done.4.refs_1_ = bf16[2,64,256]{2,1,0:T(8,128)(2,1)S(1)} collective-permute-done((bf16[2,64,256]{2,1,0:T(8,128)(2,1)S(1)}, bf16[2,64,256]{2,1,0:T(8,128)(2,1)S(1)}, u32[]{:S(2)}, u32[]{:S(2)}) %collective-permute-start.4) | collective-permute-done | bytes 65568 | tf_op jit(solution)/shard_map/ppermute | solution.py:675
  52.0 1.1 %all-to-all-done.2.refs_0_ = bf16[8,144,128]{2,1,0:T(8,128)(2,1)S(1)} async-done(((bf16[8,144,128]{2,1,0:T(8,128)(2,1)}), bf16[8,144,128]{2,1,0:T(8,128)(2,1)S(1)}, u32[]{:S(2)}, u32[]{:S(2)}) %all-to-all-start.2) | async-done | bytes 294944 | tf_op jit(solution)/shard_map/all_to_all | solution.py:664
  53.1 0.9 %collective-permute-start.6 = (bf16[1040,128]{1,0:T(8,128)(2,1)S(1)}, bf16[1040,128]{1,0:T(8,128)(2,1)S(1)}, u32[]{:S(2)}, u32[]{:S(2)}) collective-permute-start(bf16[1040,128]{1,0:T(8,128)(2,1)S(1)} %shard_map.117.refs_0_), channel_id=1, source_target_pairs={{0,2},{1,3},{2,0},{3,1},{4,6},{5,7},{6,4},{7,5},{8,10},{9,11},{10,... | collective-permute-start | bytes 798728 | tf_op jit(solution)/shard_map/ppermute | solution.py:644
  54.0 2.1 %collective-permute-start.7 = (bf16[1,64,256]{2,1,0:T(8,128)(2,1)S(1)}, bf16[1,64,256]{2,1,0:T(8,128)(2,1)S(1)}, u32[]{:S(2)}, u32[]{:S(2)}) collective-permute-start(bf16[1,64,256]{2,1,0:T(8,128)(2,1)S(1)} %get-tuple-element.69), channel_id=1, source_target_pairs={{0,16},{4,20},{8,24},{12,28},{16,0},{20,4},{24,8},{28,12},{1,17},{... | collective-permute-start | bytes 98312 | tf_op jit(solution)/shard_map/ppermute | solution.py:675
  56.2 2.7 %collective-permute-done.7.refs_2_ = bf16[1,64,256]{2,1,0:T(8,128)(2,1)S(1)} collective-permute-done((bf16[1,64,256]{2,1,0:T(8,128)(2,1)S(1)}, bf16[1,64,256]{2,1,0:T(8,128)(2,1)S(1)}, u32[]{:S(2)}, u32[]{:S(2)}) %collective-permute-start.7) | collective-permute-done | bytes 32800 | tf_op jit(solution)/shard_map/ppermute | solution.py:675
  58.8 0.5 shard_map.121.refs_4_
  59.6 1.2 %shard_map.122 = (f32[256,1024]{1,0:T(8,128)}, f32[1024,256]{1,0:T(8,128)}, f32[256,128]{1,0:T(8,128)S(1)}, bf16[64,1024]{1,0:T(8,128)(2,1)}) custom-call(bf16[1040,128]{1,0:T(8,128)(2,1)S(1)} %shard_map.117.refs_0_, bf16[1040,128]{1,0:T(8,128)(2,1)S(1)} %collective-permute-done.5.refs_1_, bf16[1040,128]{1,0:T(8,128)(2,1)S(1)} %collective-permute-done.6.refs_2_, ...), custom_call_target="tpu_custom_call" | custom-call | flops 1200000000 | bytes 4200000 | tf_op jit(solution)/shard_map/pallas_call | solution.py:75
  61.1 0.9 %shard_map.123 = (f32[256,1024]{1,0:T(8,128)}, f32[1024,256]{1,0:T(8,128)}, f32[25,256]{1,0:T(8,128)}) custom-call(bf16[1040,128]{1,0:T(8,128)(2,1)S(1)} %collective-permute-done.8.refs_0_, f32[256,128]{1,0:T(8,128)S(1)} %get-tuple-element.73.refs_1_, f32[256,1024]{1,0:T(8,128)} %get-tuple-element.74.refs_2_, ...), custom_call_target="tpu_custom_call", output_to_operand_aliasing={{0}: (2, {}), {1}: (3, {})} | custom-call | flops 1200000000 | bytes 4200000 | tf_op jit(solution)/shard_map/pallas_call | solution.py:75
  (31 shorter events, 1.2 us)
Async XLA Ops:
  0.6 9.9 %copy-start.2 = (bf16[1,64,1024]{2,1,0:T(8,128)(2,1)S(1)}, bf16[1,64,1024]{2,1,0:T(8,128)(2,1)}, u32[]{:S(2)}) copy-start(bf16[1,64,1024]{2,1,0:T(8,128)(2,1)} %param.8) | copy-start | bytes 393220
  0.6 11.5 %copy-start.6 = (bf16[25,64]{1,0:T(8,128)(2,1)S(1)}, bf16[25,64]{1,0:T(8,128)(2,1)}, u32[]{:S(2)}) copy-start(bf16[25,64]{1,0:T(8,128)(2,1)} %param.9) | copy-start | bytes 9604
  2.6 9.9 %copy-start = (bf16[256,1024]{1,0:T(8,128)(2,1)S(1)}, bf16[256,1024]{1,0:T(8,128)(2,1)}, u32[]{:S(2)}) copy-start(bf16[256,1024]{1,0:T(8,128)(2,1)} %refs_2_.4) | copy-start | bytes 1572868
  2.6 14.5 %all-to-all-start = ((bf16[8,64,256]{2,1,0:T(8,128)(2,1)}), bf16[8,64,256]{2,1,0:T(8,128)(2,1)S(1)}, u32[]{:S(2)}, u32[]{:S(2)}) async-start(bf16[8,64,256]{2,1,0:T(8,128)(2,1)} %shard_map.110.refs_5_), calls=%async_computation | async-start | bytes 524288 | tf_op jit(solution)/shard_map/all_to_all | solution.py:664
  10.5 1.9 %copy-start.3 = (s32[8,8]{1,0:T(8,128)S(1)}, s32[8,8]{1,0:T(8,128)}, u32[]{:S(2)}) copy-start(s32[8,8]{1,0:T(8,128)} %refs_9_.1) | copy-start | bytes 772
  10.5 1.9 %copy-start.4 = (s32[8,8]{1,0:T(8,128)S(1)}, s32[8,8]{1,0:T(8,128)}, u32[]{:S(2)}) copy-start(s32[8,8]{1,0:T(8,128)} %refs_10_.1) | copy-start | bytes 772
  10.5 5.0 %collective-permute-start.1 = (bf16[64,1024]{1,0:T(8,128)(2,1)S(1)}, bf16[64,1024]{1,0:T(8,128)(2,1)S(1)}, u32[]{:S(2)}, u32[]{:S(2)}) collective-permute-start(bf16[64,1024]{1,0:T(8,128)(2,1)S(1)} %bitcast.6), channel_id=1, source_target_pairs={{0,2},{1,3},{2,0},{3,1},{4,6},{5,7},{6,4},{7,5},{8,10},{9,11},{10,... | collective-permute-start | bytes 393224 | tf_op jit(solution)/shard_map/ppermute | solution.py:644
  12.1 13.6 %collective-permute-start = (bf16[64,1024]{1,0:T(8,128)(2,1)S(1)}, bf16[64,1024]{1,0:T(8,128)(2,1)S(1)}, u32[]{:S(2)}, u32[]{:S(2)}) collective-permute-start(bf16[64,1024]{1,0:T(8,128)(2,1)S(1)} %bitcast.7), channel_id=1, source_target_pairs={{0,1},{1,0},{2,3},{3,2},{4,5},{5,4},{6,7},{7,6},{8,9},{9,8},{10,11... | collective-permute-start | bytes 393224 | tf_op jit(solution)/shard_map/ppermute | solution.py:644
  15.6 10.2 %collective-permute-start.2 = (bf16[64,1024]{1,0:T(8,128)(2,1)S(1)}, bf16[64,1024]{1,0:T(8,128)(2,1)S(1)}, u32[]{:S(2)}, u32[]{:S(2)}) collective-permute-start(bf16[64,1024]{1,0:T(8,128)(2,1)S(1)} %collective-permute-done.1.refs_4_), channel_id=1, source_target_pairs={{0,1},{1,0},{2,3},{3,2},{4,5},{5,4},{6,7},{7,6},{8,9},{9,8},{10,11... | collective-permute-start | bytes 393224 | tf_op jit(solution)/shard_map/ppermute | solution.py:644
  18.4 7.4 %copy-start.1 = (bf16[1024,256]{1,0:T(8,128)(2,1)S(1)}, bf16[1024,256]{1,0:T(8,128)(2,1)}, u32[]{:S(2)}) copy-start(bf16[1024,256]{1,0:T(8,128)(2,1)} %refs_2_.5) | copy-start | bytes 1572868
  27.5 5.3 %copy-start.5 = (bf16[256,1024]{1,0:T(8,128)(2,1)}, bf16[256,1024]{1,0:T(8,128)(2,1)S(1)}, u32[]{:S(2)}) copy-start(bf16[256,1024]{1,0:T(8,128)(2,1)S(1)} %get-tuple-element.56.refs_5_) | copy-start | bytes 1572868
  27.5 12.7 %all-to-all-start.1 = ((bf16[8,128,128]{2,1,0:T(8,128)(2,1)}), bf16[8,128,128]{2,1,0:T(8,128)(2,1)S(1)}, u32[]{:S(2)}, u32[]{:S(2)}) async-start(bf16[8,128,128]{2,1,0:T(8,128)(2,1)} %bitcast.9), calls=%async_computation.1 | async-start | bytes 524288 | tf_op jit(solution)/shard_map/all_to_all | solution.py:664
  39.5 6.9 %collective-permute-start.3 = (bf16[4,64,256]{2,1,0:T(8,128)(2,1)S(1)}, bf16[4,64,256]{2,1,0:T(8,128)(2,1)S(1)}, u32[]{:S(2)}, u32[]{:S(2)}) collective-permute-start(bf16[4,64,256]{2,1,0:T(8,128)(2,1)S(1)} %get-tuple-element.60), channel_id=1, source_target_pairs={{0,8},{4,12},{8,0},{12,4},{16,24},{20,28},{24,16},{28,20},{1,9},{5... | collective-permute-start | bytes 393224 | tf_op jit(solution)/shard_map/ppermute | solution.py:675
  41.0 12.1 %all-to-all-start.2 = ((bf16[8,144,128]{2,1,0:T(8,128)(2,1)}), bf16[8,144,128]{2,1,0:T(8,128)(2,1)S(1)}, u32[]{:S(2)}, u32[]{:S(2)}) async-start(bf16[8,144,128]{2,1,0:T(8,128)(2,1)} %shard_map.116.refs_4_), calls=%async_computation.2 | async-start | bytes 589824 | tf_op jit(solution)/shard_map/all_to_all | solution.py:664
  46.4 5.6 %collective-permute-start.4 = (bf16[2,64,256]{2,1,0:T(8,128)(2,1)S(1)}, bf16[2,64,256]{2,1,0:T(8,128)(2,1)S(1)}, u32[]{:S(2)}, u32[]{:S(2)}) collective-permute-start(bf16[2,64,256]{2,1,0:T(8,128)(2,1)S(1)} %get-tuple-element.62), channel_id=1, source_target_pairs={{0,4},{4,0},{8,12},{12,8},{16,20},{20,16},{24,28},{28,24},{1,5},{5... | collective-permute-start | bytes 196616 | tf_op jit(solution)/shard_map/ppermute | solution.py:675
  53.1 6.5 %collective-permute-start.6 = (bf16[1040,128]{1,0:T(8,128)(2,1)S(1)}, bf16[1040,128]{1,0:T(8,128)(2,1)S(1)}, u32[]{:S(2)}, u32[]{:S(2)}) collective-permute-start(bf16[1040,128]{1,0:T(8,128)(2,1)S(1)} %shard_map.117.refs_0_), channel_id=1, source_target_pairs={{0,2},{1,3},{2,0},{3,1},{4,6},{5,7},{6,4},{7,5},{8,10},{9,11},{10,... | collective-permute-start | bytes 798728 | tf_op jit(solution)/shard_map/ppermute | solution.py:644
  54.0 4.8 %collective-permute-start.7 = (bf16[1,64,256]{2,1,0:T(8,128)(2,1)S(1)}, bf16[1,64,256]{2,1,0:T(8,128)(2,1)S(1)}, u32[]{:S(2)}, u32[]{:S(2)}) collective-permute-start(bf16[1,64,256]{2,1,0:T(8,128)(2,1)S(1)} %get-tuple-element.69), channel_id=1, source_target_pairs={{0,16},{4,20},{8,24},{12,28},{16,0},{20,4},{24,8},{28,12},{1,17},{... | collective-permute-start | bytes 98312 | tf_op jit(solution)/shard_map/ppermute | solution.py:675
  56.2 3.5 %collective-permute-start.5 = (bf16[1040,128]{1,0:T(8,128)(2,1)S(1)}, bf16[1040,128]{1,0:T(8,128)(2,1)S(1)}, u32[]{:S(2)}, u32[]{:S(2)}) collective-permute-start(bf16[1040,128]{1,0:T(8,128)(2,1)S(1)} %shard_map.117.refs_0_), channel_id=1, source_target_pairs={{0,1},{1,0},{2,3},{3,2},{4,5},{5,4},{6,7},{7,6},{8,9},{9,8},{10,11... | collective-permute-start | bytes 798728 | tf_op jit(solution)/shard_map/ppermute | solution.py:644
  59.6 1.5 %collective-permute-start.8 = (bf16[1040,128]{1,0:T(8,128)(2,1)S(1)}, bf16[1040,128]{1,0:T(8,128)(2,1)S(1)}, u32[]{:S(2)}, u32[]{:S(2)}) collective-permute-start(bf16[1040,128]{1,0:T(8,128)(2,1)S(1)} %collective-permute-done.6.refs_2_), channel_id=1, source_target_pairs={{0,1},{1,0},{2,3},{3,2},{4,5},{5,4},{6,7},{7,6},{8,9},{9,8},{10,11... | collective-permute-start | bytes 798728 | tf_op jit(solution)/shard_map/ppermute | solution.py:644

commit v11 on v10

--- a/solution.py
+++ b/solution.py
@@ -516,9 +516,11 @@
     gathered[slot_of(nb[6], tiles)] += dot_nt(d_row[:, LANES:], low)
     packed = dot_nt(d_side[...], spread)
     pick, slot = side_map([rot[d] for d in SIDES], edge)
+    own = jnp.concatenate(
+        [jnp.where(slot == position, packed, 0.0) for position in range(len(SIDES))], axis=0)
+    placed = dot_nt(own.astype(BF16), pick)
     for position, d in enumerate(SIDES):
-        own = jnp.where(slot == position, packed, 0.0).astype(BF16)
-        gathered[slot_of(nb[d], tiles)] += dot_nt(own, pick)
+        gathered[slot_of(nb[d], tiles)] += placed[position * channels:(position + 1) * channels, :]
     store_parts(gathered, outs)
 
 

time: 62.6 us -> 62.3 us (level)
  no operation moved by 1% of the time
where the time goes in v11:
time: 62.3 us; the launch traced here: 61.8 us
  starting transfers between devices  25.4 us (41%)
  Pallas kernels  19.9 us (32%)
  waiting for transfers between devices  8.06 us (13%)
  blocking collectives  7.33 us (12%)
  between operations  0.81 us (1%)
    pallas_call x14, Pallas kernels, call(): pl.pallas_call(run, out_shape=[SPACES[p](s, d) if p != NEAR else jax.Shap...  19.9 us
    all_to_all x3, starting transfers between devices, swap_rows(): lax.all_to_all(values, 'tile', 0, 0, tiled=True, axis_index_groups=[group])  18.6 us
    all_gather x1, blocking collectives, body(): feats = lax.all_gather(hid, 'chan', axis=0, tiled=True)  7.33 us
    ppermute x3, starting transfers between devices, swap_bit(): lax.ppermute(values, 'tile', [(t, t ^ bit) for t in range(lax.axis_size('...  4.32 us
    ppermute x3, waiting for transfers between devices, swap_bit(): lax.ppermute(values, 'tile', [(t, t ^ bit) for t in range(lax.axis_size('...  3.71 us
    all_to_all x3, waiting for transfers between devices, swap_rows(): lax.all_to_all(values, 'tile', 0, 0, tiled=True, axis_index_groups=[group])  2.75 us
    ppermute x6, starting transfers between devices, swap_chan(): lax.ppermute(values, 'chan', [(i, i ^ bit) for i in range(lax.axis_size('...  2.49 us
    ppermute x6, waiting for transfers between devices, swap_chan(): lax.ppermute(values, 'chan', [(i, i ^ bit) for i in range(lax.axis_size('...  1.6 us
  transfers between devices with their start and end apart: 12, of which 8 were waited for; matrix products, arithmetic and copies ran while one was open for 0% of the time, Pallas kernels for 25%

profile of v11, /device:TPU:0, one launch (start us, length us, event | category | flops | bytes accessed | tf_op | source)
XLA Modules:
  0.0 61.8 jit_solution(10656448280104297738)
XLA Ops:
  0.7 1.9 %shard_map.110.refs_5_ = bf16[8,64,256]{2,1,0:T(8,128)(2,1)} custom-call(bf16[64,1024]{1,0:T(8,128)(2,1)} %bitcast.10), custom_call_target="tpu_custom_call" | custom-call | flops 1000000000 | bytes 3500000 | tf_op jit(solution)/shard_map/pallas_call | solution.py:75
  2.6 8.0 %all-to-all-start = ((bf16[8,64,256]{2,1,0:T(8,128)(2,1)}), bf16[8,64,256]{2,1,0:T(8,128)(2,1)S(1)}, u32[]{:S(2)}, u32[]{:S(2)}) async-start(bf16[8,64,256]{2,1,0:T(8,128)(2,1)} %shard_map.110.refs_5_), calls=%async_computation | async-start | bytes 524288 | tf_op jit(solution)/shard_map/all_to_all | solution.py:666
  10.5 1.6 %collective-permute-start.1 = (bf16[64,1024]{1,0:T(8,128)(2,1)S(1)}, bf16[64,1024]{1,0:T(8,128)(2,1)S(1)}, u32[]{:S(2)}, u32[]{:S(2)}) collective-permute-start(bf16[64,1024]{1,0:T(8,128)(2,1)S(1)} %bitcast.6), channel_id=1, source_target_pairs={{0,2},{1,3},{2,0},{3,1},{4,6},{5,7},{6,4},{7,5},{8,10},{9,11},{10,... | collective-permute-start | bytes 393224 | tf_op jit(solution)/shard_map/ppermute | solution.py:646
  12.4 2.1 %shard_map.111 = (bf16[1024,256]{1,0:T(8,128)(2,1)S(1)}, f32[64,1024]{1,0:T(8,128)S(1)}, s32[8,8]{1,0:T(8,128)S(1)}, bf16[256,128]{1,0:T(8,128)(2,1)S(1)}, bf16[...) custom-call(bf16[256,1024]{1,0:T(8,128)(2,1)S(1)} %copy-done, ...), custom_call_target="tpu_custom_call" | custom-call | flops 2000000000 | bytes 7000000 | tf_op jit(solution)/shard_map/pallas_call | solution.py:75
  14.6 1.0 %collective-permute-done.1.refs_4_ = bf16[64,1024]{1,0:T(8,128)(2,1)S(1)} collective-permute-done((bf16[64,1024]{1,0:T(8,128)(2,1)S(1)}, bf16[64,1024]{1,0:T(8,128)(2,1)S(1)}, u32[]{:S(2)}, u32[]{:S(2)}) %collective-permute-start.1) | collective-permute-done | bytes 131104 | tf_op jit(solution)/shard_map/ppermute | solution.py:646
  15.6 1.5 %all-to-all-done.refs_7_ = bf16[8,64,256]{2,1,0:T(8,128)(2,1)S(1)} async-done(((bf16[8,64,256]{2,1,0:T(8,128)(2,1)}), bf16[8,64,256]{2,1,0:T(8,128)(2,1)S(1)}, u32[]{:S(2)}, u32[]{:S(2)}) %all-to-all-start) | async-done | bytes 262176 | tf_op jit(solution)/shard_map/all_to_all | solution.py:666
  17.1 1.3 %shard_map.112 = (bf16[64,1024]{1,0:T(8,128)(2,1)S(1)}, bf16[64,512]{1,0:T(8,128)(2,1)}) custom-call(s32[8,8]{1,0:T(8,128)S(1)} %get-tuple-element.43.refs_0_, bf16[256,128]{1,0:T(8,128)(2,1)S(1)} %get-tuple-element.44.refs_1_, bf16[256,128]{1,0:T(8,128)(2,1)S(1)} %get-tuple-element.45.refs_2_, bf16[256,256]{1,0:T(8,128)(2,1)S(1)} %get-tuple-element.46.refs_3_, ...), custom_call_target="tpu_custom_call" | custom-call | flops 1000000000 | bytes 3500000 | tf_op jit(solution)/shard_map/pallas_call | solution.py:75
  18.4 7.3 %all_gather.3.refs_6_.refs_0_ = bf16[256,1024]{1,0:T(8,128)(2,1)S(1)} all-gather(bf16[64,1024]{1,0:T(8,128)(2,1)S(1)} %get-tuple-element.51), channel_id=1, replica_groups=mesh['tile'=8,'chan'=4] {'chan'}, dimensions={0}, use_global_device_ids=true | all-gather | bytes 655360 | tf_op jit(solution)/shard_map/all_gather | solution.py:714
  25.8 1.7 %shard_map.114 = (bf16[1024,128]{1,0:T(8,128)(2,1)}, bf16[256,1024]{1,0:T(8,128)(2,1)S(1)}) custom-call(bf16[256,1024]{1,0:T(8,128)(2,1)S(1)} %all_gather.3.refs_6_.refs_0_, bf16[256,1024]{1,0:T(8,128)(2,1)S(1)} %get-tuple-element.52.refs_1_, bf16[256,256]{1,0:T(8,128)(2,1)S(1)} %get-tuple-element.53.refs_2_, bf16[256,256]{1,0:T(8,128)(2,1)S(1)} %get-tuple-element.54.refs_3_), custom_call_target="tpu_custom_call" | custom-call | flops 2200000000 | bytes 7700000 | tf_op jit(solution)/shard_map/pallas_call | solution.py:75
  27.5 5.3 %all-to-all-start.1 = ((bf16[8,128,128]{2,1,0:T(8,128)(2,1)}), bf16[8,128,128]{2,1,0:T(8,128)(2,1)S(1)}, u32[]{:S(2)}, u32[]{:S(2)}) async-start(bf16[8,128,128]{2,1,0:T(8,128)(2,1)} %bitcast.9), calls=%async_computation.1 | async-start | bytes 524288 | tf_op jit(solution)/shard_map/all_to_all | solution.py:666
  32.9 6.4 %shard_map.115 = (f32[64,1024]{1,0:T(8,128)S(1)}, bf16[16,128]{1,0:T(8,128)(2,1)S(1)}, bf16[4,64,256]{2,1,0:T(8,128)(2,1)S(1)}, bf16[4,64,256]{2,1,0:T(8,128)(2,1)S(1)}) custom-call(bf16[256,1024]{1,0:T(8,128)(2,1)S(1)} %all_gather.3.refs_6_.refs_0_, bf16[256,1024]{1,0:T(8,128)(2,1)S(1)} %get-tuple-element.52.refs_1_, bf16[256,1024]{1,0:T(8,128)(2,1)} %refs_2_.4, ...), custom_call_target="tpu_custom_call" | custom-call | flops 7500000256 | bytes 26250000 | tf_op jit(solution)/shard_map/pallas_call | solution.py:75
  39.2 0.6 %collective-permute-start.3 = (bf16[4,64,256]{2,1,0:T(8,128)(2,1)S(1)}, bf16[4,64,256]{2,1,0:T(8,128)(2,1)S(1)}, u32[]{:S(2)}, u32[]{:S(2)}) collective-permute-start(bf16[4,64,256]{2,1,0:T(8,128)(2,1)S(1)} %get-tuple-element.60), channel_id=1, source_target_pairs={{0,8},{4,12},{8,0},{12,4},{16,24},{20,28},{24,16},{28,20},{1,9},{5... | collective-permute-start | bytes 393224 | tf_op jit(solution)/shard_map/ppermute | solution.py:677
  40.2 0.8 %shard_map.116.refs_4_ = bf16[8,144,128]{2,1,0:T(8,128)(2,1)} custom-call(bf16[8,128,128]{2,1,0:T(8,128)(2,1)S(1)} %all-to-all-done.1.refs_0_, bf16[16,128]{1,0:T(8,128)(2,1)S(1)} %get-tuple-element.58.refs_1_), custom_call_target="tpu_custom_call" | custom-call | flops 1000000000 | bytes 3500000 | tf_op jit(solution)/shard_map/pallas_call | solution.py:75
  41.0 5.3 %all-to-all-start.2 = ((bf16[8,144,128]{2,1,0:T(8,128)(2,1)}), bf16[8,144,128]{2,1,0:T(8,128)(2,1)S(1)}, u32[]{:S(2)}, u32[]{:S(2)}) async-start(bf16[8,144,128]{2,1,0:T(8,128)(2,1)} %shard_map.116.refs_4_), calls=%async_computation.2 | async-start | bytes 589824 | tf_op jit(solution)/shard_map/all_to_all | solution.py:666
  46.4 1.5 %collective-permute-start.4 = (bf16[2,64,256]{2,1,0:T(8,128)(2,1)S(1)}, bf16[2,64,256]{2,1,0:T(8,128)(2,1)S(1)}, u32[]{:S(2)}, u32[]{:S(2)}) collective-permute-start(bf16[2,64,256]{2,1,0:T(8,128)(2,1)S(1)} %get-tuple-element.62), channel_id=1, source_target_pairs={{0,4},{4,0},{8,12},{12,8},{16,20},{20,16},{24,28},{28,24},{1,5},{5... | collective-permute-start | bytes 196616 | tf_op jit(solution)/shard_map/ppermute | solution.py:677
  48.0 2.9 %shard_map.118.refs_2_ = bf16[64,1024]{1,0:T(8,128)(2,1)} custom-call(bf16[256,1024]{1,0:T(8,128)(2,1)S(1)} %all_gather.3.refs_6_.refs_0_, bf16[1024,256]{1,0:T(8,128)(2,1)S(1)} %get-tuple-element.50.refs_9_.refs_0_.refs_3_.refs_1_, bf16[1024,256]{1,0:T(8,128)(2,1)S(1)} %copy-done.1, bf16[64,1024]{1,0:T(8,128)(2,1)} %bitcast.13, ...), custom_call_target="tpu_custom_call" | custom-call | flops 4000000000 | bytes 14000000 | tf_op jit(solution)/shard_map/pallas_call | solution.py:75
  50.8 1.0 %collective-permute-done.4.refs_1_ = bf16[2,64,256]{2,1,0:T(8,128)(2,1)S(1)} collective-permute-done((bf16[2,64,256]{2,1,0:T(8,128)(2,1)S(1)}, bf16[2,64,256]{2,1,0:T(8,128)(2,1)S(1)}, u32[]{:S(2)}, u32[]{:S(2)}) %collective-permute-start.4) | collective-permute-done | bytes 65568 | tf_op jit(solution)/shard_map/ppermute | solution.py:677
  51.9 0.9 %all-to-all-done.2.refs_0_ = bf16[8,144,128]{2,1,0:T(8,128)(2,1)S(1)} async-done(((bf16[8,144,128]{2,1,0:T(8,128)(2,1)}), bf16[8,144,128]{2,1,0:T(8,128)(2,1)S(1)}, u32[]{:S(2)}, u32[]{:S(2)}) %all-to-all-start.2) | async-done | bytes 294944 | tf_op jit(solution)/shard_map/all_to_all | solution.py:666
  52.9 0.9 %collective-permute-start.6 = (bf16[1040,128]{1,0:T(8,128)(2,1)S(1)}, bf16[1040,128]{1,0:T(8,128)(2,1)S(1)}, u32[]{:S(2)}, u32[]{:S(2)}) collective-permute-start(bf16[1040,128]{1,0:T(8,128)(2,1)S(1)} %shard_map.117.refs_0_), channel_id=1, source_target_pairs={{0,2},{1,3},{2,0},{3,1},{4,6},{5,7},{6,4},{7,5},{8,10},{9,11},{10,... | collective-permute-start | bytes 798728 | tf_op jit(solution)/shard_map/ppermute | solution.py:646
  53.8 2.1 %collective-permute-start.7 = (bf16[1,64,256]{2,1,0:T(8,128)(2,1)S(1)}, bf16[1,64,256]{2,1,0:T(8,128)(2,1)S(1)}, u32[]{:S(2)}, u32[]{:S(2)}) collective-permute-start(bf16[1,64,256]{2,1,0:T(8,128)(2,1)S(1)} %get-tuple-element.69), channel_id=1, source_target_pairs={{0,16},{4,20},{8,24},{12,28},{16,0},{20,4},{24,8},{28,12},{1,17},{... | collective-permute-start | bytes 98312 | tf_op jit(solution)/shard_map/ppermute | solution.py:677
  55.9 2.7 %collective-permute-done.7.refs_2_ = bf16[1,64,256]{2,1,0:T(8,128)(2,1)S(1)} collective-permute-done((bf16[1,64,256]{2,1,0:T(8,128)(2,1)S(1)}, bf16[1,64,256]{2,1,0:T(8,128)(2,1)S(1)}, u32[]{:S(2)}, u32[]{:S(2)}) %collective-permute-start.7) | collective-permute-done | bytes 32800 | tf_op jit(solution)/shard_map/ppermute | solution.py:677
  58.6 0.5 shard_map.121.refs_4_
  59.4 1.2 %shard_map.122 = (f32[256,1024]{1,0:T(8,128)}, f32[1024,256]{1,0:T(8,128)}, f32[256,128]{1,0:T(8,128)S(1)}, bf16[64,1024]{1,0:T(8,128)(2,1)}) custom-call(bf16[1040,128]{1,0:T(8,128)(2,1)S(1)} %shard_map.117.refs_0_, bf16[1040,128]{1,0:T(8,128)(2,1)S(1)} %collective-permute-done.5.refs_1_, bf16[1040,128]{1,0:T(8,128)(2,1)S(1)} %collective-permute-done.6.refs_2_, ...), custom_call_target="tpu_custom_call" | custom-call | flops 1200000000 | bytes 4200000 | tf_op jit(solution)/shard_map/pallas_call | solution.py:75
  60.9 0.9 %shard_map.123 = (f32[256,1024]{1,0:T(8,128)}, f32[1024,256]{1,0:T(8,128)}, f32[25,256]{1,0:T(8,128)}) custom-call(bf16[1040,128]{1,0:T(8,128)(2,1)S(1)} %collective-permute-done.8.refs_0_, f32[256,128]{1,0:T(8,128)S(1)} %get-tuple-element.73.refs_1_, f32[256,1024]{1,0:T(8,128)} %get-tuple-element.74.refs_2_, ...), custom_call_target="tpu_custom_call", output_to_operand_aliasing={{0}: (2, {}), {1}: (3, {})} | custom-call | flops 1200000000 | bytes 4200000 | tf_op jit(solution)/shard_map/pallas_call | solution.py:75
  (31 shorter events, 1.4 us)
Async XLA Ops:
  0.6 9.9 %copy-start.2 = (bf16[1,64,1024]{2,1,0:T(8,128)(2,1)S(1)}, bf16[1,64,1024]{2,1,0:T(8,128)(2,1)}, u32[]{:S(2)}) copy-start(bf16[1,64,1024]{2,1,0:T(8,128)(2,1)} %param.8) | copy-start | bytes 393220
  0.6 11.5 %copy-start.6 = (bf16[25,64]{1,0:T(8,128)(2,1)S(1)}, bf16[25,64]{1,0:T(8,128)(2,1)}, u32[]{:S(2)}) copy-start(bf16[25,64]{1,0:T(8,128)(2,1)} %param.9) | copy-start | bytes 9604
  2.6 9.9 %copy-start = (bf16[256,1024]{1,0:T(8,128)(2,1)S(1)}, bf16[256,1024]{1,0:T(8,128)(2,1)}, u32[]{:S(2)}) copy-start(bf16[256,1024]{1,0:T(8,128)(2,1)} %refs_2_.4) | copy-start | bytes 1572868
  2.6 14.5 %all-to-all-start = ((bf16[8,64,256]{2,1,0:T(8,128)(2,1)}), bf16[8,64,256]{2,1,0:T(8,128)(2,1)S(1)}, u32[]{:S(2)}, u32[]{:S(2)}) async-start(bf16[8,64,256]{2,1,0:T(8,128)(2,1)} %shard_map.110.refs_5_), calls=%async_computation | async-start | bytes 524288 | tf_op jit(solution)/shard_map/all_to_all | solution.py:666
  10.5 1.9 %copy-start.3 = (s32[8,8]{1,0:T(8,128)S(1)}, s32[8,8]{1,0:T(8,128)}, u32[]{:S(2)}) copy-start(s32[8,8]{1,0:T(8,128)} %refs_9_.1) | copy-start | bytes 772
  10.5 1.9 %copy-start.4 = (s32[8,8]{1,0:T(8,128)S(1)}, s32[8,8]{1,0:T(8,128)}, u32[]{:S(2)}) copy-start(s32[8,8]{1,0:T(8,128)} %refs_10_.1) | copy-start | bytes 772
  10.5 5.0 %collective-permute-start.1 = (bf16[64,1024]{1,0:T(8,128)(2,1)S(1)}, bf16[64,1024]{1,0:T(8,128)(2,1)S(1)}, u32[]{:S(2)}, u32[]{:S(2)}) collective-permute-start(bf16[64,1024]{1,0:T(8,128)(2,1)S(1)} %bitcast.6), channel_id=1, source_target_pairs={{0,2},{1,3},{2,0},{3,1},{4,6},{5,7},{6,4},{7,5},{8,10},{9,11},{10,... | collective-permute-start | bytes 393224 | tf_op jit(solution)/shard_map/ppermute | solution.py:646
  12.1 13.6 %collective-permute-start = (bf16[64,1024]{1,0:T(8,128)(2,1)S(1)}, bf16[64,1024]{1,0:T(8,128)(2,1)S(1)}, u32[]{:S(2)}, u32[]{:S(2)}) collective-permute-start(bf16[64,1024]{1,0:T(8,128)(2,1)S(1)} %bitcast.7), channel_id=1, source_target_pairs={{0,1},{1,0},{2,3},{3,2},{4,5},{5,4},{6,7},{7,6},{8,9},{9,8},{10,11... | collective-permute-start | bytes 393224 | tf_op jit(solution)/shard_map/ppermute | solution.py:646
  15.6 10.2 %collective-permute-start.2 = (bf16[64,1024]{1,0:T(8,128)(2,1)S(1)}, bf16[64,1024]{1,0:T(8,128)(2,1)S(1)}, u32[]{:S(2)}, u32[]{:S(2)}) collective-permute-start(bf16[64,1024]{1,0:T(8,128)(2,1)S(1)} %collective-permute-done.1.refs_4_), channel_id=1, source_target_pairs={{0,1},{1,0},{2,3},{3,2},{4,5},{5,4},{6,7},{7,6},{8,9},{9,8},{10,11... | collective-permute-start | bytes 393224 | tf_op jit(solution)/shard_map/ppermute | solution.py:646
  18.4 7.4 %copy-start.1 = (bf16[1024,256]{1,0:T(8,128)(2,1)S(1)}, bf16[1024,256]{1,0:T(8,128)(2,1)}, u32[]{:S(2)}) copy-start(bf16[1024,256]{1,0:T(8,128)(2,1)} %refs_2_.5) | copy-start | bytes 1572868
  27.5 5.3 %copy-start.5 = (bf16[256,1024]{1,0:T(8,128)(2,1)}, bf16[256,1024]{1,0:T(8,128)(2,1)S(1)}, u32[]{:S(2)}) copy-start(bf16[256,1024]{1,0:T(8,128)(2,1)S(1)} %get-tuple-element.56.refs_5_) | copy-start | bytes 1572868
  27.5 12.7 %all-to-all-start.1 = ((bf16[8,128,128]{2,1,0:T(8,128)(2,1)}), bf16[8,128,128]{2,1,0:T(8,128)(2,1)S(1)}, u32[]{:S(2)}, u32[]{:S(2)}) async-start(bf16[8,128,128]{2,1,0:T(8,128)(2,1)} %bitcast.9), calls=%async_computation.1 | async-start | bytes 524288 | tf_op jit(solution)/shard_map/all_to_all | solution.py:666
  39.2 7.1 %collective-permute-start.3 = (bf16[4,64,256]{2,1,0:T(8,128)(2,1)S(1)}, bf16[4,64,256]{2,1,0:T(8,128)(2,1)S(1)}, u32[]{:S(2)}, u32[]{:S(2)}) collective-permute-start(bf16[4,64,256]{2,1,0:T(8,128)(2,1)S(1)} %get-tuple-element.60), channel_id=1, source_target_pairs={{0,8},{4,12},{8,0},{12,4},{16,24},{20,28},{24,16},{28,20},{1,9},{5... | collective-permute-start | bytes 393224 | tf_op jit(solution)/shard_map/ppermute | solution.py:677
  41.0 11.8 %all-to-all-start.2 = ((bf16[8,144,128]{2,1,0:T(8,128)(2,1)}), bf16[8,144,128]{2,1,0:T(8,128)(2,1)S(1)}, u32[]{:S(2)}, u32[]{:S(2)}) async-start(bf16[8,144,128]{2,1,0:T(8,128)(2,1)} %shard_map.116.refs_4_), calls=%async_computation.2 | async-start | bytes 589824 | tf_op jit(solution)/shard_map/all_to_all | solution.py:666
  46.4 5.4 %collective-permute-start.4 = (bf16[2,64,256]{2,1,0:T(8,128)(2,1)S(1)}, bf16[2,64,256]{2,1,0:T(8,128)(2,1)S(1)}, u32[]{:S(2)}, u32[]{:S(2)}) collective-permute-start(bf16[2,64,256]{2,1,0:T(8,128)(2,1)S(1)} %get-tuple-element.62), channel_id=1, source_target_pairs={{0,4},{4,0},{8,12},{12,8},{16,20},{20,16},{24,28},{28,24},{1,5},{5... | collective-permute-start | bytes 196616 | tf_op jit(solution)/shard_map/ppermute | solution.py:677
  52.9 6.5 %collective-permute-start.6 = (bf16[1040,128]{1,0:T(8,128)(2,1)S(1)}, bf16[1040,128]{1,0:T(8,128)(2,1)S(1)}, u32[]{:S(2)}, u32[]{:S(2)}) collective-permute-start(bf16[1040,128]{1,0:T(8,128)(2,1)S(1)} %shard_map.117.refs_0_), channel_id=1, source_target_pairs={{0,2},{1,3},{2,0},{3,1},{4,6},{5,7},{6,4},{7,5},{8,10},{9,11},{10,... | collective-permute-start | bytes 798728 | tf_op jit(solution)/shard_map/ppermute | solution.py:646
  53.8 4.8 %collective-permute-start.7 = (bf16[1,64,256]{2,1,0:T(8,128)(2,1)S(1)}, bf16[1,64,256]{2,1,0:T(8,128)(2,1)S(1)}, u32[]{:S(2)}, u32[]{:S(2)}) collective-permute-start(bf16[1,64,256]{2,1,0:T(8,128)(2,1)S(1)} %get-tuple-element.69), channel_id=1, source_target_pairs={{0,16},{4,20},{8,24},{12,28},{16,0},{20,4},{24,8},{28,12},{1,17},{... | collective-permute-start | bytes 98312 | tf_op jit(solution)/shard_map/ppermute | solution.py:677
  55.9 3.5 %collective-permute-start.5 = (bf16[1040,128]{1,0:T(8,128)(2,1)S(1)}, bf16[1040,128]{1,0:T(8,128)(2,1)S(1)}, u32[]{:S(2)}, u32[]{:S(2)}) collective-permute-start(bf16[1040,128]{1,0:T(8,128)(2,1)S(1)} %shard_map.117.refs_0_), channel_id=1, source_target_pairs={{0,1},{1,0},{2,3},{3,2},{4,5},{5,4},{6,7},{7,6},{8,9},{9,8},{10,11... | collective-permute-start | bytes 798728 | tf_op jit(solution)/shard_map/ppermute | solution.py:646
  59.3 1.5 %collective-permute-start.8 = (bf16[1040,128]{1,0:T(8,128)(2,1)S(1)}, bf16[1040,128]{1,0:T(8,128)(2,1)S(1)}, u32[]{:S(2)}, u32[]{:S(2)}) collective-permute-start(bf16[1040,128]{1,0:T(8,128)(2,1)S(1)} %collective-permute-done.6.refs_2_), channel_id=1, source_target_pairs={{0,1},{1,0},{2,3},{3,2},{4,5},{5,4},{6,7},{7,6},{8,9},{9,8},{10,11... | collective-permute-start | bytes 798728 | tf_op jit(solution)/shard_map/ppermute | solution.py:646

commit v12 on v11

--- a/solution.py
+++ b/solution.py
@@ -372,7 +372,7 @@
     out.ref[...] = (x.get()[...].astype(F32) + branch.astype(BF16).astype(F32)).astype(BF16)
 
 
-def back_kernel(edge, groups, tiles, feats, cots, w_in, w_in_t, w_out, gpre_own, x, halo, cot,
+def back_kernel(edge, groups, tiles, feats, cots, w_in, w_in_t, w_out, gpre_own, x, halo, spread, cot,
                 neighbours, rotations, taps, accum_ref, tap_ref, *refs):
     outs, (gpre, grad_ref, padded_ref, side_ref, turned_all, moved_all, d_row, d_side, gathered) = (
         refs[:-9], refs[-9:])
@@ -397,7 +397,7 @@
     padded_ref[:, :LANES] = halo[:, :LANES]
     padded_ref[:, LANES:LANES + pixels] = x.get()[...]
     padded_ref[:, LANES + pixels:] = halo[:, LANES:2 * LANES]
-    spread = spread_map(edge, padded_ref.shape[1])
+    spread = spread.get()[...]
     side_ref[...] = dot(halo[:, 2 * LANES:], spread).astype(BF16)
     tap_terms(edge, grad_ref, padded_ref, side_ref, tap_ref, turned_all, moved_all)
     halo_adjoint(edge, neighbours, rotations, spread, grad_ref, taps.get(), cot.get(), accum_ref,
@@ -405,13 +405,14 @@
 
 
 def prep_kernel(edge, w_in, x, neighbours, rotations, taps, w_in_t_ref, center_ref, nb_ref,
-                *map_refs):
+                top_ref, low_ref, pick_ref, slot_ref, columns_ref, spread):
     nb_ref[...] = neighbours.get()[...]
     rot = tile_row(rotations)
     pick, slot = side_map([rot[d] for d in SIDES], edge)
-    maps = (*row_halo_maps(rot[1], rot[6], edge), pick, slot, column_map(edge))
-    for ref, values in zip(map_refs, maps):
-        ref[...] = values
+    spread.ref[...] = spread_map(edge, edge * edge + 2 * LANES)
+    spread.send()
+    top_ref[...], low_ref[...] = row_halo_maps(rot[1], rot[6], edge)
+    pick_ref[...], slot_ref[...], columns_ref[...] = pick, slot, column_map(edge)
     w_in_t_ref[...] = w_in.get()[...].astype(F32).T.astype(BF16)
     center_conv(edge, x.get(), taps.get(), center_ref)
 
@@ -702,7 +703,9 @@
         [((hidden, full), BF16, NEAR), ((channels, pixels), F32, NEAR),
          (neighbours.shape, jnp.int32, NEAR), ((rim, LANES), BF16, NEAR), ((rim, LANES), BF16, NEAR),
          ((rim, 2 * LANES), BF16, NEAR), ((1, 2 * LANES), jnp.int32, NEAR),
-         ((2 * HALO * edge, pixels), BF16, NEAR)], time=2.0, after=[(rims, RAW)])
+         ((2 * HALO * edge, pixels), BF16, NEAR), ((2 * LANES, wide), BF16, FAR)], time=2.0,
+        after=[(rims, RAW)])
+    spread = maps.pop()
     rims = swap_rows(rims)
 
     hid, halo = call(
@@ -735,7 +738,7 @@
     accum, tap_part, *border = call(
         functools.partial(back_kernel, edge, groups, tiles),
         [(feats, NEAR), (cots, NEAR), (w_in, FAR), (w_in_t, NEAR), (w_out, NEAR), (gpre, FAR), (x, FAR),
-         (halo, FAR), (cot, FAR), (neighbours, NEAR), (rotations, NEAR), (taps, NEAR)],
+         (halo, FAR), (spread, FAR), (cot, FAR), (neighbours, NEAR), (rotations, NEAR), (taps, NEAR)],
         [((channels, pixels), F32, NEAR), ((tap_rows, LANES), BF16, NEAR)] + [placed] * parts,
         [pltpu.VMEM((hidden, pixels), BF16), pltpu.VMEM((channels, pixels), BF16),
          pltpu.VMEM((channels, wide), BF16), pltpu.VMEM((channels, wide), BF16),

time: 62.3 us -> 62.2 us (level)
  no operation moved by 1% of the time
where the time goes in v12:
time: 62.2 us; the launch traced here: 61.8 us
  starting transfers between devices  25.4 us (41%)
  Pallas kernels  20.2 us (32%)
  waiting for transfers between devices  7.67 us (12%)
  blocking collectives  7.33 us (12%)
  between operations  0.81 us (1%)
    pallas_call x14, Pallas kernels, call(): pl.pallas_call(run, out_shape=[SPACES[p](s, d) if p != NEAR else jax.Shap...  20.2 us
    all_to_all x3, starting transfers between devices, swap_rows(): lax.all_to_all(values, 'tile', 0, 0, tiled=True, axis_index_groups=[group])  18.6 us
    all_gather x1, blocking collectives, body(): feats = lax.all_gather(hid, 'chan', axis=0, tiled=True)  7.33 us
    ppermute x3, starting transfers between devices, swap_bit(): lax.ppermute(values, 'tile', [(t, t ^ bit) for t in range(lax.axis_size('...  4.32 us
    ppermute x3, waiting for transfers between devices, swap_bit(): lax.ppermute(values, 'tile', [(t, t ^ bit) for t in range(lax.axis_size('...  3.71 us
    all_to_all x3, waiting for transfers between devices, swap_rows(): lax.all_to_all(values, 'tile', 0, 0, tiled=True, axis_index_groups=[group])  2.74 us
    ppermute x6, starting transfers between devices, swap_chan(): lax.ppermute(values, 'chan', [(i, i ^ bit) for i in range(lax.axis_size('...  2.5 us
  transfers between devices with their start and end apart: 12, of which 8 were waited for; matrix products, arithmetic and copies ran while one was open for 0% of the time, Pallas kernels for 25%

profile of v12, /device:TPU:0, one launch (start us, length us, event | category | flops | bytes accessed | tf_op | source)
XLA Modules:
  0.0 61.8 jit_solution(16044672114852499030)
XLA Ops:
  0.7 1.9 %shard_map.110.refs_5_ = bf16[8,64,256]{2,1,0:T(8,128)(2,1)} custom-call(bf16[64,1024]{1,0:T(8,128)(2,1)} %bitcast.10), custom_call_target="tpu_custom_call" | custom-call | flops 1000000000 | bytes 3500000 | tf_op jit(solution)/shard_map/pallas_call | solution.py:75
  2.6 8.0 %all-to-all-start = ((bf16[8,64,256]{2,1,0:T(8,128)(2,1)}), bf16[8,64,256]{2,1,0:T(8,128)(2,1)S(1)}, u32[]{:S(2)}, u32[]{:S(2)}) async-start(bf16[8,64,256]{2,1,0:T(8,128)(2,1)} %shard_map.110.refs_5_), calls=%async_computation | async-start | bytes 524288 | tf_op jit(solution)/shard_map/all_to_all | solution.py:667
  10.5 1.6 %collective-permute-start.1 = (bf16[64,1024]{1,0:T(8,128)(2,1)S(1)}, bf16[64,1024]{1,0:T(8,128)(2,1)S(1)}, u32[]{:S(2)}, u32[]{:S(2)}) collective-permute-start(bf16[64,1024]{1,0:T(8,128)(2,1)S(1)} %bitcast.6), channel_id=1, source_target_pairs={{0,2},{1,3},{2,0},{3,1},{4,6},{5,7},{6,4},{7,5},{8,10},{9,11},{10,... | collective-permute-start | bytes 393224 | tf_op jit(solution)/shard_map/ppermute | solution.py:647
  12.4 2.5 %shard_map.111 = (bf16[1024,256]{1,0:T(8,128)(2,1)S(1)}, f32[64,1024]{1,0:T(8,128)S(1)}, s32[8,8]{1,0:T(8,128)S(1)}, bf16[256,128]{1,0:T(8,128)(2,1)S(1)}, bf16[...) custom-call(bf16[256,1024]{1,0:T(8,128)(2,1)S(1)} %copy-done, ...), custom_call_target="tpu_custom_call" | custom-call | flops 2000000000 | bytes 7000000 | tf_op jit(solution)/shard_map/pallas_call | solution.py:75
  14.9 0.6 %collective-permute-done.1.refs_4_ = bf16[64,1024]{1,0:T(8,128)(2,1)S(1)} collective-permute-done((bf16[64,1024]{1,0:T(8,128)(2,1)S(1)}, bf16[64,1024]{1,0:T(8,128)(2,1)S(1)}, u32[]{:S(2)}, u32[]{:S(2)}) %collective-permute-start.1) | collective-permute-done | bytes 131104 | tf_op jit(solution)/shard_map/ppermute | solution.py:647
  15.6 1.5 %all-to-all-done.refs_7_ = bf16[8,64,256]{2,1,0:T(8,128)(2,1)S(1)} async-done(((bf16[8,64,256]{2,1,0:T(8,128)(2,1)}), bf16[8,64,256]{2,1,0:T(8,128)(2,1)S(1)}, u32[]{:S(2)}, u32[]{:S(2)}) %all-to-all-start) | async-done | bytes 262176 | tf_op jit(solution)/shard_map/all_to_all | solution.py:667
  17.1 1.3 %shard_map.112 = (bf16[64,1024]{1,0:T(8,128)(2,1)S(1)}, bf16[64,512]{1,0:T(8,128)(2,1)}) custom-call(s32[8,8]{1,0:T(8,128)S(1)} %get-tuple-element.44.refs_0_, bf16[256,128]{1,0:T(8,128)(2,1)S(1)} %get-tuple-element.45.refs_1_, bf16[256,128]{1,0:T(8,128)(2,1)S(1)} %get-tuple-element.46.refs_2_, bf16[256,256]{1,0:T(8,128)(2,1)S(1)} %get-tuple-element.47.refs_3_, ...), custom_call_target="tpu_custom_call" | custom-call | flops 1000000000 | bytes 3500000 | tf_op jit(solution)/shard_map/pallas_call | solution.py:75
  18.4 7.3 %all_gather.3.refs_6_.refs_0_ = bf16[256,1024]{1,0:T(8,128)(2,1)S(1)} all-gather(bf16[64,1024]{1,0:T(8,128)(2,1)S(1)} %get-tuple-element.52), channel_id=1, replica_groups=mesh['tile'=8,'chan'=4] {'chan'}, dimensions={0}, use_global_device_ids=true | all-gather | bytes 655360 | tf_op jit(solution)/shard_map/all_gather | solution.py:717
  25.8 1.7 %shard_map.114 = (bf16[1024,128]{1,0:T(8,128)(2,1)}, bf16[256,1024]{1,0:T(8,128)(2,1)S(1)}) custom-call(bf16[256,1024]{1,0:T(8,128)(2,1)S(1)} %all_gather.3.refs_6_.refs_0_, bf16[256,1024]{1,0:T(8,128)(2,1)S(1)} %get-tuple-element.53.refs_1_, bf16[256,256]{1,0:T(8,128)(2,1)S(1)} %get-tuple-element.54.refs_2_, bf16[256,256]{1,0:T(8,128)(2,1)S(1)} %get-tuple-element.55.refs_3_), custom_call_target="tpu_custom_call" | custom-call | flops 2200000000 | bytes 7700000 | tf_op jit(solution)/shard_map/pallas_call | solution.py:75
  27.5 5.3 %all-to-all-start.1 = ((bf16[8,128,128]{2,1,0:T(8,128)(2,1)}), bf16[8,128,128]{2,1,0:T(8,128)(2,1)S(1)}, u32[]{:S(2)}, u32[]{:S(2)}) async-start(bf16[8,128,128]{2,1,0:T(8,128)(2,1)} %bitcast.9), calls=%async_computation.1 | async-start | bytes 524288 | tf_op jit(solution)/shard_map/all_to_all | solution.py:667
  32.9 6.3 %shard_map.115 = (f32[64,1024]{1,0:T(8,128)S(1)}, bf16[16,128]{1,0:T(8,128)(2,1)S(1)}, bf16[4,64,256]{2,1,0:T(8,128)(2,1)S(1)}, bf16[4,64,256]{2,1,0:T(8,128)(2,1)S(1)}) custom-call(bf16[256,1024]{1,0:T(8,128)(2,1)S(1)} %all_gather.3.refs_6_.refs_0_, bf16[256,1024]{1,0:T(8,128)(2,1)S(1)} %get-tuple-element.53.refs_1_, bf16[256,1024]{1,0:T(8,128)(2,1)} %refs_2_.4, ...), custom_call_target="tpu_custom_call" | custom-call | flops 7500000256 | bytes 26250000 | tf_op jit(solution)/shard_map/pallas_call | solution.py:75
  39.2 0.6 %collective-permute-start.3 = (bf16[4,64,256]{2,1,0:T(8,128)(2,1)S(1)}, bf16[4,64,256]{2,1,0:T(8,128)(2,1)S(1)}, u32[]{:S(2)}, u32[]{:S(2)}) collective-permute-start(bf16[4,64,256]{2,1,0:T(8,128)(2,1)S(1)} %get-tuple-element.62), channel_id=1, source_target_pairs={{0,8},{4,12},{8,0},{12,4},{16,24},{20,28},{24,16},{28,20},{1,9},{5... | collective-permute-start | bytes 393224 | tf_op jit(solution)/shard_map/ppermute | solution.py:678
  40.2 0.8 %shard_map.116.refs_4_ = bf16[8,144,128]{2,1,0:T(8,128)(2,1)} custom-call(bf16[8,128,128]{2,1,0:T(8,128)(2,1)S(1)} %all-to-all-done.1.refs_0_, bf16[16,128]{1,0:T(8,128)(2,1)S(1)} %get-tuple-element.60.refs_1_), custom_call_target="tpu_custom_call" | custom-call | flops 1000000000 | bytes 3500000 | tf_op jit(solution)/shard_map/pallas_call | solution.py:75
  41.0 5.3 %all-to-all-start.2 = ((bf16[8,144,128]{2,1,0:T(8,128)(2,1)}), bf16[8,144,128]{2,1,0:T(8,128)(2,1)S(1)}, u32[]{:S(2)}, u32[]{:S(2)}) async-start(bf16[8,144,128]{2,1,0:T(8,128)(2,1)} %shard_map.116.refs_4_), calls=%async_computation.2 | async-start | bytes 589824 | tf_op jit(solution)/shard_map/all_to_all | solution.py:667
  46.4 1.5 %collective-permute-start.4 = (bf16[2,64,256]{2,1,0:T(8,128)(2,1)S(1)}, bf16[2,64,256]{2,1,0:T(8,128)(2,1)S(1)}, u32[]{:S(2)}, u32[]{:S(2)}) collective-permute-start(bf16[2,64,256]{2,1,0:T(8,128)(2,1)S(1)} %get-tuple-element.64), channel_id=1, source_target_pairs={{0,4},{4,0},{8,12},{12,8},{16,20},{20,16},{24,28},{28,24},{1,5},{5... | collective-permute-start | bytes 196616 | tf_op jit(solution)/shard_map/ppermute | solution.py:678
  48.0 2.9 %shard_map.118.refs_2_ = bf16[64,1024]{1,0:T(8,128)(2,1)} custom-call(bf16[256,1024]{1,0:T(8,128)(2,1)S(1)} %all_gather.3.refs_6_.refs_0_, bf16[1024,256]{1,0:T(8,128)(2,1)S(1)} %get-tuple-element.51.refs_9_.refs_0_.refs_3_.refs_1_, bf16[1024,256]{1,0:T(8,128)(2,1)S(1)} %copy-done.1, bf16[64,1024]{1,0:T(8,128)(2,1)} %bitcast.13, ...), custom_call_target="tpu_custom_call" | custom-call | flops 4000000000 | bytes 14000000 | tf_op jit(solution)/shard_map/pallas_call | solution.py:75
  50.8 1.0 %collective-permute-done.4.refs_1_ = bf16[2,64,256]{2,1,0:T(8,128)(2,1)S(1)} collective-permute-done((bf16[2,64,256]{2,1,0:T(8,128)(2,1)S(1)}, bf16[2,64,256]{2,1,0:T(8,128)(2,1)S(1)}, u32[]{:S(2)}, u32[]{:S(2)}) %collective-permute-start.4) | collective-permute-done | bytes 65568 | tf_op jit(solution)/shard_map/ppermute | solution.py:678
  51.9 0.9 %all-to-all-done.2.refs_0_ = bf16[8,144,128]{2,1,0:T(8,128)(2,1)S(1)} async-done(((bf16[8,144,128]{2,1,0:T(8,128)(2,1)}), bf16[8,144,128]{2,1,0:T(8,128)(2,1)S(1)}, u32[]{:S(2)}, u32[]{:S(2)}) %all-to-all-start.2) | async-done | bytes 294944 | tf_op jit(solution)/shard_map/all_to_all | solution.py:667
  52.8 0.9 %collective-permute-start.6 = (bf16[1040,128]{1,0:T(8,128)(2,1)S(1)}, bf16[1040,128]{1,0:T(8,128)(2,1)S(1)}, u32[]{:S(2)}, u32[]{:S(2)}) collective-permute-start(bf16[1040,128]{1,0:T(8,128)(2,1)S(1)} %shard_map.117.refs_0_), channel_id=1, source_target_pairs={{0,2},{1,3},{2,0},{3,1},{4,6},{5,7},{6,4},{7,5},{8,10},{9,11},{10,... | collective-permute-start | bytes 798728 | tf_op jit(solution)/shard_map/ppermute | solution.py:647
  53.7 2.1 %collective-permute-start.7 = (bf16[1,64,256]{2,1,0:T(8,128)(2,1)S(1)}, bf16[1,64,256]{2,1,0:T(8,128)(2,1)S(1)}, u32[]{:S(2)}, u32[]{:S(2)}) collective-permute-start(bf16[1,64,256]{2,1,0:T(8,128)(2,1)S(1)} %get-tuple-element.71), channel_id=1, source_target_pairs={{0,16},{4,20},{8,24},{12,28},{16,0},{20,4},{24,8},{28,12},{1,17},{... | collective-permute-start | bytes 98312 | tf_op jit(solution)/shard_map/ppermute | solution.py:678
  55.9 2.7 %collective-permute-done.7.refs_2_ = bf16[1,64,256]{2,1,0:T(8,128)(2,1)S(1)} collective-permute-done((bf16[1,64,256]{2,1,0:T(8,128)(2,1)S(1)}, bf16[1,64,256]{2,1,0:T(8,128)(2,1)S(1)}, u32[]{:S(2)}, u32[]{:S(2)}) %collective-permute-start.7) | collective-permute-done | bytes 32800 | tf_op jit(solution)/shard_map/ppermute | solution.py:678
  58.5 0.5 shard_map.121.refs_4_
  59.3 1.2 %shard_map.122 = (f32[256,1024]{1,0:T(8,128)}, f32[1024,256]{1,0:T(8,128)}, f32[256,128]{1,0:T(8,128)S(1)}, bf16[64,1024]{1,0:T(8,128)(2,1)}) custom-call(bf16[1040,128]{1,0:T(8,128)(2,1)S(1)} %shard_map.117.refs_0_, bf16[1040,128]{1,0:T(8,128)(2,1)S(1)} %collective-permute-done.5.refs_1_, bf16[1040,128]{1,0:T(8,128)(2,1)S(1)} %collective-permute-done.6.refs_2_, ...), custom_call_target="tpu_custom_call" | custom-call | flops 1200000000 | bytes 4200000 | tf_op jit(solution)/shard_map/pallas_call | solution.py:75
  60.8 0.9 %shard_map.123 = (f32[256,1024]{1,0:T(8,128)}, f32[1024,256]{1,0:T(8,128)}, f32[25,256]{1,0:T(8,128)}) custom-call(bf16[1040,128]{1,0:T(8,128)(2,1)S(1)} %collective-permute-done.8.refs_0_, f32[256,128]{1,0:T(8,128)S(1)} %get-tuple-element.75.refs_1_, f32[256,1024]{1,0:T(8,128)} %get-tuple-element.76.refs_2_, ...), custom_call_target="tpu_custom_call", output_to_operand_aliasing={{0}: (2, {}), {1}: (3, {})} | custom-call | flops 1200000000 | bytes 4200000 | tf_op jit(solution)/shard_map/pallas_call | solution.py:75
  (31 shorter events, 1.4 us)
Async XLA Ops:
  0.6 9.9 %copy-start.2 = (bf16[1,64,1024]{2,1,0:T(8,128)(2,1)S(1)}, bf16[1,64,1024]{2,1,0:T(8,128)(2,1)}, u32[]{:S(2)}) copy-start(bf16[1,64,1024]{2,1,0:T(8,128)(2,1)} %param.8) | copy-start | bytes 393220
  0.6 11.5 %copy-start.6 = (bf16[25,64]{1,0:T(8,128)(2,1)S(1)}, bf16[25,64]{1,0:T(8,128)(2,1)}, u32[]{:S(2)}) copy-start(bf16[25,64]{1,0:T(8,128)(2,1)} %param.9) | copy-start | bytes 9604
  2.6 9.9 %copy-start = (bf16[256,1024]{1,0:T(8,128)(2,1)S(1)}, bf16[256,1024]{1,0:T(8,128)(2,1)}, u32[]{:S(2)}) copy-start(bf16[256,1024]{1,0:T(8,128)(2,1)} %refs_2_.4) | copy-start | bytes 1572868
  2.6 14.5 %all-to-all-start = ((bf16[8,64,256]{2,1,0:T(8,128)(2,1)}), bf16[8,64,256]{2,1,0:T(8,128)(2,1)S(1)}, u32[]{:S(2)}, u32[]{:S(2)}) async-start(bf16[8,64,256]{2,1,0:T(8,128)(2,1)} %shard_map.110.refs_5_), calls=%async_computation | async-start | bytes 524288 | tf_op jit(solution)/shard_map/all_to_all | solution.py:667
  10.5 1.9 %copy-start.3 = (s32[8,8]{1,0:T(8,128)S(1)}, s32[8,8]{1,0:T(8,128)}, u32[]{:S(2)}) copy-start(s32[8,8]{1,0:T(8,128)} %refs_10_.1) | copy-start | bytes 772
  10.5 1.9 %copy-start.4 = (s32[8,8]{1,0:T(8,128)S(1)}, s32[8,8]{1,0:T(8,128)}, u32[]{:S(2)}) copy-start(s32[8,8]{1,0:T(8,128)} %refs_11_.1) | copy-start | bytes 772
  10.5 5.0 %collective-permute-start.1 = (bf16[64,1024]{1,0:T(8,128)(2,1)S(1)}, bf16[64,1024]{1,0:T(8,128)(2,1)S(1)}, u32[]{:S(2)}, u32[]{:S(2)}) collective-permute-start(bf16[64,1024]{1,0:T(8,128)(2,1)S(1)} %bitcast.6), channel_id=1, source_target_pairs={{0,2},{1,3},{2,0},{3,1},{4,6},{5,7},{6,4},{7,5},{8,10},{9,11},{10,... | collective-permute-start | bytes 393224 | tf_op jit(solution)/shard_map/ppermute | solution.py:647
  12.1 13.6 %collective-permute-start = (bf16[64,1024]{1,0:T(8,128)(2,1)S(1)}, bf16[64,1024]{1,0:T(8,128)(2,1)S(1)}, u32[]{:S(2)}, u32[]{:S(2)}) collective-permute-start(bf16[64,1024]{1,0:T(8,128)(2,1)S(1)} %bitcast.7), channel_id=1, source_target_pairs={{0,1},{1,0},{2,3},{3,2},{4,5},{5,4},{6,7},{7,6},{8,9},{9,8},{10,11... | collective-permute-start | bytes 393224 | tf_op jit(solution)/shard_map/ppermute | solution.py:647
  15.6 10.2 %collective-permute-start.2 = (bf16[64,1024]{1,0:T(8,128)(2,1)S(1)}, bf16[64,1024]{1,0:T(8,128)(2,1)S(1)}, u32[]{:S(2)}, u32[]{:S(2)}) collective-permute-start(bf16[64,1024]{1,0:T(8,128)(2,1)S(1)} %collective-permute-done.1.refs_4_), channel_id=1, source_target_pairs={{0,1},{1,0},{2,3},{3,2},{4,5},{5,4},{6,7},{7,6},{8,9},{9,8},{10,11... | collective-permute-start | bytes 393224 | tf_op jit(solution)/shard_map/ppermute | solution.py:647
  18.4 7.4 %copy-start.1 = (bf16[1024,256]{1,0:T(8,128)(2,1)S(1)}, bf16[1024,256]{1,0:T(8,128)(2,1)}, u32[]{:S(2)}) copy-start(bf16[1024,256]{1,0:T(8,128)(2,1)} %refs_2_.5) | copy-start | bytes 1572868
  27.5 5.3 %copy-start.5 = (bf16[256,1024]{1,0:T(8,128)(2,1)}, bf16[256,1024]{1,0:T(8,128)(2,1)S(1)}, u32[]{:S(2)}) copy-start(bf16[256,1024]{1,0:T(8,128)(2,1)S(1)} %get-tuple-element.57.refs_5_) | copy-start | bytes 1572868
  27.5 12.6 %all-to-all-start.1 = ((bf16[8,128,128]{2,1,0:T(8,128)(2,1)}), bf16[8,128,128]{2,1,0:T(8,128)(2,1)S(1)}, u32[]{:S(2)}, u32[]{:S(2)}) async-start(bf16[8,128,128]{2,1,0:T(8,128)(2,1)} %bitcast.9), calls=%async_computation.1 | async-start | bytes 524288 | tf_op jit(solution)/shard_map/all_to_all | solution.py:667
  39.2 7.2 %collective-permute-start.3 = (bf16[4,64,256]{2,1,0:T(8,128)(2,1)S(1)}, bf16[4,64,256]{2,1,0:T(8,128)(2,1)S(1)}, u32[]{:S(2)}, u32[]{:S(2)}) collective-permute-start(bf16[4,64,256]{2,1,0:T(8,128)(2,1)S(1)} %get-tuple-element.62), channel_id=1, source_target_pairs={{0,8},{4,12},{8,0},{12,4},{16,24},{20,28},{24,16},{28,20},{1,9},{5... | collective-permute-start | bytes 393224 | tf_op jit(solution)/shard_map/ppermute | solution.py:678
  41.0 11.7 %all-to-all-start.2 = ((bf16[8,144,128]{2,1,0:T(8,128)(2,1)}), bf16[8,144,128]{2,1,0:T(8,128)(2,1)S(1)}, u32[]{:S(2)}, u32[]{:S(2)}) async-start(bf16[8,144,128]{2,1,0:T(8,128)(2,1)} %shard_map.116.refs_4_), calls=%async_computation.2 | async-start | bytes 589824 | tf_op jit(solution)/shard_map/all_to_all | solution.py:667
  46.4 5.4 %collective-permute-start.4 = (bf16[2,64,256]{2,1,0:T(8,128)(2,1)S(1)}, bf16[2,64,256]{2,1,0:T(8,128)(2,1)S(1)}, u32[]{:S(2)}, u32[]{:S(2)}) collective-permute-start(bf16[2,64,256]{2,1,0:T(8,128)(2,1)S(1)} %get-tuple-element.64), channel_id=1, source_target_pairs={{0,4},{4,0},{8,12},{12,8},{16,20},{20,16},{24,28},{28,24},{1,5},{5... | collective-permute-start | bytes 196616 | tf_op jit(solution)/shard_map/ppermute | solution.py:678
  52.8 6.5 %collective-permute-start.6 = (bf16[1040,128]{1,0:T(8,128)(2,1)S(1)}, bf16[1040,128]{1,0:T(8,128)(2,1)S(1)}, u32[]{:S(2)}, u32[]{:S(2)}) collective-permute-start(bf16[1040,128]{1,0:T(8,128)(2,1)S(1)} %shard_map.117.refs_0_), channel_id=1, source_target_pairs={{0,2},{1,3},{2,0},{3,1},{4,6},{5,7},{6,4},{7,5},{8,10},{9,11},{10,... | collective-permute-start | bytes 798728 | tf_op jit(solution)/shard_map/ppermute | solution.py:647
  53.7 4.8 %collective-permute-start.7 = (bf16[1,64,256]{2,1,0:T(8,128)(2,1)S(1)}, bf16[1,64,256]{2,1,0:T(8,128)(2,1)S(1)}, u32[]{:S(2)}, u32[]{:S(2)}) collective-permute-start(bf16[1,64,256]{2,1,0:T(8,128)(2,1)S(1)} %get-tuple-element.71), channel_id=1, source_target_pairs={{0,16},{4,20},{8,24},{12,28},{16,0},{20,4},{24,8},{28,12},{1,17},{... | collective-permute-start | bytes 98312 | tf_op jit(solution)/shard_map/ppermute | solution.py:678
  55.9 3.4 %collective-permute-start.5 = (bf16[1040,128]{1,0:T(8,128)(2,1)S(1)}, bf16[1040,128]{1,0:T(8,128)(2,1)S(1)}, u32[]{:S(2)}, u32[]{:S(2)}) collective-permute-start(bf16[1040,128]{1,0:T(8,128)(2,1)S(1)} %shard_map.117.refs_0_), channel_id=1, source_target_pairs={{0,1},{1,0},{2,3},{3,2},{4,5},{5,4},{6,7},{7,6},{8,9},{9,8},{10,11... | collective-permute-start | bytes 798728 | tf_op jit(solution)/shard_map/ppermute | solution.py:647
  59.3 1.5 %collective-permute-start.8 = (bf16[1040,128]{1,0:T(8,128)(2,1)S(1)}, bf16[1040,128]{1,0:T(8,128)(2,1)S(1)}, u32[]{:S(2)}, u32[]{:S(2)}) collective-permute-start(bf16[1040,128]{1,0:T(8,128)(2,1)S(1)} %collective-permute-done.6.refs_2_), channel_id=1, source_target_pairs={{0,1},{1,0},{2,3},{3,2},{4,5},{5,4},{6,7},{7,6},{8,9},{9,8},{10,11... | collective-permute-start | bytes 798728 | tf_op jit(solution)/shard_map/ppermute | solution.py:647
